TPU v7x, 128 devices: a whole 4x4x4 slice. The times are simulated.
128 devices in a mesh: dp: 8 (over x, core), rows: 4 (over y), chan: 4 (over z).
Axes of the slice: x: 4, y: 4, z: 4, core: 2. Of those that a mesh axis runs over, the one named last changes fastest.
Arguments:
- features: bfloat16 [256, 24, 24, 1024], P(('dp', 'chan'), 'rows'), may hold values from -6 to 6
- counts: int32 [64], P(('dp', 'rows')), may hold values from 0 to 4, as said below
- pre_reduce: bfloat16 [1024, 1024], replicated, may hold values from -0.1875 to 0.1875
- pre_conv: bfloat16 [3, 3, 1024], replicated, may hold values from -2 to 2
- pre_expand: bfloat16 [1024, 1024], replicated, may hold values from -0.1875 to 0.1875
- pre_gain: float32 [1024], replicated, may hold values from 0.5 to 1.5
- post_reduce: bfloat16 [1024, 1024], P('chan'), may hold values from -0.1875 to 0.1875
- post_conv: bfloat16 [3, 3, 1024], replicated, may hold values from -2 to 2
- post_expand: bfloat16 [1024, 1024], P(None, 'chan'), may hold values from -0.1875 to 0.1875
- post_gain: float32 [1024], P('chan'), may hold values from 0.5 to 1.5
- readout: bfloat16 [1024, 4096], replicated, may hold values from -0.1875 to 0.1875
- cotangent: bfloat16 [256, 12, 12, 4096], P(('dp', 'rows'), None, None, 'chan'), may hold values from -6 to 6
Outputs:
- tokens: bfloat16 [256, 12, 12, 4096], P(('dp', 'rows'), None, None, 'chan')
- feature_grad: float32 [256, 24, 24, 1024], P(('dp', 'chan'), 'rows')
- pre_reduce_grad: float32 [1024, 1024], replicated
- pre_conv_grad: float32 [3, 3, 1024], replicated
- pre_expand_grad: float32 [1024, 1024], replicated
- pre_gain_grad: float32 [1024], replicated
- post_reduce_grad: float32 [1024, 1024], P('chan')
- post_conv_grad: float32 [3, 3, 1024], replicated
- post_expand_grad: float32 [1024, 1024], P(None, 'chan')
- post_gain_grad: float32 [1024], P('chan')
- readout_grad: float32 [1024, 4096], P('chan')
Inputs may be any that keep to these rules, and one draw needn't show every extreme that they name: Sample k owns slots 4 k to 4 k + 3 and uses the first counts[k] of them; some sample has 4 images and some has none.
All inputs are finite; a program needn't handle non-finite values.
Results may differ from a plain program's by a relative error of at most 0.02.
Values may be sent and summed in bfloat16 or wider, within the bound.
No kernel may reach another device: no remote copies, remote signals or barrier semaphores. Data moves between devices by JAX's collectives and lax.ppermute only.
A program may use at most 256 MiB of HBM per device.

v0:
```python
import jax
import jax.numpy as jnp
from jax import lax
from jax.sharding import PartitionSpec as P

SLOT = 4


EPS = 1e-06


def extended(cells, sides, width):
    for axis, dim in sides:
        count = lax.axis_size(axis)
        ends = count - 1
        head = lax.slice_in_dim(cells, 0, width, axis=dim)
        tail = lax.slice_in_dim(cells, cells.shape[dim] - width, cells.shape[dim], axis=dim)
        cells = jnp.concatenate(
            [
                lax.ppermute(tail, axis, [(i, (i + 1) % count) for i in range(ends)]),
                cells,
                lax.ppermute(head, axis, [((i + 1) % count, i) for i in range(ends)]),
            ],
            axis=dim,
        )
    return cells


def silu_slope(values):
    sigma = jax.nn.sigmoid(values)
    return sigma * (1.0 + values * (1.0 - sigma))


def conv_valid(padded, kernel):
    width = kernel.shape[2]
    return lax.conv_general_dilated(
        padded,
        kernel.reshape(3, 3, 1, width),
        (1, 1),
        "VALID",
        dimension_numbers=("NHWC", "HWIO", "NHWC"),
        feature_group_count=width,
        preferred_element_type=jnp.float32,
    )


def flipped(kernel):
    return kernel[::-1, ::-1]


def pad_columns(values):
    return jnp.pad(values, ((0, 0), (0, 0), (1, 1), (0, 0)))


def pad_sides(values):
    return jnp.pad(values, ((0, 0), (1, 1), (1, 1), (0, 0)))


def kernel_grad(padded, grads):
    height = grads.shape[1]
    breadth = grads.shape[2]
    kernel_rows = []
    for shift_row in range(3):
        row_terms = []
        for shift_col in range(3):
            window = padded[:, shift_row : shift_row + height, shift_col : shift_col + breadth, :]
            row_terms.append(
                jnp.einsum("abci,abci->i", window, grads, preferred_element_type=jnp.float32)
            )
        kernel_rows.append(jnp.stack(row_terms))
    return jnp.stack(kernel_rows)


def body(
    features,
    counts,
    pre_reduce,
    pre_conv,
    pre_expand,
    pre_gain,
    post_reduce,
    post_conv,
    post_expand,
    post_gain,
    readout,
    cotangent,
):
    channels = pre_reduce.shape[0]
    slots_here = features.shape[0]
    grid_rows = features.shape[1]
    grid_cols = features.shape[2]
    reduced = jnp.einsum("abcd,de->abce", features, pre_reduce, preferred_element_type=jnp.float32)
    reduced_act = jax.nn.silu(reduced).astype(jnp.bfloat16)
    rimmed = pad_columns(extended(reduced_act, (("rows", 1),), 1))
    convolved = conv_valid(rimmed, pre_conv)
    convolved_act = jax.nn.silu(convolved).astype(jnp.bfloat16)
    expanded = jnp.einsum(
        "abce,ed->abcd", convolved_act, pre_expand, preferred_element_type=jnp.float32
    )
    mean_value = jnp.mean(expanded, -1, keepdims=True)
    mean_square = jnp.mean(expanded * expanded, -1, keepdims=True)
    pre_std = lax.rsqrt(mean_square - mean_value * mean_value + EPS)
    normal_pre = (expanded - mean_value) * pre_std
    normed = normal_pre * pre_gain
    blended = features.astype(jnp.float32) + jax.nn.silu(normed)
    pooled = jnp.mean(
        blended.reshape(slots_here, grid_rows // 2, 2, grid_cols // 2, 2, channels), axis=(2, 4)
    ).astype(jnp.bfloat16)
    moved = lax.all_to_all(
        lax.all_to_all(pooled, "chan", split_axis=3, concat_axis=0, tiled=True),
        "rows",
        split_axis=0,
        concat_axis=1,
        tiled=True,
    )
    chan_index = lax.axis_index("chan")
    share = moved.shape[3]
    post_partial = jnp.einsum(
        "abcd,de->abce", moved, post_reduce, preferred_element_type=jnp.float32
    )
    post_reduced = lax.psum(post_partial, "chan")
    post_reduced_act = jax.nn.silu(post_reduced).astype(jnp.bfloat16)
    post_padded = pad_sides(post_reduced_act)
    post_convolved = conv_valid(post_padded, post_conv)
    post_convolved_act = jax.nn.silu(post_convolved).astype(jnp.bfloat16)
    post_expanded = jnp.einsum(
        "abce,ed->abcd", post_convolved_act, post_expand, preferred_element_type=jnp.float32
    )
    stat_sums = lax.psum(
        (
            jnp.sum(post_expanded, -1, keepdims=True),
            jnp.sum(post_expanded * post_expanded, -1, keepdims=True),
        ),
        "chan",
    )
    post_mean = stat_sums[0] / channels
    post_square = stat_sums[1] / channels
    post_std = lax.rsqrt(post_square - post_mean * post_mean + EPS)
    post_normal = (post_expanded - post_mean) * post_std
    post_normed = post_normal * post_gain
    refined = moved.astype(jnp.float32) + jax.nn.silu(post_normed)
    refined_low = refined.astype(jnp.bfloat16)
    readout_rows = lax.dynamic_slice_in_dim(readout, chan_index * share, share, 0)
    partial_logits = jnp.einsum(
        "abcd,de->abce", refined_low, readout_rows, preferred_element_type=jnp.float32
    )
    logits = lax.psum_scatter(partial_logits, "chan", scatter_dimension=3, tiled=True)
    token_values, gelu_pull = jax.vjp(jax.nn.gelu, logits)
    tokens = token_values.astype(jnp.bfloat16)
    samples_here = counts.shape[0]
    live = (
        (jnp.arange(SLOT)[None, :] < counts[:, None])
        .astype(jnp.float32)
        .reshape(samples_here * SLOT)
    )
    masked = cotangent.astype(jnp.float32) * live[:, None, None, None]
    logit_grad = gelu_pull(masked)[0].astype(jnp.bfloat16)
    piece = lax.all_gather(logit_grad, "chan", axis=3, tiled=True)
    start = jnp.int32(0)
    input_grad = jnp.zeros(refined.shape, jnp.float32)
    weight_grad = jnp.zeros((share, readout.shape[1]), jnp.float32)
    rows_part = lax.dynamic_slice_in_dim(readout_rows, start, piece.shape[3], 1)
    input_grad = input_grad + jnp.einsum(
        "abce,de->abcd", piece, rows_part, preferred_element_type=jnp.float32
    )
    block = jnp.einsum("abcd,abce->de", refined_low, piece, preferred_element_type=jnp.float32)
    weight_grad = lax.dynamic_update_slice_in_dim(weight_grad, block, start, 1)
    post_normed_grad = input_grad * silu_slope(post_normed)
    post_gain_grad = jnp.sum(post_normed_grad * post_normal, axis=(0, 1, 2))
    post_scaled = post_normed_grad * post_gain
    back_sums = lax.psum(
        (
            jnp.sum(post_scaled, -1, keepdims=True),
            jnp.sum(post_scaled * post_normal, -1, keepdims=True),
        ),
        "chan",
    )
    post_expanded_grad = (
        post_std * (post_scaled - back_sums[0] / channels - post_normal * (back_sums[1] / channels))
    ).astype(jnp.bfloat16)
    post_expand_grad = jnp.einsum(
        "abce,abcd->ed", post_convolved_act, post_expanded_grad, preferred_element_type=jnp.float32
    )
    post_act_partial = jnp.einsum(
        "abcd,ed->abce", post_expanded_grad, post_expand, preferred_element_type=jnp.float32
    )
    post_act_grad = lax.psum(post_act_partial, "chan")
    post_convolved_grad = (post_act_grad * silu_slope(post_convolved)).astype(jnp.bfloat16)
    post_conv_grad = kernel_grad(post_padded, post_convolved_grad)
    post_reduced_act_grad = conv_valid(pad_sides(post_convolved_grad), flipped(post_conv))
    post_reduced_grad = (post_reduced_act_grad * silu_slope(post_reduced)).astype(jnp.bfloat16)
    post_reduce_grad = jnp.einsum(
        "abcd,abce->de", moved, post_reduced_grad, preferred_element_type=jnp.float32
    )
    pooled_grad = (
        input_grad
        + jnp.einsum(
            "abce,de->abcd", post_reduced_grad, post_reduce, preferred_element_type=jnp.float32
        )
    ).astype(jnp.bfloat16)
    returned = lax.all_to_all(
        lax.all_to_all(pooled_grad, "rows", split_axis=1, concat_axis=0, tiled=True),
        "chan",
        split_axis=0,
        concat_axis=3,
        tiled=True,
    )
    blended_grad = jnp.repeat(jnp.repeat(returned.astype(jnp.float32) * 0.25, 2, axis=1), 2, axis=2)
    normed_grad = blended_grad * silu_slope(normed)
    pre_gain_grad = jnp.sum(normed_grad * normal_pre, axis=(0, 1, 2))
    pre_scaled = normed_grad * pre_gain
    expanded_grad = (
        pre_std
        * (
            pre_scaled
            - jnp.mean(pre_scaled, -1, keepdims=True)
            - normal_pre * jnp.mean(pre_scaled * normal_pre, -1, keepdims=True)
        )
    ).astype(jnp.bfloat16)
    pre_expand_grad = jnp.einsum(
        "abce,abcd->ed", convolved_act, expanded_grad, preferred_element_type=jnp.float32
    )
    convolved_act_grad = jnp.einsum(
        "abcd,ed->abce", expanded_grad, pre_expand, preferred_element_type=jnp.float32
    )
    convolved_grad = (convolved_act_grad * silu_slope(convolved)).astype(jnp.bfloat16)
    grad_padded = pad_columns(extended(convolved_grad, (("rows", 1),), 1))
    reduced_act_grad = conv_valid(grad_padded, flipped(pre_conv))
    pre_conv_grad = kernel_grad(rimmed, convolved_grad)
    reduced_grad = (reduced_act_grad * silu_slope(reduced)).astype(jnp.bfloat16)
    pre_reduce_grad = jnp.einsum(
        "abcd,abce->de", features, reduced_grad, preferred_element_type=jnp.float32
    )
    feature_grad = blended_grad + jnp.einsum(
        "abce,de->abcd", reduced_grad, pre_reduce, preferred_element_type=jnp.float32
    )
    pre_sums = lax.psum(
        (pre_reduce_grad, pre_conv_grad, pre_expand_grad, pre_gain_grad), ("dp", "rows", "chan")
    )
    post_sums = (
        lax.psum(post_reduce_grad.astype(jnp.bfloat16), ("dp", "rows")).astype(jnp.float32),
        lax.psum(post_conv_grad.astype(jnp.bfloat16), ("dp", "rows")).astype(jnp.float32),
        lax.psum(post_expand_grad.astype(jnp.bfloat16), ("dp", "rows")).astype(jnp.float32),
        lax.psum(post_gain_grad.astype(jnp.bfloat16), ("dp", "rows")).astype(jnp.float32),
        lax.psum(weight_grad.astype(jnp.bfloat16), ("dp", "rows")).astype(jnp.float32),
    )
    return (
        tokens,
        feature_grad,
        pre_sums[0],
        pre_sums[1],
        pre_sums[2],
        pre_sums[3],
        post_sums[0],
        post_sums[1],
        post_sums[2],
        post_sums[3],
        post_sums[4],
    )


def solution(mesh):
    placed = (
        P(("dp", "chan"), "rows", None, None),
        P(("dp", "rows")),
        P(),
        P(),
        P(),
        P(),
        P("chan", None),
        P(),
        P(None, "chan"),
        P("chan"),
        P(),
        P(("dp", "rows"), None, None, "chan"),
    )
    return jax.shard_map(
        body,
        mesh=mesh,
        in_specs=placed,
        out_specs=(
            P(("dp", "rows"), None, None, "chan"),
            P(("dp", "chan"), "rows", None, None),
            P(),
            P(),
            P(),
            P(),
            P("chan", None),
            P(),
            P(None, "chan"),
            P("chan"),
            P("chan", None),
        ),
        check_vma=False,
    )
```

profile of v0, /device:TPU:1, one launch (start us, length us, event | category | flops | bytes accessed | tf_op | source)
XLA Modules:
  0.0 3586.5 jit_solution(16987336699622685033)
XLA Ops:
  7.2 1.5 copy-done
  8.8 6.5 multiply_convert_fusion.5
  15.3 4.1 collective-permute-start
  20.7 6.4 collective-permute-done
  27.1 3.8 collective-permute-done.1
  31.7 584.4 %fusion.38 = f32[8,6,24,1024]{3,0,2,1:T(8,128)S(1)} fusion(bf16[8,8,24,1024]{3,2,1,0:T(8,128)(2,1)S(1)} %pad_maximum_fusion, bf16[3,3,1,1024]{3,1,0,2:T(4,128)(2,1)S(1)} %bitcast.265), kind=kOutput, calls=%fused_computation.89 | convolution fusion | flops 20643840 | bytes 7882752 | tf_op jit(solution)/shard_map/conv_general_dilated | solution.py:36
  616.1 5.2 fusion.84
  621.4 2.2 copy-done.1
  623.5 3.2 multiply_add_fusion
  626.7 6.8 reshape.96
  633.6 7.3 reduce_sum.101
  640.9 2.1 fusion.70
  643.0 6.7 copy.159
  649.6 13.8 reshape.167
  663.4 12.9 all_to_all.63
  676.3 15.6 reshape.168
  691.9 7.1 copy.303
  699.4 12.4 all_to_all.64
  711.9 3.6 fusion.72
  715.6 128.6 %all-reduce.13.cloned.1.call-done = f32[8,12,12,1024]{3,2,1,0:T(8,128)} async-done(((f32[8,12,12,1024]{3,2,1,0:T(8,128)}), f32[8,12,12,1024]{3,2,1,0:T(8,128)}) %all-reduce.13.cloned.1.call-update) | async-done | bytes 4718608 | tf_op jit(solution)/shard_map/psum | solution.py:121
  844.2 4.4 multiply_convert_fusion.1
  848.6 622.6 %fusion.50 = f32[8,12,12,1024]{3,0,2,1:T(8,128)S(1)} fusion(bf16[8,12,12,1024]{3,2,1,0:T(8,128)(2,1)S(1)} %multiply_convert_fusion.1, bf16[3,3,1,1024]{3,1,0,2:T(4,128)(2,1)S(1)} %bitcast.264), kind=kOutput, calls=%fused_computation.103 | convolution fusion | flops 18939904 | bytes 7096320 | tf_op jit(solution)/shard_map/conv_general_dilated | solution.py:36
  1471.3 5.7 fusion
  1477.0 2.9 fusion.85
  1479.9 13.4 all-reduce.5
  1493.3 2.0 add_convert_fusion.1
  1496.3 11.6 fusion.61
  1508.7 218.3 %reduce-scatter.2.cloned.1.call-done = f32[8,12,12,1024]{3,2,1,0:T(8,128)} async-done(((f32[8,12,12,4096]{3,2,1,0:T(8,128)}), f32[8,12,12,1024]{3,2,1,0:T(8,128)}) %reduce-scatter.2.cloned.1.call-update) | async-done | bytes 4718608 | tf_op jit(solution)/shard_map/reduce_scatter | solution.py:147
  1727.0 9.4 fusion.14
  1736.5 118.3 %all-gather.2.cloned.1.call-done = bf16[8,12,12,4096]{3,2,1,0:T(8,128)(2,1)} async-done(((bf16[8,12,12,1024]{3,2,1,0:T(8,128)(2,1)}), bf16[8,12,12,4096]{3,2,1,0:T(8,128)(2,1)}) %all-gather.2.cloned.1.call-update) | async-done | bytes 9437200 | tf_op jit(solution)/shard_map/all_gather | solution.py:158
  1854.7 12.1 multiply_reduce_fusion.4
  1866.8 13.8 all-reduce.4
  1880.7 2.4 multiply_convert_fusion.6
  1884.0 3.6 fusion.74
  1888.7 2.5 rev.7
  1891.1 3.9 fusion.69
  1895.0 123.4 %all-reduce.15.cloned.1.call-done = f32[8,12,12,1024]{3,2,1,0:T(8,128)} async-done(((f32[8,12,12,1024]{3,2,1,0:T(8,128)}), f32[8,12,12,1024]{3,2,1,0:T(8,128)}) %all-reduce.15.cloned.1.call-update) | async-done | bytes 4718608 | tf_op jit(solution)/shard_map/psum | solution.py:187
  2018.5 20.3 fusion.15
  2038.8 622.2 %fusion.48 = f32[8,12,12,1024]{3,0,2,1:T(8,128)S(1)} fusion(bf16[8,12,12,1024]{3,2,1,0:T(8,128)(2,1)S(1)} %get-tuple-element.121, bf16[3,3,1,1024]{3,1,0,2:T(4,128)(2,1)S(1)} %bitcast.267), kind=kOutput, calls=%fused_computation.101 | convolution fusion | flops 18939904 | bytes 7096320 | tf_op jit(solution)/shard_map/conv_general_dilated | solution.py:36
  2661.0 7.3 fusion.24
  2671.1 4.2 all-to-all-start.2
  2675.3 9.7 fusion.25
  2686.2 4.2 all-to-all-start.3
  2690.5 3.7 fusion.68
  2694.3 7.1 all-to-all-done.3
  2703.4 2.1 broadcast_in_dim.32
  2705.5 6.1 broadcast_in_dim.33
  2711.6 7.0 reshape.100
  2718.6 6.3 multiply_reduce_fusion
  2725.0 2.4 multiply_convert_fusion.3
  2727.4 16.9 fusion.26
  2744.4 3.6 collective-permute-start.2
  2747.9 1.5 collective-permute-start.3
  2749.5 11.4 convolution_bitcast_fusion.1
  2761.7 584.0 %fusion.36 = f32[8,6,24,1024]{3,0,2,1:T(8,128)S(1)} fusion(bf16[8,8,24,1024]{3,2,1,0:T(8,128)(2,1)S(1)} %pad_maximum_fusion.1, bf16[3,3,1,1024]{3,1,0,2:T(4,128)(2,1)S(1)} %bitcast.266), kind=kOutput, calls=%fused_computation.87 | convolution fusion | flops 20643840 | bytes 7882752 | tf_op jit(solution)/shard_map/conv_general_dilated | solution.py:36
  3345.7 5.4 fusion.35
  3352.6 4.4 convolution_bitcast_fusion.2
  3357.1 4.9 copy.183
  3362.3 125.1 %all-reduce.6 = (bf16[3,3,1024]{2,1,0:T(4,128)(2,1)S(1)}, bf16[256]{0:T(256)(128)(2,1)S(1)}) all-reduce(bf16[3,3,1024]{2,1,0:T(4,128)(2,1)S(1)} %pad_maximum_fusion.5, bf16[256]{0:T(256)(128)(2,1)S(1)} %copy-done.39), channel_id=1, replica_groups=mesh['dp'=8,'rows'=4,'chan'=4] {'dp','rows'}, use_global_device_ids=true, to_apply=%region_22.23 | all-reduce | flops 9472 | bytes 37888 | tf_op jit(solution)/shard_map/psum | solution.py:242
  3488.6 67.7 %all-reduce.2 = (f32[3,3,1024]{2,1,0:T(4,128)}, f32[1024]{0:T(1024)}) all-reduce(f32[3,3,1024]{2,1,0:T(4,128)S(1)} %pad_maximum_fusion.4, f32[1024]{0:T(1024)S(1)} %get-tuple-element.77), channel_id=1, replica_groups=mesh['dp'=8,'rows'=4,'chan'=4] {'dp','rows','chan'}, use_global_device_ids=true, to_apply=%region_17.18 | all-reduce | flops 10240 | bytes 81920 | tf_op jit(solution)/shard_map/psum | solution.py:237
  3556.3 6.7 fusion.63
  3563.0 4.2 convert_element_type.133
  3569.3 5.3 copy.184
  3574.6 4.8 copy.390
  (160 shorter events, 18.3 us)
Async XLA Ops:
  7.2 1.6 copy-start
  7.2 837.0 %all-reduce.13.cloned.1.call-start = ((), (), s32[]{:S(2)}) async-start(), calls=%async_computation.5 | async-start | bytes 12582912 | tf_op jit(solution)/shard_map/psum | solution.py:121
  15.3 16.1 copy-start.5
  15.3 16.4 copy-start.28
  15.3 11.8 collective-permute-start
  19.4 11.6 collective-permute-start.1
  27.1 4.2 copy-start.21
  31.0 0.7 copy-start.23
  31.3 584.8 %copy-start.9 = (bf16[8,8,24,1024]{3,2,1,0:T(8,128)(2,1)}, bf16[8,8,24,1024]{3,2,1,0:T(8,128)(2,1)S(1)}, u32[]{:S(2)}) copy-start(bf16[8,8,24,1024]{3,2,1,0:T(8,128)(2,1)S(1)} %pad_maximum_fusion) | copy-start | bytes 9437188
  31.7 584.4 %copy-start.40 = (bf16[1024,1024]{1,0:T(8,128)(2,1)S(1)}, bf16[1024,1024]{1,0:T(8,128)(2,1)}, u32[]{:S(2)}) copy-start(bf16[1024,1024]{1,0:T(8,128)(2,1)} %param.16) | copy-start | bytes 6291460
  616.1 5.2 copy-start.43
  616.1 7.4 copy-start.11
  616.1 7.4 copy-start.25
  621.3 2.2 copy-start.1
  691.9 19.9 copy-start.15
  715.5 1011.5 %reduce-scatter.2.cloned.1.call-start = ((), (), s32[]{:S(2)}) async-start(), calls=%async_computation.6 | async-start | bytes 31457280 | tf_op jit(solution)/shard_map/reduce_scatter | solution.py:147
  715.6 133.0 %copy-start.26 = (bf16[3,3,1024]{2,1,0:T(4,128)(2,1)S(1)}, bf16[3,3,1024]{2,1,0:T(4,128)(2,1)}, u32[]{:S(2)}) copy-start(bf16[3,3,1024]{2,1,0:T(4,128)(2,1)} %param.19) | copy-start | bytes 55300
  848.6 622.7 %copy-start.4 = (bf16[8,12,12,1024]{3,2,1,0:T(8,128)(2,1)}, bf16[8,12,12,1024]{3,2,1,0:T(8,128)(2,1)S(1)}, u32[]{:S(2)}) copy-start(bf16[8,12,12,1024]{3,2,1,0:T(8,128)(2,1)S(1)} %multiply_convert_fusion.1) | copy-start | bytes 7077892
  1471.3 8.6 copy-start.3
  1471.3 5.7 copy-start.19
  1477.0 2.9 copy-start.10
  1477.0 16.3 copy-start.38
  1495.4 0.9 copy-start.7
  1507.9 0.7 copy-start.41
  1507.9 346.8 %all-gather.2.cloned.1.call-start = ((), (), s32[]{:S(2)}) async-start(), calls=%async_computation.7 | async-start | bytes 15728640 | tf_op jit(solution)/shard_map/all_gather | solution.py:158
  1736.4 282.0 %all-reduce.15.cloned.1.call-start = ((), (), s32[]{:S(2)}) async-start(), calls=%async_computation.8 | async-start | bytes 12582912 | tf_op jit(solution)/shard_map/psum | solution.py:187
  1880.7 3.4 copy-start.20
  1883.2 0.9 copy-start.8
  1887.7 0.7 copy-start.27
  1887.7 1.0 copy-start.29
  2018.5 642.5 %slice-start.2 = ((s8[6291456]{0:T(1024)(128)(4,1)}), s8[2097152]{0:T(1024)(128)(4,1)S(1)}, s32[]{:S(2)}) async-start(s8[6291456]{0:T(1024)(128)(4,1)} %bitcast.244), calls=%async_computation.13 | async-start | bytes 4194304
  2038.7 622.3 %slice-start.3 = ((s8[6291456]{0:T(1024)(128)(4,1)}), s8[4194304]{0:T(1024)(128)(4,1)S(1)}, s32[]{:S(2)}) async-start(s8[6291456]{0:T(1024)(128)(4,1)} %bitcast.244), calls=%async_computation.14 | async-start | bytes 8388608
  2661.0 7.3 copy-start.16
  2661.0 7.3 copy-start.42
  2668.3 1.7 copy-start.2
  2671.1 13.8 all-to-all-start.2
  2686.2 15.1 all-to-all-start.3
  2690.4 872.5 %all-reduce.19.cloned.1.call-start = ((), (), s32[]{:S(2)}) async-start(), calls=%async_computation.10 | async-start | bytes 6291456 | tf_op jit(solution)/shard_map/psum | solution.py:241
  2694.2 875.1 %all-reduce.17.cloned.1.call-start = ((), (), s32[]{:S(2)}) async-start(), calls=%async_computation.9 | async-start | bytes 16777216 | tf_op jit(solution)/shard_map/psum | solution.py:237
  2711.6 13.4 slice-start
  2718.6 6.4 slice-start.1
  2725.0 2.4 copy-start.6
  2725.0 2.4 copy-start.22
  2725.0 2.4 copy-start.24
  2727.4 22.0 copy-start.14
  2744.4 16.5 collective-permute-start.2
  2747.9 13.0 collective-permute-start.3
  2760.9 0.7 copy-start.30
  2760.9 584.8 %slice-start.4 = ((s8[4718592]{0:T(1024)(128)(4,1)}), s8[524288]{0:T(1024)(128)(4,1)S(1)}, s32[]{:S(2)}) async-start(s8[4718592]{0:T(1024)(128)(4,1)} %bitcast.253), calls=%async_computation.15 | async-start | bytes 1048576
  2761.7 584.0 %slice-start.5 = ((s8[4718592]{0:T(1024)(128)(4,1)}), s8[4194304]{0:T(1024)(128)(4,1)S(1)}, s32[]{:S(2)}) async-start(s8[4718592]{0:T(1024)(128)(4,1)} %bitcast.253), calls=%async_computation.16 | async-start | bytes 8388608
  3345.7 6.8 copy-start.12
  3351.1 1.4 copy-start.13
  3357.0 5.0 copy-start.37
  3357.0 5.0 copy-start.36
  3357.0 5.0 copy-start.35
  3357.1 5.0 copy-start.34
  3357.1 5.0 copy-start.33
  3357.1 5.0 copy-start.32
  3357.1 5.0 copy-start.31
  3357.1 5.2 copy-start.39
  3563.0 4.2 copy-start.18
  3563.0 5.3 copy-start.17
Sparse Core Ops, SparseCore 0:
  715.7 128.4 all-reduce.12
  1508.1 218.9 reduce-scatter.1
  1736.5 118.1 all-gather.1
  1887.8 130.6 all-reduce.14
  2695.6 112.1 all-reduce.18
  3357.1 164.1 all-reduce.16
where the time goes:
time: 3590 us
  matrix products  2520 us (70%)
  waiting for transfers between devices  606 us (17%)
  blocking collectives  245 us (7%)
  local copies, waits for them, and re-layouts  96.3 us (3%)
  other arithmetic  88.2 us (2%)
    conv_general_dilated x4, matrix products, conv_valid(): lax.conv_general_dilated(padded, kernel.reshape(3, 3, 1, width), (1, 1),...  2410 us
    reduce_scatter x1, waiting for transfers between devices, body(): lax.psum_scatter(partial_logits, 'chan', scatter_dimension=3, tiled=True)  218 us
    psum x1, waiting for transfers between devices, body(): post_reduced = lax.psum(post_partial, 'chan')  129 us
    psum x1, blocking collectives, body(): lax.psum(post_conv_grad.astype(jnp.bfloat16), ('dp', 'rows'))  125 us
    psum x1, waiting for transfers between devices, body(): post_act_grad = lax.psum(post_act_partial, 'chan')  123 us
    all_gather x1, waiting for transfers between devices, body(): piece = lax.all_gather(logit_grad, 'chan', axis=3, tiled=True)  118 us
  transfers between devices with their start and end apart: 12, of which 7 were waited for; matrix products, arithmetic and copies ran while one was open for 19% of the time, Pallas kernels for 0%

commit v1 on v0

v1 whole, which is shorter than its diff:
```python
import jax
import jax.numpy as jnp
from jax import lax
from jax.sharding import Mesh, PartitionSpec as P

SLOT = 4
EPS = 1e-06
BF = jnp.bfloat16
F32 = jnp.float32
DP = ("x", "core")


def dot(a, b, dims):
    return lax.dot_general(a, b, (dims, ((), ())), preferred_element_type=F32)


def silu_slope(values):
    sigma = jax.nn.sigmoid(values)
    return sigma * (1.0 + values * (1.0 - sigma))


def conv(padded, kernel):
    rows, cols = padded.shape[1] - 2, padded.shape[2] - 2
    wide = kernel.astype(F32)
    total = 0.0
    for a in range(3):
        for b in range(3):
            total = total + padded[:, a : a + rows, b : b + cols, :].astype(F32) * wide[a, b]
    return total


def conv_grad(padded, grads):
    rows, cols = grads.shape[1], grads.shape[2]
    wide = grads.astype(F32)
    return jnp.stack(
        [
            jnp.stack(
                [
                    jnp.sum(padded[:, a : a + rows, b : b + cols, :].astype(F32) * wide, axis=(0, 1, 2))
                    for b in range(3)
                ]
            )
            for a in range(3)
        ]
    )


def pad_columns(values):
    return jnp.pad(values, ((0, 0), (0, 0), (1, 1), (0, 0)))


def pad_sides(values):
    return jnp.pad(values, ((0, 0), (1, 1), (1, 1), (0, 0)))


def halo(values):
    ends = lax.axis_size("rows") - 1
    above = lax.ppermute(values[:, -1:], "rows", [(i, i + 1) for i in range(ends)])
    below = lax.ppermute(values[:, :1], "rows", [(i + 1, i) for i in range(ends)])
    return above, below


def swap(blocks, axis):
    n = lax.axis_size(axis)
    me = lax.axis_index(axis)
    got = [lax.dynamic_index_in_dim(blocks, me, 0, keepdims=False)]
    for k in range(1, n):
        send = lax.dynamic_index_in_dim(blocks, (me + k) % n, 0, keepdims=False)
        got.append(lax.ppermute(send, axis, [(i, (i + k) % n) for i in range(n)]))
    stacked = jnp.stack(got)
    return [lax.dynamic_index_in_dim(stacked, (me - j) % n, 0, keepdims=False) for j in range(n)]


def cross(n, k):
    return [(a * n + b, ((b + k) % n) * n + a) for a in range(n) for b in range(n)]


def spread(n, k):
    return [(a * n + b, b * n + (a + k) % n) for a in range(n) for b in range(n)]


def scatter_sum(blocks, axis):
    got = lax.all_to_all(blocks, axis, 0, 0, tiled=False)
    return jnp.sum(got.astype(F32), axis=0).astype(BF)


def core_sum(blocks):
    me = lax.axis_index("core")
    keep = lax.dynamic_index_in_dim(blocks, me, 0, keepdims=False)
    send = lax.dynamic_index_in_dim(blocks, 1 - me, 0, keepdims=False)
    got = lax.ppermute(send, "core", [(0, 1), (1, 0)])
    return (keep.astype(F32) + got.astype(F32)).astype(BF)


def body(features, counts, pre_reduce, pre_conv, pre_expand, pre_gain, post_reduce, post_conv, post_expand, post_gain, readout, cotangent):
    n = lax.axis_size("chan")
    row = lax.axis_index("rows")
    chan = lax.axis_index("chan")
    ch = pre_reduce.shape[0]
    slots, high, wide = features.shape[0], features.shape[1], features.shape[2]
    part = slots // n
    cells = high * wide
    pool = wide // 2
    spots = pool * pool
    out_share = cotangent.shape[3]

    above, below = halo(features)
    shards = jnp.concatenate([post_reduce, post_expand.T], axis=1)
    full = lax.all_gather(shards, "chan", axis=0, tiled=True)
    post_reduce_all = full[:, :ch]
    post_expand_all = full[:, ch:]
    gain_all = lax.all_gather(post_gain, "chan", axis=0, tiled=True)
    live = (jnp.arange(SLOT)[None, :] < counts[:, None]).astype(F32).reshape(slots)
    masked = (cotangent.astype(F32) * live[:, None, None, None]).astype(BF).reshape(n, part * spots, out_share)
    cots = [
        lax.ppermute(lax.dynamic_index_in_dim(masked, (chan + k) % n, 0, keepdims=False), ("rows", "chan"), cross(n, k))
        for k in range(n)
    ]
    blocks_at = [(row - k) % n for k in range(n)]

    ext = jnp.concatenate([above, features, below], axis=1)
    reduced_ext = dot(ext.reshape(-1, ch), pre_reduce, ((1,), (0,))).reshape(slots, high + 2, wide, -1)
    reduced = reduced_ext[:, 1:-1]
    act_ext = jax.nn.silu(reduced_ext).astype(BF)
    rimmed = pad_columns(act_ext)
    convolved = conv(rimmed, pre_conv)
    convolved_act = jax.nn.silu(convolved).astype(BF)
    expanded = dot(convolved_act.reshape(-1, ch), pre_expand, ((1,), (0,)))
    mean_value = jnp.mean(expanded, -1, keepdims=True)
    mean_square = jnp.mean(expanded * expanded, -1, keepdims=True)
    pre_std = lax.rsqrt(mean_square - mean_value * mean_value + EPS)
    normal_pre = (expanded - mean_value) * pre_std
    normed = normal_pre * pre_gain
    blended = features.astype(F32).reshape(-1, ch) + jax.nn.silu(normed)
    pooled = jnp.mean(blended.reshape(slots, high // 2, 2, pool, 2, ch), axis=(2, 4)).astype(BF)

    moved = jnp.concatenate(swap(pooled.reshape(n, part, high // 2, pool, ch), "rows"), axis=1)
    flat = moved.reshape(part * spots, ch)

    post_reduced = dot(flat, post_reduce_all, ((1,), (0,)))
    post_act = jax.nn.silu(post_reduced).astype(BF)
    post_padded = pad_sides(post_act.reshape(part, pool, pool, ch))
    post_convolved = conv(post_padded, post_conv).reshape(-1, ch)
    post_convolved_act = jax.nn.silu(post_convolved).astype(BF)
    post_expanded = dot(post_convolved_act, post_expand_all, ((1,), (1,)))
    post_mean = jnp.mean(post_expanded, -1, keepdims=True)
    post_square = jnp.mean(post_expanded * post_expanded, -1, keepdims=True)
    post_std = lax.rsqrt(post_square - post_mean * post_mean + EPS)
    post_normal = (post_expanded - post_mean) * post_std
    post_normed = post_normal * gain_all
    refined = flat.astype(F32) + jax.nn.silu(post_normed)
    refined_low = refined.astype(BF)

    refined_grad = 0.0
    for k in range(n):
        rows_part = lax.dynamic_slice_in_dim(readout, blocks_at[k] * out_share, out_share, 1)
        logits = dot(refined_low, rows_part, ((1,), (0,)))
        pull = jax.vjp(jax.nn.gelu, logits)[1]
        piece = pull(cots[k].astype(F32))[0].astype(BF)
        refined_grad = refined_grad + dot(piece, rows_part, ((1,), (1,)))

    gathered = [lax.ppermute(refined_low, ("rows", "chan"), spread(n, k)) for k in range(n)]
    stacked = jnp.stack(gathered)
    order = [lax.dynamic_index_in_dim(stacked, (chan - j) % n, 0, keepdims=False) for j in range(n)]
    refined_here = jnp.concatenate(order, axis=0)
    columns = lax.dynamic_slice_in_dim(readout, chan * out_share, out_share, 1)
    logits_here = dot(refined_here, columns, ((1,), (0,)))
    token_values, pull_here = jax.vjp(jax.nn.gelu, logits_here)
    tokens = token_values.astype(BF).reshape(slots, pool, pool, out_share)
    piece_here = pull_here(masked.reshape(-1, out_share).astype(F32))[0].astype(BF)
    readout_grad = dot(refined_here, piece_here, ((0,), (0,)))

    post_normed_grad = refined_grad * silu_slope(post_normed)
    post_gain_grad = jnp.sum(post_normed_grad * post_normal, axis=0)
    post_scaled = post_normed_grad * gain_all
    post_expanded_grad = (
        post_std
        * (
            post_scaled
            - jnp.mean(post_scaled, -1, keepdims=True)
            - post_normal * jnp.mean(post_scaled * post_normal, -1, keepdims=True)
        )
    ).astype(BF)
    post_expand_grad_t = dot(post_expanded_grad, post_convolved_act, ((0,), (0,)))
    post_act_grad = dot(post_expanded_grad, post_expand_all, ((1,), (0,)))
    post_convolved_grad = (post_act_grad * silu_slope(post_convolved)).astype(BF).reshape(part, pool, pool, ch)
    post_conv_grad = conv_grad(post_padded, post_convolved_grad)
    post_reduced_act_grad = conv(pad_sides(post_convolved_grad), post_conv[::-1, ::-1]).reshape(-1, ch)
    post_reduced_grad = (post_reduced_act_grad * silu_slope(post_reduced)).astype(BF)
    post_reduce_grad = dot(flat, post_reduced_grad, ((0,), (0,)))
    pooled_grad = (refined_grad + dot(post_reduced_grad, post_reduce_all, ((1,), (1,)))).astype(BF)

    back = pooled_grad.reshape(part, n, high // 2, pool, ch).transpose(1, 0, 2, 3, 4)
    returned = jnp.concatenate(swap(back, "rows"), axis=0)

    share = ch // n
    eight = share // 32
    extra = jnp.zeros((n, share, 128), F32)
    extra = extra.at[:, : share // 128].set(post_gain_grad.reshape(n, share // 128, 128))
    taps = post_conv_grad.reshape(-1, 128)
    extra = extra.at[:, share // 128 : share // 128 + taps.shape[0]].set(taps[None])
    load = jnp.concatenate(
        [
            post_reduce_grad.reshape(n, share, ch),
            post_expand_grad_t.reshape(n, share, ch),
            readout_grad.reshape(n, share, out_share),
            extra,
        ],
        axis=2,
    ).astype(BF)
    load = load.reshape(n, 2, 4, 4, eight, -1).transpose(1, 2, 3, 0, 4, 5)
    load = scatter_sum(scatter_sum(core_sum(load), "x"), "rows")
    load = lax.all_to_all(load, "chan", 0, 0, tiled=False)
    summed = jnp.sum(load.astype(F32), axis=0).astype(BF)
    mine = jnp.concatenate([summed[:, : 2 * ch], summed[:, 2 * ch + out_share :]] + [load[j, :, 2 * ch : 2 * ch + out_share] for j in range(n)], axis=1)
    post_all = lax.all_gather(mine, ("core", "x", "rows"), axis=0, tiled=True).astype(F32)
    post_reduce_out = post_all[:, :ch]
    post_expand_out = post_all[:, ch : 2 * ch].T
    extra_out = post_all[:, 2 * ch : 2 * ch + 128]
    post_gain_out = extra_out[: share // 128].reshape(share)
    post_conv_out = extra_out[share // 128 : share // 128 + taps.shape[0]].reshape(3, 3, ch)
    readout_out = post_all[:, 2 * ch + 128 :]

    blended_grad = jnp.repeat(jnp.repeat(returned.astype(F32) * 0.25, 2, axis=1), 2, axis=2).reshape(-1, ch)
    normed_grad = blended_grad * silu_slope(normed)
    pre_gain_grad = jnp.sum(normed_grad * normal_pre, axis=0)
    pre_scaled = normed_grad * pre_gain
    expanded_grad = (
        pre_std
        * (
            pre_scaled
            - jnp.mean(pre_scaled, -1, keepdims=True)
            - normal_pre * jnp.mean(pre_scaled * normal_pre, -1, keepdims=True)
        )
    ).astype(BF)
    convolved_act_grad = dot(expanded_grad, pre_expand, ((1,), (1,)))
    convolved_grad = (convolved_act_grad.reshape(convolved.shape) * silu_slope(convolved)).astype(BF)
    grad_above, grad_below = halo(convolved_grad)
    pre_expand_grad = dot(convolved_act.reshape(-1, ch), expanded_grad, ((0,), (0,)))
    pre_conv_grad = conv_grad(rimmed, convolved_grad)
    grad_padded = pad_columns(jnp.concatenate([grad_above, convolved_grad, grad_below], axis=1))
    reduced_act_grad = conv(grad_padded, pre_conv[::-1, ::-1])
    reduced_grad = (reduced_act_grad * silu_slope(reduced)).astype(BF).reshape(-1, ch)
    pre_reduce_grad = dot(features.reshape(-1, ch), reduced_grad, ((0,), (0,)))
    feature_grad = (blended_grad + dot(reduced_grad, pre_reduce, ((1,), (1,)))).reshape(features.shape)

    tail = jnp.concatenate([pre_conv_grad.reshape(-1, 128), pre_gain_grad.reshape(-1, 128)], axis=0)
    tail = jnp.pad(tail, ((0, ch - tail.shape[0]), (0, 0)))
    load = jnp.concatenate([pre_reduce_grad, pre_expand_grad, tail], axis=1).astype(BF).reshape(2, 4, 4, 4, ch // 128, -1)
    load = scatter_sum(scatter_sum(scatter_sum(core_sum(load), "x"), "rows"), "chan")
    pre_all = lax.all_gather(load, ("core", "x", "rows", "chan"), axis=0, tiled=True).astype(F32)
    taps = 9 * ch // 128
    return (
        tokens,
        feature_grad,
        pre_all[:, :ch],
        pre_all[:taps, 2 * ch :].reshape(3, 3, ch),
        pre_all[:, ch : 2 * ch],
        pre_all[taps : taps + ch // 128, 2 * ch :].reshape(ch),
        post_reduce_out,
        post_conv_out,
        post_expand_out,
        post_gain_out,
        readout_out,
    )


def solution(mesh):
    grid = Mesh(mesh.devices.reshape(4, 2, 4, 4), ("x", "core", "rows", "chan"))
    images = P(("x", "core", "chan"), "rows", None, None)
    grids = P(("x", "core", "rows"), None, None, "chan")
    return jax.shard_map(
        body,
        mesh=grid,
        in_specs=(
            images,
            P(("x", "core", "rows")),
            P(),
            P(),
            P(),
            P(),
            P("chan", None),
            P(),
            P(None, "chan"),
            P("chan"),
            P(),
            grids,
        ),
        out_specs=(grids, images, P(), P(), P(), P(), P("chan", None), P(), P(None, "chan"), P("chan"), P("chan", None)),
        check_vma=False,
    )
```

time: 3590 us -> 577 us (0.16)
  matrix products: 2520 us -> 91.2 us
  waiting for transfers between devices: 606 us -> 108 us
  blocking collectives: 245 us -> 89.1 us
  starting transfers between devices: 19 us -> 59.6 us
    conv_general_dilated x4 -> x0, matrix products: 2410 us -> none  [conv_valid(): lax.conv_general_dilated(padded, kernel.reshape(3, 3, 1, width), (1, 1),...]
    psum x4 -> x0, waiting for transfers between devices: 252 us -> none  [the longest x1 129 us: body(): post_reduced = lax.psum(post_partial, 'chan')]
    psum x4 -> x0, blocking collectives: 220 us -> none  [the longest x1 125 us: body(): lax.psum(post_conv_grad.astype(jnp.bfloat16), ('dp', 'rows'))]
    reduce_scatter x1 -> x0, waiting for transfers between devices: 218 us -> none  [body(): lax.psum_scatter(partial_logits, 'chan', scatter_dimension=3, tiled=True)]
    all_gather x1 -> x3, waiting for transfers between devices: 118 us -> 34.6 us  [the longest x1 34.6 us: body(): lax.all_gather(load, ('core', 'x', 'rows', 'chan'), axis=0, tiled=True)]
    ppermute x4 -> x20, waiting for transfers between devices: 10.3 us -> 55.8 us  [the longest x6 51.8 us: swap(): got.append(lax.ppermute(send, axis, [(i, (i + k) % n) for i in range(n)]))]
    unnamed x105 -> x120, local copies, waits for them, and re-layouts: 54 us -> 15.6 us
    ppermute x4 -> x20, starting transfers between devices: 10.4 us -> 47.8 us  [the longest x4 13.1 us: body(): lax.ppermute(lax.dynamic_index_in_dim(masked, (chan + k) % n, 0, keepdims...]
  transfers between devices with their start and end apart: 12 -> 26, of which waited for: 7 -> 6; matrix products, arithmetic and copies ran while one was open for 19% -> 45% of each run, Pallas kernels for 0% -> 0%
where the time goes in v1:
time: 577 us; the launch traced here: 570 us
  waiting for transfers between devices  108 us (19%)
  local copies, waits for them, and re-layouts  106 us (18%)
  other arithmetic  101 us (18%)
  matrix products  91.2 us (16%)
  blocking collectives  89.1 us (15%)
  starting transfers between devices  59.6 us (10%)
  between operations  15.3 us (3%)
    dot_general x18, matrix products, dot(): return lax.dot_general(a, b, (dims, ((), ())), preferred_element_type=F32)  91.2 us
    all_to_all x3, blocking collectives, scatter_sum(): got = lax.all_to_all(blocks, axis, 0, 0, tiled=False)  57.7 us
    ppermute x6, waiting for transfers between devices, swap(): got.append(lax.ppermute(send, axis, [(i, (i + k) % n) for i in range(n)]))  51.8 us
    all_gather x1, waiting for transfers between devices, body(): lax.all_gather(load, ('core', 'x', 'rows', 'chan'), axis=0, tiled=True)  34.6 us
    all_gather x1, blocking collectives, body(): gain_all = lax.all_gather(post_gain, 'chan', axis=0, tiled=True)  31.4 us
    reduce_sum x2, other arithmetic, conv_grad(): jnp.sum(padded[:, a:a + rows, b:b + cols, :].astype(F32) * wide, axis=(0,...  24.5 us
    all_to_all x2, waiting for transfers between devices, scatter_sum(): got = lax.all_to_all(blocks, axis, 0, 0, tiled=False)  17.1 us
    unnamed x120, local copies, waits for them, and re-layouts  15.6 us
  transfers between devices with their start and end apart: 26, of which 6 were waited for; matrix products, arithmetic and copies ran while one was open for 45% of the time, Pallas kernels for 0%

profile of v1, /device:TPU:1, one launch (start us, length us, event | category | flops | bytes accessed | tf_op | source)
XLA Modules:
  0.0 569.6 jit_solution(8980193229276665665)
XLA Ops:
  11.9 4.1 collective-permute-start
  17.5 2.5 multiply_convert_fusion.3
  21.4 3.0 copy.64
  24.4 5.0 reshape.317
  29.4 3.1 dynamic-slice_bitcast_fusion.5
  32.5 6.0 %collective-permute-start.9 = (bf16[288,1024]{1,0:T(8,128)(2,1)}, bf16[288,1024]{1,0:T(8,128)(2,1)}, u32[]{:S(2)}, u32[]{:S(2)}) collective-permute-start(bf16[288,1024]{1,0:T(8,128)(2,1)} %get-tuple-element.128), channel_id=1, source_target_pairs={{0,0},{1,4},{2,8},{3,12},{4,1},{5,5},{6,9},{7,13},{8,2},{9,6},{10,... | collective-permute-start | bytes 1769480 | tf_op jit(solution)/shard_map/ppermute | solution.py:116
  40.9 5.8 %copy.68 = f32[8,12,12,1024]{3,2,1,0:T(8,128)} copy(bf16[8,12,12,1024]{3,0,2,1:T(8,128)(2,1)} %copy-done.4) | data formatting | bytes 7077888 | tf_op jit(solution)/shard_map/convert_element_type | solution.py:170
  46.7 31.4 %all-gather = f32[4,1,256]{2,1,0:T(1,128)S(1)} all-gather(f32[1,1,256]{2,1,0:T(1,128)S(1)} %bitcast.334), channel_id=1, replica_groups=mesh['x'=4,'core'=2,'rows'=4,'chan'=4] {'chan'}, dimensions={0}, use_global_device_ids=true | all-gather | bytes 5120 | tf_op jit(solution)/shard_map/all_gather | solution.py:112
  78.3 6.7 %reshape.336 = f32[1152,1024]{1,0:T(8,128)} reshape(f32[8,12,12,1024]{3,2,1,0:T(8,128)} %copy.68) | data formatting | bytes 9437184 | tf_op jit(solution)/shard_map/convert_element_type | solution.py:170
  86.3 8.6 %multiply_convert_fusion = (bf16[8,8,24,1024]{3,2,1,0:T(8,128)(2,1)S(1)}, f32[8,8,24,1024]{3,2,1,0:T(8,128)}) fusion(bf16[1024,1024]{1,0:T(8,128)(2,1)S(1)} %copy-done, bf16[8,1,24,1024]{3,2,1,0:T(8,128)(2,1)} %collective-permute-done.1, bf16[8,6,24,1024]{3,2,1,0:T(8,128)(2,1)} %param.16, bf16[8,1,24,1024]{3,2,1,0:T(8,128)(2,1)S(1)} %collective-permute-done), kind=kOutput, calls=%fused_computation.18 | convolution fusion | flops 3232235520 | bytes 14680064 | tf_op jit(solution)/shard_map/dot_general | solution.py:14
  94.9 9.3 %multiply_convert_fusion.5 = (bf16[8,6,24,1024]{3,2,1,0:T(8,128)(2,1)S(1)}, f32[8,6,24,1024]{3,2,1,0:T(8,128)}) fusion(f32[1024]{0:T(1024)S(1)} %bitcast.322, f32[1024]{0:T(1024)S(1)} %bitcast.321, bf16[8,8,24,1024]{3,2,1,0:T(8,128)(2,1)S(1)} %get-tuple-element.195, f32[1024]{0:T(1024)S(1)} %bitcast.320, f32[1024]{0:T(1024)S(1)} %bitcast.319, ...), kind=kLoop, calls=%fused_computation.82 | loop fusion | flops 36569088 | bytes 17338368 | tf_op jit(solution)/shard_map/convert_element_type | solution.py:127
  104.2 2.8 fusion.271
  109.2 3.3 convert_add_fusion
  112.5 7.2 %reshape.312 = f32[8,3,2,12,2,1024]{5,4,3,2,1,0:T(2,128)} reshape(f32[1152,1024]{1,0:T(8,128)} %convert_add_fusion) | data formatting | bytes 9437184 | tf_op jit(solution)/shard_map/reshape | solution.py:135
  119.6 7.3 %reduce_sum.335 = f32[8,3,12,1024]{3,2,1,0:T(8,128)} reduce(f32[8,3,2,12,2,1024]{5,4,3,2,1,0:T(2,128)} %reshape.312, f32[]{:T(128)} %constant.278.clone.1), dimensions={2,4}, to_apply=%region_2.3 | reduce | flops 884736 | bytes 5898244 | tf_op jit(solution)/shard_map/reduce_sum | solution.py:135
  130.8 4.3 copy.65
  135.0 3.6 collective-permute-start.11
  142.5 3.7 multiply_convert_fusion.11
  147.4 4.1 multiply_convert_fusion.6
  151.6 2.5 reshape.315
  154.0 2.9 fusion.272
  160.8 4.1 collective-permute-start.7
  164.8 5.7 fusion.66
  170.5 5.7 fusion.70
  178.2 5.7 fusion.74
  183.9 8.6 %multiply_reduce_fusion.5 = (bf16[1024]{0:T(1024)(128)(2,1)}, f32[288]{0:T(512)S(1)}, f32[288]{0:T(512)S(1)}, f32[288,1024]{1,0:T(8,128)}, f32[288,1024]{1,0:T(8,128)}) fusion(f32[288]{0:T(512)S(1)} %get-tuple-element.194, f32[288,1024]{1,0:T(8,128)} %copy-done.7, f32[288]{0:T(512)S(1)} %get-tuple-element.193, f32[1024]{0:T(1024)S(1)} %bitcast.284, ...), kind=kOutput, calls=%fused_computation.253 | convolution fusion | flops 1220049408 | bytes 12463616 | tf_op jit(solution)/shard_map/dot_general | solution.py:14
  196.1 4.7 multiply_reduce_fusion.4
  201.8 9.5 %fusion.95 = (f32[1024]{0:T(1024)}, f32[1024]{0:T(1024)}, f32[1024]{0:T(1024)}, f32[1024]{0:T(1024)}, f32[1024]{0:T(1024)}, /*index=5*/f32[1024]{0:T(1024)S(1)},...) fusion(bf16[2,12,12,1024]{3,2,1,0:T(8,128)(2,1)} %reshape.318, bf16[2,12,12,1024]{3,2,1,0:T(8,128)(2,1)S(1)} %reshape.314, ...), kind=kLoop, calls=%fused_computation.173 | loop fusion | flops 14737408 | bytes 2428928 | tf_op jit(solution)/shard_map/reduce_sum | solution.py:39
  218.1 2.7 collective-permute-start.15
  221.5 3.9 convolution_convert_fusion.1
  225.5 2.6 convolution_convert_fusion
  228.2 6.0 %collective-permute-start.5 = (bf16[288,1024]{1,0:T(8,128)(2,1)}, bf16[288,1024]{1,0:T(8,128)(2,1)}, u32[]{:S(2)}, u32[]{:S(2)}) collective-permute-start(bf16[288,1024]{1,0:T(8,128)(2,1)} %add_convert_fusion), channel_id=1, source_target_pairs={{0,0},{1,4},{2,8},{3,12},{4,1},{5,5},{6,9},{7,13},{8,2},{9,6},{10,... | collective-permute-start | bytes 1769480 | tf_op jit(solution)/shard_map/ppermute | solution.py:162
  234.7 51.2 %collective-permute-done.13 = bf16[2,3,12,1024]{3,2,1,0:T(8,128)(2,1)S(1)} collective-permute-done((bf16[2,3,12,1024]{3,2,1,0:T(8,128)(2,1)S(1)}, bf16[2,3,12,1024]{3,2,1,0:T(8,128)(2,1)S(1)}, u32[]{:S(2)}, u32[]{:S(2)}) %collective-permute-start.13) | collective-permute-done | bytes 147488 | tf_op jit(solution)/shard_map/ppermute | solution.py:69
  288.4 5.8 %broadcast_in_dim.7 = f32[8,6,12,2,1024]{4,3,2,1,0:T(2,128)} broadcast(f32[8,6,12,1024]{3,2,1,0:T(8,128)} %bitcast.260), dimensions={0,1,2,4} | broadcast | bytes 7077888 | tf_op jit(solution)/shard_map/broadcast_in_dim | solution.py:224
  294.2 6.9 %reshape_reshape.4 = f32[1152,1024]{1,0:T(8,128)} reshape(f32[8,6,12,2,1024]{4,3,2,1,0:T(2,128)} %broadcast_in_dim.7) | data formatting | bytes 9437184 | tf_op jit(solution)/shard_map/reshape;reshape | solution.py:224
  303.3 8.7 %multiply_convert_fusion.4 = (bf16[1152,1024]{1,0:T(8,128)(2,1)}, f32[1152,1024]{1,0:T(8,128)S(1)}) fusion(bf16[1024,4096]{1,0:T(8,128)(2,1)} %param.26, s32[]{:T(128)S(6)} %select_n.187, bf16[288,1024]{1,0:T(8,128)(2,1)S(1)} %get-tuple-element.133, bf16[288,1024]{1,0:T(8,128)(2,1)S(1)} %get-tuple-element.134, ...), kind=kOutput, calls=%fused_computation.78 | convolution fusion | flops 2435973120 | bytes 11534340 | tf_op jit(solution)/shard_map/dot_general | solution.py:14
  312.0 4.8 fusion.52
  317.8 4.6 collective-permute-start.19
  322.4 3.9 multiply_reduce_fusion
  327.9 4.3 fusion.284
  334.9 4.7 all-to-all-start.3
  339.6 15.0 %fusion.27 = (bf16[1024]{0:T(1024)(128)(2,1)S(1)}, bf16[1024]{0:T(1024)(128)(2,1)S(1)}, bf16[1024]{0:T(1024)(128)(2,1)S(1)}, bf16[1024]{0:T(1024)(128)(2,1)S(1)}...) fusion(bf16[8,8,24,1024]{3,2,1,0:T(8,128)(2,1)} %copy-done.1, ...), kind=kLoop, calls=%fused_computation.53 | loop fusion | flops 43637760 | bytes 22038528 | tf_op jit(solution)/shard_map/reduce_sum | solution.py:39
  358.5 4.1 fusion.55
  363.4 12.8 %all-to-all-done.3 = bf16[4,4,4,8,3200]{4,3,1,2,0:T(8,128)(2,1)} async-done(((bf16[4,4,4,8,3200]{4,3,1,2,0:T(8,128)(2,1)}), bf16[4,4,4,8,3200]{4,3,1,2,0:T(8,128)(2,1)}, u32[]{:S(2)}, u32[]{:S(2)}) %all-to-all-start.3) | async-done | bytes 3276832 | tf_op jit(solution)/shard_map/all_to_all | solution.py:83
  376.2 2.5 reduce_sum.365
  379.6 3.5 all-to-all-start.4
  383.2 4.6 fusion.38
  387.7 4.4 all-to-all-done.4
  392.9 3.4 all-to-all-start.5
  396.6 13.8 %fusion.26 = bf16[8,6,24,1024]{3,2,1,0:T(8,128)(2,1)} fusion(bf16[8,6,24,1024]{3,2,1,0:T(8,128)(2,1)} %copy-done.3, f32[8,8,24,1024]{3,2,1,0:T(8,128)} %get-tuple-element.196, bf16[8,8,26,1024]{3,2,1,0:T(8,128)(2,1)} %fusion.38, bf16[8,1,24,1024]{3,2,1,0:T(8,128)(2,1)} %collective-permute-done.17, bf16[8,1,24,1024]{3,2,1,0:T(8,128)(2,1)S(1)} %collective-permute-done.16, ...), kind=kLoop, calls=%fused_computation.52 | loop fusion | flops 43646976 | bytes 24416256 | tf_op jit(solution)/shard_map/convert_element_type | solution.py:243
  411.2 5.5 bitcast_convert_fusion
  417.3 4.7 collective-permute-start.18
  422.0 4.0 collective-permute-done.18
  426.5 37.5 %all_to_all.30 = bf16[4,4,4,8,2176]{4,3,2,1,0:T(8,128)(2,1)} all-to-all(bf16[4,4,4,8,2176]{4,3,2,1,0:T(8,128)(2,1)S(1)} %fusion.36), channel_id=1, replica_groups=mesh['x'=4,'core'=2,'rows'=4,'chan'=4] {'x'}, dimensions={0} | all-to-all | bytes 4456448 | tf_op jit(solution)/shard_map/all_to_all | solution.py:83
  466.0 11.0 %all_to_all.31 = bf16[4,4,8,2176]{3,2,1,0:T(8,128)(2,1)S(1)} all-to-all(bf16[4,4,8,2176]{3,2,1,0:T(8,128)(2,1)S(1)} %reduce_sum.352), channel_id=1, replica_groups=mesh['x'=4,'core'=2,'rows'=4,'chan'=4] {'rows'}, dimensions={0} | all-to-all | bytes 1114112 | tf_op jit(solution)/shard_map/all_to_all | solution.py:83
  477.1 9.2 %all_to_all.32 = bf16[4,8,2176]{2,1,0:T(8,128)(2,1)S(1)} all-to-all(bf16[4,8,2176]{2,1,0:T(8,128)(2,1)S(1)} %reduce_sum.353), channel_id=1, replica_groups=mesh['x'=4,'core'=2,'rows'=4,'chan'=4] {'chan'}, dimensions={0} | all-to-all | bytes 278528 | tf_op jit(solution)/shard_map/all_to_all | solution.py:83
  487.0 6.7 %convolution_add_fusion = f32[1152,1024]{1,0:T(8,128)} fusion(f32[1152,1024]{1,0:T(8,128)} %reshape_reshape.4, bf16[1152,1024]{1,0:T(8,128)(2,1)} %bitcast.268, bf16[1024,1024]{1,0:T(8,128)(2,1)S(1)} %copy-done), kind=kOutput, calls=%fused_computation.84 | convolution fusion | flops 2417098752 | bytes 13893632 | tf_op jit(solution)/shard_map/dot_general | solution.py:14
  493.7 4.8 reshape.316
  498.5 4.9 copy.73
  507.1 2.7 copy-done.6
  513.3 4.1 slice.503
  518.7 34.6 %all-gather.7.cloned.1.call-done = bf16[1024,2176]{1,0:T(8,128)(2,1)} async-done(((bf16[8,2176]{1,0:T(8,128)(2,1)}), bf16[1024,2176]{1,0:T(8,128)(2,1)}) %all-gather.7.cloned.1.call-update) | async-done | bytes 4456464 | tf_op jit(solution)/shard_map/all_gather | solution.py:251
  554.7 3.0 convert_element_type.386
  558.3 4.5 fusion.275
  (248 shorter events, 72.5 us)
Async XLA Ops:
  7.2 79.1 %copy-start = (bf16[1024,1024]{1,0:T(8,128)(2,1)S(1)}, bf16[1024,1024]{1,0:T(8,128)(2,1)}, u32[]{:S(2)}) copy-start(bf16[1024,1024]{1,0:T(8,128)(2,1)} %param.18) | copy-start | bytes 6291460
  7.2 135.3 %all-gather.5.cloned.1.call-start = ((), (), s32[]{:S(2)}) async-start(), calls=%async_computation.6 | async-start | bytes 5242880 | tf_op jit(solution)/shard_map/all_gather | solution.py:109
  8.6 8.7 %copy-start.47 = (s32[2]{0:T(128)S(1)}, s32[2]{0:T(128)}, u32[]{:S(2)}) copy-start(s32[2]{0:T(128)} %param.17) | copy-start | bytes 28
  11.9 74.3 %collective-permute-start = (bf16[8,1,24,1024]{3,2,1,0:T(8,128)(2,1)S(1)}, bf16[8,1,24,1024]{3,2,1,0:T(8,128)(2,1)S(1)}, u32[]{:S(2)}, u32[]{:S(2)}) collective-permute-start(bf16[8,1,24,1024]{3,2,1,0:T(8,128)(2,1)S(1)} %get-tuple-element.136), channel_id=1, source_target_pairs={{0,4},{4,8},{8,12},{1,5},{5,9},{9,13},{2,6},{6,10},{10,14},{3,7},{... | collective-permute-start | bytes 1179656 | tf_op jit(solution)/shard_map/ppermute | solution.py:58
  16.0 70.3 %collective-permute-start.1 = (bf16[8,1,24,1024]{3,2,1,0:T(8,128)(2,1)S(1)}, bf16[8,1,24,1024]{3,2,1,0:T(8,128)(2,1)}, u32[]{:S(2)}, u32[]{:S(2)}) collective-permute-start(bf16[8,1,24,1024]{3,2,1,0:T(8,128)(2,1)S(1)} %get-tuple-element.137), channel_id=1, source_target_pairs={{4,0},{8,4},{12,8},{5,1},{9,5},{13,9},{6,2},{10,6},{14,10},{7,3},{... | collective-permute-start | bytes 1179656 | tf_op jit(solution)/shard_map/ppermute | solution.py:59
  29.4 11.2 %copy-start.21 = (bf16[3,3,1024]{2,1,0:T(4,128)(2,1)S(1)}, bf16[3,3,1024]{2,1,0:T(4,128)(2,1)}, u32[]{:S(2)}) copy-start(bf16[3,3,1024]{2,1,0:T(4,128)(2,1)} %param.19) | copy-start | bytes 55300
  32.5 151.4 %collective-permute-start.9 = (bf16[288,1024]{1,0:T(8,128)(2,1)}, bf16[288,1024]{1,0:T(8,128)(2,1)}, u32[]{:S(2)}, u32[]{:S(2)}) collective-permute-start(bf16[288,1024]{1,0:T(8,128)(2,1)} %get-tuple-element.128), channel_id=1, source_target_pairs={{0,0},{1,4},{2,8},{3,12},{4,1},{5,5},{6,9},{7,13},{8,2},{9,6},{10,... | collective-permute-start | bytes 1769480 | tf_op jit(solution)/shard_map/ppermute | solution.py:116
  38.5 122.3 %collective-permute-start.12 = (bf16[288,1024]{1,0:T(8,128)(2,1)}, bf16[288,1024]{1,0:T(8,128)(2,1)}, u32[]{:S(2)}, u32[]{:S(2)}) collective-permute-start(bf16[288,1024]{1,0:T(8,128)(2,1)} %get-tuple-element.129), channel_id=1, source_target_pairs={{0,12},{1,0},{2,4},{3,8},{4,13},{5,1},{6,5},{7,9},{8,14},{9,2},{10... | collective-permute-start | bytes 1769480 | tf_op jit(solution)/shard_map/ppermute | solution.py:116
  40.9 5.8 %copy-start.44 = (f32[256]{0:T(256)S(1)}, f32[256]{0:T(256)}, u32[]{:S(2)}) copy-start(f32[256]{0:T(256)} %param.25) | copy-start | bytes 3076
  40.9 37.2 %copy-start.22 = (bf16[3,3,1024]{2,1,0:T(4,128)(2,1)S(1)}, bf16[3,3,1024]{2,1,0:T(4,128)(2,1)}, u32[]{:S(2)}) copy-start(bf16[3,3,1024]{2,1,0:T(4,128)(2,1)} %param.23) | copy-start | bytes 55300
  94.9 9.3 %copy-start.1 = (bf16[8,8,24,1024]{3,2,1,0:T(8,128)(2,1)}, bf16[8,8,24,1024]{3,2,1,0:T(8,128)(2,1)S(1)}, u32[]{:S(2)}) copy-start(bf16[8,8,24,1024]{3,2,1,0:T(8,128)(2,1)S(1)} %get-tuple-element.195) | copy-start | bytes 9437188
  94.9 9.3 %copy-start.45 = (bf16[1024,1024]{1,0:T(8,128)(2,1)S(1)}, bf16[1024,1024]{1,0:T(8,128)(2,1)}, u32[]{:S(2)}) copy-start(bf16[1024,1024]{1,0:T(8,128)(2,1)} %param.20) | copy-start | bytes 6291460
  104.1 5.0 copy-start.8
  104.2 5.0 copy-start.23
  128.6 6.4 %collective-permute-start.4 = (bf16[2,3,12,1024]{3,2,1,0:T(8,128)(2,1)S(1)}, bf16[2,3,12,1024]{3,2,1,0:T(8,128)(2,1)S(1)}, u32[]{:S(2)}, u32[]{:S(2)}) collective-permute-start(bf16[2,3,12,1024]{3,2,1,0:T(8,128)(2,1)S(1)} %get-tuple-element.152), channel_id=1, source_target_pairs={{0,12},{4,0},{8,4},{12,8},{1,13},{5,1},{9,5},{13,9},{2,14},{6,2},{... | collective-permute-start | bytes 442376 | tf_op jit(solution)/shard_map/ppermute | solution.py:69
  128.7 9.9 %collective-permute-start.3 = (bf16[2,3,12,1024]{3,2,1,0:T(8,128)(2,1)S(1)}, bf16[2,3,12,1024]{3,2,1,0:T(8,128)(2,1)S(1)}, u32[]{:S(2)}, u32[]{:S(2)}) collective-permute-start(bf16[2,3,12,1024]{3,2,1,0:T(8,128)(2,1)S(1)} %get-tuple-element.153), channel_id=1, source_target_pairs={{0,8},{4,12},{8,0},{12,4},{1,9},{5,13},{9,1},{13,5},{2,10},{6,14},... | collective-permute-start | bytes 442376 | tf_op jit(solution)/shard_map/ppermute | solution.py:69
  128.8 12.0 %collective-permute-start.2 = (bf16[2,3,12,1024]{3,2,1,0:T(8,128)(2,1)S(1)}, bf16[2,3,12,1024]{3,2,1,0:T(8,128)(2,1)S(1)}, u32[]{:S(2)}, u32[]{:S(2)}) collective-permute-start(bf16[2,3,12,1024]{3,2,1,0:T(8,128)(2,1)S(1)} %get-tuple-element.154), channel_id=1, source_target_pairs={{0,4},{4,8},{8,12},{12,0},{1,5},{5,9},{9,13},{13,1},{2,6},{6,10},{... | collective-permute-start | bytes 442376 | tf_op jit(solution)/shard_map/ppermute | solution.py:69
  135.0 35.5 %collective-permute-start.11 = (bf16[288,1024]{1,0:T(8,128)(2,1)}, bf16[288,1024]{1,0:T(8,128)(2,1)}, u32[]{:S(2)}, u32[]{:S(2)}) collective-permute-start(bf16[288,1024]{1,0:T(8,128)(2,1)} %get-tuple-element.130), channel_id=1, source_target_pairs={{0,8},{1,12},{2,0},{3,4},{4,9},{5,13},{6,1},{7,5},{8,10},{9,14},{1... | collective-permute-start | bytes 1769480 | tf_op jit(solution)/shard_map/ppermute | solution.py:116
  138.6 39.6 %collective-permute-start.10 = (bf16[288,1024]{1,0:T(8,128)(2,1)}, bf16[288,1024]{1,0:T(8,128)(2,1)}, u32[]{:S(2)}, u32[]{:S(2)}) collective-permute-start(bf16[288,1024]{1,0:T(8,128)(2,1)} %get-tuple-element.131), channel_id=1, source_target_pairs={{0,4},{1,8},{2,12},{3,0},{4,5},{5,9},{6,13},{7,1},{8,6},{9,10},{10... | collective-permute-start | bytes 1769480 | tf_op jit(solution)/shard_map/ppermute | solution.py:116
  142.4 5.0 copy-start.29
  142.4 5.0 copy-start.30
  142.4 5.0 copy-start.31
  142.4 5.0 copy-start.32
  142.4 5.0 copy-start.33
  142.4 5.0 copy-start.34
  158.3 142.8 %collective-permute-start.8 = (bf16[288,1024]{1,0:T(8,128)(2,1)}, bf16[288,1024]{1,0:T(8,128)(2,1)}, u32[]{:S(2)}, u32[]{:S(2)}) collective-permute-start(bf16[288,1024]{1,0:T(8,128)(2,1)} %add_convert_fusion), channel_id=1, source_target_pairs={{0,3},{1,7},{2,11},{3,15},{4,0},{5,4},{6,8},{7,12},{8,1},{9,5},{10... | collective-permute-start | bytes 1769480 | tf_op jit(solution)/shard_map/ppermute | solution.py:162
  160.8 140.4 %collective-permute-start.7 = (bf16[288,1024]{1,0:T(8,128)(2,1)}, bf16[288,1024]{1,0:T(8,128)(2,1)}, u32[]{:S(2)}, u32[]{:S(2)}) collective-permute-start(bf16[288,1024]{1,0:T(8,128)(2,1)} %add_convert_fusion), channel_id=1, source_target_pairs={{0,2},{1,6},{2,10},{3,14},{4,3},{5,7},{6,11},{7,15},{8,0},{9,4},{1... | collective-permute-start | bytes 1769480 | tf_op jit(solution)/shard_map/ppermute | solution.py:162
  170.5 130.6 %collective-permute-start.6 = (bf16[288,1024]{1,0:T(8,128)(2,1)}, bf16[288,1024]{1,0:T(8,128)(2,1)}, u32[]{:S(2)}, u32[]{:S(2)}) collective-permute-start(bf16[288,1024]{1,0:T(8,128)(2,1)} %add_convert_fusion), channel_id=1, source_target_pairs={{0,1},{1,5},{2,9},{3,13},{4,2},{5,6},{6,10},{7,14},{8,3},{9,7},{10... | collective-permute-start | bytes 1769480 | tf_op jit(solution)/shard_map/ppermute | solution.py:162
  196.1 5.7 %copy-start.25 = (f32[1,1,1024]{2,1,0:T(1,128)S(1)}, f32[1,1,1024]{2,1,0:T(1,128)}, u32[]{:S(2)}) copy-start(f32[1,1,1024]{2,1,0:T(1,128)} %get-tuple-element.164) | copy-start | bytes 12292
  196.1 5.7 %copy-start.26 = (f32[1,1,1024]{2,1,0:T(1,128)S(1)}, f32[1,1,1024]{2,1,0:T(1,128)}, u32[]{:S(2)}) copy-start(f32[1,1,1024]{2,1,0:T(1,128)} %get-tuple-element.165) | copy-start | bytes 12292
  196.1 5.7 %copy-start.27 = (f32[1,1,1024]{2,1,0:T(1,128)S(1)}, f32[1,1,1024]{2,1,0:T(1,128)}, u32[]{:S(2)}) copy-start(f32[1,1,1024]{2,1,0:T(1,128)} %get-tuple-element.166) | copy-start | bytes 12292
  196.1 5.7 %copy-start.28 = (f32[1,1,1024]{2,1,0:T(1,128)S(1)}, f32[1,1,1024]{2,1,0:T(1,128)}, u32[]{:S(2)}) copy-start(f32[1,1,1024]{2,1,0:T(1,128)} %get-tuple-element.167) | copy-start | bytes 12292
  218.1 7.4 %copy-start.17 = (bf16[1024,288]{1,0:T(8,128)(2,1)S(1)}, bf16[1024,288]{1,0:T(8,128)(2,1)}, u32[]{:S(2)}) copy-start(bf16[1024,288]{1,0:T(8,128)(2,1)} %copy.67) | copy-start | bytes 1769476
  218.1 7.4 %copy-start.18 = (bf16[288,1024,1,1,1,1]{1,0,2,3,4,5:T(8,128)(2,1)S(1)}, bf16[288,1024,1,1,1,1]{1,0,2,3,4,5:T(8,128)(2,1)}, u32[]{:S(2)}) copy-start(bf16[288,1024,1,1,1,1]{1,0,2,3,4,5:T(8,128)(2,1)} %reshape.344) | copy-start | bytes 1769476
  218.1 10.1 %collective-permute-start.15 = (bf16[2,3,12,1024]{3,2,1,0:T(8,128)(2,1)S(1)}, bf16[2,3,12,1024]{3,2,1,0:T(8,128)(2,1)S(1)}, u32[]{:S(2)}, u32[]{:S(2)}) collective-permute-start(bf16[2,3,12,1024]{3,2,1,0:T(8,128)(2,1)S(1)} %get-tuple-element.144), channel_id=1, source_target_pairs={{0,12},{4,0},{8,4},{12,8},{1,13},{5,1},{9,5},{13,9},{2,14},{6,2},{... | collective-permute-start | bytes 442376 | tf_op jit(solution)/shard_map/ppermute | solution.py:69
  220.8 13.4 %collective-permute-start.14 = (bf16[2,3,12,1024]{3,2,1,0:T(8,128)(2,1)S(1)}, bf16[2,3,12,1024]{3,2,1,0:T(8,128)(2,1)S(1)}, u32[]{:S(2)}, u32[]{:S(2)}) collective-permute-start(bf16[2,3,12,1024]{3,2,1,0:T(8,128)(2,1)S(1)} %get-tuple-element.145), channel_id=1, source_target_pairs={{0,8},{4,12},{8,0},{12,4},{1,9},{5,13},{9,1},{13,5},{2,10},{6,14},... | collective-permute-start | bytes 442376 | tf_op jit(solution)/shard_map/ppermute | solution.py:69
  225.5 8.7 %copy-start.43 = (bf16[1024]{0:T(1024)(128)(2,1)S(1)}, bf16[1024]{0:T(1024)(128)(2,1)}, u32[]{:S(2)}) copy-start(bf16[1024]{0:T(1024)(128)(2,1)} %get-tuple-element.104) | copy-start | bytes 6148
  228.2 72.9 %collective-permute-start.5 = (bf16[288,1024]{1,0:T(8,128)(2,1)}, bf16[288,1024]{1,0:T(8,128)(2,1)}, u32[]{:S(2)}, u32[]{:S(2)}) collective-permute-start(bf16[288,1024]{1,0:T(8,128)(2,1)} %add_convert_fusion), channel_id=1, source_target_pairs={{0,0},{1,4},{2,8},{3,12},{4,1},{5,5},{6,9},{7,13},{8,2},{9,6},{10,... | collective-permute-start | bytes 1769480 | tf_op jit(solution)/shard_map/ppermute | solution.py:162
  234.2 51.7 %collective-permute-start.13 = (bf16[2,3,12,1024]{3,2,1,0:T(8,128)(2,1)S(1)}, bf16[2,3,12,1024]{3,2,1,0:T(8,128)(2,1)S(1)}, u32[]{:S(2)}, u32[]{:S(2)}) collective-permute-start(bf16[2,3,12,1024]{3,2,1,0:T(8,128)(2,1)S(1)} %get-tuple-element.146), channel_id=1, source_target_pairs={{0,4},{4,8},{8,12},{12,0},{1,5},{5,9},{9,13},{13,1},{2,6},{6,10},{... | collective-permute-start | bytes 442376 | tf_op jit(solution)/shard_map/ppermute | solution.py:69
  303.0 9.0 %slice-start.6 = ((s8[4718592]{0:T(1024)(128)(4,1)}), s8[4194304]{0:T(1024)(128)(4,1)S(1)}, s32[]{:S(2)}) async-start(s8[4718592]{0:T(1024)(128)(4,1)} %bitcast.265), calls=%async_computation.15 | async-start | bytes 8388608
  303.3 8.7 %slice-start.7 = ((s8[4718592]{0:T(1024)(128)(4,1)}), s8[524288]{0:T(1024)(128)(4,1)S(1)}, s32[]{:S(2)}) async-start(s8[4718592]{0:T(1024)(128)(4,1)} %bitcast.265), calls=%async_computation.16 | async-start | bytes 1048576
  312.0 4.9 copy-start.12
  312.0 4.9 copy-start.13
  316.9 5.4 slice-start
  316.9 5.4 slice-start.4
  316.9 5.4 slice-start.1
  316.9 5.4 slice-start.5
  317.8 14.4 %collective-permute-start.19 = (bf16[4,4,4,8,3200]{4,3,1,0,2:T(8,128)(2,1)S(1)}, bf16[4,4,4,8,3200]{4,3,1,0,2:T(8,128)(2,1)S(1)}, u32[]{:S(2)}, u32[]{:S(2)}) collective-permute-start(bf16[4,4,4,8,3200]{4,3,1,0,2:T(8,128)(2,1)S(1)} %dynamic-slice_bitcast_fusion), channel_id=1, source_target_pairs={{0,16},{16,0},{1,17},{17,1},{2,18},{18,2},{3,19},{19,3},{4,20},{20... | collective-permute-start | bytes 9830408 | tf_op jit(solution)/shard_map/ppermute | solution.py:91
  327.9 4.3 copy-start.10
  334.9 41.3 %all-to-all-start.3 = ((bf16[4,4,4,8,3200]{4,3,1,2,0:T(8,128)(2,1)}), bf16[4,4,4,8,3200]{4,3,1,2,0:T(8,128)(2,1)}, u32[]{:S(2)}, u32[]{:S(2)}) async-start(bf16[4,4,4,8,3200]{4,3,1,2,0:T(8,128)(2,1)} %copy.70), calls=%async_computation.3 | async-start | bytes 6553600 | tf_op jit(solution)/shard_map/all_to_all | solution.py:83
  339.6 18.8 %copy-start.9 = (bf16[1024,1152]{1,0:T(8,128)(2,1)S(1)}, bf16[1024,1152]{1,0:T(8,128)(2,1)}, u32[]{:S(2)}) copy-start(bf16[1024,1152]{1,0:T(8,128)(2,1)} %copy.65) | copy-start | bytes 7077892
  339.6 18.8 %copy-start.11 = (bf16[1152,1024]{1,0:T(8,128)(2,1)S(1)}, bf16[1152,1024]{1,0:T(8,128)(2,1)}, u32[]{:S(2)}) copy-start(bf16[1152,1024]{1,0:T(8,128)(2,1)} %copy-done.10) | copy-start | bytes 7077892
  354.6 7.9 %copy-start.3 = (bf16[8,6,24,1024]{3,2,1,0:T(8,128)(2,1)}, bf16[8,6,24,1024]{3,2,1,0:T(8,128)(2,1)S(1)}, u32[]{:S(2)}) copy-start(bf16[8,6,24,1024]{3,2,1,0:T(8,128)(2,1)S(1)} %get-tuple-element.119) | copy-start | bytes 7077892
  355.8 27.3 %collective-permute-start.16 = (bf16[8,1,24,1024]{3,2,1,0:T(8,128)(2,1)}, bf16[8,1,24,1024]{3,2,1,0:T(8,128)(2,1)S(1)}, u32[]{:S(2)}, u32[]{:S(2)}) collective-permute-start(bf16[8,1,24,1024]{3,2,1,0:T(8,128)(2,1)} %get-tuple-element.126), channel_id=1, source_target_pairs={{0,4},{4,8},{8,12},{1,5},{5,9},{9,13},{2,6},{6,10},{10,14},{3,7},{... | collective-permute-start | bytes 1179656 | tf_op jit(solution)/shard_map/ppermute | solution.py:58
  357.1 26.0 %collective-permute-start.17 = (bf16[8,1,24,1024]{3,2,1,0:T(8,128)(2,1)}, bf16[8,1,24,1024]{3,2,1,0:T(8,128)(2,1)}, u32[]{:S(2)}, u32[]{:S(2)}) collective-permute-start(bf16[8,1,24,1024]{3,2,1,0:T(8,128)(2,1)} %get-tuple-element.127), channel_id=1, source_target_pairs={{4,0},{8,4},{12,8},{5,1},{9,5},{13,9},{6,2},{10,6},{14,10},{7,3},{... | collective-permute-start | bytes 1179656 | tf_op jit(solution)/shard_map/ppermute | solution.py:59
  379.6 12.5 %all-to-all-start.4 = ((bf16[4,4,8,3200]{3,2,1,0:T(8,128)(2,1)}), bf16[4,4,8,3200]{3,2,1,0:T(8,128)(2,1)S(1)}, u32[]{:S(2)}, u32[]{:S(2)}) async-start(bf16[4,4,8,3200]{3,2,1,0:T(8,128)(2,1)} %copy.72), calls=%async_computation.4 | async-start | bytes 1638400 | tf_op jit(solution)/shard_map/all_to_all | solution.py:83
  383.1 13.4 %copy-start.24 = (f32[1,1,1024]{2,1,0:T(1,128)S(1)}, f32[1,1,1024]{2,1,0:T(1,128)}, u32[]{:S(2)}) copy-start(f32[1,1,1024]{2,1,0:T(1,128)} %get-tuple-element.163) | copy-start | bytes 12292
  392.9 17.4 %all-to-all-start.5 = ((bf16[4,8,3200]{2,1,0:T(8,128)(2,1)}), bf16[4,8,3200]{2,1,0:T(8,128)(2,1)S(1)}, u32[]{:S(2)}, u32[]{:S(2)}) async-start(bf16[4,8,3200]{2,1,0:T(8,128)(2,1)} %reduce_sum.366), calls=%async_computation.5 | async-start | bytes 409600 | tf_op jit(solution)/shard_map/all_to_all | solution.py:213
  396.3 107.1 %all-gather.9.cloned.1.call-start = ((), (), s32[]{:S(2)}) async-start(), calls=%async_computation.8 | async-start | bytes 3311616 | tf_op jit(solution)/shard_map/all_gather | solution.py:216
  411.1 5.5 copy-start.16
  411.1 142.1 %all-gather.7.cloned.1.call-start = ((), (), s32[]{:S(2)}) async-start(), calls=%async_computation.7 | async-start | bytes 4491264 | tf_op jit(solution)/shard_map/all_gather | solution.py:251
  411.2 5.5 copy-start.14
  417.3 8.7 %collective-permute-start.18 = (bf16[4,4,4,8,2176]{4,3,2,1,0:T(8,128)(2,1)S(1)}, bf16[4,4,4,8,2176]{4,3,2,1,0:T(8,128)(2,1)S(1)}, u32[]{:S(2)}, u32[]{:S(2)}) collective-permute-start(bf16[4,4,4,8,2176]{4,3,2,1,0:T(8,128)(2,1)S(1)} %dynamic-slice_bitcast_fusion.1), channel_id=1, source_target_pairs={{0,16},{16,0},{1,17},{17,1},{2,18},{18,2},{3,19},{19,3},{4,20},{20... | collective-permute-start | bytes 6684680 | tf_op jit(solution)/shard_map/ppermute | solution.py:91
  553.3 5.0 slice-start.2
  (18 other events, 42.9 us)
Sparse Core Ops, SparseCore 0:
  10.9 78.1 all-gather.4
  411.3 53.6 all-gather.8
  487.1 66.1 all-gather.6

commit v2 on v1

v2 whole, which is shorter than its diff:
```python
import functools

import jax
import jax.numpy as jnp
import numpy as np
from jax import lax
from jax.experimental import pallas as pl
from jax.experimental.pallas import tpu as pltpu
from jax.sharding import Mesh, PartitionSpec as P

SLOT = 4
EPS = 1e-06
BF = jnp.bfloat16
F32 = jnp.float32
LANES = 128
VMEM_LIMIT = 56 * 1024 * 1024
NN = ((1,), (0,))
NT = ((1,), (1,))
TN = ((0,), (0,))


def dot(a, b, dims=NN):
    return lax.dot_general(a, b, (dims, ((), ())), preferred_element_type=F32)


def sigmoid(v):
    return 0.5 * jnp.tanh(0.5 * v) + 0.5


def silu(v):
    return v * sigmoid(v)


def silu_slope(v):
    s = sigmoid(v)
    return s * (1.0 + v * (1.0 - s))


def gelu_parts(v):
    c = 0.7978845608028654
    square = v * v
    t = jnp.tanh(v * (c + (c * 0.044715) * square))
    half = 0.5 * (1.0 + t)
    slope = half + 0.5 * v * (1.0 - t * t) * (c + (3.0 * c * 0.044715) * square)
    return v * half, slope


def chunks(count, body, width=LANES):
    def step(i, carry):
        body(pl.ds(pl.multiple_of(i * width, width), width))
        return carry

    lax.fori_loop(0, count, step, 0)


def call(kernel, *, grid, ins, outs, scratch=(), prefetch=0, flops=0, name):
    def spec(shape, block, index):
        if block is None:
            block, index = shape, lambda *_: (0,) * len(shape)
        return pl.BlockSpec(block, index)

    arrays = [i[0] for i in ins]
    in_specs = [spec(a.shape, b, m) for a, b, m in ins]
    out_specs = [spec(s.shape, b, m) for s, b, m in outs]
    moved = sum(a.size * a.dtype.itemsize for a in arrays) + sum(s[0].size * s[0].dtype.itemsize for s in outs)

    def run(*scalars):
        return pl.pallas_call(
            kernel,
            grid_spec=pltpu.PrefetchScalarGridSpec(
                num_scalar_prefetch=prefetch,
                grid=grid,
                in_specs=in_specs,
                out_specs=out_specs,
                scratch_shapes=list(scratch),
            ),
            out_shape=[s[0] for s in outs],
            compiler_params=pltpu.CompilerParams(
                dimension_semantics=("arbitrary",) * len(grid), vmem_limit_bytes=VMEM_LIMIT
            ),
            cost_estimate=pl.CostEstimate(flops=flops, bytes_accessed=int(moved), transcendentals=0),
            name=name,
        )(*scalars, *arrays)

    return run


def shape(dims, dtype):
    return jax.ShapeDtypeStruct(dims, dtype)


def columns_moved(t, by, first, last):
    rows = t.shape[0]
    return pltpu.roll(t, by % rows, 0) * (first if by > 0 else last)


def edge_masks(rows, width, depth):
    at = lax.broadcasted_iota(jnp.int32, (rows, LANES), 0) % (width * depth)
    return (at >= depth).astype(F32), (at < (width - 1) * depth).astype(F32)


def pre_forward(order, reduced, above, below, features, pre_reduce, taps, pre_expand, gain, pool):
    slots, cells, ch = reduced.shape
    high, wide = features.shape[1], features.shape[2]
    n = order.shape[0]
    part = slots // n

    def kernel(order_ref, red, up_ref, down_ref, feat, wr, tap, we, gn, pool_ref, conv_out, act_out, norm_out, std_out, pooled_out, halo, exp, sums):
        k = pl.program_id(0)

        @pl.when(k == 0)
        def _():
            for side, ref in enumerate((up_ref, down_ref)):
                halo[side] = dot(ref[...].reshape(slots * wide, ch), wr[...]).reshape(slots, wide, ch)

        first, last = edge_masks(wide, wide, 1)
        at = order_ref[k] * part
        for u in range(part):

            def conv(lanes):
                w = [tap[pl.ds(i, 1), lanes] for i in range(9)]
                rows = [halo[0, at + u, :, lanes]]
                rows += [red[u, pl.ds(i * wide, wide), lanes] for i in range(high)]
                rows += [halo[1, at + u, :, lanes]]
                rows = [silu(r).astype(BF).astype(F32) for r in rows]
                acts = []
                for i in range(high):
                    t = [sum(rows[i + a] * w[3 * a + b] for a in range(3)) for b in range(3)]
                    c = t[1] + columns_moved(t[0], 1, first, last) + columns_moved(t[2], -1, first, last)
                    conv_out[u, pl.ds(i * wide, wide), lanes] = c
                    acts.append(silu(c))
                act_out[u, :, lanes] = jnp.concatenate(acts, 0).astype(BF)

            chunks(ch // LANES, conv)

        exp[...] = dot(act_out[...].reshape(part * cells, ch), we[...])

        def norm(p, carry):
            u, i = p // (high // 2), p % (high // 2)
            total = [0.0] * (wide // 8)
            for half in range(2):
                f = feat[u, 2 * i + half].astype(F32)
                for t in range(wide // 8):
                    row = (2 * i + half) * wide + 8 * t
                    e = exp[pl.ds(pl.multiple_of(u * cells + row, 8), 8), :]
                    mean = jnp.mean(e, -1, keepdims=True)
                    square = jnp.mean(e * e, -1, keepdims=True)
                    std = lax.rsqrt(square - mean * mean + EPS)
                    nrm = (e - mean) * std
                    norm_out[u, pl.ds(pl.multiple_of(row, 8), 8), :] = nrm
                    std_out[u, pl.ds(pl.multiple_of(row, 8), 8), :] = std
                    total[t] = total[t] + f[8 * t : 8 * t + 8] + silu(nrm * gn[...])
            for t in range(wide // 8):
                sums[pl.ds(pl.multiple_of(p * wide + 8 * t, 8), 8), :] = total[t]
            return carry

        lax.fori_loop(0, part * high // 2, norm, 0)
        s = sums[...]
        hi = s.astype(BF)
        lo = (s - hi.astype(F32)).astype(BF)
        pooled_out[0] = (dot(pool_ref[...], hi) + dot(pool_ref[...], lo)).astype(BF)

    def by_order(rest):
        return lambda k, order: (order[k],) + (0,) * rest

    pooled_rows = pool.shape[0]
    return call(
        kernel,
        grid=(n,),
        prefetch=1,
        ins=[
            (reduced, (part, cells, ch), by_order(2)),
            (above, None, None),
            (below, None, None),
            (features, (part, high, wide, ch), by_order(3)),
            (pre_reduce, None, None),
            (taps, None, None),
            (pre_expand, None, None),
            (gain, None, None),
            (pool, None, None),
        ],
        outs=[
            (shape((slots, cells, ch), F32), (part, cells, ch), by_order(2)),
            (shape((slots, cells, ch), BF), (part, cells, ch), by_order(2)),
            (shape((slots, cells, ch), F32), (part, cells, ch), by_order(2)),
            (shape((slots, cells, 1), F32), (part, cells, 1), by_order(2)),
            (shape((n, pooled_rows, ch), BF), (1, pooled_rows, ch), lambda k, order: (k, 0, 0)),
        ],
        scratch=[
            pltpu.VMEM((2, slots, wide, ch), F32),
            pltpu.VMEM((part * cells, ch), F32),
            pltpu.VMEM((part * cells // 2, ch), F32),
        ],
        flops=2 * slots * cells * ch * ch,
        name="pre_forward",
    )(order)


def post_forward(source, moved, weights, gain, taps, pool):
    n, rows, ch = moved.shape
    total = n * rows
    depth = total // (pool * pool)
    share = ch // n

    def kernel(src, got, w, gn, tap, flat_out, red_out, act_out, conv_out, cact_out, norm_out, std_out, low_out, wide_ref):
        for r in range(n):
            wide_ref[pl.ds(r * rows, rows), :] = got[src[r]].astype(F32)
        flat_out[...] = wide_ref[...].astype(BF)
        red = 0.0
        for c in range(n):
            red = red + dot(flat_out[:, c * share : (c + 1) * share], w[c, 0])
        red_out[...] = red
        first, last = edge_masks(total, pool, depth)
        step = pool * depth

        def conv(lanes):
            x = silu(red_out[:, lanes]).astype(BF)
            act_out[:, lanes] = x
            x = x.astype(F32)
            moves = [columns_moved(x, depth, first, last), x, columns_moved(x, -depth, first, last)]
            t = [sum(moves[b] * tap[pl.ds(3 * a + b, 1), lanes] for b in range(3)) for a in range(3)]
            none = jnp.zeros((step, LANES), F32)
            c = t[1] + jnp.concatenate([none, t[0][:-step]], 0) + jnp.concatenate([t[2][step:], none], 0)
            conv_out[:, lanes] = c
            cact_out[:, lanes] = silu(c).astype(BF)

        chunks(ch // LANES, conv)
        for c in range(n):
            wide2 = dot(cact_out[...], w[c, 1], NT)
            norm_out[:, c * share : (c + 1) * share] = wide2

        def norm(i, carry):
            at = pl.ds(pl.multiple_of(i * 16, 16), 16)
            e = norm_out[at, :]
            mean = jnp.mean(e, -1, keepdims=True)
            square = jnp.mean(e * e, -1, keepdims=True)
            std = lax.rsqrt(square - mean * mean + EPS)
            nrm = (e - mean) * std
            norm_out[at, :] = nrm
            std_out[at, :] = std
            low_out[at, :] = (wide_ref[at, :] + silu(nrm * gn[...])).astype(BF)
            return carry

        lax.fori_loop(0, total // 16, norm, 0)

    wide = shape((total, ch), F32)
    narrow = shape((total, ch), BF)
    return call(
        kernel,
        grid=(1,),
        prefetch=1,
        ins=[(a, None, None) for a in (moved, weights, gain, taps)],
        outs=[(s, None, None) for s in (narrow, wide, narrow, wide, narrow, wide, shape((total, 1), F32), narrow)],
        scratch=[pltpu.VMEM((total, ch), F32)],
        flops=4 * total * ch * ch,
        name="post_forward",
    )(source)


def post_backward(source, low, readout, cots, weights, gain, taps, act, red, conv, nrm, std, pool):
    total, ch = low.shape
    n = cots.shape[0]
    share = ch // n
    out_share = cots.shape[2]
    rows = total // n
    depth = total // (pool * pool)

    def kernel(src, low_ref, ro, cot, w, gn, tap, act_ref, red_ref, conv_ref, norm_ref, std_ref, exp_out, redg_out, back_out, taps_out, gain_out, grad, cgrad):
        k = pl.program_id(0)
        logits = dot(low_ref[...], ro[...])
        piece = (cot[0].astype(F32) * gelu_parts(logits)[1]).astype(BF)
        term = dot(piece, ro[...], NT)

        @pl.when(k == 0)
        def _():
            grad[...] = term

        @pl.when(k > 0)
        def _():
            grad[...] += term

        @pl.when(k == n - 1)
        def _():
            def norm(i, total_gain):
                at = pl.ds(pl.multiple_of(i * 16, 16), 16)
                nm = norm_ref[at, :]
                ng = grad[at, :] * silu_slope(nm * gn[...])
                sc = ng * gn[...]
                one = jnp.mean(sc, -1, keepdims=True)
                two = jnp.mean(sc * nm, -1, keepdims=True)
                exp_out[at, :] = (std_ref[at, :] * (sc - one - nm * two)).astype(BF)
                g = ng * nm
                return total_gain + g[:8] + g[8:]

            gain_out[...] = lax.fori_loop(0, total // 16, norm, jnp.zeros((8, ch), F32))
            cg = 0.0
            for c in range(n):
                cg = cg + dot(exp_out[:, c * share : (c + 1) * share], w[c, 1])
            cgrad[...] = cg
            first, last = edge_masks(total, pool, depth)
            step = pool * depth

            def back(lanes):
                g = (cgrad[:, lanes] * silu_slope(conv_ref[:, lanes])).astype(BF).astype(F32)
                x = act_ref[:, lanes].astype(F32)
                moves = [columns_moved(g, -depth, first, last), g, columns_moved(g, depth, first, last)]
                none = jnp.zeros((step, LANES), F32)
                xs = [
                    jnp.concatenate([none, x[:-step]], 0),
                    x,
                    jnp.concatenate([x[step:], none], 0),
                ]
                for a in range(3):
                    for b in range(3):
                        prod = xs[a] * moves[b]
                        taps_out[3 * a + b, :, lanes] = jnp.sum(prod.reshape(total // 8, 8, LANES), 0)
                t = [sum(moves[b] * tap[pl.ds(3 * a + b, 1), lanes] for b in range(3)) for a in range(3)]
                d = t[1] + jnp.concatenate([t[0][step:], none], 0) + jnp.concatenate([none, t[2][:-step]], 0)
                redg_out[:, lanes] = (d * silu_slope(red_ref[:, lanes])).astype(BF)

            chunks(ch // LANES, back)
            for c in range(n):
                cut = slice(c * share, (c + 1) * share)
                grad[:, cut] += dot(redg_out[...], w[c, 0], NT)
            for r in range(n):
                at = pl.ds(pl.multiple_of(src[r] * rows, 8), rows)
                back_out[r] = grad[at, :].astype(BF)

    return call(
        kernel,
        grid=(n,),
        prefetch=1,
        ins=[
            (low, None, None),
            (readout, (ch, out_share), lambda k, s: (0, k)),
            (cots, (1, total, out_share), lambda k, s: (k, 0, 0)),
        ]
        + [(a, None, None) for a in (weights, gain, taps, act, red, conv, nrm, std)],
        outs=[
            (s, None, None)
            for s in (
                shape((total, ch), BF),
                shape((total, ch), BF),
                shape((n, rows, ch), BF),
                shape((9, 8, ch), F32),
                shape((8, ch), F32),
            )
        ],
        scratch=[pltpu.VMEM((total, ch), F32), pltpu.VMEM((total, ch), F32)],
        flops=2 * total * ch * (2 * out_share * n + 2 * ch),
        name="post_backward",
    )(source)


def cotangent_by_image(cotangent, select):
    rows, width = cotangent.shape
    size = select.shape[0]
    pairs = SLOT
    each = size // pairs
    per = 3

    def kernel(x, sel, out):
        for q in range(per):
            y = dot(sel[...], x[pl.ds(q * size, size), :]).astype(BF)
            for s in range(pairs):
                out[s, pl.ds(q * each, each), :] = y[s * each : (s + 1) * each]

    return call(
        kernel,
        grid=(rows // (per * size),),
        ins=[(cotangent, (per * size, width), lambda i: (i, 0)), (select, None, None)],
        outs=[(shape((pairs, rows // pairs, width), BF), (pairs, per * each, width), lambda i: (0, i, 0))],
        flops=2 * rows * size * width,
        name="cotangent_by_image",
    )()[0]


def token_block(chan, low, place, readout, cotangent, live):
    pairs, each_all, ch = low.shape
    rows, width = cotangent.shape
    size = place.shape[0]
    each = size // pairs
    per = 3

    def kernel(chan_ref, low_ref, place_ref, ro, cot, alive, tok_out, piece_out, low_out):
        for q in range(per):
            at = pl.ds(q * size, size)
            x = jnp.concatenate([low_ref[s, pl.ds(q * each, each), :] for s in range(pairs)], 0)
            low_out[at, :] = dot(place_ref[...], x).astype(BF)
        logits = dot(low_out[...], ro[...])
        value, slope = gelu_parts(logits)
        tok_out[...] = value.astype(BF)
        piece_out[...] = (cot[...].astype(F32) * alive[...] * slope).astype(BF)

    block = per * size
    row_block = lambda i, c: (i, 0)
    return call(
        kernel,
        grid=(rows // block,),
        prefetch=1,
        ins=[
            (low, (pairs, per * each, ch), lambda i, c: (0, i, 0)),
            (place, None, None),
            (readout, (ch, width), lambda i, c: (0, c[0])),
            (cotangent, (block, width), row_block),
            (live, None, None),
        ],
        outs=[
            (shape((rows, width), BF), (block, width), row_block),
            (shape((rows, width), BF), (block, width), row_block),
            (shape((rows, ch), BF), (block, ch), row_block),
        ],
        flops=2 * rows * ch * width,
        name="token_block",
    )(chan)


def pre_backward(order, returned, spread_up, nrm, std, gain, conv, pre_expand):
    slots, cells, ch = nrm.shape
    n = order.shape[0]
    part = slots // n
    wide = 24
    rows = part * cells

    def kernel(order_ref, ret, up, norm_ref, std_ref, gn, conv_ref, we, exp_out, conv_grad_out, top_out, bottom_out, gain_out, grad, cgrad):
        k = pl.program_id(0)
        grad[...] = dot(up[...], ret[0])

        def norm(i, total_gain):
            u, j = i // (cells // 16), i % (cells // 16)
            at = pl.ds(pl.multiple_of(j * 16, 16), 16)
            nm = norm_ref[u, at, :]
            ng = grad[pl.ds(pl.multiple_of(i * 16, 16), 16), :] * silu_slope(nm * gn[...])
            sc = ng * gn[...]
            one = jnp.mean(sc, -1, keepdims=True)
            two = jnp.mean(sc * nm, -1, keepdims=True)
            exp_out[u, at, :] = (std_ref[u, at, :] * (sc - one - nm * two)).astype(BF)
            g = ng * nm
            return total_gain + g[:8] + g[8:]

        gains = lax.fori_loop(0, rows // 16, norm, jnp.zeros((8, ch), F32))

        @pl.when(k == 0)
        def _():
            gain_out[...] = gains

        @pl.when(k > 0)
        def _():
            gain_out[...] += gains

        cgrad[...] = dot(exp_out[...].reshape(rows, ch), we[...], NT)
        for u in range(part):

            def slope(lanes):
                g = cgrad[pl.ds(u * cells, cells), lanes] * silu_slope(conv_ref[u, :, lanes])
                conv_grad_out[u, :, lanes] = g.astype(BF)
                top_out[u, :, lanes] = g[:wide].astype(BF)
                bottom_out[u, :, lanes] = g[cells - wide :].astype(BF)

            chunks(ch // LANES, slope)

    by_order = lambda k, order: (order[k], 0, 0)
    whole = (part, cells, ch)
    edge = (part, wide, ch)
    return call(
        kernel,
        grid=(n,),
        prefetch=1,
        ins=[
            (returned, (1,) + returned.shape[1:], lambda k, order: (k, 0, 0)),
            (spread_up, None, None),
            (nrm, whole, by_order),
            (std, (part, cells, 1), by_order),
            (gain, None, None),
            (conv, whole, by_order),
            (pre_expand, None, None),
        ],
        outs=[
            (shape((slots, cells, ch), BF), whole, by_order),
            (shape((slots, cells, ch), BF), whole, by_order),
            (shape((slots, wide, ch), BF), edge, by_order),
            (shape((slots, wide, ch), BF), edge, by_order),
            (shape((8, ch), F32), None, None),
        ],
        scratch=[pltpu.VMEM((rows, ch), F32), pltpu.VMEM((rows, ch), F32)],
        flops=2 * slots * cells * ch * ch,
        name="pre_backward",
    )(order)


def pre_conv_backward(conv_grad, above, below, reduced, taps):
    slots, cells, ch = reduced.shape
    wide = above.shape[1]
    high = cells // wide

    def kernel(cg, up, down, red, tap, redg_out, taps_out):
        step = pl.program_id(0)
        first, last = edge_masks(wide, wide, 1)

        @pl.when(step == 0)
        def _():
            taps_out[...] = jnp.zeros_like(taps_out)

        def back(lanes):
            w = [tap[pl.ds(i, 1), lanes] for i in range(9)]
            mid = cg[0, :, lanes].astype(F32)
            rows = [up[0, :, lanes].astype(F32)]
            rows += [mid[i * wide : (i + 1) * wide] for i in range(high)]
            rows += [down[0, :, lanes].astype(F32)]
            v = [red[0, pl.ds(i * wide, wide), lanes] for i in range(high)]
            s = [sigmoid(t) for t in v]
            x = [(a * b).astype(BF).astype(F32) for a, b in zip(v, s)]
            d = [0.0] * high
            sums = [0.0] * 9
            for p in range(high + 2):
                g = rows[p]
                moves = [columns_moved(g, -1, first, last), g, columns_moved(g, 1, first, last)]
                for a in range(3):
                    i = p - 1 + a - 1
                    if 0 <= i < high:
                        for b in range(3):
                            d[i] = d[i] + moves[b] * w[3 * a + b]
                            prod = x[i] * moves[b]
                            sums[3 * a + b] = sums[3 * a + b] + (prod[:8] + prod[8:16] + prod[16:])
            out = [d[i] * (s[i] * (1.0 + v[i] * (1.0 - s[i]))) for i in range(high)]
            redg_out[0, :, lanes] = jnp.concatenate(out, 0).astype(BF)
            for i in range(9):
                taps_out[i, :, lanes] += sums[i]

        chunks(ch // LANES, back)

    image = lambda i: (i, 0, 0)
    return call(
        kernel,
        grid=(slots,),
        ins=[
            (conv_grad, (1, cells, ch), image),
            (above, (1, wide, ch), image),
            (below, (1, wide, ch), image),
            (reduced, (1, cells, ch), image),
            (taps, None, None),
        ],
        outs=[
            (shape((slots, cells, ch), BF), (1, cells, ch), image),
            (shape((9, 8, ch), F32), None, None),
        ],
        flops=0,
        name="pre_conv_backward",
    )()


def feature_backward(order, reduced_grad, pre_reduce, returned, spread_up):
    slots, cells, ch = reduced_grad.shape
    n = order.shape[0]
    part = slots // n

    def kernel(order_ref, rg, wr, ret, up, out):
        g = dot(rg[...].reshape(part * cells, ch), wr[...], NT) + dot(up[...], ret[0])
        out[...] = g.reshape(part, cells, ch)

    by_order = lambda k, order: (order[k], 0, 0)
    whole = (part, cells, ch)
    return call(
        kernel,
        grid=(n,),
        prefetch=1,
        ins=[
            (reduced_grad, whole, by_order),
            (pre_reduce, None, None),
            (returned, (1,) + returned.shape[1:], lambda k, order: (k, 0, 0)),
            (spread_up, None, None),
        ],
        outs=[(shape((slots, cells, ch), F32), whole, by_order)],
        flops=2 * slots * cells * ch * ch,
        name="feature_backward",
    )(order)[0]


def spread(n, k):
    return [(a * n + b, b * n + (a + k) % n) for a in range(n) for b in range(n)]


def scatter_sum(blocks, axis):
    got = lax.all_to_all(blocks, axis, 0, 0, tiled=False)
    return jnp.sum(got.astype(F32), axis=0).astype(BF)


def core_sum(blocks):
    me = lax.axis_index("core")
    keep = lax.dynamic_index_in_dim(blocks, me, 0, keepdims=False)
    send = lax.dynamic_index_in_dim(blocks, 1 - me, 0, keepdims=False)
    got = lax.ppermute(send, "core", [(0, 1), (1, 0)])
    return (keep.astype(F32) + got.astype(F32)).astype(BF)


def pool_matrix(part, high, wide):
    half = wide // 2
    m = np.zeros((high // 2 * half * part, part * (high // 2) * wide), np.float32)
    for u in range(part):
        for i in range(high // 2):
            for j in range(wide):
                m[(i * half + j // 2) * part + u, (u * (high // 2) + i) * wide + j] = 0.25
    return m


def spread_matrix(part, high, wide):
    half = wide // 2
    m = np.zeros((part * high * wide, high // 2 * half * part), np.float32)
    for u in range(part):
        for i in range(high):
            for j in range(wide):
                m[(u * high + i) * wide + j, ((i // 2) * half + j // 2) * part + u] = 0.25
    return m


def place_matrix(cells, slots, pairs):
    per = slots // pairs
    m = np.zeros((cells * slots, cells * slots), np.float32)
    for c in range(cells):
        for s in range(slots):
            m[c * slots + s, (s // per) * cells * per + c * per + s % per] = 1.0
    return m


def body(features, counts, pre_reduce, pre_conv, pre_expand, pre_gain, post_reduce, post_conv, post_expand, post_gain, readout, cotangent):
    n = lax.axis_size("chan")
    row = lax.axis_index("rows").astype(jnp.int32)
    chan = lax.axis_index("chan").astype(jnp.int32)
    ch = pre_reduce.shape[0]
    slots, high, wide = features.shape[0], features.shape[1], features.shape[2]
    part = slots // n
    cells = high * wide
    pool = wide // 2
    share = ch // n
    out_share = cotangent.shape[3]
    steps = jnp.arange(n, dtype=jnp.int32)
    order = (row + steps) % n
    source = (chan - steps) % n
    rank = jnp.full((1,), chan, jnp.int32)
    pre_taps = pre_conv.astype(F32).reshape(9, ch)
    post_taps = post_conv.astype(F32).reshape(9, ch)
    pre_gain_row = pre_gain.reshape(1, ch)
    pool_m = jnp.asarray(pool_matrix(part, high, wide), BF)
    up_m = jnp.asarray(spread_matrix(part, high, wide), BF)
    place = jnp.asarray(place_matrix(16, slots, n), BF)

    ends = n - 1
    down_pairs = [(i, i + 1) for i in range(ends)]
    up_pairs = [(i + 1, i) for i in range(ends)]
    above = lax.ppermute(features[:, -1], "rows", down_pairs)
    below = lax.ppermute(features[:, 0], "rows", up_pairs)
    gain_hi = post_gain.astype(BF)
    gain_lo = (post_gain - gain_hi.astype(F32)).astype(BF)
    extra = jnp.zeros((16, ch), BF).at[0, :share].set(gain_hi).at[0, share : 2 * share].set(gain_lo)
    shards = jnp.concatenate([post_reduce, post_expand.T, extra], axis=0)
    full = lax.all_gather(shards, "chan", axis=0, tiled=False)
    weights = full[:, : 2 * share].reshape(n, 2, share, ch)
    gain_parts = full[:, 2 * share].astype(F32)
    post_gain_row = (gain_parts[:, :share] + gain_parts[:, share : 2 * share]).reshape(1, ch)
    live = (jnp.arange(SLOT)[None, :] < counts[:, None]).astype(F32).reshape(slots)
    select = place.T * jnp.tile(live.astype(BF), 16)[None, :]
    cot_rows = cotangent.transpose(1, 2, 0, 3).reshape(-1, out_share)
    cots = lax.all_to_all(cotangent_by_image(cot_rows, select), "chan", 0, 0, tiled=False)

    flat_features = features.reshape(slots * cells, ch)
    reduced = dot(flat_features, pre_reduce).reshape(slots, cells, ch)
    convolved, convolved_act, normal_pre, pre_std, pooled = pre_forward(
        order, reduced, above, below, features, pre_reduce, pre_taps, pre_expand, pre_gain_row, pool_m
    )

    moved = jnp.stack([lax.ppermute(pooled[k], ("rows", "chan"), spread(n, k)) for k in range(n)])
    flat, post_reduced, post_act, post_convolved, post_cact, post_normal, post_std, low = post_forward(
        source, moved, weights, post_gain_row, post_taps, pool
    )
    low_all = lax.all_gather(low, "chan", axis=0, tiled=False)
    post_expanded_grad, post_reduced_grad, back, post_taps_grad, post_gain_grad = post_backward(
        source, low, readout, cots, weights, post_gain_row, post_taps, post_act, post_reduced, post_convolved, post_normal, post_std, pool
    )

    returned = jnp.stack(
        [lax.ppermute(back[k], ("rows", "chan"), [(d, s) for s, d in spread(n, k)]) for k in range(n)]
    )
    post_reduce_grad = dot(flat, post_reduced_grad, TN).astype(BF)
    post_expand_grad_t = dot(post_expanded_grad, post_cact, TN).astype(BF)

    expanded_grad, convolved_grad, top, bottom, pre_gain_grad = pre_backward(
        order, returned, up_m, normal_pre, pre_std, pre_gain_row, convolved, pre_expand
    )
    grad_above = lax.ppermute(bottom, "rows", down_pairs)
    grad_below = lax.ppermute(top, "rows", up_pairs)
    pre_expand_grad = dot(convolved_act.reshape(-1, ch), expanded_grad.reshape(-1, ch), TN).astype(BF)
    reduced_grad, pre_taps_grad = pre_conv_backward(convolved_grad, grad_above, grad_below, reduced, pre_taps)
    pre_reduce_grad = dot(flat_features, reduced_grad.reshape(-1, ch), TN).astype(BF)
    feature_grad = feature_backward(order, reduced_grad, pre_reduce, returned, up_m).reshape(features.shape)

    alive = jnp.broadcast_to(jnp.tile(live, 48)[:, None], (48 * slots, 1))
    tokens, piece, low_here = token_block(rank, low_all, place, readout, cot_rows, alive)
    readout_grad = dot(low_here, piece, TN).astype(BF)
    tokens = tokens.reshape(pool, pool, slots, out_share).transpose(2, 0, 1, 3)

    eight = share // 32
    tail = jnp.zeros((n, share, LANES), F32)
    tail = tail.at[:, : share // LANES].set(jnp.sum(post_gain_grad, 0).reshape(n, share // LANES, LANES))
    taps_rows = jnp.sum(post_taps_grad, 1).reshape(-1, LANES)
    tail = tail.at[:, share // LANES : share // LANES + taps_rows.shape[0]].set(taps_rows[None])
    load = jnp.concatenate(
        [
            post_reduce_grad.reshape(n, share, ch),
            post_expand_grad_t.reshape(n, share, ch),
            tail.astype(BF),
            readout_grad.reshape(n, share, out_share),
        ],
        axis=2,
    )
    load = load.reshape(n, 2, 4, 4, eight, -1).transpose(1, 2, 3, 0, 4, 5)
    load = scatter_sum(scatter_sum(core_sum(load), "x"), "rows")
    load = lax.all_to_all(load, "chan", 0, 0, tiled=False)
    cut = 2 * ch + LANES
    summed = jnp.sum(load[:, :, :cut].astype(F32), axis=0).astype(BF)
    mine = jnp.concatenate([summed] + [load[j, :, cut:] for j in range(n)], axis=1)
    post_all = lax.all_gather(mine, ("core", "x", "rows"), axis=0, tiled=True).astype(F32)
    post_reduce_out = post_all[:, :ch]
    post_expand_out = post_all[:, ch : 2 * ch].T
    tail_out = post_all[:, 2 * ch : cut]
    post_gain_out = tail_out[: share // LANES].reshape(share)
    post_conv_out = tail_out[share // LANES : share // LANES + taps_rows.shape[0]].reshape(3, 3, ch)
    readout_out = post_all[:, cut:]

    tail = jnp.concatenate([jnp.sum(pre_taps_grad, 1).reshape(-1, LANES), jnp.sum(pre_gain_grad, 0).reshape(-1, LANES)], axis=0)
    tail = jnp.pad(tail, ((0, ch - tail.shape[0]), (0, 0))).astype(BF)
    load = jnp.concatenate([pre_reduce_grad, pre_expand_grad, tail], axis=1).reshape(2, 4, 4, 4, ch // 128, -1)
    load = scatter_sum(scatter_sum(scatter_sum(core_sum(load), "x"), "rows"), "chan")
    pre_all = lax.all_gather(load, ("core", "x", "rows", "chan"), axis=0, tiled=True).astype(F32)
    taps = 9 * ch // LANES
    return (
        tokens,
        feature_grad,
        pre_all[:, :ch],
        pre_all[:taps, 2 * ch :].reshape(3, 3, ch),
        pre_all[:, ch : 2 * ch],
        pre_all[taps : taps + ch // LANES, 2 * ch :].reshape(ch),
        post_reduce_out,
        post_conv_out,
        post_expand_out,
        post_gain_out,
        readout_out,
    )


def solution(mesh):
    grid = Mesh(mesh.devices.reshape(4, 2, 4, 4), ("x", "core", "rows", "chan"))
    images = P(("x", "core", "chan"), "rows", None, None)
    grids = P(("x", "core", "rows"), None, None, "chan")
    return jax.shard_map(
        body,
        mesh=grid,
        in_specs=(
            images,
            P(("x", "core", "rows")),
            P(),
            P(),
            P(),
            P(),
            P("chan", None),
            P(),
            P(None, "chan"),
            P("chan"),
            P(),
            grids,
        ),
        out_specs=(grids, images, P(), P(), P(), P(), P("chan", None), P(), P(None, "chan"), P("chan"), P("chan", None)),
        check_vma=False,
    )
```

time: 577 us -> 446 us (0.77); the launches traced: 570 us -> 444 us
  Pallas kernels: 0 us -> 109 us
  other arithmetic: 101 us -> 35.3 us
  matrix products: 91.2 us -> 30.4 us
  local copies, waits for them, and re-layouts: 106 us -> 47.3 us
  waiting for transfers between devices: 108 us -> 79.8 us
  blocking collectives: 89.1 us -> 73.6 us
    pallas_call x0 -> x8, Pallas kernels: none -> 109 us  [run(): pl.pallas_call(kernel, grid_spec=pltpu.PrefetchScalarGridSpec(num_scalar_...]
    dot_general x18 -> x6, matrix products: 91.2 us -> 30.4 us  [dot(): return lax.dot_general(a, b, (dims, ((), ())), preferred_element_type=F32)]
    convert_element_type x9 -> x3, other arithmetic: 38.3 us -> 1.62 us  [the longest x1 0.85 us: body(): gain_parts = full[:, 2 * share].astype(F32)]
    all_gather x1, waiting for transfers between devices: 34.6 us -> 0.01 us  [body(): lax.all_gather(load, ('core', 'x', 'rows', 'chan'), axis=0, tiled=True)]
    reduce_sum x5, other arithmetic: 35.7 us -> 1.95 us  [the longest x1 1.04 us: body(): jnp.sum(pre_taps_grad, 1).reshape(-1, LANES)]
    all_gather x1 -> x0, blocking collectives: 31.4 us -> none  [body(): gain_all = lax.all_gather(post_gain, 'chan', axis=0, tiled=True)]
    all_gather x1, waiting for transfers between devices: 0.01 us -> 28.5 us  [body(): lax.all_gather(mine, ('core', 'x', 'rows'), axis=0, tiled=True).astype(F32)]
    reshape x13 -> x8, local copies, waits for them, and re-layouts: 25.9 us -> 3.34 us  [the longest x1 0.65 us: body(): post_taps = post_conv.astype(F32).reshape(9, ch)]
  transfers between devices with their start and end apart: 26 -> 21, of which waited for: 6 -> 8; matrix products, arithmetic and copies ran while one was open for 45% -> 20% of each run, Pallas kernels for 0% -> 20%
where the time goes in v2:
time: 446 us; the launch traced here: 444 us
  Pallas kernels  109 us (24%)
  waiting for transfers between devices  79.8 us (18%)
  blocking collectives  73.6 us (17%)
  starting transfers between devices  54.8 us (12%)
  local copies, waits for them, and re-layouts  47.3 us (11%)
  other arithmetic  35.3 us (8%)
  matrix products  30.4 us (7%)
  between operations  14.2 us (3%)
    pallas_call x8, Pallas kernels, run(): pl.pallas_call(kernel, grid_spec=pltpu.PrefetchScalarGridSpec(num_scalar_...  109 us
    all_to_all x3, blocking collectives, scatter_sum(): got = lax.all_to_all(blocks, axis, 0, 0, tiled=False)  66 us
    ppermute x4, waiting for transfers between devices, body(): lax.ppermute(pooled[k], ('rows', 'chan'), spread(n, k))  39.2 us
    dot_general x6, matrix products, dot(): return lax.dot_general(a, b, (dims, ((), ())), preferred_element_type=F32)  30.4 us
    all_gather x1, waiting for transfers between devices, body(): lax.all_gather(mine, ('core', 'x', 'rows'), axis=0, tiled=True).astype(F32)  28.5 us
    all_to_all x2, starting transfers between devices, scatter_sum(): got = lax.all_to_all(blocks, axis, 0, 0, tiled=False)  12.1 us
    ppermute x4, starting transfers between devices, body(): lax.ppermute(back[k], ('rows', 'chan'), [(d, s) for s, d in spread(n, k)])  11.1 us
    ppermute x4, starting transfers between devices, body(): lax.ppermute(pooled[k], ('rows', 'chan'), spread(n, k))  10.5 us
  transfers between devices with their start and end apart: 21, of which 8 were waited for; matrix products, arithmetic and copies ran while one was open for 20% of the time, Pallas kernels for 20%

profile of v2, /device:TPU:1, one launch (start us, length us, event | category | flops | bytes accessed | tf_op | source)
XLA Modules:
  0.0 444.5 jit_solution(11393233100845307664)
XLA Ops:
  8.6 1.3 and_reduce_fusion
  9.9 1.2 copy.88
  11.1 2.0 broadcast_select_fusion
  13.2 1.5 scatter.15
  14.7 2.1 pad_maximum_fusion.2
  16.9 1.2 slice_bitcast_fusion.1
  18.0 4.1 collective-permute-start
  22.1 1.3 collective-permute-start.1
  24.3 4.4 cotangent_by_image.1
  28.8 5.3 %all-to-all-start = ((bf16[4,288,1024]{2,1,0:T(8,128)(2,1)}), bf16[4,288,1024]{2,1,0:T(8,128)(2,1)}, u32[]{:S(2)}, u32[]{:S(2)}) async-start(bf16[4,288,1024]{2,1,0:T(8,128)(2,1)} %cotangent_by_image.1), calls=%async_computation | async-start | bytes 4718592 | tf_op jit(solution)/shard_map/all_to_all | solution.py:663
  35.3 5.9 %fusion.2.red = f32[8,144,1024]{2,1,0:T(8,128)} fusion(bf16[8,144,1024]{2,1,0:T(8,128)(2,1)} %bitcast.133, bf16[1024,1024]{1,0:T(8,128)(2,1)S(1)} %copy-done.1), kind=kOutput, calls=%fused_computation.9 | convolution fusion | flops 2415919104 | bytes 9175040 | tf_op jit(solution)/shard_map/dot_general | solution.py:23
  41.9 22.1 %pre_forward.1 = (f32[8,144,1024]{2,1,0:T(8,128)}, bf16[8,144,1024]{2,1,0:T(8,128)(2,1)}, f32[8,144,1024]{2,1,0:T(8,128)}, f32[8,144,1]{2,1,0:T(8,128)}, bf16[4,72,1024]{2,1,0:T(8,128)(2,1)}) custom-call(s32[4]{0:T(128)} %and_select_fusion.order_ref, f32[8,144,1024]{2,1,0:T(8,128)} %fusion.2.red, bf16[8,24,1024]{2,1,0:T(8,128)(2,1)} %copy-done.6, ...), custom_call_target="tpu_custom_call" | custom-call | flops 2415919104 | bytes 24511232 | tf_op jit(solution)/shard_map/pre_forward/pallas_call | solution.py:68
  64.0 1.2 slice_bitcast_fusion.10
  65.2 3.2 collective-permute-start.4
  68.4 4.2 collective-permute-start.5
  73.3 2.5 collective-permute-start.3
  76.9 33.2 %collective-permute-done.4 = bf16[72,1024]{1,0:T(8,128)(2,1)S(1)} collective-permute-done((bf16[72,1024]{1,0:T(8,128)(2,1)S(1)}, bf16[72,1024]{1,0:T(8,128)(2,1)S(1)}, u32[]{:S(2)}, u32[]{:S(2)}) %collective-permute-start.4) | collective-permute-done | bytes 147488 | tf_op jit(solution)/shard_map/ppermute | solution.py:671
  110.1 6.0 %collective-permute-done.3 = bf16[72,1024]{1,0:T(8,128)(2,1)S(1)} collective-permute-done((bf16[72,1024]{1,0:T(8,128)(2,1)S(1)}, bf16[72,1024]{1,0:T(8,128)(2,1)S(1)}, u32[]{:S(2)}, u32[]{:S(2)}) %collective-permute-start.3) | collective-permute-done | bytes 147488 | tf_op jit(solution)/shard_map/ppermute | solution.py:671
  117.0 4.6 %slice.198 = bf16[4,512,1024]{2,1,0:T(8,128)(2,1)} slice(bf16[4,528,1024]{2,1,0:T(8,128)(2,1)} %bitcast.135), slice={[0:4], [0:512], [0:1024]} | slice | bytes 8388608 | tf_op jit(solution)/shard_map/slice | solution.py:657
  123.1 10.8 %post_forward.1 = (bf16[288,1024]{1,0:T(8,128)(2,1)}, f32[288,1024]{1,0:T(8,128)}, bf16[288,1024]{1,0:T(8,128)(2,1)}, f32[288,1024]{1,0:T(8,128)}, bf16[288,1024...) custom-call(s32[4]{0:T(128)} %and_select_fusion.1.src, ...), custom_call_target="tpu_custom_call" | custom-call | flops 1207959552 | bytes 10724480 | tf_op jit(solution)/shard_map/post_forward/pallas_call | solution.py:68
  133.9 20.6 %post_backward.1 = (bf16[288,1024]{1,0:T(8,128)(2,1)}, bf16[288,1024]{1,0:T(8,128)(2,1)}, bf16[4,72,1024]{2,1,0:T(8,128)(2,1)}, f32[9,8,1024]{2,1,0:T(8,128)}, f32[8,1024]{1,0:T(8,128)}) custom-call(s32[4]{0:T(128)} %and_select_fusion.1.src, bf16[288,1024]{1,0:T(8,128)(2,1)} %get-tuple-element.88.low_ref, bf16[1024,4096]{1,0:T(8,128)(2,1)} %ro.3, ...), custom_call_target="tpu_custom_call" | custom-call | flops 6039797760 | bytes 21800064 | tf_op jit(solution)/shard_map/post_backward/pallas_call | solution.py:68
  154.5 1.2 slice_bitcast_fusion.6
  156.6 10.1 %collective-permute-start.8 = (bf16[72,1024]{1,0:T(8,128)(2,1)S(1)}, bf16[72,1024]{1,0:T(8,128)(2,1)S(1)}, u32[]{:S(2)}, u32[]{:S(2)}) collective-permute-start(bf16[72,1024]{1,0:T(8,128)(2,1)S(1)} %get-tuple-element.191), channel_id=1, source_target_pairs={{2,0},{6,1},{10,2},{14,3},{3,4},{7,5},{11,6},{15,7},{0,8},{4,9},{8... | collective-permute-start | bytes 442376 | tf_op jit(solution)/shard_map/ppermute | solution.py:681
  166.8 2.1 collective-permute-done.8
  168.9 3.1 collective-permute-done.9
  172.9 21.2 %pre_backward.1 = (bf16[8,144,1024]{2,1,0:T(8,128)(2,1)}, bf16[8,144,1024]{2,1,0:T(8,128)(2,1)}, bf16[8,24,1024]{2,1,0:T(8,128)(2,1)}, bf16[8,24,1024]{2,1,0:T(8,128)(2,1)}, f32[8,1024]{1,0:T(8,128)}) custom-call(s32[4]{0:T(128)} %and_select_fusion.order_ref, bf16[4,72,1024]{2,1,0:T(8,128)(2,1)} %pad_maximum_fusion.4.ret, ...), custom_call_target="tpu_custom_call" | custom-call | flops 2415919104 | bytes 17712128 | tf_op jit(solution)/shard_map/pre_backward/pallas_call | solution.py:68
  194.1 3.5 collective-permute-start.10
  197.7 1.3 collective-permute-start.11
  199.9 6.7 %bitcast_convert_fusion = bf16[1024,1024]{0,1:T(8,128)(2,1)} fusion(bf16[8,144,1024]{2,1,0:T(8,128)(2,1)} %get-tuple-element.103, bf16[8,144,1024]{2,1,0:T(8,128)(2,1)} %get-tuple-element.104), kind=kOutput, calls=%fused_computation.6 | convolution fusion | flops 2416967680 | bytes 6815744 | tf_op jit(solution)/shard_map/dot_general | solution.py:23
  208.0 12.2 %pre_conv_backward.1 = (bf16[8,144,1024]{2,1,0:T(8,128)(2,1)}, f32[9,8,1024]{2,1,0:T(8,128)}) custom-call(bf16[8,144,1024]{2,1,0:T(8,128)(2,1)} %get-tuple-element.99.cg, bf16[8,24,1024]{2,1,0:T(8,128)(2,1)} %copy-done.7, bf16[8,24,1024]{2,1,0:T(8,128)(2,1)} %copy-done.8, f32[8,144,1024]{2,1,0:T(8,128)} %fusion.2.red, f32[9,1024]{1,0:T(8,128)} %reshape.279.tap), custom_call_target="tpu_custom_call" | custom-call | bytes 10555392 | tf_op jit(solution)/shard_map/pre_conv_backward/pallas_call | solution.py:68
  221.5 5.0 %convert_bitcast_fusion = bf16[1024,1024]{0,1:T(8,128)(2,1)S(1)} fusion(bf16[1152,1024]{1,0:T(8,128)(2,1)} %bitcast.137, bf16[1152,1024]{1,0:T(8,128)(2,1)S(1)} %bitcast.134), kind=kOutput, calls=%fused_computation.11 | convolution fusion | flops 2416967680 | bytes 6815744 | tf_op jit(solution)/shard_map/dot_general | solution.py:23
  226.4 2.4 pad_maximum_fusion.1
  228.8 6.6 %copy.93 = bf16[1024,2176]{1,0:T(8,128)(2,1)} copy(bf16[1024,2176]{0,1:T(8,128)(2,1)} %pad_maximum_fusion.1) | data formatting | bytes 8912896 | tf_op jit(solution)/shard_map/concatenate | solution.py:731
  235.4 1.8 dynamic-slice_bitcast_fusion
  237.2 4.2 collective-permute-start.12
  242.2 3.7 convolution_convert_fusion.2
  245.9 4.2 fusion.1
  250.1 4.1 all-to-all-start.1
  254.2 3.8 convolution_convert_fusion.1
  258.5 9.7 %token_block.1 = (bf16[1152,1024]{1,0:T(8,128)(2,1)}, bf16[1152,1024]{1,0:T(8,128)(2,1)}, bf16[1152,1024]{1,0:T(8,128)(2,1)}) custom-call(s32[1]{0:T(128)} %bitcast.chan_ref, bf16[4,288,1024]{2,1,0:T(8,128)(2,1)} %bitcast.138, bf16[128,128]{1,0:T(8,128)(2,1)} %constant.181.place_ref, bf16[1024,4096]{1,0:T(8,128)(2,1)} %ro.3, bf16[1152,1024]{1,0:T(8,128)(2,1)} %bitcast.131, ...), custom_call_target="tpu_custom_call" | custom-call | flops 2415919104 | bytes 20219392 | tf_op jit(solution)/shard_map/token_block/pallas_call | solution.py:68
  268.3 5.5 %convolution_convert_fusion = bf16[1024,1024]{1,0:T(8,128)(2,1)S(1)} fusion(bf16[1152,1024]{1,0:T(8,128)(2,1)} %get-tuple-element.113, bf16[1152,1024]{1,0:T(8,128)(2,1)} %get-tuple-element.114), kind=kOutput, calls=%fused_computation.12 | convolution fusion | flops 2416967680 | bytes 6815744 | tf_op jit(solution)/shard_map/dot_general | solution.py:23
  273.8 3.2 pad_maximum_fusion
  277.0 4.8 %all-to-all-done.1 = bf16[4,4,4,8,2176]{4,3,2,1,0:T(8,128)(2,1)S(1)} async-done(((bf16[4,4,4,8,2176]{4,3,2,1,0:T(8,128)(2,1)}), bf16[4,4,4,8,2176]{4,3,2,1,0:T(8,128)(2,1)S(1)}, u32[]{:S(2)}, u32[]{:S(2)}) %all-to-all-start.1) | async-done | bytes 2228256 | tf_op jit(solution)/shard_map/all_to_all | solution.py:584
  281.8 1.3 reduce_sum.110
  283.0 8.0 %all-to-all-start.2 = ((bf16[4,4,8,2176]{3,2,1,0:T(8,128)(2,1)}), bf16[4,4,8,2176]{3,2,1,0:T(8,128)(2,1)}, u32[]{:S(2)}, u32[]{:S(2)}) async-start(bf16[4,4,8,2176]{3,2,1,0:T(8,128)(2,1)} %reduce_sum.110), calls=%async_computation.2 | async-start | bytes 1114112 | tf_op jit(solution)/shard_map/all_to_all | solution.py:584
  291.1 3.5 constant_dynamic-slice_fusion.1
  294.6 2.0 copy.112
  296.5 1.4 collective-permute-start.13
  297.9 1.4 all-to-all-done.2
  299.3 1.1 reduce_sum.111
  300.5 7.3 %all_to_all.35 = bf16[4,8,2176]{2,1,0:T(8,128)(2,1)S(1)} all-to-all(bf16[4,8,2176]{2,1,0:T(8,128)(2,1)S(1)} %reduce_sum.111), channel_id=1, replica_groups=mesh['x'=4,'core'=2,'rows'=4,'chan'=4] {'chan'}, dimensions={0} | all-to-all | bytes 278528 | tf_op jit(solution)/shard_map/all_to_all | solution.py:584
  308.5 2.7 fusion
  311.1 39.2 %all_to_all.36 = bf16[4,4,4,8,3200]{4,3,1,2,0:T(8,128)(2,1)S(1)} all-to-all(bf16[4,4,4,8,3200]{4,3,1,2,0:T(8,128)(2,1)S(1)} %fusion), channel_id=1, replica_groups=mesh['x'=4,'core'=2,'rows'=4,'chan'=4] {'x'}, dimensions={0} | all-to-all | bytes 6553600 | tf_op jit(solution)/shard_map/all_to_all | solution.py:584
  350.3 1.6 reduce_sum.115
  351.9 1.2 copy.99
  353.1 19.6 %all_to_all.37 = bf16[4,4,8,3200]{3,2,1,0:T(8,128)(2,1)S(1)} all-to-all(bf16[4,4,8,3200]{3,2,1,0:T(8,128)(2,1)S(1)} %copy.99), channel_id=1, replica_groups=mesh['x'=4,'core'=2,'rows'=4,'chan'=4] {'rows'}, dimensions={0} | all-to-all | bytes 1638400 | tf_op jit(solution)/shard_map/all_to_all | solution.py:584
  372.9 7.6 %all_to_all.38 = bf16[4,8,3200]{2,1,0:T(8,128)(2,1)S(1)} all-to-all(bf16[4,8,3200]{2,1,0:T(8,128)(2,1)S(1)} %reduce_sum.116), channel_id=1, replica_groups=mesh['x'=4,'core'=2,'rows'=4,'chan'=4] {'chan'}, dimensions={0} | all-to-all | bytes 409600 | tf_op jit(solution)/shard_map/all_to_all | solution.py:717
  381.2 7.9 %feature_backward.1 = f32[8,144,1024]{2,1,0:T(8,128)} custom-call(s32[4]{0:T(128)} %and_select_fusion.order_ref, bf16[8,144,1024]{2,1,0:T(8,128)(2,1)} %get-tuple-element.102.rg, bf16[1024,1024]{1,0:T(8,128)(2,1)} %wr.3, bf16[4,72,1024]{2,1,0:T(8,128)(2,1)} %pad_maximum_fusion.4.ret, bf16[288,72]{1,0:T(8,128)(2,1)} %constant.170.clone.up), custom_call_target="tpu_custom_call" | custom-call | flops 2415919104 | bytes 9806336 | tf_op jit(solution)/shard_map/feature_backward/pallas_call | solution.py:68
  390.5 3.1 convert_element_type.122
  394.2 4.5 %fusion.14 = (f32[1024,1024]{1,0:T(8,128)}, f32[1024,1024]{1,0:T(8,128)}) fusion(bf16[1024,2176]{1,0:T(8,128)(2,1)S(1)} %bitcast.125), kind=kLoop, calls=%fused_computation.67 | loop fusion | bytes 16777216 | tf_op jit(solution)/shard_map/slice | solution.py:740
  398.7 28.5 %all-gather.9.cloned.1.call-done = bf16[256,6272]{1,0:T(8,128)(2,1)} async-done(((bf16[8,6272]{1,0:T(8,128)(2,1)}), bf16[256,6272]{1,0:T(8,128)(2,1)}) %all-gather.9.cloned.1.call-update) | async-done | bytes 3211280 | tf_op jit(solution)/shard_map/all_gather | solution.py:721
  427.2 2.3 convert_element_type.132
  431.2 2.5 copy.100
  434.3 2.5 slice.215
  (118 shorter events, 22.3 us)
Async XLA Ops:
  7.2 109.8 %all-gather.11.cloned.1.call-start = ((), (), s32[]{:S(2)}) async-start(), calls=%async_computation.9 | async-start | bytes 5406720 | tf_op jit(solution)/shard_map/all_gather | solution.py:656
  14.7 8.7 %copy-start.17 = (s32[2]{0:T(128)S(1)}, s32[2]{0:T(128)}, u32[]{:S(2)}) copy-start(s32[2]{0:T(128)} %param.24) | copy-start | bytes 28
  14.7 9.0 %copy-start.12 = (bf16[128,128]{0,1:T(8,128)(2,1)S(1)}, bf16[128,128]{0,1:T(8,128)(2,1)}, u32[]{:S(2)}) copy-start(bf16[128,128]{0,1:T(8,128)(2,1)} %constant.171.clone) | copy-start | bytes 98308
  18.0 23.1 %collective-permute-start = (bf16[8,24,1024]{2,1,0:T(8,128)(2,1)S(1)}, bf16[8,24,1024]{2,1,0:T(8,128)(2,1)S(1)}, u32[]{:S(2)}, u32[]{:S(2)}) collective-permute-start(bf16[8,24,1024]{2,1,0:T(8,128)(2,1)S(1)} %get-tuple-element.188), channel_id=1, source_target_pairs={{0,4},{4,8},{8,12},{1,5},{5,9},{9,13},{2,6},{6,10},{10,14},{3,7},{... | collective-permute-start | bytes 1179656 | tf_op jit(solution)/shard_map/ppermute | solution.py:650
  22.1 19.1 %collective-permute-start.1 = (bf16[8,24,1024]{2,1,0:T(8,128)(2,1)S(1)}, bf16[8,24,1024]{2,1,0:T(8,128)(2,1)}, u32[]{:S(2)}, u32[]{:S(2)}) collective-permute-start(bf16[8,24,1024]{2,1,0:T(8,128)(2,1)S(1)} %get-tuple-element.187), channel_id=1, source_target_pairs={{4,0},{8,4},{12,8},{5,1},{9,5},{13,9},{6,2},{10,6},{14,10},{7,3},{... | collective-permute-start | bytes 1179656 | tf_op jit(solution)/shard_map/ppermute | solution.py:651
  28.8 5.3 %copy-start.13 = (bf16[3,3,1024]{2,1,0:T(4,128)(2,1)S(1)}, bf16[3,3,1024]{2,1,0:T(4,128)(2,1)}, u32[]{:S(2)}) copy-start(bf16[3,3,1024]{2,1,0:T(4,128)(2,1)} %param.26) | copy-start | bytes 55300
  28.8 6.5 %copy-start.1 = (bf16[1024,1024]{1,0:T(8,128)(2,1)S(1)}, bf16[1024,1024]{1,0:T(8,128)(2,1)}, u32[]{:S(2)}) copy-start(bf16[1024,1024]{1,0:T(8,128)(2,1)} %wr.3) | copy-start | bytes 6291460
  28.8 105.1 %all-to-all-start = ((bf16[4,288,1024]{2,1,0:T(8,128)(2,1)}), bf16[4,288,1024]{2,1,0:T(8,128)(2,1)}, u32[]{:S(2)}, u32[]{:S(2)}) async-start(bf16[4,288,1024]{2,1,0:T(8,128)(2,1)} %cotangent_by_image.1), calls=%async_computation | async-start | bytes 4718592 | tf_op jit(solution)/shard_map/all_to_all | solution.py:663
  34.0 224.5 %all-gather.13.cloned.1.call-start = ((), (), s32[]{:S(2)}) async-start(), calls=%async_computation.10 | async-start | bytes 2949120 | tf_op jit(solution)/shard_map/all_gather | solution.py:675
  41.2 0.7 copy-start.6
  41.9 33.8 %copy-start.14 = (bf16[3,3,1024]{2,1,0:T(4,128)(2,1)S(1)}, bf16[3,3,1024]{2,1,0:T(4,128)(2,1)}, u32[]{:S(2)}) copy-start(bf16[3,3,1024]{2,1,0:T(4,128)(2,1)} %param.30) | copy-start | bytes 55300
  65.2 44.9 %collective-permute-start.4 = (bf16[72,1024]{1,0:T(8,128)(2,1)S(1)}, bf16[72,1024]{1,0:T(8,128)(2,1)S(1)}, u32[]{:S(2)}, u32[]{:S(2)}) collective-permute-start(bf16[72,1024]{1,0:T(8,128)(2,1)S(1)} %get-tuple-element.195), channel_id=1, source_target_pairs={{0,2},{1,6},{2,10},{3,14},{4,3},{5,7},{6,11},{7,15},{8,0},{9,4},{1... | collective-permute-start | bytes 442376 | tf_op jit(solution)/shard_map/ppermute | solution.py:671
  68.4 41.7 %collective-permute-start.5 = (bf16[72,1024]{1,0:T(8,128)(2,1)S(1)}, bf16[72,1024]{1,0:T(8,128)(2,1)S(1)}, u32[]{:S(2)}, u32[]{:S(2)}) collective-permute-start(bf16[72,1024]{1,0:T(8,128)(2,1)S(1)} %get-tuple-element.194), channel_id=1, source_target_pairs={{0,3},{1,7},{2,11},{3,15},{4,0},{5,4},{6,8},{7,12},{8,1},{9,5},{10... | collective-permute-start | bytes 442376 | tf_op jit(solution)/shard_map/ppermute | solution.py:671
  72.6 37.5 %collective-permute-start.2 = (bf16[72,1024]{1,0:T(8,128)(2,1)S(1)}, bf16[72,1024]{1,0:T(8,128)(2,1)S(1)}, u32[]{:S(2)}, u32[]{:S(2)}) collective-permute-start(bf16[72,1024]{1,0:T(8,128)(2,1)S(1)} %get-tuple-element.193), channel_id=1, source_target_pairs={{0,0},{1,4},{2,8},{3,12},{4,1},{5,5},{6,9},{7,13},{8,2},{9,6},{10,... | collective-permute-start | bytes 442376 | tf_op jit(solution)/shard_map/ppermute | solution.py:671
  73.3 42.8 %collective-permute-start.3 = (bf16[72,1024]{1,0:T(8,128)(2,1)S(1)}, bf16[72,1024]{1,0:T(8,128)(2,1)S(1)}, u32[]{:S(2)}, u32[]{:S(2)}) collective-permute-start(bf16[72,1024]{1,0:T(8,128)(2,1)S(1)} %get-tuple-element.196), channel_id=1, source_target_pairs={{0,1},{1,5},{2,9},{3,13},{4,2},{5,6},{6,10},{7,14},{8,3},{9,7},{10... | collective-permute-start | bytes 442376 | tf_op jit(solution)/shard_map/ppermute | solution.py:671
  155.7 11.1 %collective-permute-start.6 = (bf16[72,1024]{1,0:T(8,128)(2,1)S(1)}, bf16[72,1024]{1,0:T(8,128)(2,1)S(1)}, u32[]{:S(2)}, u32[]{:S(2)}) collective-permute-start(bf16[72,1024]{1,0:T(8,128)(2,1)S(1)} %get-tuple-element.189), channel_id=1, source_target_pairs={{0,0},{4,1},{8,2},{12,3},{1,4},{5,5},{9,6},{13,7},{2,8},{6,9},{10,... | collective-permute-start | bytes 442376 | tf_op jit(solution)/shard_map/ppermute | solution.py:681
  156.3 10.5 %collective-permute-start.7 = (bf16[72,1024]{1,0:T(8,128)(2,1)S(1)}, bf16[72,1024]{1,0:T(8,128)(2,1)S(1)}, u32[]{:S(2)}, u32[]{:S(2)}) collective-permute-start(bf16[72,1024]{1,0:T(8,128)(2,1)S(1)} %get-tuple-element.192), channel_id=1, source_target_pairs={{1,0},{5,1},{9,2},{13,3},{2,4},{6,5},{10,6},{14,7},{3,8},{7,9},{11... | collective-permute-start | bytes 442376 | tf_op jit(solution)/shard_map/ppermute | solution.py:681
  156.6 12.3 %collective-permute-start.8 = (bf16[72,1024]{1,0:T(8,128)(2,1)S(1)}, bf16[72,1024]{1,0:T(8,128)(2,1)S(1)}, u32[]{:S(2)}, u32[]{:S(2)}) collective-permute-start(bf16[72,1024]{1,0:T(8,128)(2,1)S(1)} %get-tuple-element.191), channel_id=1, source_target_pairs={{2,0},{6,1},{10,2},{14,3},{3,4},{7,5},{11,6},{15,7},{0,8},{4,9},{8... | collective-permute-start | bytes 442376 | tf_op jit(solution)/shard_map/ppermute | solution.py:681
  166.8 5.2 %collective-permute-start.9 = (bf16[72,1024]{1,0:T(8,128)(2,1)S(1)}, bf16[72,1024]{1,0:T(8,128)(2,1)S(1)}, u32[]{:S(2)}, u32[]{:S(2)}) collective-permute-start(bf16[72,1024]{1,0:T(8,128)(2,1)S(1)} %get-tuple-element.190), channel_id=1, source_target_pairs={{3,0},{7,1},{11,2},{15,3},{0,4},{4,5},{8,6},{12,7},{1,8},{5,9},{9,... | collective-permute-start | bytes 442376 | tf_op jit(solution)/shard_map/ppermute | solution.py:681
  194.1 12.4 %collective-permute-start.10 = (bf16[8,24,1024]{2,1,0:T(8,128)(2,1)}, bf16[8,24,1024]{2,1,0:T(8,128)(2,1)S(1)}, u32[]{:S(2)}, u32[]{:S(2)}) collective-permute-start(bf16[8,24,1024]{2,1,0:T(8,128)(2,1)} %get-tuple-element.100), channel_id=1, source_target_pairs={{0,4},{4,8},{8,12},{1,5},{5,9},{9,13},{2,6},{6,10},{10,14},{3,7},{... | collective-permute-start | bytes 1179656 | tf_op jit(solution)/shard_map/ppermute | solution.py:689
  197.7 9.6 %collective-permute-start.11 = (bf16[8,24,1024]{2,1,0:T(8,128)(2,1)}, bf16[8,24,1024]{2,1,0:T(8,128)(2,1)S(1)}, u32[]{:S(2)}, u32[]{:S(2)}) collective-permute-start(bf16[8,24,1024]{2,1,0:T(8,128)(2,1)} %get-tuple-element.101), channel_id=1, source_target_pairs={{4,0},{8,4},{12,8},{5,1},{9,5},{13,9},{6,2},{10,6},{14,10},{7,3},{... | collective-permute-start | bytes 1179656 | tf_op jit(solution)/shard_map/ppermute | solution.py:690
  206.5 0.7 copy-start.7
  207.2 0.7 copy-start.8
  208.0 13.5 %copy-start.2 = (bf16[8,6,24,1024]{3,2,1,0:T(8,128)(2,1)S(1)}, bf16[8,6,24,1024]{3,2,1,0:T(8,128)(2,1)}, u32[]{:S(2)}) copy-start(bf16[8,6,24,1024]{3,2,1,0:T(8,128)(2,1)} %feat.1) | copy-start | bytes 7077892
  221.5 5.0 %copy-start.5 = (bf16[1024,1024]{0,1:T(8,128)(2,1)S(1)}, bf16[1024,1024]{0,1:T(8,128)(2,1)}, u32[]{:S(2)}) copy-start(bf16[1024,1024]{0,1:T(8,128)(2,1)} %bitcast_convert_fusion) | copy-start | bytes 6291460
  235.4 6.8 %copy-start.16 = (bf16[288,1024]{1,0:T(8,128)(2,1)S(1)}, bf16[288,1024]{1,0:T(8,128)(2,1)}, u32[]{:S(2)}) copy-start(bf16[288,1024]{1,0:T(8,128)(2,1)} %get-tuple-element.107) | copy-start | bytes 1769476
  237.2 8.7 %collective-permute-start.12 = (bf16[4,4,4,8,2176]{4,3,2,1,0:T(8,128)(2,1)S(1)}, bf16[4,4,4,8,2176]{4,3,2,1,0:T(8,128)(2,1)}, u32[]{:S(2)}, u32[]{:S(2)}) collective-permute-start(bf16[4,4,4,8,2176]{4,3,2,1,0:T(8,128)(2,1)S(1)} %dynamic-slice_bitcast_fusion), channel_id=1, source_target_pairs={{0,16},{16,0},{1,17},{17,1},{2,18},{18,2},{3,19},{19,3},{4,20},{20... | collective-permute-start | bytes 6684680 | tf_op jit(solution)/shard_map/ppermute | solution.py:592
  250.1 4.1 copy-start.15
  250.1 31.7 %all-to-all-start.1 = ((bf16[4,4,4,8,2176]{4,3,2,1,0:T(8,128)(2,1)}), bf16[4,4,4,8,2176]{4,3,2,1,0:T(8,128)(2,1)S(1)}, u32[]{:S(2)}, u32[]{:S(2)}) async-start(bf16[4,4,4,8,2176]{4,3,2,1,0:T(8,128)(2,1)} %fusion.1), calls=%async_computation.1 | async-start | bytes 4456448 | tf_op jit(solution)/shard_map/all_to_all | solution.py:584
  254.2 3.8 copy-start.11
  254.2 3.8 copy-start.9
  268.3 5.5 %copy-start.3 = (bf16[1024,1024]{1,0:T(8,128)(2,1)S(1)}, bf16[1024,1024]{1,0:T(8,128)(2,1)}, u32[]{:S(2)}) copy-start(bf16[1024,1024]{1,0:T(8,128)(2,1)} %convolution_convert_fusion.2) | copy-start | bytes 6291460
  268.3 5.5 %copy-start.4 = (bf16[1024,1024]{1,0:T(8,128)(2,1)S(1)}, bf16[1024,1024]{1,0:T(8,128)(2,1)}, u32[]{:S(2)}) copy-start(bf16[1024,1024]{1,0:T(8,128)(2,1)} %convolution_convert_fusion.1) | copy-start | bytes 6291460
  283.0 16.3 %all-to-all-start.2 = ((bf16[4,4,8,2176]{3,2,1,0:T(8,128)(2,1)}), bf16[4,4,8,2176]{3,2,1,0:T(8,128)(2,1)}, u32[]{:S(2)}, u32[]{:S(2)}) async-start(bf16[4,4,8,2176]{3,2,1,0:T(8,128)(2,1)} %reduce_sum.110), calls=%async_computation.2 | async-start | bytes 1114112 | tf_op jit(solution)/shard_map/all_to_all | solution.py:584
  291.1 98.0 %all-gather.7.cloned.1.call-start = ((), (), s32[]{:S(2)}) async-start(), calls=%async_computation.7 | async-start | bytes 4491264 | tf_op jit(solution)/shard_map/all_gather | solution.py:733
  296.5 11.9 %collective-permute-start.13 = (bf16[4,4,4,8,3200]{4,3,1,2,0:T(8,128)(2,1)}, bf16[4,4,4,8,3200]{4,3,1,2,0:T(8,128)(2,1)}, u32[]{:S(2)}, u32[]{:S(2)}) collective-permute-start(bf16[4,4,4,8,3200]{4,3,1,2,0:T(8,128)(2,1)} %bitcast.122), channel_id=1, source_target_pairs={{0,16},{16,0},{1,17},{17,1},{2,18},{18,2},{3,19},{19,3},{4,20},{20... | collective-permute-start | bytes 9830408 | tf_op jit(solution)/shard_map/ppermute | solution.py:592
  308.4 118.8 %all-gather.9.cloned.1.call-start = ((), (), s32[]{:S(2)}) async-start(), calls=%async_computation.8 | async-start | bytes 3311616 | tf_op jit(solution)/shard_map/all_gather | solution.py:721
  380.6 0.6 copy-start.10
  389.1 5.1 %slice-start = ((s8[4456448]{0:T(1024)(128)(4,1)}), s8[262144]{0:T(1024)(128)(4,1)S(1)}, s32[]{:S(2)}) async-start(s8[4456448]{0:T(1024)(128)(4,1)} %bitcast.124), calls=%async_computation.11 | async-start | bytes 524288
  390.5 3.7 slice-start.1
  429.5 4.2 copy-start
Sparse Core Ops, SparseCore 0:
  17.0 98.1 all-gather.10
  166.9 33.4 all-gather.12
  308.5 69.4 all-gather.6
  381.3 45.7 all-gather.8

commit v3 on v2

--- a/solution.py
+++ b/solution.py
@@ -226,8 +226,11 @@
 
         chunks(ch // LANES, conv)
         for c in range(n):
-            wide2 = dot(cact_out[...], w[c, 1], NT)
-            norm_out[:, c * share : (c + 1) * share] = wide2
+            e = 0.0
+            for q in range(n):
+                cut = slice(q * share, (q + 1) * share)
+                e = e + dot(cact_out[:, cut], w[c, 1, :, cut])
+            norm_out[:, c * share : (c + 1) * share] = e
 
         def norm(i, carry):
             at = pl.ds(pl.multiple_of(i * 16, 16), 16)
@@ -293,10 +296,12 @@
                 return total_gain + g[:8] + g[8:]
 
             gain_out[...] = lax.fori_loop(0, total // 16, norm, jnp.zeros((8, ch), F32))
-            cg = 0.0
-            for c in range(n):
-                cg = cg + dot(exp_out[:, c * share : (c + 1) * share], w[c, 1])
-            cgrad[...] = cg
+            for q in range(n):
+                cut = slice(q * share, (q + 1) * share)
+                cg = 0.0
+                for c in range(n):
+                    cg = cg + dot(exp_out[:, c * share : (c + 1) * share], w[c, 1, :, cut], NT)
+                cgrad[:, cut] = cg
             first, last = edge_masks(total, pool, depth)
             step = pool * depth
 
@@ -375,17 +380,17 @@
     )()[0]
 
 
-def token_block(chan, low, place, readout, cotangent, live):
+def token_block(chan, source, low, place, readout, cotangent, live):
     pairs, each_all, ch = low.shape
     rows, width = cotangent.shape
     size = place.shape[0]
     each = size // pairs
     per = 3
 
-    def kernel(chan_ref, low_ref, place_ref, ro, cot, alive, tok_out, piece_out, low_out):
+    def kernel(chan_ref, src, low_ref, place_ref, ro, cot, alive, tok_out, piece_out, low_out):
         for q in range(per):
             at = pl.ds(q * size, size)
-            x = jnp.concatenate([low_ref[s, pl.ds(q * each, each), :] for s in range(pairs)], 0)
+            x = jnp.concatenate([low_ref[src[s], pl.ds(q * each, each), :] for s in range(pairs)], 0)
             low_out[at, :] = dot(place_ref[...], x).astype(BF)
         logits = dot(low_out[...], ro[...])
         value, slope = gelu_parts(logits)
@@ -393,15 +398,15 @@
         piece_out[...] = (cot[...].astype(F32) * alive[...] * slope).astype(BF)
 
     block = per * size
-    row_block = lambda i, c: (i, 0)
+    row_block = lambda i, c, s: (i, 0)
     return call(
         kernel,
         grid=(rows // block,),
-        prefetch=1,
+        prefetch=2,
         ins=[
-            (low, (pairs, per * each, ch), lambda i, c: (0, i, 0)),
+            (low, (pairs, per * each, ch), lambda i, c, s: (0, i, 0)),
             (place, None, None),
-            (readout, (ch, width), lambda i, c: (0, c[0])),
+            (readout, (ch, width), lambda i, c, s: (0, c[0])),
             (cotangent, (block, width), row_block),
             (live, None, None),
         ],
@@ -412,7 +417,7 @@
         ],
         flops=2 * rows * ch * width,
         name="token_block",
-    )(chan)
+    )(chan, source)
 
 
 def pre_backward(order, returned, spread_up, nrm, std, gain, conv, pre_expand):
@@ -576,21 +581,139 @@
     )(order)[0]
 
 
+def post_weight_grads(flat, reduced_grad, act, expanded_grad, n):
+    total, ch = flat.shape
+    share = ch // n
+
+    def kernel(x, g, a, e, out):
+        for c in range(n):
+            cut = slice(c * share, (c + 1) * share)
+            out[0, c] = dot(x[:, cut], g[...], TN).astype(BF)
+            for q in range(n):
+                rows = slice(q * share, (q + 1) * share)
+                out[1, c, :, rows] = dot(a[:, rows], e[:, cut], TN).astype(BF)
+
+    return call(
+        kernel,
+        grid=(1,),
+        ins=[(v, None, None) for v in (flat, reduced_grad, act, expanded_grad)],
+        outs=[(shape((2, n, share, ch), BF), None, None)],
+        flops=4 * total * ch * ch,
+        name="post_weight_grads",
+    )()[0]
+
+
 def spread(n, k):
     return [(a * n + b, b * n + (a + k) % n) for a in range(n) for b in range(n)]
 
 
-def scatter_sum(blocks, axis):
-    got = lax.all_to_all(blocks, axis, 0, 0, tiled=False)
-    return jnp.sum(got.astype(F32), axis=0).astype(BF)
-
-
-def core_sum(blocks):
-    me = lax.axis_index("core")
-    keep = lax.dynamic_index_in_dim(blocks, me, 0, keepdims=False)
-    send = lax.dynamic_index_in_dim(blocks, 1 - me, 0, keepdims=False)
-    got = lax.ppermute(send, "core", [(0, 1), (1, 0)])
-    return (keep.astype(F32) + got.astype(F32)).astype(BF)
+def other_core(values):
+    return lax.ppermute(values, "core", [(0, 1), (1, 0)])
+
+
+def small_rows(*grads):
+    ch = grads[0].shape[-1]
+    counts = [g.shape[0] if g.ndim == 3 else 1 for g in grads]
+    per = ch // LANES
+
+    def kernel(*refs):
+        out = refs[-1]
+        at = 0
+        for ref, count in zip(refs, counts):
+            for i in range(count):
+                v = jnp.sum(ref[i] if len(ref.shape) == 3 else ref[...], 0, keepdims=True)
+                for q in range(per):
+                    out[pl.ds(at, 1), :] = v[:, q * LANES : (q + 1) * LANES]
+                    at += 1
+
+    return call(
+        kernel,
+        grid=(1,),
+        ins=[(g, None, None) for g in grads],
+        outs=[(shape((sum(counts) * per, LANES), F32), None, None)],
+        name="small_rows",
+    )()[0]
+
+
+def join_halves(core, mine, theirs, small, their_small, parts):
+    rows, ch = mine[0].shape
+    half = rows // 2
+    width = len(mine) * ch + LANES
+    count = small.shape[0]
+    m = len(mine)
+
+    def kernel(core_ref, *refs):
+        own, got = refs[:m], refs[m : 2 * m]
+        sm, got_sm, out = refs[2 * m :]
+        for i in range(m):
+            out[:, i * ch : (i + 1) * ch] = (own[i][...].astype(F32) + got[i][...].astype(F32)).astype(BF)
+        first = (core_ref[0] == 0).astype(F32)
+        total = (sm[...] + got_sm[...]) * first
+        pad = jnp.zeros((half - count, LANES), F32)
+        out[:, m * ch :] = jnp.concatenate([total, pad], 0).astype(BF)
+
+    return call(
+        kernel,
+        grid=(1,),
+        prefetch=1,
+        ins=[(v, (half, ch), lambda i, c: (c[0], 0)) for v in mine]
+        + [(v, None, None) for v in (*theirs, small, their_small)],
+        outs=[(shape((half, width), BF), None, None)],
+        name="join_halves",
+    )(core)[0].reshape(parts, half // parts, width)
+
+
+def sum_and_copy(blocks):
+    parts, rows, width = blocks.shape
+
+    def kernel(x, out):
+        def cut(lanes):
+            total = jnp.sum(x[:, :, lanes].astype(F32), 0).astype(BF)
+            out[:, :, lanes] = jnp.broadcast_to(total[None], (parts, rows, LANES))
+
+        chunks(width // LANES, cut)
+
+    return call(
+        kernel,
+        grid=(1,),
+        ins=[(blocks, None, None)],
+        outs=[(shape(blocks.shape, BF), None, None)],
+        name="sum_and_copy",
+    )()[0]
+
+
+def finish_pre(core, own, got, ch):
+    half, width = own.shape
+    m = (width - LANES) // ch
+
+    def kernel(core_ref, a, b, *outs):
+        h = pl.program_id(0)
+
+        def write(ref):
+            for i in range(m):
+                outs[i][...] = ref[:, i * ch : (i + 1) * ch].astype(F32)
+
+            @pl.when(h == 0)
+            def _():
+                outs[m][...] = ref[:, m * ch :].astype(F32)
+
+        @pl.when(h == core_ref[0])
+        def _():
+            write(a)
+
+        @pl.when(h != core_ref[0])
+        def _():
+            write(b)
+
+    return call(
+        kernel,
+        grid=(2,),
+        prefetch=1,
+        ins=[(own, None, None), (got, None, None)],
+        outs=[(shape((2 * half, ch), F32), (half, ch), lambda h, c: (h, 0)) for _ in range(m)]
+        + [(shape((half, LANES), F32), None, None)],
+        name="finish_pre",
+    )(core)
 
 
 def pool_matrix(part, high, wide):
@@ -626,6 +749,8 @@
     n = lax.axis_size("chan")
     row = lax.axis_index("rows").astype(jnp.int32)
     chan = lax.axis_index("chan").astype(jnp.int32)
+    core = lax.axis_index("core").astype(jnp.int32)
+    eighth = lax.axis_index(("x", "core"))
     ch = pre_reduce.shape[0]
     slots, high, wide = features.shape[0], features.shape[1], features.shape[2]
     part = slots // n
@@ -637,6 +762,7 @@
     order = (row + steps) % n
     source = (chan - steps) % n
     rank = jnp.full((1,), chan, jnp.int32)
+    core_at = jnp.full((1,), core, jnp.int32)
     pre_taps = pre_conv.astype(F32).reshape(9, ch)
     post_taps = post_conv.astype(F32).reshape(9, ch)
     pre_gain_row = pre_gain.reshape(1, ch)
@@ -651,12 +777,14 @@
     below = lax.ppermute(features[:, 0], "rows", up_pairs)
     gain_hi = post_gain.astype(BF)
     gain_lo = (post_gain - gain_hi.astype(F32)).astype(BF)
-    extra = jnp.zeros((16, ch), BF).at[0, :share].set(gain_hi).at[0, share : 2 * share].set(gain_lo)
-    shards = jnp.concatenate([post_reduce, post_expand.T, extra], axis=0)
-    full = lax.all_gather(shards, "chan", axis=0, tiled=False)
-    weights = full[:, : 2 * share].reshape(n, 2, share, ch)
-    gain_parts = full[:, 2 * share].astype(F32)
-    post_gain_row = (gain_parts[:, :share] + gain_parts[:, share : 2 * share]).reshape(1, ch)
+    gain_row = jnp.concatenate([gain_hi, gain_lo, jnp.zeros((ch - 2 * share,), BF)])[None]
+    square = post_expand.reshape(n, share, share)
+    shards = jnp.concatenate(
+        [post_reduce, jnp.concatenate([square[q] for q in range(n)], axis=1), jnp.pad(gain_row, ((0, 63), (0, 0)))], axis=0
+    )
+    eighths = shards.reshape(8, -1, ch)
+    full = lax.all_gather(lax.dynamic_index_in_dim(eighths, eighth, 0, keepdims=False), ("chan", "x", "core"), axis=0, tiled=True)
+    full = full.reshape(n, 2 * share + 64, ch)
     live = (jnp.arange(SLOT)[None, :] < counts[:, None]).astype(F32).reshape(slots)
     select = place.T * jnp.tile(live.astype(BF), 16)[None, :]
     cot_rows = cotangent.transpose(1, 2, 0, 3).reshape(-1, out_share)
@@ -669,10 +797,13 @@
     )
 
     moved = jnp.stack([lax.ppermute(pooled[k], ("rows", "chan"), spread(n, k)) for k in range(n)])
+    weights = full[:, : 2 * share].reshape(n, 2, share, ch)
+    gain_parts = full[:, 2 * share].astype(F32)
+    post_gain_row = (gain_parts[:, :share] + gain_parts[:, share : 2 * share]).reshape(1, ch)
     flat, post_reduced, post_act, post_convolved, post_cact, post_normal, post_std, low = post_forward(
         source, moved, weights, post_gain_row, post_taps, pool
     )
-    low_all = lax.all_gather(low, "chan", axis=0, tiled=False)
+    lows = [low] + [lax.ppermute(low, "chan", [(i, (i + k) % n) for i in range(n)]) for k in range(1, n)]
     post_expanded_grad, post_reduced_grad, back, post_taps_grad, post_gain_grad = post_backward(
         source, low, readout, cots, weights, post_gain_row, post_taps, post_act, post_reduced, post_convolved, post_normal, post_std, pool
     )
@@ -680,8 +811,39 @@
     returned = jnp.stack(
         [lax.ppermute(back[k], ("rows", "chan"), [(d, s) for s, d in spread(n, k)]) for k in range(n)]
     )
-    post_reduce_grad = dot(flat, post_reduced_grad, TN).astype(BF)
-    post_expand_grad_t = dot(post_expanded_grad, post_cact, TN).astype(BF)
+
+    post_load = post_weight_grads(flat, post_reduced_grad, post_cact, post_expanded_grad, n)
+    post_keep = lax.dynamic_index_in_dim(post_load, core, 0, keepdims=False)
+    post_got = other_core(lax.dynamic_index_in_dim(post_load, 1 - core, 0, keepdims=False))
+    post_sum = lax.psum_scatter((post_keep.astype(F32) + post_got.astype(F32)).astype(BF), "chan", scatter_dimension=0, tiled=False)
+
+    alive = jnp.broadcast_to(jnp.tile(live, 48)[:, None], (48 * slots, 1))
+    tokens, piece, low_here = token_block(rank, source, jnp.stack(lows), place, readout, cot_rows, alive)
+    readout_grad = dot(low_here, piece, TN).astype(BF).reshape(n, 2, share // 2, out_share)
+    tokens = tokens.reshape(pool, pool, slots, out_share).transpose(2, 0, 1, 3)
+    read_keep = lax.dynamic_index_in_dim(readout_grad, core, 1, keepdims=False)
+    read_got = other_core(lax.dynamic_index_in_dim(readout_grad, 1 - core, 1, keepdims=False))
+    read_sum = (read_keep.astype(F32) + read_got.astype(F32)).astype(BF)
+    eight = share // 32
+    load = jnp.concatenate(
+        [
+            post_sum.reshape(4, 4, 2 * eight, ch),
+            read_sum.reshape(n, 4, 4, eight, out_share).transpose(1, 2, 0, 3, 4).reshape(4, 4, n * eight, out_share),
+        ],
+        axis=2,
+    )
+    load = lax.psum_scatter(load, "x", scatter_dimension=0, tiled=False)
+    load = lax.psum_scatter(load, "rows", scatter_dimension=0, tiled=False)
+    read_part = lax.all_to_all(load[2 * eight :].reshape(n, eight, out_share), "chan", 0, 0, tiled=False)
+    load = jnp.concatenate([load[: 2 * eight], read_part.reshape(n * eight, out_share)], axis=0)
+    half_all = lax.all_gather(load, ("x", "rows"), axis=0, tiled=False)
+    half_got = other_core(half_all)
+    first = jnp.where(core == 0, half_all, half_got).astype(F32)
+    second = jnp.where(core == 0, half_got, half_all).astype(F32)
+    post_reduce_out = first[:, : 2 * eight].reshape(share, ch)
+    post_expand_out = second[:, : 2 * eight].reshape(share, n, share).transpose(1, 0, 2).reshape(ch, share)
+    readout_out = jnp.stack([first[:, 2 * eight :], second[:, 2 * eight :]]).reshape(2, 16, n, eight, out_share)
+    readout_out = readout_out.transpose(0, 1, 3, 2, 4).reshape(share, n * out_share)
 
     expanded_grad, convolved_grad, top, bottom, pre_gain_grad = pre_backward(
         order, returned, up_m, normal_pre, pre_std, pre_gain_row, convolved, pre_expand
@@ -693,56 +855,28 @@
     pre_reduce_grad = dot(flat_features, reduced_grad.reshape(-1, ch), TN).astype(BF)
     feature_grad = feature_backward(order, reduced_grad, pre_reduce, returned, up_m).reshape(features.shape)
 
-    alive = jnp.broadcast_to(jnp.tile(live, 48)[:, None], (48 * slots, 1))
-    tokens, piece, low_here = token_block(rank, low_all, place, readout, cot_rows, alive)
-    readout_grad = dot(low_here, piece, TN).astype(BF)
-    tokens = tokens.reshape(pool, pool, slots, out_share).transpose(2, 0, 1, 3)
-
-    eight = share // 32
-    tail = jnp.zeros((n, share, LANES), F32)
-    tail = tail.at[:, : share // LANES].set(jnp.sum(post_gain_grad, 0).reshape(n, share // LANES, LANES))
-    taps_rows = jnp.sum(post_taps_grad, 1).reshape(-1, LANES)
-    tail = tail.at[:, share // LANES : share // LANES + taps_rows.shape[0]].set(taps_rows[None])
-    load = jnp.concatenate(
-        [
-            post_reduce_grad.reshape(n, share, ch),
-            post_expand_grad_t.reshape(n, share, ch),
-            tail.astype(BF),
-            readout_grad.reshape(n, share, out_share),
-        ],
-        axis=2,
-    )
-    load = load.reshape(n, 2, 4, 4, eight, -1).transpose(1, 2, 3, 0, 4, 5)
-    load = scatter_sum(scatter_sum(core_sum(load), "x"), "rows")
-    load = lax.all_to_all(load, "chan", 0, 0, tiled=False)
-    cut = 2 * ch + LANES
-    summed = jnp.sum(load[:, :, :cut].astype(F32), axis=0).astype(BF)
-    mine = jnp.concatenate([summed] + [load[j, :, cut:] for j in range(n)], axis=1)
-    post_all = lax.all_gather(mine, ("core", "x", "rows"), axis=0, tiled=True).astype(F32)
-    post_reduce_out = post_all[:, :ch]
-    post_expand_out = post_all[:, ch : 2 * ch].T
-    tail_out = post_all[:, 2 * ch : cut]
-    post_gain_out = tail_out[: share // LANES].reshape(share)
-    post_conv_out = tail_out[share // LANES : share // LANES + taps_rows.shape[0]].reshape(3, 3, ch)
-    readout_out = post_all[:, cut:]
-
-    tail = jnp.concatenate([jnp.sum(pre_taps_grad, 1).reshape(-1, LANES), jnp.sum(pre_gain_grad, 0).reshape(-1, LANES)], axis=0)
-    tail = jnp.pad(tail, ((0, ch - tail.shape[0]), (0, 0))).astype(BF)
-    load = jnp.concatenate([pre_reduce_grad, pre_expand_grad, tail], axis=1).reshape(2, 4, 4, 4, ch // 128, -1)
-    load = scatter_sum(scatter_sum(scatter_sum(core_sum(load), "x"), "rows"), "chan")
-    pre_all = lax.all_gather(load, ("core", "x", "rows", "chan"), axis=0, tiled=True).astype(F32)
-    taps = 9 * ch // LANES
+    small = small_rows(pre_taps_grad, pre_gain_grad, post_taps_grad, post_gain_grad)
+    mine = [pre_reduce_grad, pre_expand_grad]
+    theirs = [other_core(lax.dynamic_index_in_dim(g.reshape(2, ch // 2, ch), 1 - core, 0, keepdims=False)) for g in mine]
+    load = join_halves(core_at, mine, theirs, small, other_core(small), 64)
+    chips = ("x", "rows", "chan")
+    load = sum_and_copy(lax.all_to_all(load, chips, 0, 0, tiled=False))
+    load = lax.all_to_all(load, chips, 0, 0, tiled=False).reshape(ch // 2, -1)
+    pre_reduce_out, pre_expand_out, small_out = finish_pre(core_at, load, other_core(load), ch)
+    per = ch // LANES
+    cut = [0, 9 * per, 10 * per, 19 * per, 20 * per]
+    pre_conv_out, pre_gain_out, post_conv_out, post_gain_out = [small_out[a:b] for a, b in zip(cut, cut[1:])]
     return (
         tokens,
         feature_grad,
-        pre_all[:, :ch],
-        pre_all[:taps, 2 * ch :].reshape(3, 3, ch),
-        pre_all[:, ch : 2 * ch],
-        pre_all[taps : taps + ch // LANES, 2 * ch :].reshape(ch),
+        pre_reduce_out,
+        pre_conv_out.reshape(3, 3, ch),
+        pre_expand_out,
+        pre_gain_out.reshape(ch),
         post_reduce_out,
-        post_conv_out,
+        post_conv_out.reshape(3, 3, ch),
         post_expand_out,
-        post_gain_out,
+        lax.dynamic_slice_in_dim(post_gain_out.reshape(ch), chan * share, share, 0),
         readout_out,
     )
 

time: 446 us -> 455 us (1.020)
  waiting for transfers between devices: 79.8 us -> 154 us
  blocking collectives: 73.6 us -> 0 us
  Pallas kernels: 109 us -> 132 us
  starting transfers between devices: 54.8 us -> 76 us
  local copies, waits for them, and re-layouts: 47.3 us -> 31.3 us
  other arithmetic: 35.3 us -> 19.5 us
  matrix products: 30.4 us -> 21.3 us
    all_to_all x4 -> x0, blocking collectives: 73.6 us -> none  [the longest x3 66 us: scatter_sum(): got = lax.all_to_all(blocks, axis, 0, 0, tiled=False)]
    ppermute x2 -> x10, waiting for transfers between devices: 0.01 us -> 44.7 us  [the longest x3 39.6 us: body(): lax.ppermute(low, 'chan', [(i, (i + k) % n) for i in range(n)])]
    reduce_scatter x0 -> x3, waiting for transfers between devices: none -> 32.6 us  [the longest x1 32.6 us: body(): load = lax.psum_scatter(load, 'rows', scatter_dimension=0, tiled=False)]
    pallas_call x8 -> x13, Pallas kernels: 109 us -> 132 us  [run(): pl.pallas_call(kernel, grid_spec=pltpu.PrefetchScalarGridSpec(num_scalar_...]
    all_to_all x2 -> x3, waiting for transfers between devices: 6.18 us -> 26.3 us  [the longest x1 26.3 us: body(): load = lax.all_to_all(load, chips, 0, 0, tiled=False).reshape(ch // 2, -1)]
    ppermute x4, waiting for transfers between devices: 39.2 us -> 23.1 us  [body(): lax.ppermute(pooled[k], ('rows', 'chan'), spread(n, k))]
    all_to_all x2 -> x3, starting transfers between devices: 12.1 us -> 23.5 us  [the longest x1 10.3 us: body(): load = sum_and_copy(lax.all_to_all(load, chips, 0, 0, tiled=False))]
    ppermute x2 -> x10, starting transfers between devices: 5.56 us -> 16.2 us  [the longest x7 14.5 us: other_core(): return lax.ppermute(values, 'core', [(0, 1), (1, 0)])]
  transfers between devices with their start and end apart: 21 -> 31, of which waited for: 8 -> 11; matrix products, arithmetic and copies ran while one was open for 20% -> 11% of each run, Pallas kernels for 20% -> 23%
where the time goes in v3:
time: 455 us; the launch traced here: 449 us
  waiting for transfers between devices  154 us (34%)
  Pallas kernels  132 us (29%)
  starting transfers between devices  76 us (17%)
  local copies, waits for them, and re-layouts  31.3 us (7%)
  matrix products  21.3 us (5%)
  other arithmetic  19.5 us (4%)
  between operations  14.6 us (3%)
    pallas_call x13, Pallas kernels, run(): pl.pallas_call(kernel, grid_spec=pltpu.PrefetchScalarGridSpec(num_scalar_...  132 us
    ppermute x3, waiting for transfers between devices, body(): lax.ppermute(low, 'chan', [(i, (i + k) % n) for i in range(n)])  39.6 us
    reduce_scatter x1, waiting for transfers between devices, body(): load = lax.psum_scatter(load, 'rows', scatter_dimension=0, tiled=False)  32.6 us
    all_to_all x1, waiting for transfers between devices, body(): load = lax.all_to_all(load, chips, 0, 0, tiled=False).reshape(ch // 2, -1)  26.3 us
    ppermute x4, waiting for transfers between devices, body(): lax.ppermute(pooled[k], ('rows', 'chan'), spread(n, k))  23.1 us
    dot_general x4, matrix products, dot(): return lax.dot_general(a, b, (dims, ((), ())), preferred_element_type=F32)  21.3 us
    all_gather x1, waiting for transfers between devices, body(): half_all = lax.all_gather(load, ('x', 'rows'), axis=0, tiled=False)  21.1 us
    ppermute x7, starting transfers between devices, other_core(): return lax.ppermute(values, 'core', [(0, 1), (1, 0)])  14.5 us
  transfers between devices with their start and end apart: 31, of which 11 were waited for; matrix products, arithmetic and copies ran while one was open for 11% of the time, Pallas kernels for 23%

profile of v3, /device:TPU:1, one launch (start us, length us, event | category | flops | bytes accessed | tf_op | source)
XLA Modules:
  0.0 449.1 jit_solution(2399193887549664979)
XLA Ops:
  8.0 1.1 fusion.9
  9.2 1.2 fusion.5
  11.1 1.2 slice_bitcast_fusion.2
  12.2 1.3 collective-permute-start.1
  13.5 5.4 %collective-permute-start = (bf16[8,24,1024]{2,1,0:T(8,128)(2,1)S(1)}, bf16[8,24,1024]{2,1,0:T(8,128)(2,1)}, u32[]{:S(2)}, u32[]{:S(2)}) collective-permute-start(bf16[8,24,1024]{2,1,0:T(8,128)(2,1)S(1)} %get-tuple-element.78), channel_id=1, source_target_pairs={{0,4},{4,8},{8,12},{1,5},{5,9},{9,13},{2,6},{6,10},{10,14},{3,7},{... | collective-permute-start | bytes 1179656 | tf_op jit(solution)/shard_map/ppermute | solution.py:776
  19.9 4.4 cotangent_by_image.1
  24.3 5.3 %all-to-all-start = ((bf16[4,288,1024]{2,1,0:T(8,128)(2,1)}), bf16[4,288,1024]{2,1,0:T(8,128)(2,1)}, u32[]{:S(2)}, u32[]{:S(2)}) async-start(bf16[4,288,1024]{2,1,0:T(8,128)(2,1)} %cotangent_by_image.1), calls=%async_computation | async-start | bytes 4718592 | tf_op jit(solution)/shard_map/all_to_all | solution.py:791
  30.8 5.9 %fusion.3.red = f32[8,144,1024]{2,1,0:T(8,128)} fusion(bf16[8,144,1024]{2,1,0:T(8,128)(2,1)} %bitcast.139, bf16[1024,1024]{1,0:T(8,128)(2,1)S(1)} %copy-done.2), kind=kOutput, calls=%fused_computation.11 | convolution fusion | flops 2415919104 | bytes 9175040 | tf_op jit(solution)/shard_map/dot_general | solution.py:23
  37.5 22.0 %pre_forward.1 = (f32[8,144,1024]{2,1,0:T(8,128)}, bf16[8,144,1024]{2,1,0:T(8,128)(2,1)}, f32[8,144,1024]{2,1,0:T(8,128)}, f32[8,144,1]{2,1,0:T(8,128)}, bf16[4,72,1024]{2,1,0:T(8,128)(2,1)}) custom-call(s32[4]{0:T(128)} %and_select_fusion.order_ref, f32[8,144,1024]{2,1,0:T(8,128)} %fusion.3.red, bf16[8,24,1024]{2,1,0:T(8,128)(2,1)} %collective-permute-done.up_ref, ...), custom_call_target="tpu_custom_call" | custom-call | flops 2415919104 | bytes 24511232 | tf_op jit(solution)/shard_map/pre_forward/pallas_call | solution.py:68
  59.4 1.2 slice_bitcast_fusion.11
  61.3 4.6 %collective-permute-start.5 = (bf16[72,1024]{1,0:T(8,128)(2,1)S(1)}, bf16[72,1024]{1,0:T(8,128)(2,1)S(1)}, u32[]{:S(2)}, u32[]{:S(2)}) collective-permute-start(bf16[72,1024]{1,0:T(8,128)(2,1)S(1)} %get-tuple-element.84), channel_id=1, source_target_pairs={{0,3},{1,7},{2,11},{3,15},{4,0},{5,4},{6,8},{7,12},{8,1},{9,5},{10... | collective-permute-start | bytes 442376 | tf_op jit(solution)/shard_map/ppermute | solution.py:799
  66.0 3.1 collective-permute-start.4
  69.0 1.4 collective-permute-start.3
  71.5 10.8 %collective-permute-done.4 = bf16[72,1024]{1,0:T(8,128)(2,1)S(1)} collective-permute-done((bf16[72,1024]{1,0:T(8,128)(2,1)S(1)}, bf16[72,1024]{1,0:T(8,128)(2,1)S(1)}, u32[]{:S(2)}, u32[]{:S(2)}) %collective-permute-start.4) | collective-permute-done | bytes 147488 | tf_op jit(solution)/shard_map/ppermute | solution.py:799
  82.3 12.2 %collective-permute-done.3 = bf16[72,1024]{1,0:T(8,128)(2,1)S(1)} collective-permute-done((bf16[72,1024]{1,0:T(8,128)(2,1)S(1)}, bf16[72,1024]{1,0:T(8,128)(2,1)S(1)}, u32[]{:S(2)}, u32[]{:S(2)}) %collective-permute-start.3) | collective-permute-done | bytes 147488 | tf_op jit(solution)/shard_map/ppermute | solution.py:799
  95.5 4.6 %slice.121 = bf16[4,512,1024]{2,1,0:T(8,128)(2,1)} slice(bf16[4,576,1024]{2,1,0:T(8,128)(2,1)} %bitcast.141), slice={[0:4], [0:512], [0:1024]} | slice | bytes 8388608 | tf_op jit(solution)/shard_map/slice | solution.py:800
  101.6 10.7 %post_forward.1 = (bf16[288,1024]{1,0:T(8,128)(2,1)}, f32[288,1024]{1,0:T(8,128)}, bf16[288,1024]{1,0:T(8,128)(2,1)}, f32[288,1024]{1,0:T(8,128)}, bf16[288,1024...) custom-call(s32[4]{0:T(128)} %and_select_fusion.1.src, ...), custom_call_target="tpu_custom_call" | custom-call | flops 1207959552 | bytes 10724480 | tf_op jit(solution)/shard_map/post_forward/pallas_call | solution.py:68
  112.3 20.7 %post_backward.1 = (bf16[288,1024]{1,0:T(8,128)(2,1)}, bf16[288,1024]{1,0:T(8,128)(2,1)}, bf16[4,72,1024]{2,1,0:T(8,128)(2,1)}, f32[9,8,1024]{2,1,0:T(8,128)}, f32[8,1024]{1,0:T(8,128)}) custom-call(s32[4]{0:T(128)} %and_select_fusion.1.src, bf16[288,1024]{1,0:T(8,128)(2,1)} %get-tuple-element.43.low_ref, bf16[1024,4096]{1,0:T(8,128)(2,1)} %ro.3, ...), custom_call_target="tpu_custom_call" | custom-call | flops 6039797760 | bytes 21800064 | tf_op jit(solution)/shard_map/post_backward/pallas_call | solution.py:68
  133.0 6.0 %post_weight_grads.1 = bf16[2,4,256,1024]{3,2,1,0:T(8,128)(2,1)} custom-call(bf16[288,1024]{1,0:T(8,128)(2,1)} %get-tuple-element.67.x, bf16[288,1024]{1,0:T(8,128)(2,1)} %get-tuple-element.68.g, bf16[288,1024]{1,0:T(8,128)(2,1)} %get-tuple-element.69.a, bf16[288,1024]{1,0:T(8,128)(2,1)} %get-tuple-element.70.e), custom_call_target="tpu_custom_call" | custom-call | flops 1207959552 | bytes 6553600 | tf_op jit(solution)/shard_map/post_weight_grads/pallas_call | solution.py:68
  139.0 3.1 dynamic-slice_bitcast_fusion
  142.7 4.0 collective-permute-done.19
  146.7 3.9 fusion
  153.1 17.7 %collective-permute-done.8 = bf16[288,1024]{1,0:T(8,128)(2,1)S(1)} collective-permute-done((bf16[288,1024]{1,0:T(8,128)(2,1)S(1)}, bf16[288,1024]{1,0:T(8,128)(2,1)S(1)}, u32[]{:S(2)}, u32[]{:S(2)}) %collective-permute-start.8) | collective-permute-done | bytes 589856 | tf_op jit(solution)/shard_map/ppermute | solution.py:806
  170.9 1.6 collective-permute-done.7
  172.4 20.3 %collective-permute-done.6 = bf16[288,1024]{1,0:T(8,128)(2,1)S(1)} collective-permute-done((bf16[288,1024]{1,0:T(8,128)(2,1)S(1)}, bf16[288,1024]{1,0:T(8,128)(2,1)S(1)}, u32[]{:S(2)}, u32[]{:S(2)}) %collective-permute-start.6) | collective-permute-done | bytes 589856 | tf_op jit(solution)/shard_map/ppermute | solution.py:806
  192.7 1.7 pad_maximum_fusion.1.low_ref
  194.4 10.4 %token_block.1 = (bf16[1152,1024]{1,0:T(8,128)(2,1)}, bf16[1152,1024]{1,0:T(8,128)(2,1)}, bf16[1152,1024]{1,0:T(8,128)(2,1)}) custom-call(s32[1]{0:T(128)} %bitcast.chan_ref, s32[4]{0:T(128)} %and_select_fusion.1.src, bf16[4,288,1024]{2,1,0:T(8,128)(2,1)} %pad_maximum_fusion.1.low_ref, bf16[128,128]{1,0:T(8,128)(2,1)} %constant.87.place_ref, ...), custom_call_target="tpu_custom_call" | custom-call | flops 2415919104 | bytes 20219392 | tf_op jit(solution)/shard_map/token_block/pallas_call | solution.py:68
  204.8 5.3 %convolution_convert_fusion = bf16[1024,1024]{1,0:T(8,128)(2,1)S(1)} fusion(bf16[1152,1024]{1,0:T(8,128)(2,1)} %get-tuple-element.71, bf16[1152,1024]{1,0:T(8,128)(2,1)} %get-tuple-element.72), kind=kOutput, calls=%fused_computation.14 | convolution fusion | flops 2416967680 | bytes 6815744 | tf_op jit(solution)/shard_map/dot_general | solution.py:23
  210.3 2.2 collective-permute-start.20
  213.2 4.7 %collective-permute-start.12 = (bf16[72,1024]{1,0:T(8,128)(2,1)S(1)}, bf16[72,1024]{1,0:T(8,128)(2,1)S(1)}, u32[]{:S(2)}, u32[]{:S(2)}) collective-permute-start(bf16[72,1024]{1,0:T(8,128)(2,1)S(1)} %get-tuple-element.80), channel_id=1, source_target_pairs={{3,0},{7,1},{11,2},{15,3},{0,4},{4,5},{8,6},{12,7},{1,8},{5,9},{9,... | collective-permute-start | bytes 442376 | tf_op jit(solution)/shard_map/ppermute | solution.py:812
  217.9 3.4 collective-permute-start.11
  221.3 3.0 collective-permute-start.10
  224.3 6.1 %collective-permute-done.11 = bf16[72,1024]{1,0:T(8,128)(2,1)S(1)} collective-permute-done((bf16[72,1024]{1,0:T(8,128)(2,1)S(1)}, bf16[72,1024]{1,0:T(8,128)(2,1)S(1)}, u32[]{:S(2)}, u32[]{:S(2)}) %collective-permute-start.11) | collective-permute-done | bytes 147488 | tf_op jit(solution)/shard_map/ppermute | solution.py:812
  231.3 21.2 %pre_backward.1 = (bf16[8,144,1024]{2,1,0:T(8,128)(2,1)}, bf16[8,144,1024]{2,1,0:T(8,128)(2,1)}, bf16[8,24,1024]{2,1,0:T(8,128)(2,1)}, bf16[8,24,1024]{2,1,0:T(8,128)(2,1)}, f32[8,1024]{1,0:T(8,128)}) custom-call(s32[4]{0:T(128)} %and_select_fusion.order_ref, bf16[4,72,1024]{2,1,0:T(8,128)(2,1)} %pad_maximum_fusion.4.ret, ...), custom_call_target="tpu_custom_call" | custom-call | flops 2415919104 | bytes 17712128 | tf_op jit(solution)/shard_map/pre_backward/pallas_call | solution.py:68
  252.4 1.3 collective-permute-start.13
  253.8 1.3 collective-permute-start.14
  255.6 2.4 pad_maximum_fusion.2
  258.0 5.3 %bitcast_convert_fusion.refs_1_ = bf16[1024,1024]{1,0:T(8,128)(2,1)S(1)} fusion(bf16[8,144,1024]{2,1,0:T(8,128)(2,1)} %get-tuple-element.58, bf16[8,144,1024]{2,1,0:T(8,128)(2,1)} %get-tuple-element.59), kind=kOutput, calls=%fused_computation.3 | convolution fusion | flops 2416967680 | bytes 6815744 | tf_op jit(solution)/shard_map/dot_general | solution.py:23
  263.4 1.7 collective-permute-start.16
  266.0 12.2 %pre_conv_backward.1 = (bf16[8,144,1024]{2,1,0:T(8,128)(2,1)}, f32[9,8,1024]{2,1,0:T(8,128)}) custom-call(bf16[8,144,1024]{2,1,0:T(8,128)(2,1)} %get-tuple-element.54.cg, bf16[8,24,1024]{2,1,0:T(8,128)(2,1)} %copy-done.12, bf16[8,24,1024]{2,1,0:T(8,128)(2,1)} %copy-done.14, f32[8,144,1024]{2,1,0:T(8,128)} %fusion.3.red, f32[9,1024]{1,0:T(8,128)} %reshape.202.tap), custom_call_target="tpu_custom_call" | custom-call | bytes 10555392 | tf_op jit(solution)/shard_map/pre_conv_backward/pallas_call | solution.py:68
  278.2 4.9 %convolution_convert_fusion.1 = bf16[1024,1024]{0,1:T(8,128)(2,1)S(1)} fusion(bf16[1152,1024]{1,0:T(8,128)(2,1)} %bitcast.143, bf16[1152,1024]{1,0:T(8,128)(2,1)S(1)} %bitcast.140), kind=kOutput, calls=%fused_computation.15 | convolution fusion | flops 2416967680 | bytes 6815744 | tf_op jit(solution)/shard_map/dot_general | solution.py:23
  283.2 2.4 collective-permute-start.15
  285.6 1.8 small_rows.1.refs_4_
  287.9 1.1 collective-permute-done.17.refs_5_
  290.4 4.0 join_halves.1
  294.5 10.3 %all-to-all-start.1 = ((bf16[64,8,2176]{2,1,0:T(8,128)(2,1)}), bf16[64,8,2176]{2,1,0:T(8,128)(2,1)S(1)}, u32[]{:S(2)}, u32[]{:S(2)}) async-start(bf16[64,8,2176]{2,1,0:T(8,128)(2,1)} %bitcast.130), calls=%async_computation.1 | async-start | bytes 4456448 | tf_op jit(solution)/shard_map/all_to_all | solution.py:863
  305.3 32.6 %reduce-scatter.8.cloned.1.call-done = bf16[1,48,1024]{2,1,0:T(8,128)(2,1)} async-done(((bf16[4,48,1024]{2,1,0:T(8,128)(2,1)}), bf16[1,48,1024]{2,1,0:T(8,128)(2,1)}) %reduce-scatter.8.cloned.1.call-update) | async-done | bytes 98320 | tf_op jit(solution)/shard_map/reduce_scatter | solution.py:836
  337.9 1.5 slice_bitcast_fusion.12
  339.4 4.2 all-to-all-start.3
  343.7 4.4 sum_and_copy.1
  348.1 9.0 %all-to-all-start.2 = ((bf16[64,8,2176]{2,1,0:T(8,128)(2,1)}), bf16[64,8,2176]{2,1,0:T(8,128)(2,1)S(1)}, u32[]{:S(2)}, u32[]{:S(2)}) async-start(bf16[64,8,2176]{2,1,0:T(8,128)(2,1)} %sum_and_copy.1), calls=%async_computation.2 | async-start | bytes 4456448 | tf_op jit(solution)/shard_map/all_to_all | solution.py:864
  358.6 26.3 %all-to-all-done.2 = bf16[64,8,2176]{2,1,0:T(8,128)(2,1)S(1)} async-done(((bf16[64,8,2176]{2,1,0:T(8,128)(2,1)}), bf16[64,8,2176]{2,1,0:T(8,128)(2,1)S(1)}, u32[]{:S(2)}, u32[]{:S(2)}) %all-to-all-start.2) | async-done | bytes 2228256 | tf_op jit(solution)/shard_map/all_to_all | solution.py:864
  384.9 5.4 %collective-permute-start.18 = (bf16[512,2176]{1,0:T(8,128)(2,1)S(1)}, bf16[512,2176]{1,0:T(8,128)(2,1)}, u32[]{:S(2)}, u32[]{:S(2)}) collective-permute-start(bf16[512,2176]{1,0:T(8,128)(2,1)S(1)} %bitcast.128), channel_id=1, source_target_pairs={{0,16},{16,0},{1,17},{17,1},{2,18},{18,2},{3,19},{19,3},{4,20},{20... | collective-permute-start | bytes 6684680 | tf_op jit(solution)/shard_map/ppermute | solution.py:611
  390.3 21.1 %all-gather.7.cloned.1.call-done = bf16[768,1024]{1,0:T(8,128)(2,1)} async-done(((bf16[48,1024]{1,0:T(8,128)(2,1)}), bf16[768,1024]{1,0:T(8,128)(2,1)}) %all-gather.7.cloned.1.call-update) | async-done | bytes 1572880 | tf_op jit(solution)/shard_map/all_gather | solution.py:839
  411.4 1.6 collective-permute-start.21
  413.0 7.9 %feature_backward.1 = f32[8,144,1024]{2,1,0:T(8,128)} custom-call(s32[4]{0:T(128)} %and_select_fusion.order_ref, bf16[8,144,1024]{2,1,0:T(8,128)(2,1)} %get-tuple-element.57.rg, bf16[1024,1024]{1,0:T(8,128)(2,1)} %wr.3, bf16[4,72,1024]{2,1,0:T(8,128)(2,1)} %pad_maximum_fusion.4.ret, bf16[288,72]{1,0:T(8,128)(2,1)} %constant.80.clone.up), custom_call_target="tpu_custom_call" | custom-call | flops 2415919104 | bytes 9806336 | tf_op jit(solution)/shard_map/feature_backward/pallas_call | solution.py:68
  420.9 6.1 %finish_pre.1 = (f32[1024,1024]{1,0:T(8,128)}, f32[1024,1024]{1,0:T(8,128)}, f32[512,128]{1,0:T(8,128)}) custom-call(s32[1]{0:T(128)} %bitcast.36.core_ref, bf16[512,2176]{1,0:T(8,128)(2,1)} %bitcast.129, bf16[512,2176]{1,0:T(8,128)(2,1)} %collective-permute-done.18.b), custom_call_target="tpu_custom_call" | custom-call | bytes 13107200 | tf_op jit(solution)/shard_map/finish_pre/pallas_call | solution.py:68
  429.1 1.3 slice_bitcast_fusion.14
  431.0 1.8 select_convert_fusion
  432.9 1.1 slice.127
  434.0 1.8 slice_bitcast_fusion
  435.8 1.5 reshape.197
  437.3 2.5 copy.40
  439.8 2.3 pad_maximum_fusion
  (113 shorter events, 21.7 us)
Async XLA Ops:
  7.2 88.3 %all-gather.5.cloned.1.call-start = ((), (), s32[]{:S(2)}) async-start(), calls=%async_computation.10 | async-start | bytes 4866048 | tf_op jit(solution)/shard_map/all_gather | solution.py:786
  9.2 9.8 %copy-start.19 = (s32[2]{0:T(128)S(1)}, s32[2]{0:T(128)}, u32[]{:S(2)}) copy-start(s32[2]{0:T(128)} %param.16) | copy-start | bytes 28
  9.2 10.1 %copy-start.16 = (bf16[128,128]{0,1:T(8,128)(2,1)S(1)}, bf16[128,128]{0,1:T(8,128)(2,1)}, u32[]{:S(2)}) copy-start(bf16[128,128]{0,1:T(8,128)(2,1)} %constant.81.clone) | copy-start | bytes 98308
  12.2 24.5 %collective-permute-start.1 = (bf16[8,24,1024]{2,1,0:T(8,128)(2,1)S(1)}, bf16[8,24,1024]{2,1,0:T(8,128)(2,1)S(1)}, u32[]{:S(2)}, u32[]{:S(2)}) collective-permute-start(bf16[8,24,1024]{2,1,0:T(8,128)(2,1)S(1)} %get-tuple-element.77), channel_id=1, source_target_pairs={{4,0},{8,4},{12,8},{5,1},{9,5},{13,9},{6,2},{10,6},{14,10},{7,3},{... | collective-permute-start | bytes 1179656 | tf_op jit(solution)/shard_map/ppermute | solution.py:777
  13.5 23.2 %collective-permute-start = (bf16[8,24,1024]{2,1,0:T(8,128)(2,1)S(1)}, bf16[8,24,1024]{2,1,0:T(8,128)(2,1)}, u32[]{:S(2)}, u32[]{:S(2)}) collective-permute-start(bf16[8,24,1024]{2,1,0:T(8,128)(2,1)S(1)} %get-tuple-element.78), channel_id=1, source_target_pairs={{0,4},{4,8},{8,12},{1,5},{5,9},{9,13},{2,6},{6,10},{10,14},{3,7},{... | collective-permute-start | bytes 1179656 | tf_op jit(solution)/shard_map/ppermute | solution.py:776
  24.3 5.3 %copy-start.17 = (bf16[3,3,1024]{2,1,0:T(4,128)(2,1)S(1)}, bf16[3,3,1024]{2,1,0:T(4,128)(2,1)}, u32[]{:S(2)}) copy-start(bf16[3,3,1024]{2,1,0:T(4,128)(2,1)} %param.18) | copy-start | bytes 55300
  24.3 6.5 %copy-start.2 = (bf16[1024,1024]{1,0:T(8,128)(2,1)S(1)}, bf16[1024,1024]{1,0:T(8,128)(2,1)}, u32[]{:S(2)}) copy-start(bf16[1024,1024]{1,0:T(8,128)(2,1)} %wr.3) | copy-start | bytes 6291460
  24.3 88.0 %all-to-all-start = ((bf16[4,288,1024]{2,1,0:T(8,128)(2,1)}), bf16[4,288,1024]{2,1,0:T(8,128)(2,1)}, u32[]{:S(2)}, u32[]{:S(2)}) async-start(bf16[4,288,1024]{2,1,0:T(8,128)(2,1)} %cotangent_by_image.1), calls=%async_computation | async-start | bytes 4718592 | tf_op jit(solution)/shard_map/all_to_all | solution.py:791
  29.6 226.0 %reduce-scatter.4.cloned.1.call-start = ((), (), s32[]{:S(2)}) async-start(), calls=%async_computation.7 | async-start | bytes 2621440 | tf_op jit(solution)/shard_map/reduce_scatter | solution.py:818
  36.7 0.7 copy-start.13
  37.5 32.9 %copy-start.18 = (bf16[3,3,1024]{2,1,0:T(4,128)(2,1)S(1)}, bf16[3,3,1024]{2,1,0:T(4,128)(2,1)}, u32[]{:S(2)}) copy-start(bf16[3,3,1024]{2,1,0:T(4,128)(2,1)} %param.22) | copy-start | bytes 55300
  60.6 10.9 %collective-permute-start.2 = (bf16[72,1024]{1,0:T(8,128)(2,1)S(1)}, bf16[72,1024]{1,0:T(8,128)(2,1)S(1)}, u32[]{:S(2)}, u32[]{:S(2)}) collective-permute-start(bf16[72,1024]{1,0:T(8,128)(2,1)S(1)} %get-tuple-element.83), channel_id=1, source_target_pairs={{0,0},{1,4},{2,8},{3,12},{4,1},{5,5},{6,9},{7,13},{8,2},{9,6},{10,... | collective-permute-start | bytes 442376 | tf_op jit(solution)/shard_map/ppermute | solution.py:799
  61.3 10.2 %collective-permute-start.5 = (bf16[72,1024]{1,0:T(8,128)(2,1)S(1)}, bf16[72,1024]{1,0:T(8,128)(2,1)S(1)}, u32[]{:S(2)}, u32[]{:S(2)}) collective-permute-start(bf16[72,1024]{1,0:T(8,128)(2,1)S(1)} %get-tuple-element.84), channel_id=1, source_target_pairs={{0,3},{1,7},{2,11},{3,15},{4,0},{5,4},{6,8},{7,12},{8,1},{9,5},{10... | collective-permute-start | bytes 442376 | tf_op jit(solution)/shard_map/ppermute | solution.py:799
  66.0 16.4 %collective-permute-start.4 = (bf16[72,1024]{1,0:T(8,128)(2,1)S(1)}, bf16[72,1024]{1,0:T(8,128)(2,1)S(1)}, u32[]{:S(2)}, u32[]{:S(2)}) collective-permute-start(bf16[72,1024]{1,0:T(8,128)(2,1)S(1)} %get-tuple-element.85), channel_id=1, source_target_pairs={{0,2},{1,6},{2,10},{3,14},{4,3},{5,7},{6,11},{7,15},{8,0},{9,4},{1... | collective-permute-start | bytes 442376 | tf_op jit(solution)/shard_map/ppermute | solution.py:799
  69.0 25.6 %collective-permute-start.3 = (bf16[72,1024]{1,0:T(8,128)(2,1)S(1)}, bf16[72,1024]{1,0:T(8,128)(2,1)S(1)}, u32[]{:S(2)}, u32[]{:S(2)}) collective-permute-start(bf16[72,1024]{1,0:T(8,128)(2,1)S(1)} %get-tuple-element.86), channel_id=1, source_target_pairs={{0,1},{1,5},{2,9},{3,13},{4,2},{5,6},{6,10},{7,14},{8,3},{9,7},{10... | collective-permute-start | bytes 442376 | tf_op jit(solution)/shard_map/ppermute | solution.py:799
  142.1 4.6 %collective-permute-start.19 = (bf16[4,256,1024]{2,1,0:T(8,128)(2,1)}, bf16[4,256,1024]{2,1,0:T(8,128)(2,1)S(1)}, u32[]{:S(2)}, u32[]{:S(2)}) collective-permute-start(bf16[4,256,1024]{2,1,0:T(8,128)(2,1)} %dynamic-slice_bitcast_fusion), channel_id=1, source_target_pairs={{0,16},{16,0},{1,17},{17,1},{2,18},{18,2},{3,19},{19,3},{4,20},{20... | collective-permute-start | bytes 6291464 | tf_op jit(solution)/shard_map/ppermute | solution.py:611
  142.7 7.9 %copy-start.10 = (bf16[288,1024]{1,0:T(8,128)(2,1)S(1)}, bf16[288,1024]{1,0:T(8,128)(2,1)}, u32[]{:S(2)}) copy-start(bf16[288,1024]{1,0:T(8,128)(2,1)} %get-tuple-element.43.low_ref) | copy-start | bytes 1769476
  150.6 154.3 %reduce-scatter.6.cloned.1.call-start = ((), (), s32[]{:S(2)}) async-start(), calls=%async_computation.8 | async-start | bytes 1966080 | tf_op jit(solution)/shard_map/reduce_scatter | solution.py:835
  150.6 20.2 %collective-permute-start.8 = (bf16[288,1024]{1,0:T(8,128)(2,1)S(1)}, bf16[288,1024]{1,0:T(8,128)(2,1)S(1)}, u32[]{:S(2)}, u32[]{:S(2)}) collective-permute-start(bf16[288,1024]{1,0:T(8,128)(2,1)S(1)} %copy-done.10), channel_id=1, source_target_pairs={{0,3},{1,0},{2,1},{3,2},{4,7},{5,4},{6,5},{7,6},{8,11},{9,8},{10,9... | collective-permute-start | bytes 1769480 | tf_op jit(solution)/shard_map/ppermute | solution.py:806
  150.7 21.7 %collective-permute-start.7 = (bf16[288,1024]{1,0:T(8,128)(2,1)S(1)}, bf16[288,1024]{1,0:T(8,128)(2,1)S(1)}, u32[]{:S(2)}, u32[]{:S(2)}) collective-permute-start(bf16[288,1024]{1,0:T(8,128)(2,1)S(1)} %copy-done.10), channel_id=1, source_target_pairs={{0,2},{1,3},{2,0},{3,1},{4,6},{5,7},{6,4},{7,5},{8,10},{9,11},{10,... | collective-permute-start | bytes 1769480 | tf_op jit(solution)/shard_map/ppermute | solution.py:806
  151.8 40.9 %collective-permute-start.6 = (bf16[288,1024]{1,0:T(8,128)(2,1)S(1)}, bf16[288,1024]{1,0:T(8,128)(2,1)S(1)}, u32[]{:S(2)}, u32[]{:S(2)}) collective-permute-start(bf16[288,1024]{1,0:T(8,128)(2,1)S(1)} %copy-done.10), channel_id=1, source_target_pairs={{0,1},{1,2},{2,3},{3,0},{4,5},{5,6},{6,7},{7,4},{8,9},{9,10},{10,1... | collective-permute-start | bytes 1769480 | tf_op jit(solution)/shard_map/ppermute | solution.py:806
  210.2 2.3 copy-start.11
  210.3 44.8 %collective-permute-start.20 = (bf16[4,128,1024]{2,1,0:T(8,128)(2,1)S(1)}, bf16[4,128,1024]{2,1,0:T(8,128)(2,1)S(1)}, u32[]{:S(2)}, u32[]{:S(2)}) collective-permute-start(bf16[4,128,1024]{2,1,0:T(8,128)(2,1)S(1)} %dynamic-slice_bitcast_fusion.1), channel_id=1, source_target_pairs={{0,16},{16,0},{1,17},{17,1},{2,18},{18,2},{3,19},{19,3},{4,20},{20... | collective-permute-start | bytes 3145736 | tf_op jit(solution)/shard_map/ppermute | solution.py:611
  212.5 11.7 %collective-permute-start.9 = (bf16[72,1024]{1,0:T(8,128)(2,1)S(1)}, bf16[72,1024]{1,0:T(8,128)(2,1)S(1)}, u32[]{:S(2)}, u32[]{:S(2)}) collective-permute-start(bf16[72,1024]{1,0:T(8,128)(2,1)S(1)} %get-tuple-element.79), channel_id=1, source_target_pairs={{0,0},{4,1},{8,2},{12,3},{1,4},{5,5},{9,6},{13,7},{2,8},{6,9},{10,... | collective-permute-start | bytes 442376 | tf_op jit(solution)/shard_map/ppermute | solution.py:812
  213.2 11.1 %collective-permute-start.12 = (bf16[72,1024]{1,0:T(8,128)(2,1)S(1)}, bf16[72,1024]{1,0:T(8,128)(2,1)S(1)}, u32[]{:S(2)}, u32[]{:S(2)}) collective-permute-start(bf16[72,1024]{1,0:T(8,128)(2,1)S(1)} %get-tuple-element.80), channel_id=1, source_target_pairs={{3,0},{7,1},{11,2},{15,3},{0,4},{4,5},{8,6},{12,7},{1,8},{5,9},{9,... | collective-permute-start | bytes 442376 | tf_op jit(solution)/shard_map/ppermute | solution.py:812
  217.9 12.5 %collective-permute-start.11 = (bf16[72,1024]{1,0:T(8,128)(2,1)S(1)}, bf16[72,1024]{1,0:T(8,128)(2,1)S(1)}, u32[]{:S(2)}, u32[]{:S(2)}) collective-permute-start(bf16[72,1024]{1,0:T(8,128)(2,1)S(1)} %get-tuple-element.81), channel_id=1, source_target_pairs={{2,0},{6,1},{10,2},{14,3},{3,4},{7,5},{11,6},{15,7},{0,8},{4,9},{8... | collective-permute-start | bytes 442376 | tf_op jit(solution)/shard_map/ppermute | solution.py:812
  221.3 9.1 %collective-permute-start.10 = (bf16[72,1024]{1,0:T(8,128)(2,1)S(1)}, bf16[72,1024]{1,0:T(8,128)(2,1)S(1)}, u32[]{:S(2)}, u32[]{:S(2)}) collective-permute-start(bf16[72,1024]{1,0:T(8,128)(2,1)S(1)} %get-tuple-element.82), channel_id=1, source_target_pairs={{1,0},{5,1},{9,2},{13,3},{2,4},{6,5},{10,6},{14,7},{3,8},{7,9},{11... | collective-permute-start | bytes 442376 | tf_op jit(solution)/shard_map/ppermute | solution.py:812
  252.4 12.7 %collective-permute-start.13 = (bf16[8,24,1024]{2,1,0:T(8,128)(2,1)}, bf16[8,24,1024]{2,1,0:T(8,128)(2,1)S(1)}, u32[]{:S(2)}, u32[]{:S(2)}) collective-permute-start(bf16[8,24,1024]{2,1,0:T(8,128)(2,1)} %get-tuple-element.55), channel_id=1, source_target_pairs={{0,4},{4,8},{8,12},{1,5},{5,9},{9,13},{2,6},{6,10},{10,14},{3,7},{... | collective-permute-start | bytes 1179656 | tf_op jit(solution)/shard_map/ppermute | solution.py:851
  253.8 11.3 %collective-permute-start.14 = (bf16[8,24,1024]{2,1,0:T(8,128)(2,1)}, bf16[8,24,1024]{2,1,0:T(8,128)(2,1)S(1)}, u32[]{:S(2)}, u32[]{:S(2)}) collective-permute-start(bf16[8,24,1024]{2,1,0:T(8,128)(2,1)} %get-tuple-element.56), channel_id=1, source_target_pairs={{4,0},{8,4},{12,8},{5,1},{9,5},{13,9},{6,2},{10,6},{14,10},{7,3},{... | collective-permute-start | bytes 1179656 | tf_op jit(solution)/shard_map/ppermute | solution.py:852
  263.3 14.9 %copy-start.4 = (bf16[1024,1024]{1,0:T(8,128)(2,1)}, bf16[1024,1024]{1,0:T(8,128)(2,1)S(1)}, u32[]{:S(2)}) copy-start(bf16[1024,1024]{1,0:T(8,128)(2,1)S(1)} %bitcast_convert_fusion.refs_1_) | copy-start | bytes 6291460
  263.4 25.6 %collective-permute-start.16 = (bf16[512,1024]{1,0:T(8,128)(2,1)S(1)}, bf16[512,1024]{1,0:T(8,128)(2,1)S(1)}, u32[]{:S(2)}, u32[]{:S(2)}) collective-permute-start(bf16[512,1024]{1,0:T(8,128)(2,1)S(1)} %dynamic-slice_bitcast_fusion.2), channel_id=1, source_target_pairs={{0,16},{16,0},{1,17},{17,1},{2,18},{18,2},{3,19},{19,3},{4,20},{20... | collective-permute-start | bytes 3145736 | tf_op jit(solution)/shard_map/ppermute | solution.py:611
  265.1 0.7 copy-start.12
  265.1 0.9 copy-start.14
  266.0 12.2 %copy-start.6 = (bf16[8,6,24,1024]{3,2,1,0:T(8,128)(2,1)S(1)}, bf16[8,6,24,1024]{3,2,1,0:T(8,128)(2,1)}, u32[]{:S(2)}) copy-start(bf16[8,6,24,1024]{3,2,1,0:T(8,128)(2,1)} %feat.1) | copy-start | bytes 7077892
  283.1 6.0 %copy-start.5 = (bf16[1024,1024]{0,1:T(8,128)(2,1)}, bf16[1024,1024]{0,1:T(8,128)(2,1)S(1)}, u32[]{:S(2)}) copy-start(bf16[1024,1024]{0,1:T(8,128)(2,1)S(1)} %convolution_convert_fusion.1) | copy-start | bytes 6291460
  283.2 5.9 %collective-permute-start.15 = (bf16[512,1024]{1,0:T(8,128)(2,1)S(1)}, bf16[512,1024]{1,0:T(8,128)(2,1)S(1)}, u32[]{:S(2)}, u32[]{:S(2)}) collective-permute-start(bf16[512,1024]{1,0:T(8,128)(2,1)S(1)} %dynamic-slice_bitcast_fusion.3), channel_id=1, source_target_pairs={{0,16},{16,0},{1,17},{17,1},{2,18},{18,2},{3,19},{19,3},{4,20},{20... | collective-permute-start | bytes 3145736 | tf_op jit(solution)/shard_map/ppermute | solution.py:611
  287.5 1.6 collective-permute-start.17
  289.1 0.6 copy-start.15
  289.1 1.0 copy-start.8
  289.1 1.3 copy-start.9
  294.5 45.0 %all-to-all-start.1 = ((bf16[64,8,2176]{2,1,0:T(8,128)(2,1)}), bf16[64,8,2176]{2,1,0:T(8,128)(2,1)S(1)}, u32[]{:S(2)}, u32[]{:S(2)}) async-start(bf16[64,8,2176]{2,1,0:T(8,128)(2,1)} %bitcast.130), calls=%async_computation.1 | async-start | bytes 4456448 | tf_op jit(solution)/shard_map/all_to_all | solution.py:863
  304.8 33.2 %reduce-scatter.8.cloned.1.call-start = ((), (), s32[]{:S(2)}) async-start(), calls=%async_computation.9 | async-start | bytes 491520 | tf_op jit(solution)/shard_map/reduce_scatter | solution.py:836
  339.4 4.2 copy-start.1
  339.4 8.7 %all-to-all-start.3 = ((bf16[4,8,1024]{2,1,0:T(8,128)(2,1)}), bf16[4,8,1024]{2,1,0:T(8,128)(2,1)S(1)}, u32[]{:S(2)}, u32[]{:S(2)}) async-start(bf16[4,8,1024]{2,1,0:T(8,128)(2,1)} %slice_bitcast_fusion.12), calls=%async_computation.6 | async-start | bytes 131072 | tf_op jit(solution)/shard_map/all_to_all | solution.py:837
  348.1 36.7 %all-to-all-start.2 = ((bf16[64,8,2176]{2,1,0:T(8,128)(2,1)}), bf16[64,8,2176]{2,1,0:T(8,128)(2,1)S(1)}, u32[]{:S(2)}, u32[]{:S(2)}) async-start(bf16[64,8,2176]{2,1,0:T(8,128)(2,1)} %sum_and_copy.1), calls=%async_computation.2 | async-start | bytes 4456448 | tf_op jit(solution)/shard_map/all_to_all | solution.py:864
  357.1 54.3 %all-gather.7.cloned.1.call-start = ((), (), s32[]{:S(2)}) async-start(), calls=%async_computation.11 | async-start | bytes 1671168 | tf_op jit(solution)/shard_map/all_gather | solution.py:839
  384.9 36.0 %copy-start = (bf16[64,8,2176]{2,1,0:T(8,128)(2,1)}, bf16[64,8,2176]{2,1,0:T(8,128)(2,1)S(1)}, u32[]{:S(2)}) copy-start(bf16[64,8,2176]{2,1,0:T(8,128)(2,1)S(1)} %all-to-all-done.2) | copy-start | bytes 6684676
  384.9 36.0 %collective-permute-start.18 = (bf16[512,2176]{1,0:T(8,128)(2,1)S(1)}, bf16[512,2176]{1,0:T(8,128)(2,1)}, u32[]{:S(2)}, u32[]{:S(2)}) collective-permute-start(bf16[512,2176]{1,0:T(8,128)(2,1)S(1)} %bitcast.128), channel_id=1, source_target_pairs={{0,16},{16,0},{1,17},{17,1},{2,18},{18,2},{3,19},{19,3},{4,20},{20... | collective-permute-start | bytes 6684680 | tf_op jit(solution)/shard_map/ppermute | solution.py:611
  411.4 19.6 %collective-permute-start.21 = (bf16[16,48,1024]{2,1,0:T(8,128)(2,1)}, bf16[16,48,1024]{2,1,0:T(8,128)(2,1)}, u32[]{:S(2)}, u32[]{:S(2)}) collective-permute-start(bf16[16,48,1024]{2,1,0:T(8,128)(2,1)} %bitcast.146), channel_id=1, source_target_pairs={{0,16},{16,0},{1,17},{17,1},{2,18},{18,2},{3,19},{19,3},{4,20},{20... | collective-permute-start | bytes 4718600 | tf_op jit(solution)/shard_map/ppermute | solution.py:611
  420.9 10.1 %copy-start.7 = (bf16[768,1024]{1,0:T(8,128)(2,1)S(1)}, bf16[768,1024]{1,0:T(8,128)(2,1)}, u32[]{:S(2)}) copy-start(bf16[768,1024]{1,0:T(8,128)(2,1)} %all-gather.7.cloned.1.call-done) | copy-start | bytes 4718596
  437.3 2.6 copy-start.3
Sparse Core Ops, SparseCore 0:
  11.2 58.9 all-gather.4
  150.7 47.4 reduce-scatter.3
  258.2 28.6 reduce-scatter.5
  307.8 30.0 reduce-scatter.7
  360.4 50.9 all-gather.6

commit v4 on v3

--- a/solution.py
+++ b/solution.py
@@ -53,7 +53,7 @@
     lax.fori_loop(0, count, step, 0)
 
 
-def call(kernel, *, grid, ins, outs, scratch=(), prefetch=0, flops=0, name):
+def call(kernel, *, grid, ins, outs, scratch=(), prefetch=0, name):
     def spec(shape, block, index):
         if block is None:
             block, index = shape, lambda *_: (0,) * len(shape)
@@ -62,7 +62,6 @@
     arrays = [i[0] for i in ins]
     in_specs = [spec(a.shape, b, m) for a, b, m in ins]
     out_specs = [spec(s.shape, b, m) for s, b, m in outs]
-    moved = sum(a.size * a.dtype.itemsize for a in arrays) + sum(s[0].size * s[0].dtype.itemsize for s in outs)
 
     def run(*scalars):
         return pl.pallas_call(
@@ -78,7 +77,7 @@
             compiler_params=pltpu.CompilerParams(
                 dimension_semantics=("arbitrary",) * len(grid), vmem_limit_bytes=VMEM_LIMIT
             ),
-            cost_estimate=pl.CostEstimate(flops=flops, bytes_accessed=int(moved), transcendentals=0),
+            cost_estimate=pl.CostEstimate(flops=1, bytes_accessed=1, transcendentals=0),
             name=name,
         )(*scalars, *arrays)
 
@@ -105,7 +104,8 @@
     n = order.shape[0]
     part = slots // n
 
-    def kernel(order_ref, red, up_ref, down_ref, feat, wr, tap, we, gn, pool_ref, conv_out, act_out, norm_out, std_out, pooled_out, halo, exp, sums):
+    def kernel(order_ref, red, up_ref, down_ref, feat, wr, tap, we, gn, pool_ref, conv_out, act_out, norm_out, std_out, *rest):
+        pooled_out, (halo, exp, sums) = rest[:-3], rest[-3:]
         k = pl.program_id(0)
 
         @pl.when(k == 0)
@@ -158,7 +158,12 @@
         s = sums[...]
         hi = s.astype(BF)
         lo = (s - hi.astype(F32)).astype(BF)
-        pooled_out[0] = (dot(pool_ref[...], hi) + dot(pool_ref[...], lo)).astype(BF)
+        pooled = (dot(pool_ref[...], hi) + dot(pool_ref[...], lo)).astype(BF)
+        for i in range(n):
+
+            @pl.when(k == i)
+            def _():
+                pooled_out[i][...] = pooled
 
     def by_order(rest):
         return lambda k, order: (order[k],) + (0,) * rest
@@ -184,31 +189,39 @@
             (shape((slots, cells, ch), BF), (part, cells, ch), by_order(2)),
             (shape((slots, cells, ch), F32), (part, cells, ch), by_order(2)),
             (shape((slots, cells, 1), F32), (part, cells, 1), by_order(2)),
-            (shape((n, pooled_rows, ch), BF), (1, pooled_rows, ch), lambda k, order: (k, 0, 0)),
-        ],
+        ]
+        + [(shape((pooled_rows, ch), BF), None, None)] * n,
         scratch=[
             pltpu.VMEM((2, slots, wide, ch), F32),
             pltpu.VMEM((part * cells, ch), F32),
             pltpu.VMEM((part * cells // 2, ch), F32),
         ],
-        flops=2 * slots * cells * ch * ch,
         name="pre_forward",
     )(order)
 
 
-def post_forward(source, moved, weights, gain, taps, pool):
-    n, rows, ch = moved.shape
+def gain_row(w, n, share):
+    at = 2 * share
+    parts = [w[c, at : at + 16, :].astype(F32)[:1] for c in range(n)]
+    return jnp.concatenate([p[:, :share] + p[:, share : 2 * share] for p in parts], 1)
+
+
+def post_forward(source, moved, weights, taps, pool):
+    n, (rows, ch) = len(moved), moved[0].shape
     total = n * rows
     depth = total // (pool * pool)
     share = ch // n
 
-    def kernel(src, got, w, gn, tap, flat_out, red_out, act_out, conv_out, cact_out, norm_out, std_out, low_out, wide_ref):
-        for r in range(n):
-            wide_ref[pl.ds(r * rows, rows), :] = got[src[r]].astype(F32)
+    def kernel(src, *refs):
+        got, (w, tap, flat_out, red_out, act_out, conv_out, cact_out, norm_out, std_out, low_out, wide_ref) = refs[:n], refs[n:]
+        for k in range(n):
+            at = pl.multiple_of(src[k] * rows, 8)
+            wide_ref[pl.ds(at, rows), :] = got[k][...].astype(F32)
+        gain = gain_row(w, n, share)
         flat_out[...] = wide_ref[...].astype(BF)
         red = 0.0
         for c in range(n):
-            red = red + dot(flat_out[:, c * share : (c + 1) * share], w[c, 0])
+            red = red + dot(flat_out[:, c * share : (c + 1) * share], w[c, :share])
         red_out[...] = red
         first, last = edge_masks(total, pool, depth)
         step = pool * depth
@@ -229,7 +242,7 @@
             e = 0.0
             for q in range(n):
                 cut = slice(q * share, (q + 1) * share)
-                e = e + dot(cact_out[:, cut], w[c, 1, :, cut])
+                e = e + dot(cact_out[:, cut], w[c, share : 2 * share, cut])
             norm_out[:, c * share : (c + 1) * share] = e
 
         def norm(i, carry):
@@ -241,7 +254,7 @@
             nrm = (e - mean) * std
             norm_out[at, :] = nrm
             std_out[at, :] = std
-            low_out[at, :] = (wide_ref[at, :] + silu(nrm * gn[...])).astype(BF)
+            low_out[at, :] = (wide_ref[at, :] + silu(nrm * gain)).astype(BF)
             return carry
 
         lax.fori_loop(0, total // 16, norm, 0)
@@ -252,15 +265,14 @@
         kernel,
         grid=(1,),
         prefetch=1,
-        ins=[(a, None, None) for a in (moved, weights, gain, taps)],
+        ins=[(a, None, None) for a in (*moved, weights, taps)],
         outs=[(s, None, None) for s in (narrow, wide, narrow, wide, narrow, wide, shape((total, 1), F32), narrow)],
         scratch=[pltpu.VMEM((total, ch), F32)],
-        flops=4 * total * ch * ch,
         name="post_forward",
     )(source)
 
 
-def post_backward(source, low, readout, cots, weights, gain, taps, act, red, conv, nrm, std, pool):
+def post_backward(source, low, readout, cots, weights, taps, act, red, conv, nrm, std, pool):
     total, ch = low.shape
     n = cots.shape[0]
     share = ch // n
@@ -268,7 +280,8 @@
     rows = total // n
     depth = total // (pool * pool)
 
-    def kernel(src, low_ref, ro, cot, w, gn, tap, act_ref, red_ref, conv_ref, norm_ref, std_ref, exp_out, redg_out, back_out, taps_out, gain_out, grad, cgrad):
+    def kernel(src, low_ref, ro, cot, w, tap, act_ref, red_ref, conv_ref, norm_ref, std_ref, exp_out, redg_out, taps_out, gain_out, *rest):
+        back_out, (grad, cgrad) = rest[:n], rest[n:]
         k = pl.program_id(0)
         logits = dot(low_ref[...], ro[...])
         piece = (cot[0].astype(F32) * gelu_parts(logits)[1]).astype(BF)
@@ -284,11 +297,13 @@
 
         @pl.when(k == n - 1)
         def _():
+            gain = gain_row(w, n, share)
+
             def norm(i, total_gain):
                 at = pl.ds(pl.multiple_of(i * 16, 16), 16)
                 nm = norm_ref[at, :]
-                ng = grad[at, :] * silu_slope(nm * gn[...])
-                sc = ng * gn[...]
+                ng = grad[at, :] * silu_slope(nm * gain)
+                sc = ng * gain
                 one = jnp.mean(sc, -1, keepdims=True)
                 two = jnp.mean(sc * nm, -1, keepdims=True)
                 exp_out[at, :] = (std_ref[at, :] * (sc - one - nm * two)).astype(BF)
@@ -300,7 +315,7 @@
                 cut = slice(q * share, (q + 1) * share)
                 cg = 0.0
                 for c in range(n):
-                    cg = cg + dot(exp_out[:, c * share : (c + 1) * share], w[c, 1, :, cut], NT)
+                    cg = cg + dot(exp_out[:, c * share : (c + 1) * share], w[c, share : 2 * share, cut], NT)
                 cgrad[:, cut] = cg
             first, last = edge_masks(total, pool, depth)
             step = pool * depth
@@ -326,10 +341,10 @@
             chunks(ch // LANES, back)
             for c in range(n):
                 cut = slice(c * share, (c + 1) * share)
-                grad[:, cut] += dot(redg_out[...], w[c, 0], NT)
+                grad[:, cut] += dot(redg_out[...], w[c, :share], NT)
             for r in range(n):
                 at = pl.ds(pl.multiple_of(src[r] * rows, 8), rows)
-                back_out[r] = grad[at, :].astype(BF)
+                back_out[r][...] = grad[at, :].astype(BF)
 
     return call(
         kernel,
@@ -340,19 +355,18 @@
             (readout, (ch, out_share), lambda k, s: (0, k)),
             (cots, (1, total, out_share), lambda k, s: (k, 0, 0)),
         ]
-        + [(a, None, None) for a in (weights, gain, taps, act, red, conv, nrm, std)],
+        + [(a, None, None) for a in (weights, taps, act, red, conv, nrm, std)],
         outs=[
             (s, None, None)
             for s in (
                 shape((total, ch), BF),
                 shape((total, ch), BF),
-                shape((n, rows, ch), BF),
                 shape((9, 8, ch), F32),
                 shape((8, ch), F32),
+                *[shape((rows, ch), BF)] * n,
             )
         ],
         scratch=[pltpu.VMEM((total, ch), F32), pltpu.VMEM((total, ch), F32)],
-        flops=2 * total * ch * (2 * out_share * n + 2 * ch),
         name="post_backward",
     )(source)
 
@@ -375,22 +389,24 @@
         grid=(rows // (per * size),),
         ins=[(cotangent, (per * size, width), lambda i: (i, 0)), (select, None, None)],
         outs=[(shape((pairs, rows // pairs, width), BF), (pairs, per * each, width), lambda i: (0, i, 0))],
-        flops=2 * rows * size * width,
         name="cotangent_by_image",
     )()[0]
 
 
 def token_block(chan, source, low, place, readout, cotangent, live):
-    pairs, each_all, ch = low.shape
+    pairs, ch = len(low), low[0].shape[1]
     rows, width = cotangent.shape
     size = place.shape[0]
     each = size // pairs
     per = 3
 
-    def kernel(chan_ref, src, low_ref, place_ref, ro, cot, alive, tok_out, piece_out, low_out):
+    def kernel(chan_ref, src, *refs):
+        lows, (place_ref, ro, cot, alive, tok_out, piece_out, low_out, by_pair) = refs[:pairs], refs[pairs:]
+        for k in range(pairs):
+            by_pair[src[k]] = lows[k][...]
         for q in range(per):
             at = pl.ds(q * size, size)
-            x = jnp.concatenate([low_ref[src[s], pl.ds(q * each, each), :] for s in range(pairs)], 0)
+            x = jnp.concatenate([by_pair[s, pl.ds(q * each, each), :] for s in range(pairs)], 0)
             low_out[at, :] = dot(place_ref[...], x).astype(BF)
         logits = dot(low_out[...], ro[...])
         value, slope = gelu_parts(logits)
@@ -404,7 +420,7 @@
         grid=(rows // block,),
         prefetch=2,
         ins=[
-            (low, (pairs, per * each, ch), lambda i, c, s: (0, i, 0)),
+            *[(v, (per * each, ch), lambda i, c, s: (i, 0)) for v in low],
             (place, None, None),
             (readout, (ch, width), lambda i, c, s: (0, c[0])),
             (cotangent, (block, width), row_block),
@@ -415,7 +431,7 @@
             (shape((rows, width), BF), (block, width), row_block),
             (shape((rows, ch), BF), (block, ch), row_block),
         ],
-        flops=2 * rows * ch * width,
+        scratch=[pltpu.VMEM((pairs, per * each, ch), BF)],
         name="token_block",
     )(chan, source)
 
@@ -427,9 +443,15 @@
     wide = 24
     rows = part * cells
 
-    def kernel(order_ref, ret, up, norm_ref, std_ref, gn, conv_ref, we, exp_out, conv_grad_out, top_out, bottom_out, gain_out, grad, cgrad):
+    def kernel(order_ref, *refs):
+        ret, refs = refs[:n], refs[n:]
+        up, norm_ref, std_ref, gn, conv_ref, we, exp_out, conv_grad_out, top_out, bottom_out, gain_out, grad, cgrad = refs
         k = pl.program_id(0)
-        grad[...] = dot(up[...], ret[0])
+        for i in range(n):
+
+            @pl.when(k == i)
+            def _():
+                grad[...] = dot(up[...], ret[i][...])
 
         def norm(i, total_gain):
             u, j = i // (cells // 16), i % (cells // 16)
@@ -472,7 +494,7 @@
         grid=(n,),
         prefetch=1,
         ins=[
-            (returned, (1,) + returned.shape[1:], lambda k, order: (k, 0, 0)),
+            *[(r, None, None) for r in returned],
             (spread_up, None, None),
             (nrm, whole, by_order),
             (std, (part, cells, 1), by_order),
@@ -488,7 +510,6 @@
             (shape((8, ch), F32), None, None),
         ],
         scratch=[pltpu.VMEM((rows, ch), F32), pltpu.VMEM((rows, ch), F32)],
-        flops=2 * slots * cells * ch * ch,
         name="pre_backward",
     )(order)
 
@@ -549,7 +570,6 @@
             (shape((slots, cells, ch), BF), (1, cells, ch), image),
             (shape((9, 8, ch), F32), None, None),
         ],
-        flops=0,
         name="pre_conv_backward",
     )()
 
@@ -559,9 +579,16 @@
     n = order.shape[0]
     part = slots // n
 
-    def kernel(order_ref, rg, wr, ret, up, out):
-        g = dot(rg[...].reshape(part * cells, ch), wr[...], NT) + dot(up[...], ret[0])
-        out[...] = g.reshape(part, cells, ch)
+    def kernel(order_ref, rg, wr, up, *refs):
+        ret, out = refs[:n], refs[n]
+        k = pl.program_id(0)
+        for i in range(n):
+
+            @pl.when(k == i)
+            def _():
+                out[...] = dot(up[...], ret[i][...]).reshape(part, cells, ch)
+
+        out[...] += dot(rg[...].reshape(part * cells, ch), wr[...], NT).reshape(part, cells, ch)
 
     by_order = lambda k, order: (order[k], 0, 0)
     whole = (part, cells, ch)
@@ -572,11 +599,10 @@
         ins=[
             (reduced_grad, whole, by_order),
             (pre_reduce, None, None),
-            (returned, (1,) + returned.shape[1:], lambda k, order: (k, 0, 0)),
             (spread_up, None, None),
+            *[(r, None, None) for r in returned],
         ],
         outs=[(shape((slots, cells, ch), F32), whole, by_order)],
-        flops=2 * slots * cells * ch * ch,
         name="feature_backward",
     )(order)[0]
 
@@ -588,17 +614,16 @@
     def kernel(x, g, a, e, out):
         for c in range(n):
             cut = slice(c * share, (c + 1) * share)
-            out[0, c] = dot(x[:, cut], g[...], TN).astype(BF)
+            out[c, :, :ch] = dot(x[:, cut], g[...], TN).astype(BF)
             for q in range(n):
                 rows = slice(q * share, (q + 1) * share)
-                out[1, c, :, rows] = dot(a[:, rows], e[:, cut], TN).astype(BF)
+                out[c, :, ch + q * share : ch + (q + 1) * share] = dot(a[:, rows], e[:, cut], TN).astype(BF)
 
     return call(
         kernel,
         grid=(1,),
         ins=[(v, None, None) for v in (flat, reduced_grad, act, expanded_grad)],
-        outs=[(shape((2, n, share, ch), BF), None, None)],
-        flops=4 * total * ch * ch,
+        outs=[(shape((n, share, 2 * ch), BF), None, None)],
         name="post_weight_grads",
     )()[0]
 
@@ -714,6 +739,37 @@
         + [(shape((half, LANES), F32), None, None)],
         name="finish_pre",
     )(core)
+
+
+def finish_post(gathered, n, share):
+    groups, rows, ch = gathered.shape
+    eight = share // groups
+    per = 4
+
+    def kernel(x, reduce_out, expand_out, read_out):
+        for g in range(per):
+            at = pl.ds(g * eight, eight)
+            v = x[g].astype(F32)
+            reduce_out[at, :] = v[:eight]
+            for q in range(n):
+                expand_out[q, at, :] = v[eight : 2 * eight, q * share : (q + 1) * share]
+                read_out[at, q * ch : (q + 1) * ch] = v[(2 + q) * eight : (3 + q) * eight]
+
+    return call(
+        kernel,
+        grid=(groups // per,),
+        ins=[(gathered, (per, rows, ch), lambda i: (i, 0, 0))],
+        outs=[
+            (shape((share, ch), F32), (per * eight, ch), lambda i: (i, 0)),
+            (shape((n, share, share), F32), (n, per * eight, share), lambda i: (0, i, 0)),
+            (shape((share, n * ch), F32), (per * eight, n * ch), lambda i: (i, 0)),
+        ],
+        name="finish_post",
+    )()
+
+
+def after(values, *earlier):
+    return lax.optimization_barrier((values, *earlier))[0]
 
 
 def pool_matrix(part, high, wide):
@@ -792,68 +848,60 @@
 
     flat_features = features.reshape(slots * cells, ch)
     reduced = dot(flat_features, pre_reduce).reshape(slots, cells, ch)
-    convolved, convolved_act, normal_pre, pre_std, pooled = pre_forward(
+    convolved, convolved_act, normal_pre, pre_std, *pooled = pre_forward(
         order, reduced, above, below, features, pre_reduce, pre_taps, pre_expand, pre_gain_row, pool_m
     )
 
-    moved = jnp.stack([lax.ppermute(pooled[k], ("rows", "chan"), spread(n, k)) for k in range(n)])
-    weights = full[:, : 2 * share].reshape(n, 2, share, ch)
-    gain_parts = full[:, 2 * share].astype(F32)
-    post_gain_row = (gain_parts[:, :share] + gain_parts[:, share : 2 * share]).reshape(1, ch)
+    moved = [lax.ppermute(pooled[k], ("rows", "chan"), spread(n, k)) for k in range(n)]
     flat, post_reduced, post_act, post_convolved, post_cact, post_normal, post_std, low = post_forward(
-        source, moved, weights, post_gain_row, post_taps, pool
+        source, moved, full, post_taps, pool
     )
     lows = [low] + [lax.ppermute(low, "chan", [(i, (i + k) % n) for i in range(n)]) for k in range(1, n)]
-    post_expanded_grad, post_reduced_grad, back, post_taps_grad, post_gain_grad = post_backward(
-        source, low, readout, cots, weights, post_gain_row, post_taps, post_act, post_reduced, post_convolved, post_normal, post_std, pool
+    post_expanded_grad, post_reduced_grad, post_taps_grad, post_gain_grad, *back = post_backward(
+        source, low, readout, cots, full, post_taps, post_act, post_reduced, post_convolved, post_normal, post_std, pool
     )
 
-    returned = jnp.stack(
-        [lax.ppermute(back[k], ("rows", "chan"), [(d, s) for s, d in spread(n, k)]) for k in range(n)]
-    )
+    returned = [lax.ppermute(back[k], ("rows", "chan"), [(d, s) for s, d in spread(n, k)]) for k in range(n)]
 
     post_load = post_weight_grads(flat, post_reduced_grad, post_cact, post_expanded_grad, n)
-    post_keep = lax.dynamic_index_in_dim(post_load, core, 0, keepdims=False)
-    post_got = other_core(lax.dynamic_index_in_dim(post_load, 1 - core, 0, keepdims=False))
-    post_sum = lax.psum_scatter((post_keep.astype(F32) + post_got.astype(F32)).astype(BF), "chan", scatter_dimension=0, tiled=False)
+    post_sum = lax.psum_scatter(post_load, "chan", scatter_dimension=0, tiled=False)
 
     alive = jnp.broadcast_to(jnp.tile(live, 48)[:, None], (48 * slots, 1))
-    tokens, piece, low_here = token_block(rank, source, jnp.stack(lows), place, readout, cot_rows, alive)
-    readout_grad = dot(low_here, piece, TN).astype(BF).reshape(n, 2, share // 2, out_share)
+    lows = after(lows, post_load)
+    tokens, piece, low_here = token_block(rank, source, lows, place, readout, cot_rows, alive)
+    readout_grad = dot(low_here, piece, TN).astype(BF)
     tokens = tokens.reshape(pool, pool, slots, out_share).transpose(2, 0, 1, 3)
-    read_keep = lax.dynamic_index_in_dim(readout_grad, core, 1, keepdims=False)
-    read_got = other_core(lax.dynamic_index_in_dim(readout_grad, 1 - core, 1, keepdims=False))
-    read_sum = (read_keep.astype(F32) + read_got.astype(F32)).astype(BF)
-    eight = share // 32
-    load = jnp.concatenate(
-        [
-            post_sum.reshape(4, 4, 2 * eight, ch),
-            read_sum.reshape(n, 4, 4, eight, out_share).transpose(1, 2, 0, 3, 4).reshape(4, 4, n * eight, out_share),
-        ],
-        axis=2,
-    )
-    load = lax.psum_scatter(load, "x", scatter_dimension=0, tiled=False)
-    load = lax.psum_scatter(load, "rows", scatter_dimension=0, tiled=False)
-    read_part = lax.all_to_all(load[2 * eight :].reshape(n, eight, out_share), "chan", 0, 0, tiled=False)
-    load = jnp.concatenate([load[: 2 * eight], read_part.reshape(n * eight, out_share)], axis=0)
-    half_all = lax.all_gather(load, ("x", "rows"), axis=0, tiled=False)
-    half_got = other_core(half_all)
-    first = jnp.where(core == 0, half_all, half_got).astype(F32)
-    second = jnp.where(core == 0, half_got, half_all).astype(F32)
-    post_reduce_out = first[:, : 2 * eight].reshape(share, ch)
-    post_expand_out = second[:, : 2 * eight].reshape(share, n, share).transpose(1, 0, 2).reshape(ch, share)
-    readout_out = jnp.stack([first[:, 2 * eight :], second[:, 2 * eight :]]).reshape(2, 16, n, eight, out_share)
-    readout_out = readout_out.transpose(0, 1, 3, 2, 4).reshape(share, n * out_share)
-
+
+    returned = after(returned, readout_grad)
     expanded_grad, convolved_grad, top, bottom, pre_gain_grad = pre_backward(
         order, returned, up_m, normal_pre, pre_std, pre_gain_row, convolved, pre_expand
     )
     grad_above = lax.ppermute(bottom, "rows", down_pairs)
     grad_below = lax.ppermute(top, "rows", up_pairs)
-    pre_expand_grad = dot(convolved_act.reshape(-1, ch), expanded_grad.reshape(-1, ch), TN).astype(BF)
+
+    eight = share // 32
+    read_rows = after(readout_grad, bottom).reshape(n, 8, 4, eight, out_share).transpose(1, 2, 0, 3, 4)
+    load = jnp.concatenate(
+        [
+            post_sum[:, :ch].reshape(8, 4, eight, ch),
+            post_sum[:, ch:].reshape(8, 4, eight, ch),
+            read_rows.reshape(8, 4, n * eight, out_share),
+        ],
+        axis=2,
+    )
+    load = lax.psum_scatter(load, ("x", "core"), scatter_dimension=0, tiled=False)
+    load = lax.psum_scatter(load, "rows", scatter_dimension=0, tiled=False)
+    read_part = lax.all_to_all(load[2 * eight :].reshape(n, eight, out_share), "chan", 0, 0, tiled=False)
+    load = jnp.concatenate([load[: 2 * eight], read_part.reshape(n * eight, out_share)], axis=0)
+    gathered = lax.all_gather(load, ("x", "core", "rows"), axis=0, tiled=False)
+    post_reduce_out, post_expand_out, readout_out = finish_post(gathered, n, share)
+
+    act_rows = after(convolved_act, bottom).reshape(-1, ch)
+    pre_expand_grad = dot(act_rows, expanded_grad.reshape(-1, ch), TN).astype(BF)
+    convolved_grad = after(convolved_grad, pre_expand_grad)
     reduced_grad, pre_taps_grad = pre_conv_backward(convolved_grad, grad_above, grad_below, reduced, pre_taps)
     pre_reduce_grad = dot(flat_features, reduced_grad.reshape(-1, ch), TN).astype(BF)
-    feature_grad = feature_backward(order, reduced_grad, pre_reduce, returned, up_m).reshape(features.shape)
+    feature_grad = feature_backward(order, after(reduced_grad, pre_reduce_grad), pre_reduce, returned, up_m).reshape(features.shape)
 
     small = small_rows(pre_taps_grad, pre_gain_grad, post_taps_grad, post_gain_grad)
     mine = [pre_reduce_grad, pre_expand_grad]
@@ -875,7 +923,7 @@
         pre_gain_out.reshape(ch),
         post_reduce_out,
         post_conv_out.reshape(3, 3, ch),
-        post_expand_out,
+        post_expand_out.reshape(ch, share),
         lax.dynamic_slice_in_dim(post_gain_out.reshape(ch), chan * share, share, 0),
         readout_out,
     )

time: 455 us -> 425 us (0.934)
  waiting for transfers between devices: 154 us -> 96.1 us
  blocking collectives: 0 us -> 47.4 us
  other arithmetic: 19.5 us -> 5.94 us
  Pallas kernels: 132 us -> 141 us
  starting transfers between devices: 76 us -> 69.9 us
    all_to_all x0 -> x1, blocking collectives: none -> 47.4 us  [body(): load = lax.all_to_all(load, chips, 0, 0, tiled=False).reshape(ch // 2, -1)]
    all_to_all x1 -> x0, waiting for transfers between devices: 26.3 us -> none  [body(): load = lax.all_to_all(load, chips, 0, 0, tiled=False).reshape(ch // 2, -1)]
    all_to_all x1, waiting for transfers between devices: 0.01 us -> 24.5 us  [body(): load = sum_and_copy(lax.all_to_all(load, chips, 0, 0, tiled=False))]
    all_gather x1, waiting for transfers between devices: 21.1 us -> 0.01 us  [body(): gathered = lax.all_gather(load, ('x', 'core', 'rows'), axis=0, tiled=False)]
    reduce_scatter x1, waiting for transfers between devices: 32.6 us -> 16.5 us  [body(): load = lax.psum_scatter(load, 'rows', scatter_dimension=0, tiled=False)]
    all_to_all x1 -> x0, starting transfers between devices: 8.99 us -> none  [body(): load = lax.all_to_all(load, chips, 0, 0, tiled=False).reshape(ch // 2, -1)]
    pallas_call x13 -> x14, Pallas kernels: 132 us -> 141 us  [run(): pl.pallas_call(kernel, grid_spec=pltpu.PrefetchScalarGridSpec(num_scalar_...]
    ppermute x4, waiting for transfers between devices: 23.1 us -> 14.8 us  [body(): lax.ppermute(pooled[k], ('rows', 'chan'), spread(n, k))]
  transfers between devices with their start and end apart: 31 -> 27, of which waited for: 11 -> 6; matrix products, arithmetic and copies ran while one was open for 11% -> 9% of each run, Pallas kernels for 23% -> 25%
where the time goes in v4:
time: 425 us; the launch traced here: 423 us
  Pallas kernels  141 us (33%)
  waiting for transfers between devices  96.1 us (23%)
  starting transfers between devices  69.9 us (16%)
  blocking collectives  47.4 us (11%)
  local copies, waits for them, and re-layouts  26.8 us (6%)
  matrix products  22.6 us (5%)
  between operations  14.1 us (3%)
  other arithmetic  5.94 us (1%)
    pallas_call x14, Pallas kernels, run(): pl.pallas_call(kernel, grid_spec=pltpu.PrefetchScalarGridSpec(num_scalar_...  141 us
    all_to_all x1, blocking collectives, body(): load = lax.all_to_all(load, chips, 0, 0, tiled=False).reshape(ch // 2, -1)  47.4 us
    ppermute x3, waiting for transfers between devices, body(): lax.ppermute(low, 'chan', [(i, (i + k) % n) for i in range(n)])  38.4 us
    all_to_all x1, waiting for transfers between devices, body(): load = sum_and_copy(lax.all_to_all(load, chips, 0, 0, tiled=False))  24.5 us
    dot_general x4, matrix products, dot(): return lax.dot_general(a, b, (dims, ((), ())), preferred_element_type=F32)  22.6 us
    reduce_scatter x1, waiting for transfers between devices, body(): load = lax.psum_scatter(load, 'rows', scatter_dimension=0, tiled=False)  16.5 us
    ppermute x4, waiting for transfers between devices, body(): lax.ppermute(pooled[k], ('rows', 'chan'), spread(n, k))  14.8 us
    ppermute x4, starting transfers between devices, body(): lax.ppermute(back[k], ('rows', 'chan'), [(d, s) for s, d in spread(n, k)])  11.1 us
  transfers between devices with their start and end apart: 27, of which 6 were waited for; matrix products, arithmetic and copies ran while one was open for 9% of the time, Pallas kernels for 25%

profile of v4, /device:TPU:1, one launch (start us, length us, event | category | flops | bytes accessed | tf_op | source)
XLA Modules:
  0.0 423.4 jit_solution(17020729306972783463)
XLA Ops:
  7.3 0.8 subtract_convert_fusion
  8.0 1.1 fusion.7
  9.2 1.2 fusion.3
  12.2 4.4 %cotangent_by_image.1 = bf16[4,288,1024]{2,1,0:T(8,128)(2,1)} custom-call(bf16[1152,1024]{1,0:T(8,128)(2,1)} %bitcast.70, bf16[128,128]{1,0:T(8,128)(2,1)} %copy.32.sel), custom_call_target="tpu_custom_call" | custom-call | flops 1 | bytes 1 | tf_op jit(solution)/shard_map/cotangent_by_image/pallas_call | solution.py:67
  16.6 5.9 %all-to-all-start = ((bf16[4,288,1024]{2,1,0:T(8,128)(2,1)}), bf16[4,288,1024]{2,1,0:T(8,128)(2,1)S(1)}, u32[]{:S(2)}, u32[]{:S(2)}) async-start(bf16[4,288,1024]{2,1,0:T(8,128)(2,1)} %cotangent_by_image.1), calls=%async_computation | async-start | bytes 4718592 | tf_op jit(solution)/shard_map/all_to_all | solution.py:847
  22.5 1.2 slice_bitcast_fusion
  23.6 1.3 collective-permute-start.1
  24.9 4.8 %collective-permute-start = (bf16[8,24,1024]{2,1,0:T(8,128)(2,1)S(1)}, bf16[8,24,1024]{2,1,0:T(8,128)(2,1)}, u32[]{:S(2)}, u32[]{:S(2)}) collective-permute-start(bf16[8,24,1024]{2,1,0:T(8,128)(2,1)S(1)} %get-tuple-element.118), channel_id=1, source_target_pairs={{0,4},{4,8},{8,12},{1,5},{5,9},{9,13},{2,6},{6,10},{10,14},{3,7},{... | collective-permute-start | bytes 1179656 | tf_op jit(solution)/shard_map/ppermute | solution.py:832
  29.7 1.4 reshape.175.tap
  31.6 7.1 %fusion.1.red = f32[8,144,1024]{2,1,0:T(8,128)} fusion(bf16[8,144,1024]{2,1,0:T(8,128)(2,1)} %bitcast.80, bf16[1024,1024]{1,0:T(8,128)(2,1)} %wr.3), kind=kOutput, calls=%fused_computation.4 | convolution fusion | flops 2415919104 | bytes 9175040 | tf_op jit(solution)/shard_map/dot_general | solution.py:23
  39.5 22.5 %pre_forward.1 = (f32[8,144,1024]{2,1,0:T(8,128)}, bf16[8,144,1024]{2,1,0:T(8,128)(2,1)}, f32[8,144,1024]{2,1,0:T(8,128)}, f32[8,144,1]{2,1,0:T(8,128)}, bf16[72...) custom-call(s32[4]{0:T(128)} %and_select_fusion.order_ref, ...), custom_call_target="tpu_custom_call" | custom-call | flops 1 | bytes 1 | tf_op jit(solution)/shard_map/pre_forward/pallas_call | solution.py:67
  62.0 1.6 collective-permute-start.2
  63.5 2.1 collective-permute-start.3
  65.7 4.5 %collective-permute-start.4 = (bf16[72,1024]{1,0:T(8,128)(2,1)}, bf16[72,1024]{1,0:T(8,128)(2,1)S(1)}, u32[]{:S(2)}, u32[]{:S(2)}) collective-permute-start(bf16[72,1024]{1,0:T(8,128)(2,1)} %get-tuple-element.65), channel_id=1, source_target_pairs={{0,2},{1,6},{2,10},{3,14},{4,3},{5,7},{6,11},{7,15},{8,0},{9,4},{1... | collective-permute-start | bytes 442376 | tf_op jit(solution)/shard_map/ppermute | solution.py:855
  70.2 2.4 collective-permute-start.5
  73.8 14.8 %collective-permute-done.3.refs_1_ = bf16[72,1024]{1,0:T(8,128)(2,1)S(1)} collective-permute-done((bf16[72,1024]{1,0:T(8,128)(2,1)}, bf16[72,1024]{1,0:T(8,128)(2,1)S(1)}, u32[]{:S(2)}, u32[]{:S(2)}) %collective-permute-start.3) | collective-permute-done | bytes 147488 | tf_op jit(solution)/shard_map/ppermute | solution.py:855
  89.4 11.1 %post_forward.1 = (bf16[288,1024]{1,0:T(8,128)(2,1)}, f32[288,1024]{1,0:T(8,128)}, bf16[288,1024]{1,0:T(8,128)(2,1)}, f32[288,1024]{1,0:T(8,128)}, bf16[288,1024...) custom-call(s32[4]{0:T(128)} %and_select_fusion.1.src, ...), custom_call_target="tpu_custom_call" | custom-call | flops 1 | bytes 1 | tf_op jit(solution)/shard_map/post_forward/pallas_call | solution.py:67
  100.4 1.4 copy-done
  101.8 20.8 %post_backward.1 = (bf16[288,1024]{1,0:T(8,128)(2,1)}, bf16[288,1024]{1,0:T(8,128)(2,1)}, f32[9,8,1024]{2,1,0:T(8,128)}, f32[8,1024]{1,0:T(8,128)}, bf16[72,1024...) custom-call(s32[4]{0:T(128)} %and_select_fusion.1.src, ...), custom_call_target="tpu_custom_call" | custom-call | flops 1 | bytes 1 | tf_op jit(solution)/shard_map/post_backward/pallas_call | solution.py:67
  122.7 6.0 %post_weight_grads.1 = bf16[4,256,2048]{2,1,0:T(8,128)(2,1)} custom-call(bf16[288,1024]{1,0:T(8,128)(2,1)} %get-tuple-element.68.x, bf16[288,1024]{1,0:T(8,128)(2,1)} %get-tuple-element.74.g, bf16[288,1024]{1,0:T(8,128)(2,1)} %get-tuple-element.75.a, bf16[288,1024]{1,0:T(8,128)(2,1)} %get-tuple-element.76.e), custom_call_target="tpu_custom_call" | custom-call | flops 1 | bytes 1 | tf_op jit(solution)/shard_map/post_weight_grads/pallas_call | solution.py:67
  128.8 1.0 copy-done.6
  129.7 3.5 collective-permute-start.8
  133.2 5.4 %collective-permute-start.7 = (bf16[288,1024]{1,0:T(8,128)(2,1)S(1)}, bf16[288,1024]{1,0:T(8,128)(2,1)S(1)}, u32[]{:S(2)}, u32[]{:S(2)}) collective-permute-start(bf16[288,1024]{1,0:T(8,128)(2,1)S(1)} %copy-done.6), channel_id=1, source_target_pairs={{0,2},{1,3},{2,0},{3,1},{4,6},{5,7},{6,4},{7,5},{8,10},{9,11},{10,... | collective-permute-start | bytes 1769480 | tf_op jit(solution)/shard_map/ppermute | solution.py:859
  138.7 0.9 collective-permute-start.6
  139.5 0.8 broadcast_in_dim_tile.5.refs_7_
  140.3 1.6 collective-permute-start.9
  141.9 4.6 %collective-permute-start.10 = (bf16[72,1024]{1,0:T(8,128)(2,1)S(1)}, bf16[72,1024]{1,0:T(8,128)(2,1)S(1)}, u32[]{:S(2)}, u32[]{:S(2)}) collective-permute-start(bf16[72,1024]{1,0:T(8,128)(2,1)S(1)} %copy-done.28), channel_id=1, source_target_pairs={{1,0},{5,1},{9,2},{13,3},{2,4},{6,5},{10,6},{14,7},{3,8},{7,9},{11... | collective-permute-start | bytes 442376 | tf_op jit(solution)/shard_map/ppermute | solution.py:864
  146.5 5.0 %collective-permute-start.11 = (bf16[72,1024]{1,0:T(8,128)(2,1)S(1)}, bf16[72,1024]{1,0:T(8,128)(2,1)S(1)}, u32[]{:S(2)}, u32[]{:S(2)}) collective-permute-start(bf16[72,1024]{1,0:T(8,128)(2,1)S(1)} %copy-done.27), channel_id=1, source_target_pairs={{2,0},{6,1},{10,2},{14,3},{3,4},{7,5},{11,6},{15,7},{0,8},{4,9},{8... | collective-permute-start | bytes 442376 | tf_op jit(solution)/shard_map/ppermute | solution.py:864
  151.5 13.1 %collective-permute-done.7.refs_2_ = bf16[288,1024]{1,0:T(8,128)(2,1)S(1)} collective-permute-done((bf16[288,1024]{1,0:T(8,128)(2,1)S(1)}, bf16[288,1024]{1,0:T(8,128)(2,1)S(1)}, u32[]{:S(2)}, u32[]{:S(2)}) %collective-permute-start.7) | collective-permute-done | bytes 589856 | tf_op jit(solution)/shard_map/ppermute | solution.py:859
  164.6 25.3 %collective-permute-done.6.refs_1_ = bf16[288,1024]{1,0:T(8,128)(2,1)S(1)} collective-permute-done((bf16[288,1024]{1,0:T(8,128)(2,1)S(1)}, bf16[288,1024]{1,0:T(8,128)(2,1)S(1)}, u32[]{:S(2)}, u32[]{:S(2)}) %collective-permute-start.6) | collective-permute-done | bytes 589856 | tf_op jit(solution)/shard_map/ppermute | solution.py:859
  189.8 0.8 copy-done.10
  190.7 10.8 %token_block.1 = (bf16[1152,1024]{1,0:T(8,128)(2,1)}, bf16[1152,1024]{1,0:T(8,128)(2,1)}, bf16[1152,1024]{1,0:T(8,128)(2,1)}) custom-call(s32[1]{0:T(128)} %bitcast.chan_ref, s32[4]{0:T(128)} %and_select_fusion.1.src, bf16[288,1024]{1,0:T(8,128)(2,1)} %get-tuple-element.77.low_ref.refs_0_, bf16[288,1024]{1,0:T(8,128)(2,1)} %copy-done.10, ...), custom_call_target="tpu_custom_call" | custom-call | flops 1 | bytes 1 | tf_op jit(solution)/shard_map/token_block/pallas_call | solution.py:67
  201.5 5.3 %convolution_convert_fusion.1 = bf16[1024,1024]{1,0:T(8,128)(2,1)S(1)} fusion(bf16[1152,1024]{1,0:T(8,128)(2,1)} %get-tuple-element.86, bf16[1152,1024]{1,0:T(8,128)(2,1)} %get-tuple-element.87), kind=kOutput, calls=%fused_computation.8 | convolution fusion | flops 2416967680 | bytes 6815744 | tf_op jit(solution)/shard_map/dot_general | solution.py:23
  207.6 21.5 %pre_backward.1 = (bf16[8,144,1024]{2,1,0:T(8,128)(2,1)}, bf16[8,144,1024]{2,1,0:T(8,128)(2,1)}, bf16[8,24,1024]{2,1,0:T(8,128)(2,1)}, bf16[8,24,1024]{2,1,0:T(8,128)(2,1)}, f32[8,1024]{1,0:T(8,128)}) custom-call(s32[4]{0:T(128)} %and_select_fusion.order_ref, bf16[72,1024]{1,0:T(8,128)(2,1)} %copy-done.11, bf16[72,1024]{1,0:T(8,128)(2,1)} %copy-done.12, ...), custom_call_target="tpu_custom_call" | custom-call | flops 1 | bytes 1 | tf_op jit(solution)/shard_map/pre_backward/pallas_call | solution.py:67
  229.4 1.3 fusion.6
  230.6 2.1 pad_maximum_fusion
  232.8 0.9 copy-done.25
  233.8 1.3 collective-permute-start.13
  235.1 1.3 collective-permute-start.14
  236.4 5.3 %bitcast_convert_fusion.refs_1_ = bf16[1024,1024]{1,0:T(8,128)(2,1)S(1)} fusion(bf16[8,144,1024]{2,1,0:T(8,128)(2,1)} %get-tuple-element.98, bf16[8,144,1024]{2,1,0:T(8,128)(2,1)} %get-tuple-element.99), kind=kOutput, calls=%fused_computation | convolution fusion | flops 2416967680 | bytes 6815744 | tf_op jit(solution)/shard_map/dot_general | solution.py:23
  241.7 1.1 dynamic-slice_bitcast_fusion
  242.8 5.4 %collective-permute-start.16 = (bf16[512,1024]{1,0:T(8,128)(2,1)}, bf16[512,1024]{1,0:T(8,128)(2,1)S(1)}, u32[]{:S(2)}, u32[]{:S(2)}) collective-permute-start(bf16[512,1024]{1,0:T(8,128)(2,1)} %dynamic-slice_bitcast_fusion), channel_id=1, source_target_pairs={{0,16},{16,0},{1,17},{17,1},{2,18},{18,2},{3,19},{19,3},{4,20},{20... | collective-permute-start | bytes 3145736 | tf_op jit(solution)/shard_map/ppermute | solution.py:636
  249.7 12.1 %pre_conv_backward.1 = (bf16[8,144,1024]{2,1,0:T(8,128)(2,1)}, f32[9,8,1024]{2,1,0:T(8,128)}) custom-call(bf16[8,144,1024]{2,1,0:T(8,128)(2,1)} %get-tuple-element.100.cg, bf16[8,24,1024]{2,1,0:T(8,128)(2,1)} %copy-done.16, bf16[8,24,1024]{2,1,0:T(8,128)(2,1)} %copy-done.17, f32[8,144,1024]{2,1,0:T(8,128)} %fusion.1.red, f32[9,1024]{1,0:T(8,128)} %reshape.175.tap), custom_call_target="tpu_custom_call" | custom-call | flops 1 | bytes 1 | tf_op jit(solution)/shard_map/pre_conv_backward/pallas_call | solution.py:67
  261.8 4.8 %convolution_convert_fusion = bf16[1024,1024]{0,1:T(8,128)(2,1)S(1)} fusion(bf16[1152,1024]{1,0:T(8,128)(2,1)} %bitcast.83, bf16[1152,1024]{1,0:T(8,128)(2,1)S(1)} %bitcast.81), kind=kOutput, calls=%fused_computation.7 | convolution fusion | flops 2416967680 | bytes 6815744 | tf_op jit(solution)/shard_map/dot_general | solution.py:23
  266.7 1.8 reduce-scatter.6.cloned.1.call-done
  268.5 1.0 dynamic-slice_bitcast_fusion.1
  269.5 3.6 collective-permute-start.15
  273.1 1.8 small_rows.1.refs_4_
  274.9 16.5 %reduce-scatter.8.cloned.1.call-done = bf16[1,48,1024]{2,1,0:T(8,128)(2,1)} async-done(((bf16[4,48,1024]{2,1,0:T(8,128)(2,1)}), bf16[1,48,1024]{2,1,0:T(8,128)(2,1)}) %reduce-scatter.8.cloned.1.call-update) | async-done | bytes 98320 | tf_op jit(solution)/shard_map/reduce_scatter | solution.py:893
  291.4 1.5 slice_bitcast_fusion.2
  292.9 4.1 all-to-all-start.3
  298.0 4.0 join_halves.1
  302.1 8.6 %all-to-all-start.1 = ((bf16[64,8,2176]{2,1,0:T(8,128)(2,1)}), bf16[64,8,2176]{2,1,0:T(8,128)(2,1)S(1)}, u32[]{:S(2)}, u32[]{:S(2)}) async-start(bf16[64,8,2176]{2,1,0:T(8,128)(2,1)} %bitcast.74), calls=%async_computation.1 | async-start | bytes 4456448 | tf_op jit(solution)/shard_map/all_to_all | solution.py:911
  310.7 0.8 slice_bitcast_fusion.3
  312.2 24.5 %all-to-all-done.1.x = bf16[64,8,2176]{2,1,0:T(8,128)(2,1)S(1)} async-done(((bf16[64,8,2176]{2,1,0:T(8,128)(2,1)}), bf16[64,8,2176]{2,1,0:T(8,128)(2,1)S(1)}, u32[]{:S(2)}, u32[]{:S(2)}) %all-to-all-start.1) | async-done | bytes 2228256 | tf_op jit(solution)/shard_map/all_to_all | solution.py:911
  336.6 1.4 copy-done.2
  338.0 4.4 %sum_and_copy.1 = bf16[64,8,2176]{2,1,0:T(8,128)(2,1)} custom-call(bf16[64,8,2176]{2,1,0:T(8,128)(2,1)} %copy-done.2), custom_call_target="tpu_custom_call" | custom-call | flops 1 | bytes 1 | tf_op jit(solution)/shard_map/sum_and_copy/pallas_call | solution.py:67
  342.4 47.4 %all_to_all.20 = bf16[64,8,2176]{2,1,0:T(8,128)(2,1)S(1)} all-to-all(bf16[64,8,2176]{2,1,0:T(8,128)(2,1)} %sum_and_copy.1), channel_id=1, replica_groups=mesh['x'=4,'core'=2,'rows'=4,'chan'=4] {'x','rows','chan'}, dimensions={0} | all-to-all | bytes 4456448 | tf_op jit(solution)/shard_map/all_to_all | solution.py:912
  389.8 2.0 collective-permute-start.18
  391.8 8.5 %feature_backward.1 = f32[8,144,1024]{2,1,0:T(8,128)} custom-call(s32[4]{0:T(128)} %and_select_fusion.order_ref, bf16[8,144,1024]{2,1,0:T(8,128)(2,1)} %get-tuple-element.103.rg, bf16[1024,1024]{1,0:T(8,128)(2,1)} %wr.3, bf16[288,72]{1,0:T(8,128)(2,1)} %constant.68.clone.refs_4_.up, bf16[72,1024]{1,0:T(8,128)(2,1)} %copy-done.11, ...), custom_call_target="tpu_custom_call" | custom-call | flops 1 | bytes 1 | tf_op jit(solution)/shard_map/feature_backward/pallas_call | solution.py:67
  400.3 6.0 %finish_pre.1 = (f32[1024,1024]{1,0:T(8,128)}, f32[1024,1024]{1,0:T(8,128)}, f32[512,128]{1,0:T(8,128)}) custom-call(s32[1]{0:T(128)} %bitcast.18.core_ref, bf16[512,2176]{1,0:T(8,128)(2,1)} %bitcast.73, bf16[512,2176]{1,0:T(8,128)(2,1)} %collective-permute-done.18.b), custom_call_target="tpu_custom_call" | custom-call | flops 1 | bytes 1 | tf_op jit(solution)/shard_map/finish_pre/pallas_call | solution.py:67
  406.3 0.8 fusion.8
  408.3 1.3 slice_bitcast_fusion.4
  410.3 6.6 %finish_post.1 = (f32[256,1024]{1,0:T(8,128)}, f32[4,256,256]{2,1,0:T(8,128)}, f32[256,4096]{1,0:T(8,128)}) custom-call(bf16[32,48,1024]{2,1,0:T(8,128)(2,1)} %bitcast.82), custom_call_target="tpu_custom_call" | custom-call | flops 1 | bytes 1 | tf_op jit(solution)/shard_map/finish_post/pallas_call | solution.py:67
  (108 shorter events, 11.3 us)
Async XLA Ops:
  7.2 4.2 copy-start.22
  7.2 3.9 copy-start.29
  7.2 81.4 %all-gather.5.cloned.1.call-start = ((), (), s32[]{:S(2)}) async-start(), calls=%async_computation.10 | async-start | bytes 4866048 | tf_op jit(solution)/shard_map/all_gather | solution.py:842
  16.6 83.8 %all-to-all-start = ((bf16[4,288,1024]{2,1,0:T(8,128)(2,1)}), bf16[4,288,1024]{2,1,0:T(8,128)(2,1)S(1)}, u32[]{:S(2)}, u32[]{:S(2)}) async-start(bf16[4,288,1024]{2,1,0:T(8,128)(2,1)} %cotangent_by_image.1), calls=%async_computation | async-start | bytes 4718592 | tf_op jit(solution)/shard_map/all_to_all | solution.py:847
  22.5 206.9 %reduce-scatter.4.cloned.1.call-start = ((), (), s32[]{:S(2)}) async-start(), calls=%async_computation.7 | async-start | bytes 5242880 | tf_op jit(solution)/shard_map/reduce_scatter | solution.py:867
  23.6 15.1 %collective-permute-start.1 = (bf16[8,24,1024]{2,1,0:T(8,128)(2,1)S(1)}, bf16[8,24,1024]{2,1,0:T(8,128)(2,1)S(1)}, u32[]{:S(2)}, u32[]{:S(2)}) collective-permute-start(bf16[8,24,1024]{2,1,0:T(8,128)(2,1)S(1)} %get-tuple-element.117), channel_id=1, source_target_pairs={{4,0},{8,4},{12,8},{5,1},{9,5},{13,9},{6,2},{10,6},{14,10},{7,3},{... | collective-permute-start | bytes 1179656 | tf_op jit(solution)/shard_map/ppermute | solution.py:833
  24.9 13.8 %collective-permute-start = (bf16[8,24,1024]{2,1,0:T(8,128)(2,1)S(1)}, bf16[8,24,1024]{2,1,0:T(8,128)(2,1)}, u32[]{:S(2)}, u32[]{:S(2)}) collective-permute-start(bf16[8,24,1024]{2,1,0:T(8,128)(2,1)S(1)} %get-tuple-element.118), channel_id=1, source_target_pairs={{0,4},{4,8},{8,12},{1,5},{5,9},{9,13},{2,6},{6,10},{10,14},{3,7},{... | collective-permute-start | bytes 1179656 | tf_op jit(solution)/shard_map/ppermute | solution.py:832
  38.7 0.7 copy-start.15
  39.5 33.1 %copy-start.24 = (bf16[3,3,1024]{2,1,0:T(4,128)(2,1)S(1)}, bf16[3,3,1024]{2,1,0:T(4,128)(2,1)}, u32[]{:S(2)}) copy-start(bf16[3,3,1024]{2,1,0:T(4,128)(2,1)} %param.22) | copy-start | bytes 55300
  62.0 11.8 %collective-permute-start.2 = (bf16[72,1024]{1,0:T(8,128)(2,1)}, bf16[72,1024]{1,0:T(8,128)(2,1)S(1)}, u32[]{:S(2)}, u32[]{:S(2)}) collective-permute-start(bf16[72,1024]{1,0:T(8,128)(2,1)} %get-tuple-element.63), channel_id=1, source_target_pairs={{0,0},{1,4},{2,8},{3,12},{4,1},{5,5},{6,9},{7,13},{8,2},{9,6},{10,... | collective-permute-start | bytes 442376 | tf_op jit(solution)/shard_map/ppermute | solution.py:855
  63.5 25.1 %collective-permute-start.3 = (bf16[72,1024]{1,0:T(8,128)(2,1)}, bf16[72,1024]{1,0:T(8,128)(2,1)S(1)}, u32[]{:S(2)}, u32[]{:S(2)}) collective-permute-start(bf16[72,1024]{1,0:T(8,128)(2,1)} %get-tuple-element.64), channel_id=1, source_target_pairs={{0,1},{1,5},{2,9},{3,13},{4,2},{5,6},{6,10},{7,14},{8,3},{9,7},{10... | collective-permute-start | bytes 442376 | tf_op jit(solution)/shard_map/ppermute | solution.py:855
  65.7 22.9 %collective-permute-start.4 = (bf16[72,1024]{1,0:T(8,128)(2,1)}, bf16[72,1024]{1,0:T(8,128)(2,1)S(1)}, u32[]{:S(2)}, u32[]{:S(2)}) collective-permute-start(bf16[72,1024]{1,0:T(8,128)(2,1)} %get-tuple-element.65), channel_id=1, source_target_pairs={{0,2},{1,6},{2,10},{3,14},{4,3},{5,7},{6,11},{7,15},{8,0},{9,4},{1... | collective-permute-start | bytes 442376 | tf_op jit(solution)/shard_map/ppermute | solution.py:855
  70.2 18.4 %collective-permute-start.5 = (bf16[72,1024]{1,0:T(8,128)(2,1)}, bf16[72,1024]{1,0:T(8,128)(2,1)S(1)}, u32[]{:S(2)}, u32[]{:S(2)}) collective-permute-start(bf16[72,1024]{1,0:T(8,128)(2,1)} %get-tuple-element.66), channel_id=1, source_target_pairs={{0,3},{1,7},{2,11},{3,15},{4,0},{5,4},{6,8},{7,12},{8,1},{9,5},{10... | collective-permute-start | bytes 442376 | tf_op jit(solution)/shard_map/ppermute | solution.py:855
  73.8 14.9 %copy-start.18 = (bf16[72,1024]{1,0:T(8,128)(2,1)}, bf16[72,1024]{1,0:T(8,128)(2,1)S(1)}, u32[]{:S(2)}) copy-start(bf16[72,1024]{1,0:T(8,128)(2,1)S(1)} %collective-permute-done.2.refs_0_) | copy-start | bytes 442372
  88.6 0.7 copy-start.19
  88.6 0.7 copy-start.20
  88.6 0.7 copy-start.21
  100.4 1.4 copy-start
  128.7 1.1 copy-start.6
  128.7 13.2 %copy-start.28 = (bf16[72,1024]{1,0:T(8,128)(2,1)S(1)}, bf16[72,1024]{1,0:T(8,128)(2,1)}, u32[]{:S(2)}) copy-start(bf16[72,1024]{1,0:T(8,128)(2,1)} %get-tuple-element.83) | copy-start | bytes 442372
  128.7 17.8 %copy-start.27 = (bf16[72,1024]{1,0:T(8,128)(2,1)S(1)}, bf16[72,1024]{1,0:T(8,128)(2,1)}, u32[]{:S(2)}) copy-start(bf16[72,1024]{1,0:T(8,128)(2,1)} %get-tuple-element.84) | copy-start | bytes 442372
  128.7 35.9 %copy-start.26 = (bf16[72,1024]{1,0:T(8,128)(2,1)S(1)}, bf16[72,1024]{1,0:T(8,128)(2,1)}, u32[]{:S(2)}) copy-start(bf16[72,1024]{1,0:T(8,128)(2,1)} %get-tuple-element.85) | copy-start | bytes 442372
  128.7 139.8 %reduce-scatter.6.cloned.1.call-start = ((), (), s32[]{:S(2)}) async-start(), calls=%async_computation.8 | async-start | bytes 3538944 | tf_op jit(solution)/shard_map/reduce_scatter | solution.py:892
  129.7 16.8 %collective-permute-start.8 = (bf16[288,1024]{1,0:T(8,128)(2,1)S(1)}, bf16[288,1024]{1,0:T(8,128)(2,1)S(1)}, u32[]{:S(2)}, u32[]{:S(2)}) collective-permute-start(bf16[288,1024]{1,0:T(8,128)(2,1)S(1)} %copy-done.6), channel_id=1, source_target_pairs={{0,3},{1,0},{2,1},{3,2},{4,7},{5,4},{6,5},{7,6},{8,11},{9,8},{10,9... | collective-permute-start | bytes 1769480 | tf_op jit(solution)/shard_map/ppermute | solution.py:859
  133.2 31.3 %collective-permute-start.7 = (bf16[288,1024]{1,0:T(8,128)(2,1)S(1)}, bf16[288,1024]{1,0:T(8,128)(2,1)S(1)}, u32[]{:S(2)}, u32[]{:S(2)}) collective-permute-start(bf16[288,1024]{1,0:T(8,128)(2,1)S(1)} %copy-done.6), channel_id=1, source_target_pairs={{0,2},{1,3},{2,0},{3,1},{4,6},{5,7},{6,4},{7,5},{8,10},{9,11},{10,... | collective-permute-start | bytes 1769480 | tf_op jit(solution)/shard_map/ppermute | solution.py:859
  138.7 51.2 %collective-permute-start.6 = (bf16[288,1024]{1,0:T(8,128)(2,1)S(1)}, bf16[288,1024]{1,0:T(8,128)(2,1)S(1)}, u32[]{:S(2)}, u32[]{:S(2)}) collective-permute-start(bf16[288,1024]{1,0:T(8,128)(2,1)S(1)} %copy-done.6), channel_id=1, source_target_pairs={{0,1},{1,2},{2,3},{3,0},{4,5},{5,6},{6,7},{7,4},{8,9},{9,10},{10,1... | collective-permute-start | bytes 1769480 | tf_op jit(solution)/shard_map/ppermute | solution.py:859
  140.3 66.5 %collective-permute-start.9 = (bf16[72,1024]{1,0:T(8,128)(2,1)}, bf16[72,1024]{1,0:T(8,128)(2,1)S(1)}, u32[]{:S(2)}, u32[]{:S(2)}) collective-permute-start(bf16[72,1024]{1,0:T(8,128)(2,1)} %get-tuple-element.82), channel_id=1, source_target_pairs={{0,0},{4,1},{8,2},{12,3},{1,4},{5,5},{9,6},{13,7},{2,8},{6,9},{10,... | collective-permute-start | bytes 442376 | tf_op jit(solution)/shard_map/ppermute | solution.py:864
  141.9 64.9 %collective-permute-start.10 = (bf16[72,1024]{1,0:T(8,128)(2,1)S(1)}, bf16[72,1024]{1,0:T(8,128)(2,1)S(1)}, u32[]{:S(2)}, u32[]{:S(2)}) collective-permute-start(bf16[72,1024]{1,0:T(8,128)(2,1)S(1)} %copy-done.28), channel_id=1, source_target_pairs={{1,0},{5,1},{9,2},{13,3},{2,4},{6,5},{10,6},{14,7},{3,8},{7,9},{11... | collective-permute-start | bytes 442376 | tf_op jit(solution)/shard_map/ppermute | solution.py:864
  146.5 43.3 %copy-start.8 = (bf16[288,1024]{1,0:T(8,128)(2,1)}, bf16[288,1024]{1,0:T(8,128)(2,1)S(1)}, u32[]{:S(2)}) copy-start(bf16[288,1024]{1,0:T(8,128)(2,1)S(1)} %collective-permute-done.8.refs_3_) | copy-start | bytes 1769476
  146.5 60.3 %collective-permute-start.11 = (bf16[72,1024]{1,0:T(8,128)(2,1)S(1)}, bf16[72,1024]{1,0:T(8,128)(2,1)S(1)}, u32[]{:S(2)}, u32[]{:S(2)}) collective-permute-start(bf16[72,1024]{1,0:T(8,128)(2,1)S(1)} %copy-done.27), channel_id=1, source_target_pairs={{2,0},{6,1},{10,2},{14,3},{3,4},{7,5},{11,6},{15,7},{0,8},{4,9},{8... | collective-permute-start | bytes 442376 | tf_op jit(solution)/shard_map/ppermute | solution.py:864
  164.6 25.3 %copy-start.9 = (bf16[288,1024]{1,0:T(8,128)(2,1)}, bf16[288,1024]{1,0:T(8,128)(2,1)S(1)}, u32[]{:S(2)}) copy-start(bf16[288,1024]{1,0:T(8,128)(2,1)S(1)} %collective-permute-done.7.refs_2_) | copy-start | bytes 1769476
  164.6 42.3 %collective-permute-start.12 = (bf16[72,1024]{1,0:T(8,128)(2,1)S(1)}, bf16[72,1024]{1,0:T(8,128)(2,1)S(1)}, u32[]{:S(2)}, u32[]{:S(2)}) collective-permute-start(bf16[72,1024]{1,0:T(8,128)(2,1)S(1)} %copy-done.26), channel_id=1, source_target_pairs={{3,0},{7,1},{11,2},{15,3},{0,4},{4,5},{8,6},{12,7},{1,8},{5,9},{9,... | collective-permute-start | bytes 442376 | tf_op jit(solution)/shard_map/ppermute | solution.py:864
  189.8 0.8 copy-start.10
  206.8 0.7 copy-start.11
  206.8 0.7 copy-start.12
  206.8 0.7 copy-start.13
  206.8 0.8 copy-start.14
  232.8 1.0 copy-start.25
  232.8 58.6 %reduce-scatter.8.cloned.1.call-start = ((), (), s32[]{:S(2)}) async-start(), calls=%async_computation.9 | async-start | bytes 491520 | tf_op jit(solution)/shard_map/reduce_scatter | solution.py:893
  233.8 14.4 %collective-permute-start.13 = (bf16[8,24,1024]{2,1,0:T(8,128)(2,1)S(1)}, bf16[8,24,1024]{2,1,0:T(8,128)(2,1)S(1)}, u32[]{:S(2)}, u32[]{:S(2)}) collective-permute-start(bf16[8,24,1024]{2,1,0:T(8,128)(2,1)S(1)} %copy-done.25), channel_id=1, source_target_pairs={{0,4},{4,8},{8,12},{1,5},{5,9},{9,13},{2,6},{6,10},{10,14},{3,7},{... | collective-permute-start | bytes 1179656 | tf_op jit(solution)/shard_map/ppermute | solution.py:879
  235.1 13.1 %collective-permute-start.14 = (bf16[8,24,1024]{2,1,0:T(8,128)(2,1)}, bf16[8,24,1024]{2,1,0:T(8,128)(2,1)S(1)}, u32[]{:S(2)}, u32[]{:S(2)}) collective-permute-start(bf16[8,24,1024]{2,1,0:T(8,128)(2,1)} %get-tuple-element.101), channel_id=1, source_target_pairs={{4,0},{8,4},{12,8},{5,1},{9,5},{13,9},{6,2},{10,6},{14,10},{7,3},{... | collective-permute-start | bytes 1179656 | tf_op jit(solution)/shard_map/ppermute | solution.py:880
  241.7 20.1 %copy-start.3 = (bf16[1024,1024]{1,0:T(8,128)(2,1)}, bf16[1024,1024]{1,0:T(8,128)(2,1)S(1)}, u32[]{:S(2)}) copy-start(bf16[1024,1024]{1,0:T(8,128)(2,1)S(1)} %bitcast_convert_fusion.refs_1_) | copy-start | bytes 6291460
  242.8 19.0 %copy-start.5 = (bf16[8,6,24,1024]{3,2,1,0:T(8,128)(2,1)S(1)}, bf16[8,6,24,1024]{3,2,1,0:T(8,128)(2,1)}, u32[]{:S(2)}) copy-start(bf16[8,6,24,1024]{3,2,1,0:T(8,128)(2,1)} %feat.1) | copy-start | bytes 7077892
  242.8 54.2 %collective-permute-start.16 = (bf16[512,1024]{1,0:T(8,128)(2,1)}, bf16[512,1024]{1,0:T(8,128)(2,1)S(1)}, u32[]{:S(2)}, u32[]{:S(2)}) collective-permute-start(bf16[512,1024]{1,0:T(8,128)(2,1)} %dynamic-slice_bitcast_fusion), channel_id=1, source_target_pairs={{0,16},{16,0},{1,17},{17,1},{2,18},{18,2},{3,19},{19,3},{4,20},{20... | collective-permute-start | bytes 3145736 | tf_op jit(solution)/shard_map/ppermute | solution.py:636
  248.2 0.7 copy-start.17
  248.9 0.7 copy-start.16
  266.7 30.4 %copy-start.4 = (bf16[1024,1024]{0,1:T(8,128)(2,1)}, bf16[1024,1024]{0,1:T(8,128)(2,1)S(1)}, u32[]{:S(2)}) copy-start(bf16[1024,1024]{0,1:T(8,128)(2,1)S(1)} %convolution_convert_fusion) | copy-start | bytes 6291460
  269.5 27.5 %collective-permute-start.15 = (bf16[512,1024]{1,0:T(8,128)(2,1)}, bf16[512,1024]{1,0:T(8,128)(2,1)}, u32[]{:S(2)}, u32[]{:S(2)}) collective-permute-start(bf16[512,1024]{1,0:T(8,128)(2,1)} %dynamic-slice_bitcast_fusion.1), channel_id=1, source_target_pairs={{0,16},{16,0},{1,17},{17,1},{2,18},{18,2},{3,19},{19,3},{4,20},{20... | collective-permute-start | bytes 3145736 | tf_op jit(solution)/shard_map/ppermute | solution.py:636
  274.9 22.1 %collective-permute-start.17 = (f32[160,128]{1,0:T(8,128)}, f32[160,128]{1,0:T(8,128)S(1)}, u32[]{:S(2)}, u32[]{:S(2)}) collective-permute-start(f32[160,128]{1,0:T(8,128)} %small_rows.1.refs_4_), channel_id=1, source_target_pairs={{0,16},{16,0},{1,17},{17,1},{2,18},{18,2},{3,19},{19,3},{4,20},{20... | collective-permute-start | bytes 245768 | tf_op jit(solution)/shard_map/ppermute | solution.py:636
  292.9 9.2 %all-to-all-start.3 = ((bf16[4,8,1024]{2,1,0:T(8,128)(2,1)}), bf16[4,8,1024]{2,1,0:T(8,128)(2,1)S(1)}, u32[]{:S(2)}, u32[]{:S(2)}) async-start(bf16[4,8,1024]{2,1,0:T(8,128)(2,1)} %slice_bitcast_fusion.2), calls=%async_computation.6 | async-start | bytes 131072 | tf_op jit(solution)/shard_map/all_to_all | solution.py:894
  297.0 0.6 copy-start.23
  297.0 1.0 copy-start.7
  302.1 34.6 %all-to-all-start.1 = ((bf16[64,8,2176]{2,1,0:T(8,128)(2,1)}), bf16[64,8,2176]{2,1,0:T(8,128)(2,1)S(1)}, u32[]{:S(2)}, u32[]{:S(2)}) async-start(bf16[64,8,2176]{2,1,0:T(8,128)(2,1)} %bitcast.74), calls=%async_computation.1 | async-start | bytes 4456448 | tf_op jit(solution)/shard_map/all_to_all | solution.py:911
  310.7 99.6 %all-gather.7.cloned.1.call-start = ((), (), s32[]{:S(2)}) async-start(), calls=%async_computation.11 | async-start | bytes 3244032 | tf_op jit(solution)/shard_map/all_gather | solution.py:896
  336.6 1.4 copy-start.2
  389.8 10.5 %copy-start.1 = (bf16[64,8,2176]{2,1,0:T(8,128)(2,1)}, bf16[64,8,2176]{2,1,0:T(8,128)(2,1)S(1)}, u32[]{:S(2)}) copy-start(bf16[64,8,2176]{2,1,0:T(8,128)(2,1)S(1)} %all_to_all.20) | copy-start | bytes 6684676
  389.8 10.5 %collective-permute-start.18 = (bf16[512,2176]{1,0:T(8,128)(2,1)S(1)}, bf16[512,2176]{1,0:T(8,128)(2,1)}, u32[]{:S(2)}, u32[]{:S(2)}) collective-permute-start(bf16[512,2176]{1,0:T(8,128)(2,1)S(1)} %bitcast.72), channel_id=1, source_target_pairs={{0,16},{16,0},{1,17},{17,1},{2,18},{18,2},{3,19},{19,3},{4,20},{20... | collective-permute-start | bytes 6684680 | tf_op jit(solution)/shard_map/ppermute | solution.py:636
Sparse Core Ops, SparseCore 0:
  11.2 56.4 all-gather.4
  128.8 77.9 reduce-scatter.3
  232.9 35.5 reduce-scatter.5
  270.8 20.5 reduce-scatter.7
  314.1 74.7 all-gather.6

commit v5 on v4

--- a/solution.py
+++ b/solution.py
@@ -53,14 +53,14 @@
     lax.fori_loop(0, count, step, 0)
 
 
-def call(kernel, *, grid, ins, outs, scratch=(), prefetch=0, name):
+def call(kernel, *, grid, ins, outs, scratch=(), prefetch=0, aliased=(), cost=1, name):
     def spec(shape, block, index):
         if block is None:
             block, index = shape, lambda *_: (0,) * len(shape)
         return pl.BlockSpec(block, index)
 
-    arrays = [i[0] for i in ins]
-    in_specs = [spec(a.shape, b, m) for a, b, m in ins]
+    arrays = [i[0] for i in ins] + list(aliased)
+    in_specs = [spec(a.shape, b, m) for a, b, m in ins] + [pl.BlockSpec(memory_space=pl.ANY)] * len(aliased)
     out_specs = [spec(s.shape, b, m) for s, b, m in outs]
 
     def run(*scalars):
@@ -77,7 +77,8 @@
             compiler_params=pltpu.CompilerParams(
                 dimension_semantics=("arbitrary",) * len(grid), vmem_limit_bytes=VMEM_LIMIT
             ),
-            cost_estimate=pl.CostEstimate(flops=1, bytes_accessed=1, transcendentals=0),
+            input_output_aliases={prefetch + len(ins) + i: i for i in range(len(aliased))},
+            cost_estimate=pl.CostEstimate(flops=cost, bytes_accessed=1, transcendentals=0),
             name=name,
         )(*scalars, *arrays)
 
@@ -98,30 +99,27 @@
     return (at >= depth).astype(F32), (at < (width - 1) * depth).astype(F32)
 
 
-def pre_forward(order, reduced, above, below, features, pre_reduce, taps, pre_expand, gain, pool):
-    slots, cells, ch = reduced.shape
-    high, wide = features.shape[1], features.shape[2]
+def pre_forward(order, above, below, features, pre_reduce, taps, pre_expand, gain, pool, earlier=()):
+    slots, high, wide, ch = features.shape
+    cells = high * wide
     n = order.shape[0]
-    part = slots // n
-
-    def kernel(order_ref, red, up_ref, down_ref, feat, wr, tap, we, gn, pool_ref, conv_out, act_out, norm_out, std_out, *rest):
-        pooled_out, (halo, exp, sums) = rest[:-3], rest[-3:]
+    part = 2
+
+    def kernel(order_ref, up_ref, down_ref, feat, wr, tap, we, gn, pool_ref, *rest):
+        red, conv_out, act_out, norm_out, std_out, *rest = rest[len(earlier) :]
+        pooled_out, (halo, exp, sums) = rest[:n], rest[n:]
         k = pl.program_id(0)
-
-        @pl.when(k == 0)
-        def _():
-            for side, ref in enumerate((up_ref, down_ref)):
-                halo[side] = dot(ref[...].reshape(slots * wide, ch), wr[...]).reshape(slots, wide, ch)
-
+        red[...] = dot(feat[...].reshape(part * cells, ch), wr[...]).reshape(part, cells, ch)
+        for side, ref in enumerate((up_ref, down_ref)):
+            halo[side] = dot(ref[...].reshape(part * wide, ch), wr[...]).reshape(part, wide, ch)
         first, last = edge_masks(wide, wide, 1)
-        at = order_ref[k] * part
         for u in range(part):
 
             def conv(lanes):
                 w = [tap[pl.ds(i, 1), lanes] for i in range(9)]
-                rows = [halo[0, at + u, :, lanes]]
+                rows = [halo[0, u, :, lanes]]
                 rows += [red[u, pl.ds(i * wide, wide), lanes] for i in range(high)]
-                rows += [halo[1, at + u, :, lanes]]
+                rows += [halo[1, u, :, lanes]]
                 rows = [silu(r).astype(BF).astype(F32) for r in rows]
                 acts = []
                 for i in range(high):
@@ -169,14 +167,14 @@
         return lambda k, order: (order[k],) + (0,) * rest
 
     pooled_rows = pool.shape[0]
+    block = (part, cells, ch)
     return call(
         kernel,
         grid=(n,),
         prefetch=1,
         ins=[
-            (reduced, (part, cells, ch), by_order(2)),
-            (above, None, None),
-            (below, None, None),
+            (above, (part, wide, ch), by_order(2)),
+            (below, (part, wide, ch), by_order(2)),
             (features, (part, high, wide, ch), by_order(3)),
             (pre_reduce, None, None),
             (taps, None, None),
@@ -185,17 +183,19 @@
             (pool, None, None),
         ],
         outs=[
-            (shape((slots, cells, ch), F32), (part, cells, ch), by_order(2)),
-            (shape((slots, cells, ch), BF), (part, cells, ch), by_order(2)),
-            (shape((slots, cells, ch), F32), (part, cells, ch), by_order(2)),
+            (shape((slots, cells, ch), F32), block, by_order(2)),
+            (shape((slots, cells, ch), F32), block, by_order(2)),
+            (shape((slots, cells, ch), BF), block, by_order(2)),
+            (shape((slots, cells, ch), F32), block, by_order(2)),
             (shape((slots, cells, 1), F32), (part, cells, 1), by_order(2)),
         ]
         + [(shape((pooled_rows, ch), BF), None, None)] * n,
         scratch=[
-            pltpu.VMEM((2, slots, wide, ch), F32),
+            pltpu.VMEM((2, part, wide, ch), F32),
             pltpu.VMEM((part * cells, ch), F32),
             pltpu.VMEM((part * cells // 2, ch), F32),
         ],
+        aliased=earlier,
         name="pre_forward",
     )(order)
 
@@ -272,16 +272,11 @@
     )(source)
 
 
-def post_backward(source, low, readout, cots, weights, taps, act, red, conv, nrm, std, pool):
+def readout_backward(low, readout, cots):
     total, ch = low.shape
-    n = cots.shape[0]
-    share = ch // n
-    out_share = cots.shape[2]
-    rows = total // n
-    depth = total // (pool * pool)
-
-    def kernel(src, low_ref, ro, cot, w, tap, act_ref, red_ref, conv_ref, norm_ref, std_ref, exp_out, redg_out, taps_out, gain_out, *rest):
-        back_out, (grad, cgrad) = rest[:n], rest[n:]
+    n, _, out_share = cots.shape
+
+    def kernel(low_ref, ro, cot, grad):
         k = pl.program_id(0)
         logits = dot(low_ref[...], ro[...])
         piece = (cot[0].astype(F32) * gelu_parts(logits)[1]).astype(BF)
@@ -295,67 +290,82 @@
         def _():
             grad[...] += term
 
-        @pl.when(k == n - 1)
-        def _():
-            gain = gain_row(w, n, share)
-
-            def norm(i, total_gain):
-                at = pl.ds(pl.multiple_of(i * 16, 16), 16)
-                nm = norm_ref[at, :]
-                ng = grad[at, :] * silu_slope(nm * gain)
-                sc = ng * gain
-                one = jnp.mean(sc, -1, keepdims=True)
-                two = jnp.mean(sc * nm, -1, keepdims=True)
-                exp_out[at, :] = (std_ref[at, :] * (sc - one - nm * two)).astype(BF)
-                g = ng * nm
-                return total_gain + g[:8] + g[8:]
-
-            gain_out[...] = lax.fori_loop(0, total // 16, norm, jnp.zeros((8, ch), F32))
-            for q in range(n):
-                cut = slice(q * share, (q + 1) * share)
-                cg = 0.0
-                for c in range(n):
-                    cg = cg + dot(exp_out[:, c * share : (c + 1) * share], w[c, share : 2 * share, cut], NT)
-                cgrad[:, cut] = cg
-            first, last = edge_masks(total, pool, depth)
-            step = pool * depth
-
-            def back(lanes):
-                g = (cgrad[:, lanes] * silu_slope(conv_ref[:, lanes])).astype(BF).astype(F32)
-                x = act_ref[:, lanes].astype(F32)
-                moves = [columns_moved(g, -depth, first, last), g, columns_moved(g, depth, first, last)]
-                none = jnp.zeros((step, LANES), F32)
-                xs = [
-                    jnp.concatenate([none, x[:-step]], 0),
-                    x,
-                    jnp.concatenate([x[step:], none], 0),
-                ]
-                for a in range(3):
-                    for b in range(3):
-                        prod = xs[a] * moves[b]
-                        taps_out[3 * a + b, :, lanes] = jnp.sum(prod.reshape(total // 8, 8, LANES), 0)
-                t = [sum(moves[b] * tap[pl.ds(3 * a + b, 1), lanes] for b in range(3)) for a in range(3)]
-                d = t[1] + jnp.concatenate([t[0][step:], none], 0) + jnp.concatenate([none, t[2][:-step]], 0)
-                redg_out[:, lanes] = (d * silu_slope(red_ref[:, lanes])).astype(BF)
-
-            chunks(ch // LANES, back)
-            for c in range(n):
-                cut = slice(c * share, (c + 1) * share)
-                grad[:, cut] += dot(redg_out[...], w[c, :share], NT)
-            for r in range(n):
-                at = pl.ds(pl.multiple_of(src[r] * rows, 8), rows)
-                back_out[r][...] = grad[at, :].astype(BF)
-
     return call(
         kernel,
         grid=(n,),
-        prefetch=1,
         ins=[
             (low, None, None),
-            (readout, (ch, out_share), lambda k, s: (0, k)),
-            (cots, (1, total, out_share), lambda k, s: (k, 0, 0)),
-        ]
-        + [(a, None, None) for a in (weights, taps, act, red, conv, nrm, std)],
+            (readout, (ch, out_share), lambda k: (0, k)),
+            (cots, (1, total, out_share), lambda k: (k, 0, 0)),
+        ],
+        outs=[(shape((total, ch), F32), None, None)],
+        name="readout_backward",
+    )()[0]
+
+
+def post_backward(source, refined_grad, weights, taps, act, red, conv, nrm, std, pool):
+    total, ch = act.shape
+    n = weights.shape[0]
+    share = ch // n
+    rows = total // n
+    depth = total // (pool * pool)
+
+    def kernel(src, rg, w, tap, act_ref, red_ref, conv_ref, norm_ref, std_ref, exp_out, redg_out, taps_out, gain_out, *rest):
+        back_out, (grad, cgrad) = rest[:n], rest[n:]
+        gain = gain_row(w, n, share)
+
+        def norm(i, total_gain):
+            at = pl.ds(pl.multiple_of(i * 16, 16), 16)
+            nm = norm_ref[at, :]
+            ng = rg[at, :] * silu_slope(nm * gain)
+            sc = ng * gain
+            one = jnp.mean(sc, -1, keepdims=True)
+            two = jnp.mean(sc * nm, -1, keepdims=True)
+            exp_out[at, :] = (std_ref[at, :] * (sc - one - nm * two)).astype(BF)
+            g = ng * nm
+            return total_gain + g[:8] + g[8:]
+
+        gain_out[...] = lax.fori_loop(0, total // 16, norm, jnp.zeros((8, ch), F32))
+        for q in range(n):
+            cut = slice(q * share, (q + 1) * share)
+            cg = 0.0
+            for c in range(n):
+                cg = cg + dot(exp_out[:, c * share : (c + 1) * share], w[c, share : 2 * share, cut], NT)
+            cgrad[:, cut] = cg
+        first, last = edge_masks(total, pool, depth)
+        step = pool * depth
+
+        def back(lanes):
+            g = (cgrad[:, lanes] * silu_slope(conv_ref[:, lanes])).astype(BF).astype(F32)
+            x = act_ref[:, lanes].astype(F32)
+            moves = [columns_moved(g, -depth, first, last), g, columns_moved(g, depth, first, last)]
+            none = jnp.zeros((step, LANES), F32)
+            xs = [
+                jnp.concatenate([none, x[:-step]], 0),
+                x,
+                jnp.concatenate([x[step:], none], 0),
+            ]
+            for a in range(3):
+                for b in range(3):
+                    prod = xs[a] * moves[b]
+                    taps_out[3 * a + b, :, lanes] = jnp.sum(prod.reshape(total // 8, 8, LANES), 0)
+            t = [sum(moves[b] * tap[pl.ds(3 * a + b, 1), lanes] for b in range(3)) for a in range(3)]
+            d = t[1] + jnp.concatenate([t[0][step:], none], 0) + jnp.concatenate([none, t[2][:-step]], 0)
+            redg_out[:, lanes] = (d * silu_slope(red_ref[:, lanes])).astype(BF)
+
+        chunks(ch // LANES, back)
+        for c in range(n):
+            cut = slice(c * share, (c + 1) * share)
+            grad[:, cut] = rg[:, cut] + dot(redg_out[...], w[c, :share], NT)
+        for r in range(n):
+            at = pl.ds(pl.multiple_of(src[r] * rows, 8), rows)
+            back_out[r][...] = grad[at, :].astype(BF)
+
+    return call(
+        kernel,
+        grid=(1,),
+        prefetch=1,
+        ins=[(a, None, None) for a in (refined_grad, weights, taps, act, red, conv, nrm, std)],
         outs=[
             (s, None, None)
             for s in (
@@ -603,6 +613,7 @@
             *[(r, None, None) for r in returned],
         ],
         outs=[(shape((slots, cells, ch), F32), whole, by_order)],
+        cost=9 * 10**9,
         name="feature_backward",
     )(order)[0]
 
@@ -610,21 +621,46 @@
 def post_weight_grads(flat, reduced_grad, act, expanded_grad, n):
     total, ch = flat.shape
     share = ch // n
+    rows = share // 8
 
     def kernel(x, g, a, e, out):
         for c in range(n):
             cut = slice(c * share, (c + 1) * share)
-            out[c, :, :ch] = dot(x[:, cut], g[...], TN).astype(BF)
+            v = dot(x[:, cut], g[...], TN).astype(BF)
+            for d in range(8):
+                out[d, c, :, :ch] = v[d * rows : (d + 1) * rows]
             for q in range(n):
-                rows = slice(q * share, (q + 1) * share)
-                out[c, :, ch + q * share : ch + (q + 1) * share] = dot(a[:, rows], e[:, cut], TN).astype(BF)
+                v = dot(a[:, q * share : (q + 1) * share], e[:, cut], TN).astype(BF)
+                for d in range(8):
+                    out[d, c, :, ch + q * share : ch + (q + 1) * share] = v[d * rows : (d + 1) * rows]
 
     return call(
         kernel,
         grid=(1,),
         ins=[(v, None, None) for v in (flat, reduced_grad, act, expanded_grad)],
-        outs=[(shape((n, share, 2 * ch), BF), None, None)],
+        outs=[(shape((8, n, rows, 3 * ch), BF), (8, n, rows, 2 * ch), lambda i: (0, 0, 0, 0))],
         name="post_weight_grads",
+    )()[0]
+
+
+def readout_weight_grad(low, piece, load):
+    total, ch = low.shape
+    width = piece.shape[1]
+    parts, n, rows, _ = load.shape
+    share = ch // n
+
+    def kernel(x, g, old, out):
+        v = dot(x[...], g[...], TN).astype(BF)
+        for d in range(parts):
+            out[d, 0] = v[d * rows : (d + 1) * rows]
+
+    return call(
+        kernel,
+        grid=(n,),
+        ins=[(low, (total, share), lambda c: (0, c)), (piece, None, None)],
+        outs=[(shape(load.shape, BF), (parts, 1, rows, width), lambda c: (0, c, 0, 2))],
+        aliased=(load,),
+        name="readout_weight_grad",
     )()[0]
 
 
@@ -741,29 +777,27 @@
     )(core)
 
 
-def finish_post(gathered, n, share):
-    groups, rows, ch = gathered.shape
-    eight = share // groups
-    per = 4
+def finish_post(gathered, n):
+    share, width = gathered.shape
+    ch = width // (n + 2)
+    per = 64
 
     def kernel(x, reduce_out, expand_out, read_out):
-        for g in range(per):
-            at = pl.ds(g * eight, eight)
-            v = x[g].astype(F32)
-            reduce_out[at, :] = v[:eight]
-            for q in range(n):
-                expand_out[q, at, :] = v[eight : 2 * eight, q * share : (q + 1) * share]
-                read_out[at, q * ch : (q + 1) * ch] = v[(2 + q) * eight : (3 + q) * eight]
-
-    return call(
-        kernel,
-        grid=(groups // per,),
-        ins=[(gathered, (per, rows, ch), lambda i: (i, 0, 0))],
+        reduce_out[...] = x[:, :ch].astype(F32)
+        for q in range(n):
+            expand_out[q] = x[:, ch + q * share : ch + (q + 1) * share].astype(F32)
+        read_out[...] = x[:, 2 * ch :].astype(F32)
+
+    return call(
+        kernel,
+        grid=(share // per,),
+        ins=[(gathered, (per, width), lambda i: (i, 0))],
         outs=[
-            (shape((share, ch), F32), (per * eight, ch), lambda i: (i, 0)),
-            (shape((n, share, share), F32), (n, per * eight, share), lambda i: (0, i, 0)),
-            (shape((share, n * ch), F32), (per * eight, n * ch), lambda i: (i, 0)),
-        ],
+            (shape((share, ch), F32), (per, ch), lambda i: (i, 0)),
+            (shape((n, share, share), F32), (n, per, share), lambda i: (0, i, 0)),
+            (shape((share, n * ch), F32), (per, n * ch), lambda i: (i, 0)),
+        ],
+        cost=6 * 10**9,
         name="finish_post",
     )()
 
@@ -847,55 +881,44 @@
     cots = lax.all_to_all(cotangent_by_image(cot_rows, select), "chan", 0, 0, tiled=False)
 
     flat_features = features.reshape(slots * cells, ch)
-    reduced = dot(flat_features, pre_reduce).reshape(slots, cells, ch)
-    convolved, convolved_act, normal_pre, pre_std, *pooled = pre_forward(
-        order, reduced, above, below, features, pre_reduce, pre_taps, pre_expand, pre_gain_row, pool_m
-    )
+    fixed = (features, pre_reduce, pre_taps, pre_expand, pre_gain_row, pool_m)
+    half = n // 2
+    kept, pooled = (), []
+    for h in range(2):
+        *kept, = pre_forward(order[h * half : (h + 1) * half], above, below, *fixed, earlier=tuple(kept))
+        pooled += kept[5:]
+        kept = kept[:5]
+    reduced, convolved, convolved_act, normal_pre, pre_std = kept
 
     moved = [lax.ppermute(pooled[k], ("rows", "chan"), spread(n, k)) for k in range(n)]
     flat, post_reduced, post_act, post_convolved, post_cact, post_normal, post_std, low = post_forward(
         source, moved, full, post_taps, pool
     )
     lows = [low] + [lax.ppermute(low, "chan", [(i, (i + k) % n) for i in range(n)]) for k in range(1, n)]
+    refined_grad = readout_backward(low, readout, cots)
+    refined_grad, lows[1], lows[3] = lax.optimization_barrier((refined_grad, lows[1], lows[3]))
     post_expanded_grad, post_reduced_grad, post_taps_grad, post_gain_grad, *back = post_backward(
-        source, low, readout, cots, full, post_taps, post_act, post_reduced, post_convolved, post_normal, post_std, pool
+        source, refined_grad, full, post_taps, post_act, post_reduced, post_convolved, post_normal, post_std, pool
     )
 
     returned = [lax.ppermute(back[k], ("rows", "chan"), [(d, s) for s, d in spread(n, k)]) for k in range(n)]
 
-    post_load = post_weight_grads(flat, post_reduced_grad, post_cact, post_expanded_grad, n)
-    post_sum = lax.psum_scatter(post_load, "chan", scatter_dimension=0, tiled=False)
+    load = post_weight_grads(flat, post_reduced_grad, post_cact, post_expanded_grad, n)
 
     alive = jnp.broadcast_to(jnp.tile(live, 48)[:, None], (48 * slots, 1))
-    lows = after(lows, post_load)
+    lows = after(lows, load)
     tokens, piece, low_here = token_block(rank, source, lows, place, readout, cot_rows, alive)
-    readout_grad = dot(low_here, piece, TN).astype(BF)
+    load = readout_weight_grad(low_here, piece, load)
     tokens = tokens.reshape(pool, pool, slots, out_share).transpose(2, 0, 1, 3)
-
-    returned = after(returned, readout_grad)
+    returned = after(returned, load)
+    eight = share // 32
+    rest = lax.psum_scatter(load, ("x", "core"), scatter_dimension=0, tiled=False)
+
     expanded_grad, convolved_grad, top, bottom, pre_gain_grad = pre_backward(
         order, returned, up_m, normal_pre, pre_std, pre_gain_row, convolved, pre_expand
     )
     grad_above = lax.ppermute(bottom, "rows", down_pairs)
     grad_below = lax.ppermute(top, "rows", up_pairs)
-
-    eight = share // 32
-    read_rows = after(readout_grad, bottom).reshape(n, 8, 4, eight, out_share).transpose(1, 2, 0, 3, 4)
-    load = jnp.concatenate(
-        [
-            post_sum[:, :ch].reshape(8, 4, eight, ch),
-            post_sum[:, ch:].reshape(8, 4, eight, ch),
-            read_rows.reshape(8, 4, n * eight, out_share),
-        ],
-        axis=2,
-    )
-    load = lax.psum_scatter(load, ("x", "core"), scatter_dimension=0, tiled=False)
-    load = lax.psum_scatter(load, "rows", scatter_dimension=0, tiled=False)
-    read_part = lax.all_to_all(load[2 * eight :].reshape(n, eight, out_share), "chan", 0, 0, tiled=False)
-    load = jnp.concatenate([load[: 2 * eight], read_part.reshape(n * eight, out_share)], axis=0)
-    gathered = lax.all_gather(load, ("x", "core", "rows"), axis=0, tiled=False)
-    post_reduce_out, post_expand_out, readout_out = finish_post(gathered, n, share)
-
     act_rows = after(convolved_act, bottom).reshape(-1, ch)
     pre_expand_grad = dot(act_rows, expanded_grad.reshape(-1, ch), TN).astype(BF)
     convolved_grad = after(convolved_grad, pre_expand_grad)
@@ -908,7 +931,17 @@
     theirs = [other_core(lax.dynamic_index_in_dim(g.reshape(2, ch // 2, ch), 1 - core, 0, keepdims=False)) for g in mine]
     load = join_halves(core_at, mine, theirs, small, other_core(small), 64)
     chips = ("x", "rows", "chan")
-    load = sum_and_copy(lax.all_to_all(load, chips, 0, 0, tiled=False))
+    pieces = after(lax.all_to_all(load, chips, 0, 0, tiled=False), feature_grad)
+
+    rest = after(rest, load).reshape(n, 4, eight, 3 * ch).transpose(1, 0, 2, 3)
+    rest = lax.psum_scatter(rest, "rows", scatter_dimension=0, tiled=False)
+    rest = lax.all_to_all(rest, "chan", 0, 0, tiled=False)
+    summed = jnp.sum(rest[:, :, : 2 * ch].astype(F32), axis=0).astype(BF)
+    rest = jnp.concatenate([summed] + [rest[c, :, 2 * ch :] for c in range(n)], axis=1)
+    rest = lax.all_gather(rest, ("x", "core", "rows"), axis=0, tiled=True)
+    post_reduce_out, post_expand_out, readout_out = finish_post(rest, n)
+
+    load = sum_and_copy(pieces)
     load = lax.all_to_all(load, chips, 0, 0, tiled=False).reshape(ch // 2, -1)
     pre_reduce_out, pre_expand_out, small_out = finish_pre(core_at, load, other_core(load), ch)
     per = ch // LANES

time: 425 us -> 396 us (0.932)
  waiting for transfers between devices: 96.1 us -> 60 us
  Pallas kernels: 141 us -> 158 us
  matrix products: 22.6 us -> 9.66 us
  blocking collectives: 47.4 us -> 56 us
    ppermute x3, waiting for transfers between devices: 38.4 us -> 0.01 us  [body(): lax.ppermute(low, 'chan', [(i, (i + k) % n) for i in range(n)])]
    pallas_call x14 -> x17, Pallas kernels: 141 us -> 158 us  [run(): pl.pallas_call(kernel, grid_spec=pltpu.PrefetchScalarGridSpec(num_scalar_...]
    dot_general x4 -> x2, matrix products: 22.6 us -> 9.66 us  [dot(): return lax.dot_general(a, b, (dims, ((), ())), preferred_element_type=F32)]
    ppermute x4, waiting for transfers between devices: 14.8 us -> 4.27 us  [body(): lax.ppermute(pooled[k], ('rows', 'chan'), spread(n, k))]
    all_to_all x0 -> x1, blocking collectives: none -> 9.31 us  [body(): rest = lax.all_to_all(rest, 'chan', 0, 0, tiled=False)]
    all_to_all x2 -> x1, waiting for transfers between devices: 24.5 us -> 17.2 us  [body(): pieces = after(lax.all_to_all(load, chips, 0, 0, tiled=False), feature_grad)]
    all_to_all x2 -> x1, starting transfers between devices: 12.7 us -> 6.49 us  [body(): pieces = after(lax.all_to_all(load, chips, 0, 0, tiled=False), feature_grad)]
    ppermute x4, starting transfers between devices: 11.1 us -> 16.4 us  [body(): lax.ppermute(back[k], ('rows', 'chan'), [(d, s) for s, d in spread(n, k)])]
  transfers between devices with their start and end apart: 27 -> 25, of which waited for: 6 -> 11; matrix products, arithmetic and copies ran while one was open for 9% -> 6% of each run, Pallas kernels for 25% -> 34%
where the time goes in v5:
time: 396 us; the launch traced here: 394 us
  Pallas kernels  158 us (40%)
  starting transfers between devices  69.5 us (18%)
  waiting for transfers between devices  60 us (15%)
  blocking collectives  56 us (14%)
  local copies, waits for them, and re-layouts  24.2 us (6%)
  between operations  14.2 us (4%)
  matrix products  9.66 us (2%)
    pallas_call x17, Pallas kernels, run(): pl.pallas_call(kernel, grid_spec=pltpu.PrefetchScalarGridSpec(num_scalar_...  158 us
    all_to_all x1, blocking collectives, body(): load = lax.all_to_all(load, chips, 0, 0, tiled=False).reshape(ch // 2, -1)  46.6 us
    reduce_scatter x1, waiting for transfers between devices, body(): rest = lax.psum_scatter(rest, 'rows', scatter_dimension=0, tiled=False)  20.1 us
    all_to_all x1, waiting for transfers between devices, body(): pieces = after(lax.all_to_all(load, chips, 0, 0, tiled=False), feature_grad)  17.2 us
    ppermute x4, starting transfers between devices, body(): lax.ppermute(back[k], ('rows', 'chan'), [(d, s) for s, d in spread(n, k)])  16.4 us
    ppermute x4, starting transfers between devices, other_core(): return lax.ppermute(values, 'core', [(0, 1), (1, 0)])  13 us
    ppermute x4, starting transfers between devices, body(): lax.ppermute(pooled[k], ('rows', 'chan'), spread(n, k))  10.5 us
    dot_general x2, matrix products, dot(): return lax.dot_general(a, b, (dims, ((), ())), preferred_element_type=F32)  9.66 us
  transfers between devices with their start and end apart: 25, of which 11 were waited for; matrix products, arithmetic and copies ran while one was open for 6% of the time, Pallas kernels for 34%

profile of v5, /device:TPU:1, one launch (start us, length us, event | category | flops | bytes accessed | tf_op | source)
XLA Modules:
  0.0 394.3 jit_solution(12708886820665993187)
XLA Ops:
  7.2 0.8 subtract_convert_fusion
  8.0 1.1 fusion.8
  9.2 1.2 fusion.1
  12.2 4.5 %cotangent_by_image.1 = bf16[4,288,1024]{2,1,0:T(8,128)(2,1)} custom-call(bf16[1152,1024]{1,0:T(8,128)(2,1)} %bitcast.71, bf16[128,128]{1,0:T(8,128)(2,1)} %copy.37.sel), custom_call_target="tpu_custom_call" | custom-call | flops 1 | bytes 1 | tf_op jit(solution)/shard_map/cotangent_by_image/pallas_call | solution.py:67
  16.6 5.8 %all-to-all-start = ((bf16[4,288,1024]{2,1,0:T(8,128)(2,1)}), bf16[4,288,1024]{2,1,0:T(8,128)(2,1)S(1)}, u32[]{:S(2)}, u32[]{:S(2)}) async-start(bf16[4,288,1024]{2,1,0:T(8,128)(2,1)} %cotangent_by_image.1), calls=%async_computation | async-start | bytes 4718592 | tf_op jit(solution)/shard_map/all_to_all | solution.py:881
  22.5 1.9 slice_bitcast_fusion
  24.4 3.2 collective-permute-start
  27.6 1.3 collective-permute-start.1
  28.9 1.4 reshape.149.tap
  30.9 4.4 %collective-permute-done.up_ref = bf16[8,24,1024]{2,1,0:T(8,128)(2,1)S(1)} collective-permute-done((bf16[8,24,1024]{2,1,0:T(8,128)(2,1)}, bf16[8,24,1024]{2,1,0:T(8,128)(2,1)S(1)}, u32[]{:S(2)}, u32[]{:S(2)}) %collective-permute-start) | collective-permute-done | bytes 393248 | tf_op jit(solution)/shard_map/ppermute | solution.py:866
  35.3 3.5 collective-permute-done.1.down_ref
  38.9 0.7 copy-done.8
  39.6 16.1 %pre_forward.2 = (f32[8,144,1024]{2,1,0:T(8,128)}, f32[8,144,1024]{2,1,0:T(8,128)}, bf16[8,144,1024]{2,1,0:T(8,128)(2,1)}, f32[8,144,1024]{2,1,0:T(8,128)}, f32[...) custom-call(s32[2]{0:T(128)} %get-tuple-element.148.order_ref, ...), custom_call_target="tpu_custom_call" | custom-call | flops 1 | bytes 1 | tf_op jit(solution)/shard_map/pre_forward/pallas_call | solution.py:67
  55.7 1.6 collective-permute-start.2
  57.3 2.9 collective-permute-start.3
  60.2 16.4 %pre_forward.3 = (f32[8,144,1024]{2,1,0:T(8,128)}, f32[8,144,1024]{2,1,0:T(8,128)}, bf16[8,144,1024]{2,1,0:T(8,128)(2,1)}, f32[8,144,1024]{2,1,0:T(8,128)}, f32[...) custom-call(s32[2]{0:T(128)} %get-tuple-element.147.order_ref, ...), custom_call_target="tpu_custom_call", output_to_operand_aliasing={{0}: (9, {}), {1}: (10, {}), {2}: (11, {}), {3}: (12, {}), ... | custom-call | flops 1 | bytes 1 | tf_op jit(solution)/shard_map/pre_forward/pallas_call | solution.py:67
  76.6 4.2 %collective-permute-start.4 = (bf16[72,1024]{1,0:T(8,128)(2,1)}, bf16[72,1024]{1,0:T(8,128)(2,1)S(1)}, u32[]{:S(2)}, u32[]{:S(2)}) collective-permute-start(bf16[72,1024]{1,0:T(8,128)(2,1)} %get-tuple-element.80), channel_id=1, source_target_pairs={{0,2},{1,6},{2,10},{3,14},{4,3},{5,7},{6,11},{7,15},{8,0},{9,4},{1... | collective-permute-start | bytes 442376 | tf_op jit(solution)/shard_map/ppermute | solution.py:893
  80.8 1.8 collective-permute-start.5
  83.8 1.0 collective-permute-done.4.refs_2_
  84.8 3.3 collective-permute-done.5.refs_3_
  88.7 11.1 %post_forward.1 = (bf16[288,1024]{1,0:T(8,128)(2,1)}, f32[288,1024]{1,0:T(8,128)}, bf16[288,1024]{1,0:T(8,128)(2,1)}, f32[288,1024]{1,0:T(8,128)}, bf16[288,1024...) custom-call(s32[4]{0:T(128)} %and_select_fusion.1.src, ...), custom_call_target="tpu_custom_call" | custom-call | flops 1 | bytes 1 | tf_op jit(solution)/shard_map/post_forward/pallas_call | solution.py:67
  99.8 2.0 collective-permute-start.6
  101.8 5.0 %collective-permute-start.7 = (bf16[288,1024]{1,0:T(8,128)(2,1)}, bf16[288,1024]{1,0:T(8,128)(2,1)S(1)}, u32[]{:S(2)}, u32[]{:S(2)}) collective-permute-start(bf16[288,1024]{1,0:T(8,128)(2,1)} %get-tuple-element.95.low_ref.refs_0_), channel_id=1, source_target_pairs={{0,3},{1,0},{2,1},{3,2},{4,7},{5,4},{6,5},{7,6},{8,11},{9,8},{10,9... | collective-permute-start | bytes 1769480 | tf_op jit(solution)/shard_map/ppermute | solution.py:897
  106.8 1.2 collective-permute-start.8
  108.6 1.6 broadcast_in_dim_tile.5.refs_7_
  110.1 1.4 copy-done.1
  111.5 10.9 %readout_backward.1.rg = f32[288,1024]{1,0:T(8,128)} custom-call(bf16[288,1024]{1,0:T(8,128)(2,1)} %get-tuple-element.95.low_ref.refs_0_, bf16[1024,4096]{1,0:T(8,128)(2,1)} %refs_5_.1, bf16[4,288,1024]{2,1,0:T(8,128)(2,1)} %copy-done.1), custom_call_target="tpu_custom_call" | custom-call | flops 1 | bytes 1 | tf_op jit(solution)/shard_map/readout_backward/pallas_call | solution.py:67
  122.4 12.3 %post_backward.1 = (bf16[288,1024]{1,0:T(8,128)(2,1)}, bf16[288,1024]{1,0:T(8,128)(2,1)}, f32[9,8,1024]{2,1,0:T(8,128)}, f32[8,1024]{1,0:T(8,128)}, bf16[72,1024...) custom-call(s32[4]{0:T(128)} %and_select_fusion.1.src, ...), custom_call_target="tpu_custom_call" | custom-call | flops 1 | bytes 1 | tf_op jit(solution)/shard_map/post_backward/pallas_call | solution.py:67
  134.7 6.0 %post_weight_grads.1.old = bf16[8,4,32,3072]{3,2,1,0:T(8,128)(2,1)} custom-call(bf16[288,1024]{1,0:T(8,128)(2,1)} %get-tuple-element.85.x, bf16[288,1024]{1,0:T(8,128)(2,1)} %get-tuple-element.92.g, bf16[288,1024]{1,0:T(8,128)(2,1)} %get-tuple-element.93.a, bf16[288,1024]{1,0:T(8,128)(2,1)} %get-tuple-element.94.e), custom_call_target="tpu_custom_call" | custom-call | flops 1 | bytes 1 | tf_op jit(solution)/shard_map/post_weight_grads/pallas_call | solution.py:67
  140.7 10.8 %token_block.1 = (bf16[1152,1024]{1,0:T(8,128)(2,1)}, bf16[1152,1024]{1,0:T(8,128)(2,1)}, bf16[1152,1024]{1,0:T(8,128)(2,1)}) custom-call(s32[1]{0:T(128)} %bitcast.chan_ref, s32[4]{0:T(128)} %and_select_fusion.1.src, bf16[288,1024]{1,0:T(8,128)(2,1)} %get-tuple-element.95.low_ref.refs_0_, bf16[288,1024]{1,0:T(8,128)(2,1)} %copy-done.11, ...), custom_call_target="tpu_custom_call" | custom-call | flops 1 | bytes 1 | tf_op jit(solution)/shard_map/token_block/pallas_call | solution.py:67
  151.5 6.7 %readout_weight_grad.1 = bf16[8,4,32,3072]{3,2,1,0:T(8,128)(2,1)} custom-call(bf16[1152,1024]{1,0:T(8,128)(2,1)} %get-tuple-element.104.x, bf16[1152,1024]{1,0:T(8,128)(2,1)} %get-tuple-element.105.g, bf16[8,4,32,3072]{3,2,1,0:T(8,128)(2,1)} %post_weight_grads.1.old), custom_call_target="tpu_custom_call", output_to_operand_aliasing={{}: (2, {})} | custom-call | flops 1 | bytes 1 | tf_op jit(solution)/shard_map/readout_weight_grad/pallas_call | solution.py:67
  158.3 0.8 copy-done.31
  159.8 13.9 %collective-permute-start.10 = (bf16[72,1024]{1,0:T(8,128)(2,1)S(1)}, bf16[72,1024]{1,0:T(8,128)(2,1)S(1)}, u32[]{:S(2)}, u32[]{:S(2)}) collective-permute-start(bf16[72,1024]{1,0:T(8,128)(2,1)S(1)} %copy-done.30), channel_id=1, source_target_pairs={{1,0},{5,1},{9,2},{13,3},{2,4},{6,5},{10,6},{14,7},{3,8},{7,9},{11... | collective-permute-start | bytes 442376 | tf_op jit(solution)/shard_map/ppermute | solution.py:904
  173.7 1.9 collective-permute-start.12
  175.6 1.7 collective-permute-done.10.refs_1_
  177.2 2.0 collective-permute-done.11.refs_2_
  179.3 1.5 collective-permute-done.12.refs_3_
  181.4 21.6 %pre_backward.1 = (bf16[8,144,1024]{2,1,0:T(8,128)(2,1)}, bf16[8,144,1024]{2,1,0:T(8,128)(2,1)}, bf16[8,24,1024]{2,1,0:T(8,128)(2,1)}, bf16[8,24,1024]{2,1,0:T(8,128)(2,1)}, f32[8,1024]{1,0:T(8,128)}) custom-call(s32[4]{0:T(128)} %copy-done.27, bf16[72,1024]{1,0:T(8,128)(2,1)} %copy-done.20, bf16[72,1024]{1,0:T(8,128)(2,1)} %copy-done.21, ...), custom_call_target="tpu_custom_call" | custom-call | flops 1 | bytes 1 | tf_op jit(solution)/shard_map/pre_backward/pallas_call | solution.py:67
  203.0 3.0 collective-permute-start.13
  206.0 1.5 collective-permute-start.14
  207.5 4.8 %bitcast_convert_fusion.refs_1_ = bf16[1024,1024]{1,0:T(8,128)(2,1)S(1)} fusion(bf16[8,144,1024]{2,1,0:T(8,128)(2,1)S(1)} %copy-done.6, bf16[8,144,1024]{2,1,0:T(8,128)(2,1)} %get-tuple-element.117), kind=kOutput, calls=%fused_computation | convolution fusion | flops 2416967680 | bytes 6815744 | tf_op jit(solution)/shard_map/dot_general | solution.py:23
  212.4 7.2 %collective-permute-start.16 = (bf16[512,1024]{1,0:T(8,128)(2,1)S(1)}, bf16[512,1024]{1,0:T(8,128)(2,1)S(1)}, u32[]{:S(2)}, u32[]{:S(2)}) collective-permute-start(bf16[512,1024]{1,0:T(8,128)(2,1)S(1)} %dynamic-slice_bitcast_fusion), channel_id=1, source_target_pairs={{0,16},{16,0},{1,17},{17,1},{2,18},{18,2},{3,19},{19,3},{4,20},{20... | collective-permute-start | bytes 3145736 | tf_op jit(solution)/shard_map/ppermute | solution.py:672
  219.7 0.7 copy-done.13
  220.5 12.2 %pre_conv_backward.1 = (bf16[8,144,1024]{2,1,0:T(8,128)(2,1)}, f32[9,8,1024]{2,1,0:T(8,128)}) custom-call(bf16[8,144,1024]{2,1,0:T(8,128)(2,1)} %get-tuple-element.118.cg, bf16[8,24,1024]{2,1,0:T(8,128)(2,1)} %copy-done.13, bf16[8,24,1024]{2,1,0:T(8,128)(2,1)} %copy-done.14, f32[8,144,1024]{2,1,0:T(8,128)} %get-tuple-element.120.red, f32[9,1024]{1,0:T(8,128)} %reshape.149.tap), custom_call_target="tpu_custom_call" | custom-call | flops 1 | bytes 1 | tf_op jit(solution)/shard_map/pre_conv_backward/pallas_call | solution.py:67
  232.8 4.8 %convolution_convert_fusion = bf16[1024,1024]{0,1:T(8,128)(2,1)S(1)} fusion(bf16[1152,1024]{1,0:T(8,128)(2,1)} %bitcast.85, bf16[1152,1024]{1,0:T(8,128)(2,1)S(1)} %bitcast.70), kind=kOutput, calls=%fused_computation.3 | convolution fusion | flops 2416967680 | bytes 6815744 | tf_op jit(solution)/shard_map/dot_general | solution.py:23
  237.7 3.3 collective-permute-start.15
  241.0 1.8 small_rows.1.refs_4_
  243.3 1.1 collective-permute-done.17.refs_5_
  245.8 4.0 %join_halves.1 = bf16[512,2176]{1,0:T(8,128)(2,1)} custom-call(s32[1]{0:T(128)} %bitcast.16.core_ref, bf16[1024,1024]{1,0:T(8,128)(2,1)} %bitcast.77, bf16[1024,1024]{1,0:T(8,128)(2,1)} %copy-done.4, bf16[512,1024]{1,0:T(8,128)(2,1)} %copy-done.10, bf16[512,1024]{1,0:T(8,128)(2,1)} %copy-done.9, f32[160,128]{1,0:T(8,128)} %small_rows.1.refs_4_, ...), custom_call_target="tpu_custom_call" | custom-call | flops 1 | bytes 1 | tf_op jit(solution)/shard_map/join_halves/pallas_call | solution.py:67
  249.8 2.1 copy_bitcast_fusion
  251.9 20.1 %reduce-scatter.5.cloned.1.call-done = bf16[1,4,8,3072]{3,2,1,0:T(8,128)(2,1)} async-done(((bf16[4,4,8,3072]{3,2,1,0:T(8,128)(2,1)}), bf16[1,4,8,3072]{3,2,1,0:T(8,128)(2,1)}) %reduce-scatter.5.cloned.1.call-update) | async-done | bytes 196624 | tf_op jit(solution)/shard_map/reduce_scatter | solution.py:937
  272.0 9.3 %all_to_all.20 = bf16[4,8,3072]{2,1,0:T(8,128)(2,1)S(1)} all-to-all(bf16[4,8,3072]{2,1,0:T(8,128)(2,1)} %bitcast.80), channel_id=1, replica_groups=mesh['x'=4,'core'=2,'rows'=4,'chan'=4] {'chan'}, dimensions={0} | all-to-all | bytes 393216 | tf_op jit(solution)/shard_map/all_to_all | solution.py:938
  281.3 6.5 %all-to-all-start.1 = ((bf16[64,8,2176]{2,1,0:T(8,128)(2,1)}), bf16[64,8,2176]{2,1,0:T(8,128)(2,1)S(1)}, u32[]{:S(2)}, u32[]{:S(2)}) async-start(bf16[64,8,2176]{2,1,0:T(8,128)(2,1)} %bitcast.21), calls=%async_computation.1 | async-start | bytes 4456448 | tf_op jit(solution)/shard_map/all_to_all | solution.py:934
  288.6 8.5 %feature_backward.1 = f32[8,144,1024]{2,1,0:T(8,128)} custom-call(s32[4]{0:T(128)} %copy-done.27, bf16[8,144,1024]{2,1,0:T(8,128)(2,1)} %get-tuple-element.122.rg, bf16[1024,1024]{1,0:T(8,128)(2,1)} %wr.5, bf16[288,72]{1,0:T(8,128)(2,1)} %constant.70.clone.refs_4_.up, bf16[72,1024]{1,0:T(8,128)(2,1)} %copy-done.20, bf16[72,1024]{1,0:T(8,128)(2,1)} %copy-done.21, ...), custom_call_target="tpu_custom_call" | custom-call | flops 8999999488 | bytes 1 | tf_op jit(solution)/shard_map/feature_backward/pallas_call | solution.py:67
  297.1 17.2 %all-to-all-done.1.x = bf16[64,8,2176]{2,1,0:T(8,128)(2,1)S(1)} async-done(((bf16[64,8,2176]{2,1,0:T(8,128)(2,1)}), bf16[64,8,2176]{2,1,0:T(8,128)(2,1)S(1)}, u32[]{:S(2)}, u32[]{:S(2)}) %all-to-all-start.1) | async-done | bytes 2228256 | tf_op jit(solution)/shard_map/all_to_all | solution.py:934
  314.3 1.4 copy-done.2
  315.6 4.5 %sum_and_copy.1 = bf16[64,8,2176]{2,1,0:T(8,128)(2,1)} custom-call(bf16[64,8,2176]{2,1,0:T(8,128)(2,1)} %copy-done.2), custom_call_target="tpu_custom_call" | custom-call | flops 1 | bytes 1 | tf_op jit(solution)/shard_map/sum_and_copy/pallas_call | solution.py:67
  320.1 46.6 %all_to_all.21 = bf16[64,8,2176]{2,1,0:T(8,128)(2,1)S(1)} all-to-all(bf16[64,8,2176]{2,1,0:T(8,128)(2,1)} %sum_and_copy.1), channel_id=1, replica_groups=mesh['x'=4,'core'=2,'rows'=4,'chan'=4] {'x','rows','chan'}, dimensions={0} | all-to-all | bytes 4456448 | tf_op jit(solution)/shard_map/all_to_all | solution.py:945
  366.7 2.0 collective-permute-start.18
  368.8 4.1 %collective-permute-done.18.b = bf16[512,2176]{1,0:T(8,128)(2,1)} collective-permute-done((bf16[512,2176]{1,0:T(8,128)(2,1)S(1)}, bf16[512,2176]{1,0:T(8,128)(2,1)}, u32[]{:S(2)}, u32[]{:S(2)}) %collective-permute-start.18) | collective-permute-done | bytes 2228256 | tf_op jit(solution)/shard_map/ppermute | solution.py:672
  372.9 5.9 %finish_pre.1 = (f32[1024,1024]{1,0:T(8,128)}, f32[1024,1024]{1,0:T(8,128)}, f32[512,128]{1,0:T(8,128)}) custom-call(s32[1]{0:T(128)} %bitcast.16.core_ref, bf16[512,2176]{1,0:T(8,128)(2,1)} %bitcast.74, bf16[512,2176]{1,0:T(8,128)(2,1)} %collective-permute-done.18.b), custom_call_target="tpu_custom_call" | custom-call | flops 1 | bytes 1 | tf_op jit(solution)/shard_map/finish_pre/pallas_call | solution.py:67
  378.8 0.8 fusion.9
  380.9 1.3 slice_bitcast_fusion.6
  382.8 5.0 %finish_post.1 = (f32[256,1024]{1,0:T(8,128)}, f32[4,256,256]{2,1,0:T(8,128)}, f32[256,4096]{1,0:T(8,128)}) custom-call(bf16[256,6144]{1,0:T(8,128)(2,1)} %all-gather.4.cloned.1.call-done.x), custom_call_target="tpu_custom_call" | custom-call | flops 6000000000 | bytes 1 | tf_op jit(solution)/shard_map/finish_post/pallas_call | solution.py:67
  (113 shorter events, 11.1 us)
Async XLA Ops:
  7.2 4.2 %copy-start.24 = (bf16[128,128]{1,0:T(8,128)(2,1)S(1)}, bf16[128,128]{1,0:T(8,128)(2,1)}, u32[]{:S(2)}) copy-start(bf16[128,128]{1,0:T(8,128)(2,1)} %constant.71.clone.refs_4_) | copy-start | bytes 98308
  7.2 3.9 copy-start.32
  7.2 80.9 %all-gather.6.cloned.1.call-start = ((), (), s32[]{:S(2)}) async-start(), calls=%async_computation.9 | async-start | bytes 4866048 | tf_op jit(solution)/shard_map/all_gather | solution.py:876
  16.6 93.5 %all-to-all-start = ((bf16[4,288,1024]{2,1,0:T(8,128)(2,1)}), bf16[4,288,1024]{2,1,0:T(8,128)(2,1)S(1)}, u32[]{:S(2)}, u32[]{:S(2)}) async-start(bf16[4,288,1024]{2,1,0:T(8,128)(2,1)} %cotangent_by_image.1), calls=%async_computation | async-start | bytes 4718592 | tf_op jit(solution)/shard_map/all_to_all | solution.py:881
  22.5 227.4 %reduce-scatter.3.cloned.1.call-start = ((), (), s32[]{:S(2)}) async-start(), calls=%async_computation.6 | async-start | bytes 7077888 | tf_op jit(solution)/shard_map/reduce_scatter | solution.py:915
  24.4 10.9 %collective-permute-start = (bf16[8,24,1024]{2,1,0:T(8,128)(2,1)}, bf16[8,24,1024]{2,1,0:T(8,128)(2,1)S(1)}, u32[]{:S(2)}, u32[]{:S(2)}) collective-permute-start(bf16[8,24,1024]{2,1,0:T(8,128)(2,1)} %get-tuple-element.138), channel_id=1, source_target_pairs={{0,4},{4,8},{8,12},{1,5},{5,9},{9,13},{2,6},{6,10},{10,14},{3,7},{... | collective-permute-start | bytes 1179656 | tf_op jit(solution)/shard_map/ppermute | solution.py:866
  27.6 11.2 %collective-permute-start.1 = (bf16[8,24,1024]{2,1,0:T(8,128)(2,1)S(1)}, bf16[8,24,1024]{2,1,0:T(8,128)(2,1)S(1)}, u32[]{:S(2)}, u32[]{:S(2)}) collective-permute-start(bf16[8,24,1024]{2,1,0:T(8,128)(2,1)S(1)} %get-tuple-element.137), channel_id=1, source_target_pairs={{4,0},{8,4},{12,8},{5,1},{9,5},{13,9},{6,2},{10,6},{14,10},{7,3},{... | collective-permute-start | bytes 1179656 | tf_op jit(solution)/shard_map/ppermute | solution.py:867
  30.3 25.4 %copy-start.27 = (s32[4]{0:T(128)}, s32[4]{0:T(128)S(1)}, u32[]{:S(2)}) copy-start(s32[4]{0:T(128)S(1)} %and_select_fusion.order_ref) | copy-start | bytes 52
  35.3 3.5 copy-start.7
  38.9 0.7 copy-start.8
  55.7 28.0 %collective-permute-start.2 = (bf16[72,1024]{1,0:T(8,128)(2,1)}, bf16[72,1024]{1,0:T(8,128)(2,1)S(1)}, u32[]{:S(2)}, u32[]{:S(2)}) collective-permute-start(bf16[72,1024]{1,0:T(8,128)(2,1)} %get-tuple-element.73), channel_id=1, source_target_pairs={{0,0},{1,4},{2,8},{3,12},{4,1},{5,5},{6,9},{7,13},{8,2},{9,6},{10,... | collective-permute-start | bytes 442376 | tf_op jit(solution)/shard_map/ppermute | solution.py:893
  57.3 26.5 %collective-permute-start.3 = (bf16[72,1024]{1,0:T(8,128)(2,1)}, bf16[72,1024]{1,0:T(8,128)(2,1)S(1)}, u32[]{:S(2)}, u32[]{:S(2)}) collective-permute-start(bf16[72,1024]{1,0:T(8,128)(2,1)} %get-tuple-element.74), channel_id=1, source_target_pairs={{0,1},{1,5},{2,9},{3,13},{4,2},{5,6},{6,10},{7,14},{8,3},{9,7},{10... | collective-permute-start | bytes 442376 | tf_op jit(solution)/shard_map/ppermute | solution.py:893
  60.2 22.4 %copy-start.26 = (bf16[3,3,1024]{2,1,0:T(4,128)(2,1)S(1)}, bf16[3,3,1024]{2,1,0:T(4,128)(2,1)}, u32[]{:S(2)}) copy-start(bf16[3,3,1024]{2,1,0:T(4,128)(2,1)} %param.22) | copy-start | bytes 55300
  76.6 8.2 %collective-permute-start.4 = (bf16[72,1024]{1,0:T(8,128)(2,1)}, bf16[72,1024]{1,0:T(8,128)(2,1)S(1)}, u32[]{:S(2)}, u32[]{:S(2)}) collective-permute-start(bf16[72,1024]{1,0:T(8,128)(2,1)} %get-tuple-element.80), channel_id=1, source_target_pairs={{0,2},{1,6},{2,10},{3,14},{4,3},{5,7},{6,11},{7,15},{8,0},{9,4},{1... | collective-permute-start | bytes 442376 | tf_op jit(solution)/shard_map/ppermute | solution.py:893
  80.8 7.3 %collective-permute-start.5 = (bf16[72,1024]{1,0:T(8,128)(2,1)}, bf16[72,1024]{1,0:T(8,128)(2,1)S(1)}, u32[]{:S(2)}, u32[]{:S(2)}) collective-permute-start(bf16[72,1024]{1,0:T(8,128)(2,1)} %get-tuple-element.81), channel_id=1, source_target_pairs={{0,3},{1,7},{2,11},{3,15},{4,0},{5,4},{6,8},{7,12},{8,1},{9,5},{10... | collective-permute-start | bytes 442376 | tf_op jit(solution)/shard_map/ppermute | solution.py:893
  83.8 4.3 %copy-start.16 = (bf16[72,1024]{1,0:T(8,128)(2,1)}, bf16[72,1024]{1,0:T(8,128)(2,1)S(1)}, u32[]{:S(2)}) copy-start(bf16[72,1024]{1,0:T(8,128)(2,1)S(1)} %collective-permute-done.2.refs_0_) | copy-start | bytes 442372
  83.8 4.3 %copy-start.17 = (bf16[72,1024]{1,0:T(8,128)(2,1)}, bf16[72,1024]{1,0:T(8,128)(2,1)S(1)}, u32[]{:S(2)}) copy-start(bf16[72,1024]{1,0:T(8,128)(2,1)S(1)} %collective-permute-done.3.refs_1_) | copy-start | bytes 442372
  84.8 3.3 copy-start.18
  88.1 0.7 copy-start.19
  99.8 22.6 %collective-permute-start.6 = (bf16[288,1024]{1,0:T(8,128)(2,1)}, bf16[288,1024]{1,0:T(8,128)(2,1)S(1)}, u32[]{:S(2)}, u32[]{:S(2)}) collective-permute-start(bf16[288,1024]{1,0:T(8,128)(2,1)} %get-tuple-element.95.low_ref.refs_0_), channel_id=1, source_target_pairs={{0,1},{1,2},{2,3},{3,0},{4,5},{5,6},{6,7},{7,4},{8,9},{9,10},{10,1... | collective-permute-start | bytes 1769480 | tf_op jit(solution)/shard_map/ppermute | solution.py:897
  101.8 20.6 %collective-permute-start.7 = (bf16[288,1024]{1,0:T(8,128)(2,1)}, bf16[288,1024]{1,0:T(8,128)(2,1)S(1)}, u32[]{:S(2)}, u32[]{:S(2)}) collective-permute-start(bf16[288,1024]{1,0:T(8,128)(2,1)} %get-tuple-element.95.low_ref.refs_0_), channel_id=1, source_target_pairs={{0,3},{1,0},{2,1},{3,2},{4,7},{5,4},{6,5},{7,6},{8,11},{9,8},{10,9... | collective-permute-start | bytes 1769480 | tf_op jit(solution)/shard_map/ppermute | solution.py:897
  106.8 33.9 %collective-permute-start.8 = (bf16[288,1024]{1,0:T(8,128)(2,1)}, bf16[288,1024]{1,0:T(8,128)(2,1)}, u32[]{:S(2)}, u32[]{:S(2)}) collective-permute-start(bf16[288,1024]{1,0:T(8,128)(2,1)} %get-tuple-element.95.low_ref.refs_0_), channel_id=1, source_target_pairs={{0,2},{1,3},{2,0},{3,1},{4,6},{5,7},{6,4},{7,5},{8,10},{9,11},{10,... | collective-permute-start | bytes 1769480 | tf_op jit(solution)/shard_map/ppermute | solution.py:897
  110.1 1.4 copy-start.1
  122.4 12.3 %copy-start.11 = (bf16[288,1024]{1,0:T(8,128)(2,1)}, bf16[288,1024]{1,0:T(8,128)(2,1)S(1)}, u32[]{:S(2)}) copy-start(bf16[288,1024]{1,0:T(8,128)(2,1)S(1)} %collective-permute-done.6.refs_1_) | copy-start | bytes 1769476
  122.4 12.3 %copy-start.12 = (bf16[288,1024]{1,0:T(8,128)(2,1)}, bf16[288,1024]{1,0:T(8,128)(2,1)S(1)}, u32[]{:S(2)}) copy-start(bf16[288,1024]{1,0:T(8,128)(2,1)S(1)} %collective-permute-done.7.refs_3_) | copy-start | bytes 1769476
  158.2 0.9 copy-start.31
  158.2 1.6 copy-start.30
  158.2 15.5 %copy-start.29 = (bf16[72,1024]{1,0:T(8,128)(2,1)S(1)}, bf16[72,1024]{1,0:T(8,128)(2,1)}, u32[]{:S(2)}) copy-start(bf16[72,1024]{1,0:T(8,128)(2,1)} %get-tuple-element.102) | copy-start | bytes 442372
  158.2 15.5 %copy-start.28 = (bf16[72,1024]{1,0:T(8,128)(2,1)S(1)}, bf16[72,1024]{1,0:T(8,128)(2,1)}, u32[]{:S(2)}) copy-start(bf16[72,1024]{1,0:T(8,128)(2,1)} %get-tuple-element.103) | copy-start | bytes 442372
  158.2 113.7 %reduce-scatter.5.cloned.1.call-start = ((), (), s32[]{:S(2)}) async-start(), calls=%async_computation.7 | async-start | bytes 983040 | tf_op jit(solution)/shard_map/reduce_scatter | solution.py:937
  159.1 16.5 %collective-permute-start.9 = (bf16[72,1024]{1,0:T(8,128)(2,1)S(1)}, bf16[72,1024]{1,0:T(8,128)(2,1)S(1)}, u32[]{:S(2)}, u32[]{:S(2)}) collective-permute-start(bf16[72,1024]{1,0:T(8,128)(2,1)S(1)} %copy-done.31), channel_id=1, source_target_pairs={{0,0},{4,1},{8,2},{12,3},{1,4},{5,5},{9,6},{13,7},{2,8},{6,9},{10,... | collective-permute-start | bytes 442376 | tf_op jit(solution)/shard_map/ppermute | solution.py:904
  159.8 17.4 %collective-permute-start.10 = (bf16[72,1024]{1,0:T(8,128)(2,1)S(1)}, bf16[72,1024]{1,0:T(8,128)(2,1)S(1)}, u32[]{:S(2)}, u32[]{:S(2)}) collective-permute-start(bf16[72,1024]{1,0:T(8,128)(2,1)S(1)} %copy-done.30), channel_id=1, source_target_pairs={{1,0},{5,1},{9,2},{13,3},{2,4},{6,5},{10,6},{14,7},{3,8},{7,9},{11... | collective-permute-start | bytes 442376 | tf_op jit(solution)/shard_map/ppermute | solution.py:904
  173.7 5.6 %collective-permute-start.11 = (bf16[72,1024]{1,0:T(8,128)(2,1)S(1)}, bf16[72,1024]{1,0:T(8,128)(2,1)S(1)}, u32[]{:S(2)}, u32[]{:S(2)}) collective-permute-start(bf16[72,1024]{1,0:T(8,128)(2,1)S(1)} %copy-done.29), channel_id=1, source_target_pairs={{2,0},{6,1},{10,2},{14,3},{3,4},{7,5},{11,6},{15,7},{0,8},{4,9},{8... | collective-permute-start | bytes 442376 | tf_op jit(solution)/shard_map/ppermute | solution.py:904
  173.7 7.1 %collective-permute-start.12 = (bf16[72,1024]{1,0:T(8,128)(2,1)S(1)}, bf16[72,1024]{1,0:T(8,128)(2,1)S(1)}, u32[]{:S(2)}, u32[]{:S(2)}) collective-permute-start(bf16[72,1024]{1,0:T(8,128)(2,1)S(1)} %copy-done.28), channel_id=1, source_target_pairs={{3,0},{7,1},{11,2},{15,3},{0,4},{4,5},{8,6},{12,7},{1,8},{5,9},{9,... | collective-permute-start | bytes 442376 | tf_op jit(solution)/shard_map/ppermute | solution.py:904
  175.6 5.2 %copy-start.20 = (bf16[72,1024]{1,0:T(8,128)(2,1)}, bf16[72,1024]{1,0:T(8,128)(2,1)S(1)}, u32[]{:S(2)}) copy-start(bf16[72,1024]{1,0:T(8,128)(2,1)S(1)} %collective-permute-done.9.refs_0_) | copy-start | bytes 442372
  177.2 3.5 copy-start.21
  179.3 1.5 copy-start.22
  180.7 0.6 copy-start.23
  181.4 26.1 %copy-start.6 = (bf16[8,144,1024]{2,1,0:T(8,128)(2,1)S(1)}, bf16[8,144,1024]{2,1,0:T(8,128)(2,1)}, u32[]{:S(2)}) copy-start(bf16[8,144,1024]{2,1,0:T(8,128)(2,1)} %get-tuple-element.116) | copy-start | bytes 7077892
  203.0 16.7 %collective-permute-start.13 = (bf16[8,24,1024]{2,1,0:T(8,128)(2,1)}, bf16[8,24,1024]{2,1,0:T(8,128)(2,1)S(1)}, u32[]{:S(2)}, u32[]{:S(2)}) collective-permute-start(bf16[8,24,1024]{2,1,0:T(8,128)(2,1)} %get-tuple-element.115), channel_id=1, source_target_pairs={{0,4},{4,8},{8,12},{1,5},{5,9},{9,13},{2,6},{6,10},{10,14},{3,7},{... | collective-permute-start | bytes 1179656 | tf_op jit(solution)/shard_map/ppermute | solution.py:920
  206.0 13.7 %collective-permute-start.14 = (bf16[8,24,1024]{2,1,0:T(8,128)(2,1)}, bf16[8,24,1024]{2,1,0:T(8,128)(2,1)S(1)}, u32[]{:S(2)}, u32[]{:S(2)}) collective-permute-start(bf16[8,24,1024]{2,1,0:T(8,128)(2,1)} %get-tuple-element.119), channel_id=1, source_target_pairs={{4,0},{8,4},{12,8},{5,1},{9,5},{13,9},{6,2},{10,6},{14,10},{7,3},{... | collective-permute-start | bytes 1179656 | tf_op jit(solution)/shard_map/ppermute | solution.py:921
  212.3 20.4 %copy-start.4 = (bf16[1024,1024]{1,0:T(8,128)(2,1)}, bf16[1024,1024]{1,0:T(8,128)(2,1)S(1)}, u32[]{:S(2)}) copy-start(bf16[1024,1024]{1,0:T(8,128)(2,1)S(1)} %bitcast_convert_fusion.refs_1_) | copy-start | bytes 6291460
  212.4 32.0 %collective-permute-start.16 = (bf16[512,1024]{1,0:T(8,128)(2,1)S(1)}, bf16[512,1024]{1,0:T(8,128)(2,1)S(1)}, u32[]{:S(2)}, u32[]{:S(2)}) collective-permute-start(bf16[512,1024]{1,0:T(8,128)(2,1)S(1)} %dynamic-slice_bitcast_fusion), channel_id=1, source_target_pairs={{0,16},{16,0},{1,17},{17,1},{2,18},{18,2},{3,19},{19,3},{4,20},{20... | collective-permute-start | bytes 3145736 | tf_op jit(solution)/shard_map/ppermute | solution.py:672
  219.7 0.7 copy-start.13
  219.7 0.9 copy-start.14
  220.5 12.2 %copy-start = (bf16[8,6,24,1024]{3,2,1,0:T(8,128)(2,1)S(1)}, bf16[8,6,24,1024]{3,2,1,0:T(8,128)(2,1)}, u32[]{:S(2)}) copy-start(bf16[8,6,24,1024]{3,2,1,0:T(8,128)(2,1)} %feat.3) | copy-start | bytes 7077892
  237.6 6.9 %copy-start.5 = (bf16[1024,1024]{0,1:T(8,128)(2,1)}, bf16[1024,1024]{0,1:T(8,128)(2,1)S(1)}, u32[]{:S(2)}) copy-start(bf16[1024,1024]{0,1:T(8,128)(2,1)S(1)} %convolution_convert_fusion) | copy-start | bytes 6291460
  237.7 6.8 %collective-permute-start.15 = (bf16[512,1024]{1,0:T(8,128)(2,1)S(1)}, bf16[512,1024]{1,0:T(8,128)(2,1)S(1)}, u32[]{:S(2)}, u32[]{:S(2)}) collective-permute-start(bf16[512,1024]{1,0:T(8,128)(2,1)S(1)} %dynamic-slice_bitcast_fusion.1), channel_id=1, source_target_pairs={{0,16},{16,0},{1,17},{17,1},{2,18},{18,2},{3,19},{19,3},{4,20},{20... | collective-permute-start | bytes 3145736 | tf_op jit(solution)/shard_map/ppermute | solution.py:672
  242.8 1.6 collective-permute-start.17
  244.5 0.6 copy-start.25
  244.5 1.0 copy-start.9
  244.5 1.3 copy-start.10
  281.3 33.0 %all-to-all-start.1 = ((bf16[64,8,2176]{2,1,0:T(8,128)(2,1)}), bf16[64,8,2176]{2,1,0:T(8,128)(2,1)S(1)}, u32[]{:S(2)}, u32[]{:S(2)}) async-start(bf16[64,8,2176]{2,1,0:T(8,128)(2,1)} %bitcast.21), calls=%async_computation.1 | async-start | bytes 4456448 | tf_op jit(solution)/shard_map/all_to_all | solution.py:934
  287.8 95.0 %all-gather.4.cloned.1.call-start = ((), (), s32[]{:S(2)}) async-start(), calls=%async_computation.8 | async-start | bytes 3244032 | tf_op jit(solution)/shard_map/all_gather | solution.py:941
  287.9 0.6 copy-start.15
  314.3 1.4 copy-start.2
  366.7 6.1 %copy-start.3 = (bf16[64,8,2176]{2,1,0:T(8,128)(2,1)}, bf16[64,8,2176]{2,1,0:T(8,128)(2,1)S(1)}, u32[]{:S(2)}) copy-start(bf16[64,8,2176]{2,1,0:T(8,128)(2,1)S(1)} %all_to_all.21) | copy-start | bytes 6684676
  366.7 6.1 %collective-permute-start.18 = (bf16[512,2176]{1,0:T(8,128)(2,1)S(1)}, bf16[512,2176]{1,0:T(8,128)(2,1)}, u32[]{:S(2)}, u32[]{:S(2)}) collective-permute-start(bf16[512,2176]{1,0:T(8,128)(2,1)S(1)} %bitcast.73), channel_id=1, source_target_pairs={{0,16},{16,0},{1,17},{17,1},{2,18},{18,2},{3,19},{19,3},{4,20},{20... | collective-permute-start | bytes 6684680 | tf_op jit(solution)/shard_map/ppermute | solution.py:672
Sparse Core Ops, SparseCore 0:
  11.2 61.4 all-gather.5
  158.4 54.4 reduce-scatter.2
  252.0 19.8 reduce-scatter.4
  291.2 74.5 all-gather.3

commit v6 on v5

--- a/solution.py
+++ b/solution.py
@@ -99,17 +99,16 @@
     return (at >= depth).astype(F32), (at < (width - 1) * depth).astype(F32)
 
 
-def pre_forward(order, above, below, features, pre_reduce, taps, pre_expand, gain, pool, earlier=()):
+def pre_forward(order, reduced, above, below, features, pre_reduce, taps, pre_expand, gain, pool, earlier=()):
     slots, high, wide, ch = features.shape
     cells = high * wide
     n = order.shape[0]
     part = 2
 
-    def kernel(order_ref, up_ref, down_ref, feat, wr, tap, we, gn, pool_ref, *rest):
-        red, conv_out, act_out, norm_out, std_out, *rest = rest[len(earlier) :]
+    def kernel(order_ref, red, up_ref, down_ref, feat, wr, tap, we, gn, pool_ref, *rest):
+        conv_out, act_out, norm_out, std_out, *rest = rest[len(earlier) :]
         pooled_out, (halo, exp, sums) = rest[:n], rest[n:]
         k = pl.program_id(0)
-        red[...] = dot(feat[...].reshape(part * cells, ch), wr[...]).reshape(part, cells, ch)
         for side, ref in enumerate((up_ref, down_ref)):
             halo[side] = dot(ref[...].reshape(part * wide, ch), wr[...]).reshape(part, wide, ch)
         first, last = edge_masks(wide, wide, 1)
@@ -173,6 +172,7 @@
         grid=(n,),
         prefetch=1,
         ins=[
+            (reduced, block, by_order(2)),
             (above, (part, wide, ch), by_order(2)),
             (below, (part, wide, ch), by_order(2)),
             (features, (part, high, wide, ch), by_order(3)),
@@ -183,7 +183,6 @@
             (pool, None, None),
         ],
         outs=[
-            (shape((slots, cells, ch), F32), block, by_order(2)),
             (shape((slots, cells, ch), F32), block, by_order(2)),
             (shape((slots, cells, ch), BF), block, by_order(2)),
             (shape((slots, cells, ch), F32), block, by_order(2)),
@@ -743,38 +742,26 @@
     )()[0]
 
 
-def finish_pre(core, own, got, ch):
-    half, width = own.shape
+def finish_pre(place, half_rows, ch, earlier=()):
+    half, width = half_rows.shape
     m = (width - LANES) // ch
 
-    def kernel(core_ref, a, b, *outs):
-        h = pl.program_id(0)
-
-        def write(ref):
-            for i in range(m):
-                outs[i][...] = ref[:, i * ch : (i + 1) * ch].astype(F32)
-
-            @pl.when(h == 0)
-            def _():
-                outs[m][...] = ref[:, m * ch :].astype(F32)
-
-        @pl.when(h == core_ref[0])
-        def _():
-            write(a)
-
-        @pl.when(h != core_ref[0])
-        def _():
-            write(b)
-
-    return call(
-        kernel,
-        grid=(2,),
+    def kernel(place_ref, x, *outs):
+        outs = outs[len(earlier) :]
+        for i in range(m):
+            outs[i][...] = x[:, i * ch : (i + 1) * ch].astype(F32)
+        outs[m][...] = x[:, m * ch :].astype(F32)
+
+    return call(
+        kernel,
+        grid=(1,),
         prefetch=1,
-        ins=[(own, None, None), (got, None, None)],
-        outs=[(shape((2 * half, ch), F32), (half, ch), lambda h, c: (h, 0)) for _ in range(m)]
+        ins=[(half_rows, None, None)],
+        outs=[(shape((2 * half, ch), F32), (half, ch), lambda i, c: (c[0], 0)) for _ in range(m)]
         + [(shape((half, LANES), F32), None, None)],
+        aliased=earlier,
         name="finish_pre",
-    )(core)
+    )(place)
 
 
 def finish_post(gathered, n):
@@ -875,20 +862,21 @@
     eighths = shards.reshape(8, -1, ch)
     full = lax.all_gather(lax.dynamic_index_in_dim(eighths, eighth, 0, keepdims=False), ("chan", "x", "core"), axis=0, tiled=True)
     full = full.reshape(n, 2 * share + 64, ch)
+    flat_features = features.reshape(slots * cells, ch)
+    reduced = dot(flat_features, pre_reduce).reshape(slots, cells, ch)
     live = (jnp.arange(SLOT)[None, :] < counts[:, None]).astype(F32).reshape(slots)
     select = place.T * jnp.tile(live.astype(BF), 16)[None, :]
     cot_rows = cotangent.transpose(1, 2, 0, 3).reshape(-1, out_share)
-    cots = lax.all_to_all(cotangent_by_image(cot_rows, select), "chan", 0, 0, tiled=False)
-
-    flat_features = features.reshape(slots * cells, ch)
-    fixed = (features, pre_reduce, pre_taps, pre_expand, pre_gain_row, pool_m)
+    cots = lax.all_to_all(cotangent_by_image(after(cot_rows, reduced), select), "chan", 0, 0, tiled=False)
+
+    fixed = (reduced, above, below, features, pre_reduce, pre_taps, pre_expand, pre_gain_row, pool_m)
     half = n // 2
     kept, pooled = (), []
     for h in range(2):
-        *kept, = pre_forward(order[h * half : (h + 1) * half], above, below, *fixed, earlier=tuple(kept))
-        pooled += kept[5:]
-        kept = kept[:5]
-    reduced, convolved, convolved_act, normal_pre, pre_std = kept
+        *kept, = pre_forward(order[h * half : (h + 1) * half], *fixed, earlier=tuple(kept))
+        pooled += kept[4:]
+        kept = kept[:4]
+    convolved, convolved_act, normal_pre, pre_std = kept
 
     moved = [lax.ppermute(pooled[k], ("rows", "chan"), spread(n, k)) for k in range(n)]
     flat, post_reduced, post_act, post_convolved, post_cact, post_normal, post_std, low = post_forward(
@@ -906,9 +894,9 @@
     load = post_weight_grads(flat, post_reduced_grad, post_cact, post_expanded_grad, n)
 
     alive = jnp.broadcast_to(jnp.tile(live, 48)[:, None], (48 * slots, 1))
-    lows = after(lows, load)
+    lows = after(lows, load, returned[:2])
     tokens, piece, low_here = token_block(rank, source, lows, place, readout, cot_rows, alive)
-    load = readout_weight_grad(low_here, piece, load)
+    load = readout_weight_grad(low_here, after(piece, returned[2:]), load)
     tokens = tokens.reshape(pool, pool, slots, out_share).transpose(2, 0, 1, 3)
     returned = after(returned, load)
     eight = share // 32
@@ -923,19 +911,21 @@
     pre_expand_grad = dot(act_rows, expanded_grad.reshape(-1, ch), TN).astype(BF)
     convolved_grad = after(convolved_grad, pre_expand_grad)
     reduced_grad, pre_taps_grad = pre_conv_backward(convolved_grad, grad_above, grad_below, reduced, pre_taps)
+    rest = after(rest, reduced_grad).reshape(n, 4, eight, 3 * ch).transpose(1, 0, 2, 3)
+    small = small_rows(pre_taps_grad, pre_gain_grad, post_taps_grad, post_gain_grad)
+    flat_features = after(flat_features, rest, small)
+    rest = lax.psum_scatter(rest, "rows", scatter_dimension=0, tiled=False)
+
     pre_reduce_grad = dot(flat_features, reduced_grad.reshape(-1, ch), TN).astype(BF)
     feature_grad = feature_backward(order, after(reduced_grad, pre_reduce_grad), pre_reduce, returned, up_m).reshape(features.shape)
 
-    small = small_rows(pre_taps_grad, pre_gain_grad, post_taps_grad, post_gain_grad)
     mine = [pre_reduce_grad, pre_expand_grad]
     theirs = [other_core(lax.dynamic_index_in_dim(g.reshape(2, ch // 2, ch), 1 - core, 0, keepdims=False)) for g in mine]
     load = join_halves(core_at, mine, theirs, small, other_core(small), 64)
     chips = ("x", "rows", "chan")
     pieces = after(lax.all_to_all(load, chips, 0, 0, tiled=False), feature_grad)
 
-    rest = after(rest, load).reshape(n, 4, eight, 3 * ch).transpose(1, 0, 2, 3)
-    rest = lax.psum_scatter(rest, "rows", scatter_dimension=0, tiled=False)
-    rest = lax.all_to_all(rest, "chan", 0, 0, tiled=False)
+    rest = lax.all_to_all(after(rest, feature_grad), "chan", 0, 0, tiled=False)
     summed = jnp.sum(rest[:, :, : 2 * ch].astype(F32), axis=0).astype(BF)
     rest = jnp.concatenate([summed] + [rest[c, :, 2 * ch :] for c in range(n)], axis=1)
     rest = lax.all_gather(rest, ("x", "core", "rows"), axis=0, tiled=True)
@@ -943,7 +933,11 @@
 
     load = sum_and_copy(pieces)
     load = lax.all_to_all(load, chips, 0, 0, tiled=False).reshape(ch // 2, -1)
-    pre_reduce_out, pre_expand_out, small_out = finish_pre(core_at, load, other_core(load), ch)
+    theirs = other_core(load)
+    *own, small_own = finish_pre(core_at, load, ch)
+    theirs = after(theirs, small_own)
+    pre_reduce_out, pre_expand_out, small_their = finish_pre(1 - core_at, theirs, ch, earlier=tuple(own))
+    small_out = jnp.where(core == 0, small_own, small_their)
     per = ch // LANES
     cut = [0, 9 * per, 10 * per, 19 * per, 20 * per]
     pre_conv_out, pre_gain_out, post_conv_out, post_gain_out = [small_out[a:b] for a, b in zip(cut, cut[1:])]

time: 396 us -> 388 us (0.980)
  blocking collectives: 56 us -> 43.2 us
  waiting for transfers between devices: 60 us -> 48.1 us
  starting transfers between devices: 69.5 us -> 78 us
  matrix products: 9.66 us -> 15.5 us
    reduce_scatter x1, waiting for transfers between devices: 20.1 us -> 6.8 us  [body(): rest = lax.psum_scatter(rest, 'rows', scatter_dimension=0, tiled=False)]
    all_to_all x1 -> x0, blocking collectives: 9.31 us -> none  [body(): rest = lax.all_to_all(rest, 'chan', 0, 0, tiled=False)]
    all_to_all x1, waiting for transfers between devices: 17.2 us -> 25.5 us  [body(): pieces = after(lax.all_to_all(load, chips, 0, 0, tiled=False), feature_grad)]
    dot_general x2 -> x3, matrix products: 9.66 us -> 15.5 us  [dot(): return lax.dot_general(a, b, (dims, ((), ())), preferred_element_type=F32)]
    ppermute x4, waiting for transfers between devices: 5.16 us -> 0.01 us  [body(): lax.ppermute(back[k], ('rows', 'chan'), [(d, s) for s, d in spread(n, k)])]
    ppermute x4, starting transfers between devices: 13 us -> 7.89 us  [other_core(): return lax.ppermute(values, 'core', [(0, 1), (1, 0)])]
    all_to_all x1 -> x2, starting transfers between devices: 5.85 us -> 10.1 us  [the longest x1 5.99 us: body(): lax.all_to_all(cotangent_by_image(after(cot_rows, reduced), select), 'cha...]
    unnamed x70 -> x72, local copies, waits for them, and re-layouts: 8.51 us -> 12.6 us
  transfers between devices with their start and end apart: 25 -> 26, of which waited for: 11 -> 10; matrix products, arithmetic and copies ran while one was open for 6% -> 8% of each run, Pallas kernels for 34% -> 38%
where the time goes in v6:
time: 388 us; the launch traced here: 386 us
  Pallas kernels  158 us (41%)
  starting transfers between devices  78 us (20%)
  waiting for transfers between devices  48.1 us (12%)
  blocking collectives  43.2 us (11%)
  local copies, waits for them, and re-layouts  24.5 us (6%)
  matrix products  15.5 us (4%)
  between operations  14.2 us (4%)
  other arithmetic  4.63 us (1%)
    pallas_call x18, Pallas kernels, run(): pl.pallas_call(kernel, grid_spec=pltpu.PrefetchScalarGridSpec(num_scalar_...  158 us
    all_to_all x1, blocking collectives, body(): load = lax.all_to_all(load, chips, 0, 0, tiled=False).reshape(ch // 2, -1)  43.2 us
    all_to_all x1, waiting for transfers between devices, body(): pieces = after(lax.all_to_all(load, chips, 0, 0, tiled=False), feature_grad)  25.5 us
    ppermute x4, starting transfers between devices, body(): lax.ppermute(back[k], ('rows', 'chan'), [(d, s) for s, d in spread(n, k)])  19.2 us
    dot_general x3, matrix products, dot(): return lax.dot_general(a, b, (dims, ((), ())), preferred_element_type=F32)  15.5 us
    unnamed x72, local copies, waits for them, and re-layouts  12.6 us
    ppermute x4, starting transfers between devices, body(): lax.ppermute(pooled[k], ('rows', 'chan'), spread(n, k))  11.5 us
    all_to_all x1, starting transfers between devices, body(): pieces = after(lax.all_to_all(load, chips, 0, 0, tiled=False), feature_grad)  8.89 us
  transfers between devices with their start and end apart: 26, of which 10 were waited for; matrix products, arithmetic and copies ran while one was open for 8% of the time, Pallas kernels for 38%

profile of v6, /device:TPU:1, one launch (start us, length us, event | category | flops | bytes accessed | tf_op | source)
XLA Modules:
  0.0 385.7 jit_solution(9895896687355750398)
XLA Ops:
  7.2 0.8 subtract_convert_fusion
  8.1 1.1 fusion.10
  9.3 1.2 fusion.3
  11.2 5.8 %fusion.1.red = f32[8,144,1024]{2,1,0:T(8,128)} fusion(bf16[8,144,1024]{2,1,0:T(8,128)(2,1)S(1)} %bitcast.73, bf16[1024,1024]{1,0:T(8,128)(2,1)} %wr.5), kind=kOutput, calls=%fused_computation.3 | convolution fusion | flops 2415919104 | bytes 9175040 | tf_op jit(solution)/shard_map/dot_general | solution.py:23
  18.1 4.4 %cotangent_by_image.1 = bf16[4,288,1024]{2,1,0:T(8,128)(2,1)} custom-call(bf16[1152,1024]{1,0:T(8,128)(2,1)} %bitcast.75, bf16[128,128]{1,0:T(8,128)(2,1)} %copy.38.sel), custom_call_target="tpu_custom_call" | custom-call | flops 1 | bytes 1 | tf_op jit(solution)/shard_map/cotangent_by_image/pallas_call | solution.py:67
  22.5 6.0 %all-to-all-start = ((bf16[4,288,1024]{2,1,0:T(8,128)(2,1)}), bf16[4,288,1024]{2,1,0:T(8,128)(2,1)}, u32[]{:S(2)}, u32[]{:S(2)}) async-start(bf16[4,288,1024]{2,1,0:T(8,128)(2,1)} %cotangent_by_image.1), calls=%async_computation | async-start | bytes 4718592 | tf_op jit(solution)/shard_map/all_to_all | solution.py:870
  28.6 3.2 collective-permute-start
  31.8 1.3 collective-permute-start.1
  34.4 4.9 %collective-permute-done.up_ref = bf16[8,24,1024]{2,1,0:T(8,128)(2,1)S(1)} collective-permute-done((bf16[8,24,1024]{2,1,0:T(8,128)(2,1)S(1)}, bf16[8,24,1024]{2,1,0:T(8,128)(2,1)S(1)}, u32[]{:S(2)}, u32[]{:S(2)}) %collective-permute-start) | collective-permute-done | bytes 393248 | tf_op jit(solution)/shard_map/ppermute | solution.py:853
  39.2 3.9 %collective-permute-done.1.down_ref = bf16[8,24,1024]{2,1,0:T(8,128)(2,1)S(1)} collective-permute-done((bf16[8,24,1024]{2,1,0:T(8,128)(2,1)S(1)}, bf16[8,24,1024]{2,1,0:T(8,128)(2,1)S(1)}, u32[]{:S(2)}, u32[]{:S(2)}) %collective-permute-start.1) | collective-permute-done | bytes 393248 | tf_op jit(solution)/shard_map/ppermute | solution.py:854
  43.2 0.7 copy-done.8
  43.9 15.2 %pre_forward.2 = (f32[8,144,1024]{2,1,0:T(8,128)}, bf16[8,144,1024]{2,1,0:T(8,128)(2,1)}, f32[8,144,1024]{2,1,0:T(8,128)}, f32[8,144,1]{2,1,0:T(8,128)}, bf16[72...) custom-call(s32[2]{0:T(128)} %get-tuple-element.160.order_ref, f32[8,144,1024]{2,1,0:T(8,128)} %fusion.1.red, ...), custom_call_target="tpu_custom_call" | custom-call | flops 1 | bytes 1 | tf_op jit(solution)/shard_map/pre_forward/pallas_call | solution.py:67
  59.1 1.6 collective-permute-start.2
  60.7 2.9 collective-permute-start.3
  63.6 15.0 %pre_forward.3 = (f32[8,144,1024]{2,1,0:T(8,128)}, bf16[8,144,1024]{2,1,0:T(8,128)(2,1)}, f32[8,144,1024]{2,1,0:T(8,128)}, f32[8,144,1]{2,1,0:T(8,128)}, bf16[72...) custom-call(s32[2]{0:T(128)} %get-tuple-element.159.order_ref, ...), custom_call_target="tpu_custom_call", output_to_operand_aliasing={{0}: (10, {}), {1}: (11, {}), {2}: (12, {}), {3}: (13, {})} | custom-call | flops 1 | bytes 1 | tf_op jit(solution)/shard_map/pre_forward/pallas_call | solution.py:67
  78.6 4.6 %collective-permute-start.4 = (bf16[72,1024]{1,0:T(8,128)(2,1)}, bf16[72,1024]{1,0:T(8,128)(2,1)S(1)}, u32[]{:S(2)}, u32[]{:S(2)}) collective-permute-start(bf16[72,1024]{1,0:T(8,128)(2,1)} %get-tuple-element.85), channel_id=1, source_target_pairs={{0,2},{1,6},{2,10},{3,14},{4,3},{5,7},{6,11},{7,15},{8,0},{9,4},{1... | collective-permute-start | bytes 442376 | tf_op jit(solution)/shard_map/ppermute | solution.py:881
  83.2 2.5 collective-permute-start.5
  87.3 4.3 %collective-permute-done.5.refs_3_ = bf16[72,1024]{1,0:T(8,128)(2,1)S(1)} collective-permute-done((bf16[72,1024]{1,0:T(8,128)(2,1)}, bf16[72,1024]{1,0:T(8,128)(2,1)S(1)}, u32[]{:S(2)}, u32[]{:S(2)}) %collective-permute-start.5) | collective-permute-done | bytes 147488 | tf_op jit(solution)/shard_map/ppermute | solution.py:881
  92.3 11.1 %post_forward.1 = (bf16[288,1024]{1,0:T(8,128)(2,1)}, f32[288,1024]{1,0:T(8,128)}, bf16[288,1024]{1,0:T(8,128)(2,1)}, f32[288,1024]{1,0:T(8,128)}, bf16[288,1024...) custom-call(s32[4]{0:T(128)} %and_select_fusion.1.src, ...), custom_call_target="tpu_custom_call" | custom-call | flops 1 | bytes 1 | tf_op jit(solution)/shard_map/post_forward/pallas_call | solution.py:67
  103.4 1.9 collective-permute-start.6
  105.3 4.9 %collective-permute-start.7 = (bf16[288,1024]{1,0:T(8,128)(2,1)}, bf16[288,1024]{1,0:T(8,128)(2,1)S(1)}, u32[]{:S(2)}, u32[]{:S(2)}) collective-permute-start(bf16[288,1024]{1,0:T(8,128)(2,1)} %get-tuple-element.103.low_ref.refs_0_), channel_id=1, source_target_pairs={{0,3},{1,0},{2,1},{3,2},{4,7},{5,4},{6,5},{7,6},{8,11},{9,8},{10,9... | collective-permute-start | bytes 1769480 | tf_op jit(solution)/shard_map/ppermute | solution.py:885
  110.2 1.2 collective-permute-start.8
  111.4 10.8 %readout_backward.1.rg = f32[288,1024]{1,0:T(8,128)} custom-call(bf16[288,1024]{1,0:T(8,128)(2,1)} %get-tuple-element.103.low_ref.refs_0_, bf16[1024,4096]{1,0:T(8,128)(2,1)} %refs_5_.1, bf16[4,288,1024]{2,1,0:T(8,128)(2,1)} %all-to-all-done.cot), custom_call_target="tpu_custom_call" | custom-call | flops 1 | bytes 1 | tf_op jit(solution)/shard_map/readout_backward/pallas_call | solution.py:67
  123.2 12.3 %post_backward.1 = (bf16[288,1024]{1,0:T(8,128)(2,1)}, bf16[288,1024]{1,0:T(8,128)(2,1)}, f32[9,8,1024]{2,1,0:T(8,128)}, f32[8,1024]{1,0:T(8,128)}, bf16[72,1024...) custom-call(s32[4]{0:T(128)} %and_select_fusion.1.src, ...), custom_call_target="tpu_custom_call" | custom-call | flops 1 | bytes 1 | tf_op jit(solution)/shard_map/post_backward/pallas_call | solution.py:67
  135.4 1.6 collective-permute-start.9
  137.0 15.9 %collective-permute-start.10 = (bf16[72,1024]{1,0:T(8,128)(2,1)}, bf16[72,1024]{1,0:T(8,128)(2,1)S(1)}, u32[]{:S(2)}, u32[]{:S(2)}) collective-permute-start(bf16[72,1024]{1,0:T(8,128)(2,1)} %get-tuple-element.102), channel_id=1, source_target_pairs={{1,0},{5,1},{9,2},{13,3},{2,4},{6,5},{10,6},{14,7},{3,8},{7,9},{11... | collective-permute-start | bytes 442376 | tf_op jit(solution)/shard_map/ppermute | solution.py:892
  152.9 1.7 collective-permute-start.12
  154.6 0.8 broadcast_in_dim_tile.5.refs_7_
  155.4 6.0 %post_weight_grads.1.old = bf16[8,4,32,3072]{3,2,1,0:T(8,128)(2,1)} custom-call(bf16[288,1024]{1,0:T(8,128)(2,1)} %get-tuple-element.91.x, bf16[288,1024]{1,0:T(8,128)(2,1)} %get-tuple-element.98.g, bf16[288,1024]{1,0:T(8,128)(2,1)} %get-tuple-element.99.a, bf16[288,1024]{1,0:T(8,128)(2,1)} %get-tuple-element.100.e), custom_call_target="tpu_custom_call" | custom-call | flops 1 | bytes 1 | tf_op jit(solution)/shard_map/post_weight_grads/pallas_call | solution.py:67
  161.5 0.8 copy-done.14
  162.3 10.8 %token_block.1 = (bf16[1152,1024]{1,0:T(8,128)(2,1)}, bf16[1152,1024]{1,0:T(8,128)(2,1)}, bf16[1152,1024]{1,0:T(8,128)(2,1)}) custom-call(s32[1]{0:T(128)} %bitcast.chan_ref, s32[4]{0:T(128)} %and_select_fusion.1.src, bf16[288,1024]{1,0:T(8,128)(2,1)} %get-tuple-element.103.low_ref.refs_0_, bf16[288,1024]{1,0:T(8,128)(2,1)} %copy-done.12, ...), custom_call_target="tpu_custom_call" | custom-call | flops 1 | bytes 1 | tf_op jit(solution)/shard_map/token_block/pallas_call | solution.py:67
  173.1 6.7 %readout_weight_grad.1 = bf16[8,4,32,3072]{3,2,1,0:T(8,128)(2,1)} custom-call(bf16[1152,1024]{1,0:T(8,128)(2,1)} %get-tuple-element.110.x, bf16[1152,1024]{1,0:T(8,128)(2,1)} %get-tuple-element.112.g, bf16[8,4,32,3072]{3,2,1,0:T(8,128)(2,1)} %post_weight_grads.1.old), custom_call_target="tpu_custom_call", output_to_operand_aliasing={{}: (2, {})} | custom-call | flops 1 | bytes 1 | tf_op jit(solution)/shard_map/readout_weight_grad/pallas_call | solution.py:67
  179.9 21.6 %pre_backward.1 = (bf16[8,144,1024]{2,1,0:T(8,128)(2,1)}, bf16[8,144,1024]{2,1,0:T(8,128)(2,1)}, bf16[8,24,1024]{2,1,0:T(8,128)(2,1)}, bf16[8,24,1024]{2,1,0:T(8,128)(2,1)}, f32[8,1024]{1,0:T(8,128)}) custom-call(s32[4]{0:T(128)} %copy-done.32, bf16[72,1024]{1,0:T(8,128)(2,1)} %copy-done.24, bf16[72,1024]{1,0:T(8,128)(2,1)} %copy-done.25, ...), custom_call_target="tpu_custom_call" | custom-call | flops 1 | bytes 1 | tf_op jit(solution)/shard_map/pre_backward/pallas_call | solution.py:67
  201.5 6.2 %collective-permute-start.13 = (bf16[8,24,1024]{2,1,0:T(8,128)(2,1)}, bf16[8,24,1024]{2,1,0:T(8,128)(2,1)S(1)}, u32[]{:S(2)}, u32[]{:S(2)}) collective-permute-start(bf16[8,24,1024]{2,1,0:T(8,128)(2,1)} %get-tuple-element.122), channel_id=1, source_target_pairs={{0,4},{4,8},{8,12},{1,5},{5,9},{9,13},{2,6},{6,10},{10,14},{3,7},{... | collective-permute-start | bytes 1179656 | tf_op jit(solution)/shard_map/ppermute | solution.py:908
  207.7 1.5 collective-permute-start.14
  209.2 4.9 %bitcast_convert_fusion.refs_1_ = bf16[1024,1024]{1,0:T(8,128)(2,1)S(1)} fusion(bf16[8,144,1024]{2,1,0:T(8,128)(2,1)S(1)} %copy-done.6, bf16[8,144,1024]{2,1,0:T(8,128)(2,1)} %get-tuple-element.124), kind=kOutput, calls=%fused_computation | convolution fusion | flops 2416967680 | bytes 6815744 | tf_op jit(solution)/shard_map/dot_general | solution.py:23
  214.1 1.4 copy-done.4
  215.5 1.0 dynamic-slice_bitcast_fusion
  216.5 2.7 collective-permute-start.16
  219.3 0.7 copy-done.15
  220.0 0.7 copy-done.16
  220.8 12.1 %pre_conv_backward.1 = (bf16[8,144,1024]{2,1,0:T(8,128)(2,1)}, f32[9,8,1024]{2,1,0:T(8,128)}) custom-call(bf16[8,144,1024]{2,1,0:T(8,128)(2,1)} %get-tuple-element.125.cg, bf16[8,24,1024]{2,1,0:T(8,128)(2,1)} %copy-done.15, bf16[8,24,1024]{2,1,0:T(8,128)(2,1)} %copy-done.16, f32[8,144,1024]{2,1,0:T(8,128)} %fusion.1.red, f32[9,1024]{1,0:T(8,128)} %reshape.152.tap), custom_call_target="tpu_custom_call" | custom-call | flops 1 | bytes 1 | tf_op jit(solution)/shard_map/pre_conv_backward/pallas_call | solution.py:67
  232.9 2.0 small_rows.1.refs_4_
  234.9 2.1 copy_bitcast_fusion
  237.0 4.8 %convolution_convert_fusion.refs_0_ = bf16[1024,1024]{1,0:T(8,128)(2,1)S(1)} fusion(bf16[1152,1024]{1,0:T(8,128)(2,1)S(1)} %bitcast.74, bf16[1152,1024]{1,0:T(8,128)(2,1)} %bitcast.89), kind=kOutput, calls=%fused_computation.5 | convolution fusion | flops 2416967680 | bytes 6815744 | tf_op jit(solution)/shard_map/dot_general | solution.py:23
  241.8 1.3 copy-done.5
  243.2 1.4 collective-permute-start.15
  244.6 8.5 %feature_backward.1 = f32[8,144,1024]{2,1,0:T(8,128)} custom-call(s32[4]{0:T(128)} %copy-done.32, bf16[8,144,1024]{2,1,0:T(8,128)(2,1)} %get-tuple-element.134.rg, bf16[1024,1024]{1,0:T(8,128)(2,1)} %wr.5, bf16[288,72]{1,0:T(8,128)(2,1)} %constant.72.clone.refs_4_.up, bf16[72,1024]{1,0:T(8,128)(2,1)} %copy-done.24, bf16[72,1024]{1,0:T(8,128)(2,1)} %copy-done.25, ...), custom_call_target="tpu_custom_call" | custom-call | flops 8999999488 | bytes 1 | tf_op jit(solution)/shard_map/feature_backward/pallas_call | solution.py:67
  253.1 6.8 %reduce-scatter.5.cloned.1.call-done = bf16[1,4,8,3072]{3,2,1,0:T(8,128)(2,1)} async-done(((bf16[4,4,8,3072]{3,2,1,0:T(8,128)(2,1)}), bf16[1,4,8,3072]{3,2,1,0:T(8,128)(2,1)}) %reduce-scatter.5.cloned.1.call-update) | async-done | bytes 196624 | tf_op jit(solution)/shard_map/reduce_scatter | solution.py:917
  259.9 4.2 %all-to-all-start.3 = ((bf16[4,8,3072]{2,1,0:T(8,128)(2,1)}), bf16[4,8,3072]{2,1,0:T(8,128)(2,1)S(1)}, u32[]{:S(2)}, u32[]{:S(2)}) async-start(bf16[4,8,3072]{2,1,0:T(8,128)(2,1)} %bitcast.84), calls=%async_computation.5 | async-start | bytes 393216 | tf_op jit(solution)/shard_map/all_to_all | solution.py:928
  264.1 2.0 collective-permute-start.17
  266.0 0.9 collective-permute-done.17.refs_5_
  268.3 4.0 %join_halves.1 = bf16[512,2176]{1,0:T(8,128)(2,1)} custom-call(s32[1]{0:T(128)} %bitcast.20.core_ref.place_ref, bf16[1024,1024]{1,0:T(8,128)(2,1)} %copy-done.5, bf16[1024,1024]{1,0:T(8,128)(2,1)} %copy-done.4, bf16[512,1024]{1,0:T(8,128)(2,1)} %copy-done.10, bf16[512,1024]{1,0:T(8,128)(2,1)} %copy-done.9, f32[160,128]{1,0:T(8,128)} %small_rows.1.refs_4_, ...), custom_call_target="tpu_custom_call" | custom-call | flops 1 | bytes 1 | tf_op jit(solution)/shard_map/join_halves/pallas_call | solution.py:67
  273.0 8.9 %all-to-all-start.1 = ((bf16[64,8,2176]{2,1,0:T(8,128)(2,1)}), bf16[64,8,2176]{2,1,0:T(8,128)(2,1)S(1)}, u32[]{:S(2)}, u32[]{:S(2)}) async-start(bf16[64,8,2176]{2,1,0:T(8,128)(2,1)} %bitcast.77), calls=%async_computation.2 | async-start | bytes 4456448 | tf_op jit(solution)/shard_map/all_to_all | solution.py:926
  282.0 0.9 slice_reduce_fusion
  286.5 25.5 %all-to-all-done.1.x = bf16[64,8,2176]{2,1,0:T(8,128)(2,1)S(1)} async-done(((bf16[64,8,2176]{2,1,0:T(8,128)(2,1)}), bf16[64,8,2176]{2,1,0:T(8,128)(2,1)S(1)}, u32[]{:S(2)}, u32[]{:S(2)}) %all-to-all-start.1) | async-done | bytes 2228256 | tf_op jit(solution)/shard_map/all_to_all | solution.py:926
  311.9 1.4 copy-done.2
  313.3 4.4 %sum_and_copy.1 = bf16[64,8,2176]{2,1,0:T(8,128)(2,1)} custom-call(bf16[64,8,2176]{2,1,0:T(8,128)(2,1)} %copy-done.2), custom_call_target="tpu_custom_call" | custom-call | flops 1 | bytes 1 | tf_op jit(solution)/shard_map/sum_and_copy/pallas_call | solution.py:67
  317.7 43.2 %all_to_all.20 = bf16[64,8,2176]{2,1,0:T(8,128)(2,1)S(1)} all-to-all(bf16[64,8,2176]{2,1,0:T(8,128)(2,1)} %sum_and_copy.1), channel_id=1, replica_groups=mesh['x'=4,'core'=2,'rows'=4,'chan'=4] {'x','rows','chan'}, dimensions={0} | all-to-all | bytes 4456448 | tf_op jit(solution)/shard_map/all_to_all | solution.py:935
  361.0 1.8 collective-permute-start.18
  362.8 3.8 finish_pre.2
  366.9 3.9 %finish_pre.3 = (f32[1024,1024]{1,0:T(8,128)}, f32[1024,1024]{1,0:T(8,128)}, f32[512,128]{1,0:T(8,128)}) custom-call(s32[1]{0:T(128)S(6)} %sub.19.place_ref, bf16[512,2176]{1,0:T(8,128)(2,1)} %collective-permute-done.18.x, f32[1024,1024]{1,0:T(8,128)} %get-tuple-element.138.outs_0_, ...), custom_call_target="tpu_custom_call", output_to_operand_aliasing={{0}: (2, {}), {1}: (3, {})} | custom-call | flops 1 | bytes 1 | tf_op jit(solution)/shard_map/finish_pre/pallas_call | solution.py:67
  370.7 1.0 broadcast_select_fusion
  374.2 5.0 %finish_post.1 = (f32[256,1024]{1,0:T(8,128)}, f32[4,256,256]{2,1,0:T(8,128)}, f32[256,4096]{1,0:T(8,128)}) custom-call(bf16[256,6144]{1,0:T(8,128)(2,1)} %all-gather.4.cloned.1.call-done.x), custom_call_target="tpu_custom_call" | custom-call | flops 6000000000 | bytes 1 | tf_op jit(solution)/shard_map/finish_post/pallas_call | solution.py:67
  (119 shorter events, 15.0 us)
Async XLA Ops:
  7.2 4.0 %copy-start = (bf16[8,6,24,1024]{3,2,1,0:T(8,128)(2,1)S(1)}, bf16[8,6,24,1024]{3,2,1,0:T(8,128)(2,1)}, u32[]{:S(2)}) copy-start(bf16[8,6,24,1024]{3,2,1,0:T(8,128)(2,1)} %feat.3) | copy-start | bytes 7077892
  7.2 84.4 %all-gather.6.cloned.1.call-start = ((), (), s32[]{:S(2)}) async-start(), calls=%async_computation.9 | async-start | bytes 4866048 | tf_op jit(solution)/shard_map/all_gather | solution.py:863
  11.2 5.8 %copy-start.33 = (s32[2]{0:T(128)S(1)}, s32[2]{0:T(128)}, u32[]{:S(2)}) copy-start(s32[2]{0:T(128)} %param.16) | copy-start | bytes 28
  11.2 6.1 %copy-start.28 = (bf16[128,128]{1,0:T(8,128)(2,1)S(1)}, bf16[128,128]{1,0:T(8,128)(2,1)}, u32[]{:S(2)}) copy-start(bf16[128,128]{1,0:T(8,128)(2,1)} %constant.73.clone.refs_4_) | copy-start | bytes 98308
  22.5 10.6 %copy-start.30 = (bf16[3,3,1024]{2,1,0:T(4,128)(2,1)S(1)}, bf16[3,3,1024]{2,1,0:T(4,128)(2,1)}, u32[]{:S(2)}) copy-start(bf16[3,3,1024]{2,1,0:T(4,128)(2,1)} %param.18) | copy-start | bytes 55300
  22.5 88.9 %all-to-all-start = ((bf16[4,288,1024]{2,1,0:T(8,128)(2,1)}), bf16[4,288,1024]{2,1,0:T(8,128)(2,1)}, u32[]{:S(2)}, u32[]{:S(2)}) async-start(bf16[4,288,1024]{2,1,0:T(8,128)(2,1)} %cotangent_by_image.1), calls=%async_computation | async-start | bytes 4718592 | tf_op jit(solution)/shard_map/all_to_all | solution.py:870
  28.5 206.4 %reduce-scatter.3.cloned.1.call-start = ((), (), s32[]{:S(2)}) async-start(), calls=%async_computation.6 | async-start | bytes 7077888 | tf_op jit(solution)/shard_map/reduce_scatter | solution.py:903
  28.6 10.6 %collective-permute-start = (bf16[8,24,1024]{2,1,0:T(8,128)(2,1)S(1)}, bf16[8,24,1024]{2,1,0:T(8,128)(2,1)S(1)}, u32[]{:S(2)}, u32[]{:S(2)}) collective-permute-start(bf16[8,24,1024]{2,1,0:T(8,128)(2,1)S(1)} %get-tuple-element.150), channel_id=1, source_target_pairs={{0,4},{4,8},{8,12},{1,5},{5,9},{9,13},{2,6},{6,10},{10,14},{3,7},{... | collective-permute-start | bytes 1179656 | tf_op jit(solution)/shard_map/ppermute | solution.py:853
  31.8 11.4 %collective-permute-start.1 = (bf16[8,24,1024]{2,1,0:T(8,128)(2,1)S(1)}, bf16[8,24,1024]{2,1,0:T(8,128)(2,1)S(1)}, u32[]{:S(2)}, u32[]{:S(2)}) collective-permute-start(bf16[8,24,1024]{2,1,0:T(8,128)(2,1)S(1)} %get-tuple-element.149), channel_id=1, source_target_pairs={{4,0},{8,4},{12,8},{5,1},{9,5},{13,9},{6,2},{10,6},{14,10},{7,3},{... | collective-permute-start | bytes 1179656 | tf_op jit(solution)/shard_map/ppermute | solution.py:854
  33.8 25.3 %copy-start.32 = (s32[4]{0:T(128)}, s32[4]{0:T(128)S(1)}, u32[]{:S(2)}) copy-start(s32[4]{0:T(128)S(1)} %and_select_fusion.order_ref) | copy-start | bytes 52
  39.2 4.0 %copy-start.7 = (bf16[8,24,1024]{2,1,0:T(8,128)(2,1)}, bf16[8,24,1024]{2,1,0:T(8,128)(2,1)S(1)}, u32[]{:S(2)}) copy-start(bf16[8,24,1024]{2,1,0:T(8,128)(2,1)S(1)} %collective-permute-done.up_ref) | copy-start | bytes 1179652
  43.2 0.7 copy-start.8
  59.1 27.7 %collective-permute-start.2 = (bf16[72,1024]{1,0:T(8,128)(2,1)}, bf16[72,1024]{1,0:T(8,128)(2,1)S(1)}, u32[]{:S(2)}, u32[]{:S(2)}) collective-permute-start(bf16[72,1024]{1,0:T(8,128)(2,1)} %get-tuple-element.79), channel_id=1, source_target_pairs={{0,0},{1,4},{2,8},{3,12},{4,1},{5,5},{6,9},{7,13},{8,2},{9,6},{10,... | collective-permute-start | bytes 442376 | tf_op jit(solution)/shard_map/ppermute | solution.py:881
  60.7 26.1 %collective-permute-start.3 = (bf16[72,1024]{1,0:T(8,128)(2,1)}, bf16[72,1024]{1,0:T(8,128)(2,1)S(1)}, u32[]{:S(2)}, u32[]{:S(2)}) collective-permute-start(bf16[72,1024]{1,0:T(8,128)(2,1)} %get-tuple-element.80), channel_id=1, source_target_pairs={{0,1},{1,5},{2,9},{3,13},{4,2},{5,6},{6,10},{7,14},{8,3},{9,7},{10... | collective-permute-start | bytes 442376 | tf_op jit(solution)/shard_map/ppermute | solution.py:881
  63.6 22.0 %copy-start.31 = (bf16[3,3,1024]{2,1,0:T(4,128)(2,1)S(1)}, bf16[3,3,1024]{2,1,0:T(4,128)(2,1)}, u32[]{:S(2)}) copy-start(bf16[3,3,1024]{2,1,0:T(4,128)(2,1)} %param.22) | copy-start | bytes 55300
  78.6 8.7 %collective-permute-start.4 = (bf16[72,1024]{1,0:T(8,128)(2,1)}, bf16[72,1024]{1,0:T(8,128)(2,1)S(1)}, u32[]{:S(2)}, u32[]{:S(2)}) collective-permute-start(bf16[72,1024]{1,0:T(8,128)(2,1)} %get-tuple-element.85), channel_id=1, source_target_pairs={{0,2},{1,6},{2,10},{3,14},{4,3},{5,7},{6,11},{7,15},{8,0},{9,4},{1... | collective-permute-start | bytes 442376 | tf_op jit(solution)/shard_map/ppermute | solution.py:881
  83.2 8.4 %collective-permute-start.5 = (bf16[72,1024]{1,0:T(8,128)(2,1)}, bf16[72,1024]{1,0:T(8,128)(2,1)S(1)}, u32[]{:S(2)}, u32[]{:S(2)}) collective-permute-start(bf16[72,1024]{1,0:T(8,128)(2,1)} %get-tuple-element.86), channel_id=1, source_target_pairs={{0,3},{1,7},{2,11},{3,15},{4,0},{5,4},{6,8},{7,12},{8,1},{9,5},{10... | collective-permute-start | bytes 442376 | tf_op jit(solution)/shard_map/ppermute | solution.py:881
  86.8 4.8 %copy-start.20 = (bf16[72,1024]{1,0:T(8,128)(2,1)}, bf16[72,1024]{1,0:T(8,128)(2,1)S(1)}, u32[]{:S(2)}) copy-start(bf16[72,1024]{1,0:T(8,128)(2,1)S(1)} %collective-permute-done.2.refs_0_) | copy-start | bytes 442372
  86.8 4.8 %copy-start.21 = (bf16[72,1024]{1,0:T(8,128)(2,1)}, bf16[72,1024]{1,0:T(8,128)(2,1)S(1)}, u32[]{:S(2)}) copy-start(bf16[72,1024]{1,0:T(8,128)(2,1)S(1)} %collective-permute-done.3.refs_1_) | copy-start | bytes 442372
  87.3 4.3 %copy-start.22 = (bf16[72,1024]{1,0:T(8,128)(2,1)}, bf16[72,1024]{1,0:T(8,128)(2,1)S(1)}, u32[]{:S(2)}) copy-start(bf16[72,1024]{1,0:T(8,128)(2,1)S(1)} %collective-permute-done.4.refs_2_) | copy-start | bytes 442372
  91.6 0.7 copy-start.23
  103.4 19.5 %collective-permute-start.6 = (bf16[288,1024]{1,0:T(8,128)(2,1)}, bf16[288,1024]{1,0:T(8,128)(2,1)S(1)}, u32[]{:S(2)}, u32[]{:S(2)}) collective-permute-start(bf16[288,1024]{1,0:T(8,128)(2,1)} %get-tuple-element.103.low_ref.refs_0_), channel_id=1, source_target_pairs={{0,1},{1,2},{2,3},{3,0},{4,5},{5,6},{6,7},{7,4},{8,9},{9,10},{10,1... | collective-permute-start | bytes 1769480 | tf_op jit(solution)/shard_map/ppermute | solution.py:885
  105.3 17.8 %collective-permute-start.7 = (bf16[288,1024]{1,0:T(8,128)(2,1)}, bf16[288,1024]{1,0:T(8,128)(2,1)S(1)}, u32[]{:S(2)}, u32[]{:S(2)}) collective-permute-start(bf16[288,1024]{1,0:T(8,128)(2,1)} %get-tuple-element.103.low_ref.refs_0_), channel_id=1, source_target_pairs={{0,3},{1,0},{2,1},{3,2},{4,7},{5,4},{6,5},{7,6},{8,11},{9,8},{10,9... | collective-permute-start | bytes 1769480 | tf_op jit(solution)/shard_map/ppermute | solution.py:885
  110.2 51.3 %collective-permute-start.8 = (bf16[288,1024]{1,0:T(8,128)(2,1)}, bf16[288,1024]{1,0:T(8,128)(2,1)S(1)}, u32[]{:S(2)}, u32[]{:S(2)}) collective-permute-start(bf16[288,1024]{1,0:T(8,128)(2,1)} %get-tuple-element.103.low_ref.refs_0_), channel_id=1, source_target_pairs={{0,2},{1,3},{2,0},{3,1},{4,6},{5,7},{6,4},{7,5},{8,10},{9,11},{10,... | collective-permute-start | bytes 1769480 | tf_op jit(solution)/shard_map/ppermute | solution.py:885
  122.9 12.6 %copy-start.12 = (bf16[288,1024]{1,0:T(8,128)(2,1)}, bf16[288,1024]{1,0:T(8,128)(2,1)S(1)}, u32[]{:S(2)}) copy-start(bf16[288,1024]{1,0:T(8,128)(2,1)S(1)} %collective-permute-done.6.refs_1_) | copy-start | bytes 1769476
  123.2 12.3 %copy-start.13 = (bf16[288,1024]{1,0:T(8,128)(2,1)}, bf16[288,1024]{1,0:T(8,128)(2,1)S(1)}, u32[]{:S(2)}) copy-start(bf16[288,1024]{1,0:T(8,128)(2,1)S(1)} %collective-permute-done.7.refs_3_) | copy-start | bytes 1769476
  135.4 26.0 %collective-permute-start.9 = (bf16[72,1024]{1,0:T(8,128)(2,1)}, bf16[72,1024]{1,0:T(8,128)(2,1)S(1)}, u32[]{:S(2)}, u32[]{:S(2)}) collective-permute-start(bf16[72,1024]{1,0:T(8,128)(2,1)} %get-tuple-element.101), channel_id=1, source_target_pairs={{0,0},{4,1},{8,2},{12,3},{1,4},{5,5},{9,6},{13,7},{2,8},{6,9},{10,... | collective-permute-start | bytes 442376 | tf_op jit(solution)/shard_map/ppermute | solution.py:892
  137.0 24.5 %collective-permute-start.10 = (bf16[72,1024]{1,0:T(8,128)(2,1)}, bf16[72,1024]{1,0:T(8,128)(2,1)S(1)}, u32[]{:S(2)}, u32[]{:S(2)}) collective-permute-start(bf16[72,1024]{1,0:T(8,128)(2,1)} %get-tuple-element.102), channel_id=1, source_target_pairs={{1,0},{5,1},{9,2},{13,3},{2,4},{6,5},{10,6},{14,7},{3,8},{7,9},{11... | collective-permute-start | bytes 442376 | tf_op jit(solution)/shard_map/ppermute | solution.py:892
  152.9 20.2 %collective-permute-start.11 = (bf16[72,1024]{1,0:T(8,128)(2,1)}, bf16[72,1024]{1,0:T(8,128)(2,1)S(1)}, u32[]{:S(2)}, u32[]{:S(2)}) collective-permute-start(bf16[72,1024]{1,0:T(8,128)(2,1)} %get-tuple-element.108), channel_id=1, source_target_pairs={{2,0},{6,1},{10,2},{14,3},{3,4},{7,5},{11,6},{15,7},{0,8},{4,9},{8... | collective-permute-start | bytes 442376 | tf_op jit(solution)/shard_map/ppermute | solution.py:892
  152.9 20.2 %collective-permute-start.12 = (bf16[72,1024]{1,0:T(8,128)(2,1)}, bf16[72,1024]{1,0:T(8,128)(2,1)S(1)}, u32[]{:S(2)}, u32[]{:S(2)}) collective-permute-start(bf16[72,1024]{1,0:T(8,128)(2,1)} %get-tuple-element.109), channel_id=1, source_target_pairs={{3,0},{7,1},{11,2},{15,3},{0,4},{4,5},{8,6},{12,7},{1,8},{5,9},{9,... | collective-permute-start | bytes 442376 | tf_op jit(solution)/shard_map/ppermute | solution.py:892
  161.4 0.8 copy-start.14
  161.5 11.6 %copy-start.24 = (bf16[72,1024]{1,0:T(8,128)(2,1)}, bf16[72,1024]{1,0:T(8,128)(2,1)S(1)}, u32[]{:S(2)}) copy-start(bf16[72,1024]{1,0:T(8,128)(2,1)S(1)} %collective-permute-done.9.refs_0_) | copy-start | bytes 442372
  161.5 11.6 %copy-start.25 = (bf16[72,1024]{1,0:T(8,128)(2,1)}, bf16[72,1024]{1,0:T(8,128)(2,1)S(1)}, u32[]{:S(2)}) copy-start(bf16[72,1024]{1,0:T(8,128)(2,1)S(1)} %collective-permute-done.10.refs_1_) | copy-start | bytes 442372
  173.1 6.8 %copy-start.26 = (bf16[72,1024]{1,0:T(8,128)(2,1)}, bf16[72,1024]{1,0:T(8,128)(2,1)S(1)}, u32[]{:S(2)}) copy-start(bf16[72,1024]{1,0:T(8,128)(2,1)S(1)} %collective-permute-done.11.refs_2_) | copy-start | bytes 442372
  173.1 6.7 %copy-start.27 = (bf16[72,1024]{1,0:T(8,128)(2,1)}, bf16[72,1024]{1,0:T(8,128)(2,1)S(1)}, u32[]{:S(2)}) copy-start(bf16[72,1024]{1,0:T(8,128)(2,1)S(1)} %collective-permute-done.12.refs_3_) | copy-start | bytes 442372
  179.8 80.1 %reduce-scatter.5.cloned.1.call-start = ((), (), s32[]{:S(2)}) async-start(), calls=%async_computation.7 | async-start | bytes 983040 | tf_op jit(solution)/shard_map/reduce_scatter | solution.py:917
  179.9 29.3 %copy-start.6 = (bf16[8,144,1024]{2,1,0:T(8,128)(2,1)S(1)}, bf16[8,144,1024]{2,1,0:T(8,128)(2,1)}, u32[]{:S(2)}) copy-start(bf16[8,144,1024]{2,1,0:T(8,128)(2,1)} %get-tuple-element.123) | copy-start | bytes 7077892
  201.5 17.7 %collective-permute-start.13 = (bf16[8,24,1024]{2,1,0:T(8,128)(2,1)}, bf16[8,24,1024]{2,1,0:T(8,128)(2,1)S(1)}, u32[]{:S(2)}, u32[]{:S(2)}) collective-permute-start(bf16[8,24,1024]{2,1,0:T(8,128)(2,1)} %get-tuple-element.122), channel_id=1, source_target_pairs={{0,4},{4,8},{8,12},{1,5},{5,9},{9,13},{2,6},{6,10},{10,14},{3,7},{... | collective-permute-start | bytes 1179656 | tf_op jit(solution)/shard_map/ppermute | solution.py:908
  207.7 11.6 %collective-permute-start.14 = (bf16[8,24,1024]{2,1,0:T(8,128)(2,1)}, bf16[8,24,1024]{2,1,0:T(8,128)(2,1)S(1)}, u32[]{:S(2)}, u32[]{:S(2)}) collective-permute-start(bf16[8,24,1024]{2,1,0:T(8,128)(2,1)} %get-tuple-element.126), channel_id=1, source_target_pairs={{4,0},{8,4},{12,8},{5,1},{9,5},{13,9},{6,2},{10,6},{14,10},{7,3},{... | collective-permute-start | bytes 1179656 | tf_op jit(solution)/shard_map/ppermute | solution.py:909
  214.1 1.4 copy-start.4
  216.5 50.4 %collective-permute-start.16 = (bf16[512,1024]{1,0:T(8,128)(2,1)}, bf16[512,1024]{1,0:T(8,128)(2,1)S(1)}, u32[]{:S(2)}, u32[]{:S(2)}) collective-permute-start(bf16[512,1024]{1,0:T(8,128)(2,1)} %dynamic-slice_bitcast_fusion), channel_id=1, source_target_pairs={{0,16},{16,0},{1,17},{17,1},{2,18},{18,2},{3,19},{19,3},{4,20},{20... | collective-permute-start | bytes 3145736 | tf_op jit(solution)/shard_map/ppermute | solution.py:671
  219.3 0.7 copy-start.15
  220.0 0.7 copy-start.16
  232.9 4.1 %copy-start.1 = (bf16[8,6,24,1024]{3,2,1,0:T(8,128)(2,1)S(1)}, bf16[8,6,24,1024]{3,2,1,0:T(8,128)(2,1)}, u32[]{:S(2)}) copy-start(bf16[8,6,24,1024]{3,2,1,0:T(8,128)(2,1)} %feat.3) | copy-start | bytes 7077892
  241.8 1.3 copy-start.5
  243.2 20.8 %copy-start.17 = (f32[160,128]{1,0:T(8,128)S(1)}, f32[160,128]{1,0:T(8,128)}, u32[]{:S(2)}) copy-start(f32[160,128]{1,0:T(8,128)} %small_rows.1.refs_4_) | copy-start | bytes 245764
  243.2 23.8 %collective-permute-start.15 = (bf16[512,1024]{1,0:T(8,128)(2,1)S(1)}, bf16[512,1024]{1,0:T(8,128)(2,1)S(1)}, u32[]{:S(2)}, u32[]{:S(2)}) collective-permute-start(bf16[512,1024]{1,0:T(8,128)(2,1)S(1)} %dynamic-slice_bitcast_fusion.1), channel_id=1, source_target_pairs={{0,16},{16,0},{1,17},{17,1},{2,18},{18,2},{3,19},{19,3},{4,20},{20... | collective-permute-start | bytes 3145736 | tf_op jit(solution)/shard_map/ppermute | solution.py:671
  259.9 12.4 %all-to-all-start.3 = ((bf16[4,8,3072]{2,1,0:T(8,128)(2,1)}), bf16[4,8,3072]{2,1,0:T(8,128)(2,1)S(1)}, u32[]{:S(2)}, u32[]{:S(2)}) async-start(bf16[4,8,3072]{2,1,0:T(8,128)(2,1)} %bitcast.84), calls=%async_computation.5 | async-start | bytes 393216 | tf_op jit(solution)/shard_map/all_to_all | solution.py:928
  264.1 2.9 collective-permute-start.17
  267.0 0.6 copy-start.29
  267.0 1.0 copy-start.9
  267.0 1.3 copy-start.10
  272.3 0.7 copy-start.11
  273.0 38.9 %all-to-all-start.1 = ((bf16[64,8,2176]{2,1,0:T(8,128)(2,1)}), bf16[64,8,2176]{2,1,0:T(8,128)(2,1)S(1)}, u32[]{:S(2)}, u32[]{:S(2)}) async-start(bf16[64,8,2176]{2,1,0:T(8,128)(2,1)} %bitcast.77), calls=%async_computation.2 | async-start | bytes 4456448 | tf_op jit(solution)/shard_map/all_to_all | solution.py:926
  281.9 92.3 %all-gather.4.cloned.1.call-start = ((), (), s32[]{:S(2)}) async-start(), calls=%async_computation.8 | async-start | bytes 3244032 | tf_op jit(solution)/shard_map/all_gather | solution.py:931
  285.8 0.6 copy-start.19
  311.9 1.4 copy-start.2
  361.0 1.8 copy-start.3
  361.0 5.9 %collective-permute-start.18 = (bf16[512,2176]{1,0:T(8,128)(2,1)S(1)}, bf16[512,2176]{1,0:T(8,128)(2,1)}, u32[]{:S(2)}, u32[]{:S(2)}) collective-permute-start(bf16[512,2176]{1,0:T(8,128)(2,1)S(1)} %bitcast.78), channel_id=1, source_target_pairs={{0,16},{16,0},{1,17},{17,1},{2,18},{18,2},{3,19},{19,3},{4,20},{20... | collective-permute-start | bytes 6684680 | tf_op jit(solution)/shard_map/ppermute | solution.py:671
  366.9 3.9 %copy-start.18 = (f32[512,128]{1,0:T(8,128)S(1)}, f32[512,128]{1,0:T(8,128)}, u32[]{:S(2)}) copy-start(f32[512,128]{1,0:T(8,128)} %get-tuple-element.136) | copy-start | bytes 786436
Sparse Core Ops, SparseCore 0:
  11.3 59.0 all-gather.5
  180.0 47.4 reduce-scatter.2
  237.1 22.7 reduce-scatter.4
  286.6 71.2 all-gather.3

commit v7 on v6

--- a/solution.py
+++ b/solution.py
@@ -271,35 +271,31 @@
     )(source)
 
 
-def readout_backward(low, readout, cots):
+def readout_backward(source, low, readout, cots):
     total, ch = low.shape
-    n, _, out_share = cots.shape
-
-    def kernel(low_ref, ro, cot, grad):
+    n, out_share = len(cots), cots[0].shape[1]
+
+    def kernel(src, low_ref, ro, *rest):
+        cot, grad = rest[:n], rest[n]
         k = pl.program_id(0)
         logits = dot(low_ref[...], ro[...])
-        piece = (cot[0].astype(F32) * gelu_parts(logits)[1]).astype(BF)
-        term = dot(piece, ro[...], NT)
-
-        @pl.when(k == 0)
-        def _():
-            grad[...] = term
-
-        @pl.when(k > 0)
-        def _():
-            grad[...] += term
+        slope = gelu_parts(logits)[1]
+        for i in range(n):
+
+            @pl.when(k == i)
+            def _():
+                piece = (cot[i][...].astype(F32) * slope).astype(BF)
+                term = dot(piece, ro[...], NT)
+                grad[...] = term if i == 0 else grad[...] + term
 
     return call(
         kernel,
         grid=(n,),
-        ins=[
-            (low, None, None),
-            (readout, (ch, out_share), lambda k: (0, k)),
-            (cots, (1, total, out_share), lambda k: (k, 0, 0)),
-        ],
+        prefetch=1,
+        ins=[(low, None, None), (readout, (ch, out_share), lambda k, s: (0, s[k]))] + [(c, None, None) for c in cots],
         outs=[(shape((total, ch), F32), None, None)],
         name="readout_backward",
-    )()[0]
+    )(source)[0]
 
 
 def post_backward(source, refined_grad, weights, taps, act, red, conv, nrm, std, pool):
@@ -380,26 +376,25 @@
     )(source)
 
 
-def cotangent_by_image(cotangent, select):
+def cotangent_by_image(cotangent, select, pairs):
     rows, width = cotangent.shape
     size = select.shape[0]
-    pairs = SLOT
     each = size // pairs
     per = 3
 
-    def kernel(x, sel, out):
+    def kernel(x, sel, *outs):
         for q in range(per):
             y = dot(sel[...], x[pl.ds(q * size, size), :]).astype(BF)
             for s in range(pairs):
-                out[s, pl.ds(q * each, each), :] = y[s * each : (s + 1) * each]
+                outs[s][pl.ds(q * each, each), :] = y[s * each : (s + 1) * each]
 
     return call(
         kernel,
         grid=(rows // (per * size),),
         ins=[(cotangent, (per * size, width), lambda i: (i, 0)), (select, None, None)],
-        outs=[(shape((pairs, rows // pairs, width), BF), (pairs, per * each, width), lambda i: (0, i, 0))],
+        outs=[(shape((rows // pairs, width), BF), (per * each, width), lambda i: (i, 0))] * pairs,
         name="cotangent_by_image",
-    )()[0]
+    )()
 
 
 def token_block(chan, source, low, place, readout, cotangent, live):
@@ -579,6 +574,7 @@
             (shape((slots, cells, ch), BF), (1, cells, ch), image),
             (shape((9, 8, ch), F32), None, None),
         ],
+        cost=12 * 10**9,
         name="pre_conv_backward",
     )()
 
@@ -667,6 +663,14 @@
     return [(a * n + b, b * n + (a + k) % n) for a in range(n) for b in range(n)]
 
 
+def cross(n, k):
+    return [(a * n + b, ((b + k) % n) * n + a) for a in range(n) for b in range(n)]
+
+
+def turn(n, k):
+    return [(i, (i + k) % n) for i in range(n)]
+
+
 def other_core(values):
     return lax.ppermute(values, "core", [(0, 1), (1, 0)])
 
@@ -695,29 +699,25 @@
     )()[0]
 
 
-def join_halves(core, mine, theirs, small, their_small, parts):
-    rows, ch = mine[0].shape
+def join_halves(core, mine, theirs, parts, small=()):
+    rows, ch = mine.shape
     half = rows // 2
-    width = len(mine) * ch + LANES
-    count = small.shape[0]
-    m = len(mine)
-
-    def kernel(core_ref, *refs):
-        own, got = refs[:m], refs[m : 2 * m]
-        sm, got_sm, out = refs[2 * m :]
-        for i in range(m):
-            out[:, i * ch : (i + 1) * ch] = (own[i][...].astype(F32) + got[i][...].astype(F32)).astype(BF)
-        first = (core_ref[0] == 0).astype(F32)
-        total = (sm[...] + got_sm[...]) * first
-        pad = jnp.zeros((half - count, LANES), F32)
-        out[:, m * ch :] = jnp.concatenate([total, pad], 0).astype(BF)
+    width = ch + (LANES if small else 0)
+
+    def kernel(core_ref, own, got, *refs):
+        out = refs[-1]
+        out[:, :ch] = (own[...].astype(F32) + got[...].astype(F32)).astype(BF)
+        if small:
+            first = (core_ref[0] == 0).astype(F32)
+            total = (refs[0][...] + refs[1][...]) * first
+            pad = jnp.zeros((half - total.shape[0], LANES), F32)
+            out[:, ch:] = jnp.concatenate([total, pad], 0).astype(BF)
 
     return call(
         kernel,
         grid=(1,),
         prefetch=1,
-        ins=[(v, (half, ch), lambda i, c: (c[0], 0)) for v in mine]
-        + [(v, None, None) for v in (*theirs, small, their_small)],
+        ins=[(mine, (half, ch), lambda i, c: (c[0], 0)), (theirs, None, None)] + [(v, None, None) for v in small],
         outs=[(shape((half, width), BF), None, None)],
         name="join_halves",
     )(core)[0].reshape(parts, half // parts, width)
@@ -744,49 +744,53 @@
 
 def finish_pre(place, half_rows, ch, earlier=()):
     half, width = half_rows.shape
-    m = (width - LANES) // ch
+    more = width > ch
 
     def kernel(place_ref, x, *outs):
         outs = outs[len(earlier) :]
-        for i in range(m):
-            outs[i][...] = x[:, i * ch : (i + 1) * ch].astype(F32)
-        outs[m][...] = x[:, m * ch :].astype(F32)
+        outs[0][...] = x[:, :ch].astype(F32)
+        if more:
+            outs[1][...] = x[:, ch:].astype(F32)
 
     return call(
         kernel,
         grid=(1,),
         prefetch=1,
         ins=[(half_rows, None, None)],
-        outs=[(shape((2 * half, ch), F32), (half, ch), lambda i, c: (c[0], 0)) for _ in range(m)]
-        + [(shape((half, LANES), F32), None, None)],
+        outs=[(shape((2 * half, ch), F32), (half, ch), lambda i, c: (c[0], 0))]
+        + ([(shape((half, width - ch), F32), None, None)] if more else []),
         aliased=earlier,
         name="finish_pre",
     )(place)
 
 
-def finish_post(gathered, n):
-    share, width = gathered.shape
+def finish_post(place, gathered, n, earlier=()):
+    groups, per, width = gathered.shape
+    share = 2 * groups * per
     ch = width // (n + 2)
-    per = 64
-
-    def kernel(x, reduce_out, expand_out, read_out):
-        reduce_out[...] = x[:, :ch].astype(F32)
+
+    def kernel(place_ref, x, *outs):
+        reduce_out, expand_out, read_out = outs[len(earlier) :]
+        reduce_out[...] = x[0, :, :ch].astype(F32)
         for q in range(n):
-            expand_out[q] = x[:, ch + q * share : ch + (q + 1) * share].astype(F32)
-        read_out[...] = x[:, 2 * ch :].astype(F32)
-
-    return call(
-        kernel,
-        grid=(share // per,),
-        ins=[(gathered, (per, width), lambda i: (i, 0))],
+            expand_out[q] = x[0, :, ch + q * share : ch + (q + 1) * share].astype(F32)
+        read_out[...] = x[0, :, 2 * ch :].astype(F32)
+
+    at = lambda i, c: (2 * i + c[0], 0)
+    return call(
+        kernel,
+        grid=(groups,),
+        prefetch=1,
+        ins=[(gathered, (1, per, width), lambda i, c: (i, 0, 0))],
         outs=[
-            (shape((share, ch), F32), (per, ch), lambda i: (i, 0)),
-            (shape((n, share, share), F32), (n, per, share), lambda i: (0, i, 0)),
-            (shape((share, n * ch), F32), (per, n * ch), lambda i: (i, 0)),
+            (shape((share, ch), F32), (per, ch), at),
+            (shape((n, share, share), F32), (n, per, share), lambda i, c: (0, 2 * i + c[0], 0)),
+            (shape((share, n * ch), F32), (per, n * ch), at),
         ],
-        cost=6 * 10**9,
+        aliased=earlier,
+        cost=3 * 10**9,
         name="finish_post",
-    )()
+    )(place)
 
 
 def after(values, *earlier):
@@ -837,7 +841,8 @@
     out_share = cotangent.shape[3]
     steps = jnp.arange(n, dtype=jnp.int32)
     order = (row + steps) % n
-    source = (chan - steps) % n
+    source = (row - steps) % n
+    lows_at = (chan - steps) % n
     rank = jnp.full((1,), chan, jnp.int32)
     core_at = jnp.full((1,), core, jnp.int32)
     pre_taps = pre_conv.astype(F32).reshape(9, ch)
@@ -865,37 +870,40 @@
     flat_features = features.reshape(slots * cells, ch)
     reduced = dot(flat_features, pre_reduce).reshape(slots, cells, ch)
     live = (jnp.arange(SLOT)[None, :] < counts[:, None]).astype(F32).reshape(slots)
-    select = place.T * jnp.tile(live.astype(BF), 16)[None, :]
+    size = 16 * slots
+    at = lax.broadcasted_iota(jnp.int32, (size, size), 0)
+    column = lax.broadcasted_iota(jnp.int32, (size, size), 1)
+    each = size // n
+    wanted = (at % each) // part * slots + part * ((chan + at // each) % n) + at % part
+    select = jnp.where(column == wanted, jnp.tile(live, 16)[None, :], 0.0).astype(BF)
     cot_rows = cotangent.transpose(1, 2, 0, 3).reshape(-1, out_share)
-    cots = lax.all_to_all(cotangent_by_image(after(cot_rows, reduced), select), "chan", 0, 0, tiled=False)
-
-    fixed = (reduced, above, below, features, pre_reduce, pre_taps, pre_expand, pre_gain_row, pool_m)
-    half = n // 2
-    kept, pooled = (), []
-    for h in range(2):
-        *kept, = pre_forward(order[h * half : (h + 1) * half], *fixed, earlier=tuple(kept))
-        pooled += kept[4:]
-        kept = kept[:4]
-    convolved, convolved_act, normal_pre, pre_std = kept
-
-    moved = [lax.ppermute(pooled[k], ("rows", "chan"), spread(n, k)) for k in range(n)]
+    sends = cotangent_by_image(after(cot_rows, reduced, above, below), select, n)
+    cots = [lax.ppermute(sends[k], ("rows", "chan"), cross(n, k)) for k in range(n)]
+
+    convolved, convolved_act, normal_pre, pre_std, *pooled = pre_forward(
+        order, reduced, above, below, features, pre_reduce, pre_taps, pre_expand, pre_gain_row, pool_m
+    )
+
+    moved = [pooled[0]] + [lax.ppermute(pooled[k], "rows", turn(n, k)) for k in range(1, n)]
     flat, post_reduced, post_act, post_convolved, post_cact, post_normal, post_std, low = post_forward(
         source, moved, full, post_taps, pool
     )
-    lows = [low] + [lax.ppermute(low, "chan", [(i, (i + k) % n) for i in range(n)]) for k in range(1, n)]
-    refined_grad = readout_backward(low, readout, cots)
-    refined_grad, lows[1], lows[3] = lax.optimization_barrier((refined_grad, lows[1], lows[3]))
+    refined_grad = readout_backward(source, low, readout, cots)
+    lows = [lax.ppermute(low, ("rows", "chan"), spread(n, k)) for k in range(n - 1)]
+    lows += [lax.ppermute(after(low, refined_grad), ("rows", "chan"), spread(n, n - 1))]
+    refined_grad, lows[0] = lax.optimization_barrier((refined_grad, lows[0]))
     post_expanded_grad, post_reduced_grad, post_taps_grad, post_gain_grad, *back = post_backward(
         source, refined_grad, full, post_taps, post_act, post_reduced, post_convolved, post_normal, post_std, pool
     )
 
-    returned = [lax.ppermute(back[k], ("rows", "chan"), [(d, s) for s, d in spread(n, k)]) for k in range(n)]
-
+    returned = [back[0]] + [lax.ppermute(back[k], "rows", turn(n, -k)) for k in range(1, n)]
+
+    flat = after(flat, lows[1], lows[2])
     load = post_weight_grads(flat, post_reduced_grad, post_cact, post_expanded_grad, n)
 
     alive = jnp.broadcast_to(jnp.tile(live, 48)[:, None], (48 * slots, 1))
-    lows = after(lows, load, returned[:2])
-    tokens, piece, low_here = token_block(rank, source, lows, place, readout, cot_rows, alive)
+    lows = after(lows, load, returned[1])
+    tokens, piece, low_here = token_block(rank, lows_at, lows, place, readout, cot_rows, alive)
     load = readout_weight_grad(low_here, after(piece, returned[2:]), load)
     tokens = tokens.reshape(pool, pool, slots, out_share).transpose(2, 0, 1, 3)
     returned = after(returned, load)
@@ -907,37 +915,50 @@
     )
     grad_above = lax.ppermute(bottom, "rows", down_pairs)
     grad_below = lax.ppermute(top, "rows", up_pairs)
+    chips = ("x", "rows", "chan")
+
+    def halves(grad):
+        return other_core(lax.dynamic_index_in_dim(grad.reshape(2, ch // 2, ch), 1 - core, 0, keepdims=False))
+
     act_rows = after(convolved_act, bottom).reshape(-1, ch)
     pre_expand_grad = dot(act_rows, expanded_grad.reshape(-1, ch), TN).astype(BF)
-    convolved_grad = after(convolved_grad, pre_expand_grad)
+    expand_load = join_halves(core_at, pre_expand_grad, halves(pre_expand_grad), 64)
+    expand_parts = lax.all_to_all(expand_load, chips, 0, 0, tiled=False)
+    convolved_grad = after(convolved_grad, expand_load)
     reduced_grad, pre_taps_grad = pre_conv_backward(convolved_grad, grad_above, grad_below, reduced, pre_taps)
+
     rest = after(rest, reduced_grad).reshape(n, 4, eight, 3 * ch).transpose(1, 0, 2, 3)
     small = small_rows(pre_taps_grad, pre_gain_grad, post_taps_grad, post_gain_grad)
-    flat_features = after(flat_features, rest, small)
+    expand_parts = sum_and_copy(after(expand_parts, rest, small))
+    flat_features = after(flat_features, expand_parts)
     rest = lax.psum_scatter(rest, "rows", scatter_dimension=0, tiled=False)
+    expand_all = lax.all_to_all(expand_parts, chips, 0, 0, tiled=False).reshape(ch // 2, -1)
 
     pre_reduce_grad = dot(flat_features, reduced_grad.reshape(-1, ch), TN).astype(BF)
-    feature_grad = feature_backward(order, after(reduced_grad, pre_reduce_grad), pre_reduce, returned, up_m).reshape(features.shape)
-
-    mine = [pre_reduce_grad, pre_expand_grad]
-    theirs = [other_core(lax.dynamic_index_in_dim(g.reshape(2, ch // 2, ch), 1 - core, 0, keepdims=False)) for g in mine]
-    load = join_halves(core_at, mine, theirs, small, other_core(small), 64)
-    chips = ("x", "rows", "chan")
-    pieces = after(lax.all_to_all(load, chips, 0, 0, tiled=False), feature_grad)
+    reduce_load = join_halves(core_at, pre_reduce_grad, halves(pre_reduce_grad), 64, (small, other_core(small)))
+    reduce_parts = lax.all_to_all(reduce_load, chips, 0, 0, tiled=False)
+    feature_grad = feature_backward(order, after(reduced_grad, reduce_load), pre_reduce, returned, up_m).reshape(features.shape)
 
     rest = lax.all_to_all(after(rest, feature_grad), "chan", 0, 0, tiled=False)
     summed = jnp.sum(rest[:, :, : 2 * ch].astype(F32), axis=0).astype(BF)
     rest = jnp.concatenate([summed] + [rest[c, :, 2 * ch :] for c in range(n)], axis=1)
-    rest = lax.all_gather(rest, ("x", "core", "rows"), axis=0, tiled=True)
-    post_reduce_out, post_expand_out, readout_out = finish_post(rest, n)
-
-    load = sum_and_copy(pieces)
-    load = lax.all_to_all(load, chips, 0, 0, tiled=False).reshape(ch // 2, -1)
-    theirs = other_core(load)
-    *own, small_own = finish_pre(core_at, load, ch)
-    theirs = after(theirs, small_own)
-    pre_reduce_out, pre_expand_out, small_their = finish_pre(1 - core_at, theirs, ch, earlier=tuple(own))
-    small_out = jnp.where(core == 0, small_own, small_their)
+    reduce_parts = sum_and_copy(after(reduce_parts, rest))
+    rest = lax.all_gather(rest, ("x", "rows"), axis=0, tiled=False).reshape(4, 4 * eight, -1)
+    reduce_all = lax.all_to_all(reduce_parts, chips, 0, 0, tiled=False).reshape(ch // 2, -1)
+
+    def finish(kernel, values, *sizes):
+        theirs = other_core(values)
+        own = kernel(core_at, values, *sizes)
+        theirs = after(theirs, *own)
+        return own, theirs
+
+    own, theirs = finish(finish_pre, after(expand_all, reduce_parts), ch)
+    pre_expand_out = finish_pre(1 - core_at, theirs, ch, earlier=tuple(own))[0]
+    own, theirs = finish(finish_pre, reduce_all, ch)
+    pre_reduce_out, small_their = finish_pre(1 - core_at, theirs, ch, earlier=tuple(own[:1]))
+    small_out = jnp.where(core == 0, own[1], small_their)
+    own, theirs = finish(finish_post, rest, n)
+    post_reduce_out, post_expand_out, readout_out = finish_post(1 - core_at, theirs, n, earlier=tuple(own))
     per = ch // LANES
     cut = [0, 9 * per, 10 * per, 19 * per, 20 * per]
     pre_conv_out, pre_gain_out, post_conv_out, post_gain_out = [small_out[a:b] for a, b in zip(cut, cut[1:])]

time: 388 us -> 469 us (1.21)
  starting transfers between devices: 78 us -> 133 us
  waiting for transfers between devices: 48.1 us -> 78 us
  blocking collectives: 43.2 us -> 34.9 us
  Pallas kernels: 158 us -> 163 us
    ppermute x11 -> x14, waiting for transfers between devices: 5.72 us -> 42.9 us  [the longest x3 29.6 us: body(): lax.ppermute(pooled[k], 'rows', turn(n, k))]
    ppermute x11 -> x14, starting transfers between devices: 38.7 us -> 71.6 us  [the longest x3 41.2 us: body(): lax.ppermute(back[k], 'rows', turn(n, -k))]
    all_to_all x3, starting transfers between devices: 19 us -> 30.9 us  [the longest x1 17.2 us: body(): expand_parts = lax.all_to_all(expand_load, chips, 0, 0, tiled=False)]
    all_to_all x1 -> x2, blocking collectives: 43.2 us -> 34.9 us  [the longest x1 25.5 us: body(): lax.all_to_all(reduce_parts, chips, 0, 0, tiled=False).reshape(ch // 2, -1)]
    ppermute x4 -> x6, starting transfers between devices: 7.89 us -> 13.7 us  [other_core(): return lax.ppermute(values, 'core', [(0, 1), (1, 0)])]
    pallas_call x18 -> x22, Pallas kernels: 158 us -> 163 us  [run(): pl.pallas_call(kernel, grid_spec=pltpu.PrefetchScalarGridSpec(num_scalar_...]
    ppermute x1, waiting for transfers between devices: 4.86 us -> 0.01 us  [body(): above = lax.ppermute(features[:, -1], 'rows', down_pairs)]
    unnamed x72 -> x76, local copies, waits for them, and re-layouts: 12.6 us -> 10.5 us
  transfers between devices with their start and end apart: 26 -> 31, of which waited for: 10 -> 12; matrix products, arithmetic and copies ran while one was open for 8% -> 5% of each run, Pallas kernels for 38% -> 32%
where the time goes in v7:
time: 469 us; the launch traced here: 467 us
  Pallas kernels  163 us (35%)
  starting transfers between devices  133 us (28%)
  waiting for transfers between devices  78 us (17%)
  blocking collectives  34.9 us (7%)
  local copies, waits for them, and re-layouts  21 us (4%)
  matrix products  16 us (3%)
  between operations  14.2 us (3%)
  other arithmetic  7.83 us (2%)
    pallas_call x22, Pallas kernels, run(): pl.pallas_call(kernel, grid_spec=pltpu.PrefetchScalarGridSpec(num_scalar_...  163 us
    ppermute x3, starting transfers between devices, body(): lax.ppermute(back[k], 'rows', turn(n, -k))  41.2 us
    ppermute x3, waiting for transfers between devices, body(): lax.ppermute(pooled[k], 'rows', turn(n, k))  29.6 us
    all_to_all x1, blocking collectives, body(): lax.all_to_all(reduce_parts, chips, 0, 0, tiled=False).reshape(ch // 2, -1)  25.5 us
    all_to_all x1, starting transfers between devices, body(): expand_parts = lax.all_to_all(expand_load, chips, 0, 0, tiled=False)  17.2 us
    dot_general x3, matrix products, dot(): return lax.dot_general(a, b, (dims, ((), ())), preferred_element_type=F32)  16 us
    all_to_all x1, waiting for transfers between devices, body(): reduce_parts = lax.all_to_all(reduce_load, chips, 0, 0, tiled=False)  15 us
    ppermute x6, starting transfers between devices, other_core(): return lax.ppermute(values, 'core', [(0, 1), (1, 0)])  13.7 us
  transfers between devices with their start and end apart: 31, of which 12 were waited for; matrix products, arithmetic and copies ran while one was open for 5% of the time, Pallas kernels for 32%

profile of v7, /device:TPU:1, one launch (start us, length us, event | category | flops | bytes accessed | tf_op | source)
XLA Modules:
  0.0 467.4 jit_solution(10273585500516150848)
XLA Ops:
  8.1 1.1 fusion.22
  9.3 1.2 fusion.3
  11.3 4.1 collective-permute-start
  15.3 1.3 collective-permute-start.1
  18.3 5.8 %fusion.1.red = f32[8,144,1024]{2,1,0:T(8,128)} fusion(bf16[8,144,1024]{2,1,0:T(8,128)(2,1)S(1)} %bitcast.82, bf16[1024,1024]{1,0:T(8,128)(2,1)} %wr.3), kind=kOutput, calls=%fused_computation.3 | convolution fusion | flops 2415919104 | bytes 9175040 | tf_op jit(solution)/shard_map/dot_general | solution.py:23
  25.0 1.5 select_convert_fusion.sel
  27.0 4.4 cotangent_by_image.1
  31.4 1.7 collective-permute-start.5
  34.3 24.7 %pre_forward.1 = (f32[8,144,1024]{2,1,0:T(8,128)}, bf16[8,144,1024]{2,1,0:T(8,128)(2,1)}, f32[8,144,1024]{2,1,0:T(8,128)}, f32[8,144,1]{2,1,0:T(8,128)}, bf16[72...) custom-call(s32[4]{0:T(128)} %and_select_fusion.order_ref, ...), custom_call_target="tpu_custom_call" | custom-call | flops 1 | bytes 1 | tf_op jit(solution)/shard_map/pre_forward/pallas_call | solution.py:67
  59.0 3.1 collective-permute-start.2
  62.1 3.1 collective-permute-start.6
  65.3 2.0 collective-permute-start.7
  67.2 2.5 collective-permute-start.8
  69.8 2.3 collective-permute-start.3
  72.1 27.1 %collective-permute-done.3.refs_2_ = bf16[72,1024]{1,0:T(8,128)(2,1)S(1)} collective-permute-done((bf16[72,1024]{1,0:T(8,128)(2,1)}, bf16[72,1024]{1,0:T(8,128)(2,1)S(1)}, u32[]{:S(2)}, u32[]{:S(2)}) %collective-permute-start.3) | collective-permute-done | bytes 147488 | tf_op jit(solution)/shard_map/ppermute | solution.py:887
  99.1 2.3 collective-permute-start.4
  102.6 2.5 collective-permute-done.4.refs_3_
  105.8 11.1 %post_forward.1 = (bf16[288,1024]{1,0:T(8,128)(2,1)}, f32[288,1024]{1,0:T(8,128)}, bf16[288,1024]{1,0:T(8,128)(2,1)}, f32[288,1024]{1,0:T(8,128)}, bf16[288,1024...) custom-call(s32[4]{0:T(128)} %and_select_fusion.1.src, ...), custom_call_target="tpu_custom_call" | custom-call | flops 1 | bytes 1 | tf_op jit(solution)/shard_map/post_forward/pallas_call | solution.py:67
  116.8 1.8 collective-permute-start.9
  118.7 4.5 collective-permute-start.10
  123.2 1.2 collective-permute-start.11
  126.0 12.5 %readout_backward.1.rg = f32[288,1024]{1,0:T(8,128)} custom-call(s32[4]{0:T(128)} %and_select_fusion.1.src, bf16[288,1024]{1,0:T(8,128)(2,1)} %get-tuple-element.96.low_ref, bf16[1024,4096]{1,0:T(8,128)(2,1)} %refs_5_.1, bf16[288,1024]{1,0:T(8,128)(2,1)} %copy-done.10, bf16[288,1024]{1,0:T(8,128)(2,1)} %copy-done.12, bf16[288,1024]{1,0:T(8,128)(2,1)} %copy-done.13, ...), custom_call_target="tpu_custom_call" | custom-call | flops 1 | bytes 1 | tf_op jit(solution)/shard_map/readout_backward/pallas_call | solution.py:67
  138.5 5.9 %collective-permute-start.12 = (bf16[288,1024]{1,0:T(8,128)(2,1)S(1)}, bf16[288,1024]{1,0:T(8,128)(2,1)S(1)}, u32[]{:S(2)}, u32[]{:S(2)}) collective-permute-start(bf16[288,1024]{1,0:T(8,128)(2,1)S(1)} %copy-done.11), channel_id=1, source_target_pairs={{0,3},{1,7},{2,11},{3,15},{4,0},{5,4},{6,8},{7,12},{8,1},{9,5},{10... | collective-permute-start | bytes 1769480 | tf_op jit(solution)/shard_map/ppermute | solution.py:893
  144.4 12.2 %post_backward.1 = (bf16[288,1024]{1,0:T(8,128)(2,1)}, bf16[288,1024]{1,0:T(8,128)(2,1)}, f32[9,8,1024]{2,1,0:T(8,128)}, f32[8,1024]{1,0:T(8,128)}, bf16[72,1024...) custom-call(s32[4]{0:T(128)} %and_select_fusion.1.src, ...), custom_call_target="tpu_custom_call" | custom-call | flops 1 | bytes 1 | tf_op jit(solution)/shard_map/post_backward/pallas_call | solution.py:67
  156.6 41.2 %collective-permute-start.13 = (bf16[72,1024]{1,0:T(8,128)(2,1)}, bf16[72,1024]{1,0:T(8,128)(2,1)S(1)}, u32[]{:S(2)}, u32[]{:S(2)}) collective-permute-start(bf16[72,1024]{1,0:T(8,128)(2,1)} %get-tuple-element.108), channel_id=1, source_target_pairs={{0,12},{4,0},{8,4},{12,8},{1,13},{5,1},{9,5},{13,9},{2,14},{6,2},{... | collective-permute-start | bytes 442376 | tf_op jit(solution)/shard_map/ppermute | solution.py:899
  197.8 1.1 collective-permute-done.10.refs_1_
  200.4 6.0 %post_weight_grads.1.old = bf16[8,4,32,3072]{3,2,1,0:T(8,128)(2,1)} custom-call(bf16[288,1024]{1,0:T(8,128)(2,1)} %get-tuple-element.98.x, bf16[288,1024]{1,0:T(8,128)(2,1)} %get-tuple-element.105.g, bf16[288,1024]{1,0:T(8,128)(2,1)} %get-tuple-element.106.a, bf16[288,1024]{1,0:T(8,128)(2,1)} %get-tuple-element.107.e), custom_call_target="tpu_custom_call" | custom-call | flops 1 | bytes 1 | tf_op jit(solution)/shard_map/post_weight_grads/pallas_call | solution.py:67
  207.2 10.8 %token_block.1 = (bf16[1152,1024]{1,0:T(8,128)(2,1)}, bf16[1152,1024]{1,0:T(8,128)(2,1)}, bf16[1152,1024]{1,0:T(8,128)(2,1)}) custom-call(s32[1]{0:T(128)} %bitcast.chan_ref, s32[4]{0:T(128)} %and_select_fusion.2.src, bf16[288,1024]{1,0:T(8,128)(2,1)} %copy-done.15, bf16[288,1024]{1,0:T(8,128)(2,1)} %collective-permute-done.10.refs_1_, ...), custom_call_target="tpu_custom_call" | custom-call | flops 1 | bytes 1 | tf_op jit(solution)/shard_map/token_block/pallas_call | solution.py:67
  218.0 12.0 %collective-permute-done.15.refs_3_ = bf16[72,1024]{1,0:T(8,128)(2,1)S(1)} collective-permute-done((bf16[72,1024]{1,0:T(8,128)(2,1)}, bf16[72,1024]{1,0:T(8,128)(2,1)S(1)}, u32[]{:S(2)}, u32[]{:S(2)}) %collective-permute-start.15) | collective-permute-done | bytes 147488 | tf_op jit(solution)/shard_map/ppermute | solution.py:899
  230.1 6.7 %readout_weight_grad.1 = bf16[8,4,32,3072]{3,2,1,0:T(8,128)(2,1)} custom-call(bf16[1152,1024]{1,0:T(8,128)(2,1)} %get-tuple-element.117.x, bf16[1152,1024]{1,0:T(8,128)(2,1)} %get-tuple-element.119.g, bf16[8,4,32,3072]{3,2,1,0:T(8,128)(2,1)} %post_weight_grads.1.old), custom_call_target="tpu_custom_call", output_to_operand_aliasing={{}: (2, {})} | custom-call | flops 1 | bytes 1 | tf_op jit(solution)/shard_map/readout_weight_grad/pallas_call | solution.py:67
  236.8 21.6 %pre_backward.1 = (bf16[8,144,1024]{2,1,0:T(8,128)(2,1)}, bf16[8,144,1024]{2,1,0:T(8,128)(2,1)}, bf16[8,24,1024]{2,1,0:T(8,128)(2,1)}, bf16[8,24,1024]{2,1,0:T(8,128)(2,1)}, f32[8,1024]{1,0:T(8,128)}) custom-call(s32[4]{0:T(128)} %and_select_fusion.order_ref, bf16[72,1024]{1,0:T(8,128)(2,1)} %get-tuple-element.120.refs_0_, bf16[72,1024]{1,0:T(8,128)(2,1)} %copy-done.24, ...), custom_call_target="tpu_custom_call" | custom-call | flops 1 | bytes 1 | tf_op jit(solution)/shard_map/pre_backward/pallas_call | solution.py:67
  258.4 4.9 %bitcast_convert_fusion.own = bf16[1024,1024]{1,0:T(8,128)(2,1)S(1)} fusion(bf16[8,144,1024]{2,1,0:T(8,128)(2,1)S(1)} %copy-done.30, bf16[8,144,1024]{2,1,0:T(8,128)(2,1)} %get-tuple-element.131), kind=kOutput, calls=%fused_computation | convolution fusion | flops 2416967680 | bytes 6815744 | tf_op jit(solution)/shard_map/dot_general | solution.py:23
  263.4 2.8 collective-permute-start.16
  266.2 9.3 %collective-permute-start.17 = (bf16[8,24,1024]{2,1,0:T(8,128)(2,1)S(1)}, bf16[8,24,1024]{2,1,0:T(8,128)(2,1)S(1)}, u32[]{:S(2)}, u32[]{:S(2)}) collective-permute-start(bf16[8,24,1024]{2,1,0:T(8,128)(2,1)S(1)} %copy-done.32), channel_id=1, source_target_pairs={{0,4},{4,8},{8,12},{1,5},{5,9},{9,13},{2,6},{6,10},{10,14},{3,7},{... | collective-permute-start | bytes 1179656 | tf_op jit(solution)/shard_map/ppermute | solution.py:916
  275.5 1.3 collective-permute-start.18
  277.8 2.8 join_halves.2
  280.6 17.2 %all-to-all-start = ((bf16[64,8,1024]{2,1,0:T(8,128)(2,1)}), bf16[64,8,1024]{2,1,0:T(8,128)(2,1)S(1)}, u32[]{:S(2)}, u32[]{:S(2)}) async-start(bf16[64,8,1024]{2,1,0:T(8,128)(2,1)} %bitcast.80), calls=%async_computation | async-start | bytes 2097152 | tf_op jit(solution)/shard_map/all_to_all | solution.py:926
  299.7 12.1 %pre_conv_backward.1 = (bf16[8,144,1024]{2,1,0:T(8,128)(2,1)}, f32[9,8,1024]{2,1,0:T(8,128)}) custom-call(bf16[8,144,1024]{2,1,0:T(8,128)(2,1)} %get-tuple-element.132.cg, bf16[8,24,1024]{2,1,0:T(8,128)(2,1)} %copy-done.33, bf16[8,24,1024]{2,1,0:T(8,128)(2,1)} %copy-done.34, f32[8,144,1024]{2,1,0:T(8,128)} %fusion.1.red, f32[9,1024]{1,0:T(8,128)} %reshape.154.tap), custom_call_target="tpu_custom_call" | custom-call | flops 12000000000 | bytes 1 | tf_op jit(solution)/shard_map/pre_conv_backward/pallas_call | solution.py:67
  311.8 1.8 small_rows.1.refs_0_
  313.6 2.1 copy_bitcast_fusion
  316.6 3.0 sum_and_copy.2
  319.7 5.3 %convolution_convert_fusion.own = bf16[1024,1024]{1,0:T(8,128)(2,1)S(1)} fusion(bf16[1152,1024]{1,0:T(8,128)(2,1)} %bitcast.81, bf16[1152,1024]{1,0:T(8,128)(2,1)} %bitcast.94), kind=kOutput, calls=%fused_computation.5 | convolution fusion | flops 2416967680 | bytes 6815744 | tf_op jit(solution)/shard_map/dot_general | solution.py:23
  325.0 1.0 dynamic-slice_bitcast_fusion
  326.0 1.7 collective-permute-start.19
  327.9 2.1 collective-permute-done.20.refs_1_
  331.6 2.8 join_halves.3
  334.4 8.6 %feature_backward.1 = f32[8,144,1024]{2,1,0:T(8,128)} custom-call(s32[4]{0:T(128)} %and_select_fusion.order_ref, bf16[8,144,1024]{2,1,0:T(8,128)(2,1)} %get-tuple-element.142.rg, bf16[1024,1024]{1,0:T(8,128)(2,1)} %wr.3, bf16[288,72]{1,0:T(8,128)(2,1)} %constant.131.clone.refs_4_.up, bf16[72,1024]{1,0:T(8,128)(2,1)} %get-tuple-element.120.refs_0_, ...), custom_call_target="tpu_custom_call" | custom-call | flops 8999999488 | bytes 1 | tf_op jit(solution)/shard_map/feature_backward/pallas_call | solution.py:67
  343.0 6.2 %reduce-scatter.5.cloned.1.call-done = bf16[1,4,8,3072]{3,2,1,0:T(8,128)(2,1)} async-done(((bf16[4,4,8,3072]{3,2,1,0:T(8,128)(2,1)}), bf16[1,4,8,3072]{3,2,1,0:T(8,128)(2,1)}) %reduce-scatter.5.cloned.1.call-update) | async-done | bytes 196624 | tf_op jit(solution)/shard_map/reduce_scatter | solution.py:934
  349.2 9.3 %all_to_all.25 = bf16[4,8,3072]{2,1,0:T(8,128)(2,1)S(1)} all-to-all(bf16[4,8,3072]{2,1,0:T(8,128)(2,1)} %bitcast.87), channel_id=1, replica_groups=mesh['x'=4,'core'=2,'rows'=4,'chan'=4] {'chan'}, dimensions={0} | all-to-all | bytes 393216 | tf_op jit(solution)/shard_map/all_to_all | solution.py:942
  358.6 6.5 %all-to-all-start.1 = ((bf16[64,8,1152]{2,1,0:T(8,128)(2,1)}), bf16[64,8,1152]{2,1,0:T(8,128)(2,1)S(1)}, u32[]{:S(2)}, u32[]{:S(2)}) async-start(bf16[64,8,1152]{2,1,0:T(8,128)(2,1)} %bitcast.24), calls=%async_computation.2 | async-start | bytes 2359296 | tf_op jit(solution)/shard_map/all_to_all | solution.py:939
  365.9 15.0 %all-to-all-done.1.x = bf16[64,8,1152]{2,1,0:T(8,128)(2,1)S(1)} async-done(((bf16[64,8,1152]{2,1,0:T(8,128)(2,1)}), bf16[64,8,1152]{2,1,0:T(8,128)(2,1)S(1)}, u32[]{:S(2)}, u32[]{:S(2)}) %all-to-all-start.1) | async-done | bytes 1179680 | tf_op jit(solution)/shard_map/all_to_all | solution.py:939
  381.9 3.1 sum_and_copy.3
  385.0 25.5 %all_to_all.26 = bf16[64,8,1152]{2,1,0:T(8,128)(2,1)S(1)} all-to-all(bf16[64,8,1152]{2,1,0:T(8,128)(2,1)} %sum_and_copy.3), channel_id=1, replica_groups=mesh['x'=4,'core'=2,'rows'=4,'chan'=4] {'x','rows','chan'}, dimensions={0} | all-to-all | bytes 2359296 | tf_op jit(solution)/shard_map/all_to_all | solution.py:947
  410.5 7.2 %all-to-all-start.4 = ((bf16[64,8,1024]{2,1,0:T(8,128)(2,1)}), bf16[64,8,1024]{2,1,0:T(8,128)(2,1)S(1)}, u32[]{:S(2)}, u32[]{:S(2)}) async-start(bf16[64,8,1024]{2,1,0:T(8,128)(2,1)} %sum_and_copy.2), calls=%async_computation.6 | async-start | bytes 2097152 | tf_op jit(solution)/shard_map/all_to_all | solution.py:935
  417.7 3.8 collective-permute-start.21
  421.5 10.4 %all-to-all-done.4 = bf16[64,8,1024]{2,1,0:T(8,128)(2,1)S(1)} async-done(((bf16[64,8,1024]{2,1,0:T(8,128)(2,1)}), bf16[64,8,1024]{2,1,0:T(8,128)(2,1)S(1)}, u32[]{:S(2)}, u32[]{:S(2)}) %all-to-all-start.4) | async-done | bytes 1048608 | tf_op jit(solution)/shard_map/all_to_all | solution.py:935
  431.9 5.3 %collective-permute-start.22 = (bf16[512,1024]{1,0:T(8,128)(2,1)S(1)}, bf16[512,1024]{1,0:T(8,128)(2,1)}, u32[]{:S(2)}, u32[]{:S(2)}) collective-permute-start(bf16[512,1024]{1,0:T(8,128)(2,1)S(1)} %bitcast.83), channel_id=1, source_target_pairs={{0,16},{16,0},{1,17},{17,1},{2,18},{18,2},{3,19},{19,3},{4,20},{20... | collective-permute-start | bytes 3145736 | tf_op jit(solution)/shard_map/ppermute | solution.py:675
  437.3 2.7 finish_pre.6.outs_0_
  440.3 2.7 finish_pre.7
  443.0 2.8 finish_pre.4
  445.8 1.0 copy-done.7
  446.8 2.8 finish_pre.5
  453.1 3.8 finish_post.2
  457.0 3.9 finish_post.3
  (141 shorter events, 22.9 us)
Async XLA Ops:
  7.2 4.0 copy-start.5
  7.2 97.9 %all-gather.5.cloned.1.call-start = ((), (), s32[]{:S(2)}) async-start(), calls=%async_computation.9 | async-start | bytes 4866048 | tf_op jit(solution)/shard_map/all_gather | solution.py:868
  9.3 8.4 %copy-start.35 = (s32[2]{0:T(128)S(1)}, s32[2]{0:T(128)}, u32[]{:S(2)}) copy-start(s32[2]{0:T(128)} %param.16) | copy-start | bytes 28
  11.2 302.4 %reduce-scatter.3.cloned.1.call-start = ((), (), s32[]{:S(2)}) async-start(), calls=%async_computation.7 | async-start | bytes 7077888 | tf_op jit(solution)/shard_map/reduce_scatter | solution.py:911
  11.3 15.3 %collective-permute-start = (bf16[8,24,1024]{2,1,0:T(8,128)(2,1)S(1)}, bf16[8,24,1024]{2,1,0:T(8,128)(2,1)S(1)}, u32[]{:S(2)}, u32[]{:S(2)}) collective-permute-start(bf16[8,24,1024]{2,1,0:T(8,128)(2,1)S(1)} %get-tuple-element.162), channel_id=1, source_target_pairs={{0,4},{4,8},{8,12},{1,5},{5,9},{9,13},{2,6},{6,10},{10,14},{3,7},{... | collective-permute-start | bytes 1179656 | tf_op jit(solution)/shard_map/ppermute | solution.py:858
  15.3 11.7 %collective-permute-start.1 = (bf16[8,24,1024]{2,1,0:T(8,128)(2,1)S(1)}, bf16[8,24,1024]{2,1,0:T(8,128)(2,1)}, u32[]{:S(2)}, u32[]{:S(2)}) collective-permute-start(bf16[8,24,1024]{2,1,0:T(8,128)(2,1)S(1)} %get-tuple-element.161), channel_id=1, source_target_pairs={{4,0},{8,4},{12,8},{5,1},{9,5},{13,9},{6,2},{10,6},{14,10},{7,3},{... | collective-permute-start | bytes 1179656 | tf_op jit(solution)/shard_map/ppermute | solution.py:859
  24.1 9.1 %copy-start.28 = (bf16[3,3,1024]{2,1,0:T(4,128)(2,1)S(1)}, bf16[3,3,1024]{2,1,0:T(4,128)(2,1)}, u32[]{:S(2)}) copy-start(bf16[3,3,1024]{2,1,0:T(4,128)(2,1)} %param.18) | copy-start | bytes 55300
  26.5 7.8 %copy-start.17 = (bf16[8,24,1024]{2,1,0:T(8,128)(2,1)}, bf16[8,24,1024]{2,1,0:T(8,128)(2,1)S(1)}, u32[]{:S(2)}) copy-start(bf16[8,24,1024]{2,1,0:T(8,128)(2,1)S(1)} %collective-permute-done.up_ref) | copy-start | bytes 1179652
  31.4 87.2 %collective-permute-start.5 = (bf16[288,1024]{1,0:T(8,128)(2,1)}, bf16[288,1024]{1,0:T(8,128)(2,1)S(1)}, u32[]{:S(2)}, u32[]{:S(2)}) collective-permute-start(bf16[288,1024]{1,0:T(8,128)(2,1)} %get-tuple-element.91), channel_id=1, source_target_pairs={{0,0},{1,4},{2,8},{3,12},{4,1},{5,5},{6,9},{7,13},{8,2},{9,6},{10,... | collective-permute-start | bytes 1769480 | tf_op jit(solution)/shard_map/ppermute | solution.py:881
  34.3 67.1 %copy-start.29 = (bf16[3,3,1024]{2,1,0:T(4,128)(2,1)S(1)}, bf16[3,3,1024]{2,1,0:T(4,128)(2,1)}, u32[]{:S(2)}) copy-start(bf16[3,3,1024]{2,1,0:T(4,128)(2,1)} %param.22) | copy-start | bytes 55300
  59.0 10.7 %collective-permute-start.2 = (bf16[72,1024]{1,0:T(8,128)(2,1)}, bf16[72,1024]{1,0:T(8,128)(2,1)S(1)}, u32[]{:S(2)}, u32[]{:S(2)}) collective-permute-start(bf16[72,1024]{1,0:T(8,128)(2,1)} %get-tuple-element.86), channel_id=1, source_target_pairs={{0,4},{4,8},{8,12},{12,0},{1,5},{5,9},{9,13},{13,1},{2,6},{6,10},{... | collective-permute-start | bytes 442376 | tf_op jit(solution)/shard_map/ppermute | solution.py:887
  62.1 61.1 %collective-permute-start.6 = (bf16[288,1024]{1,0:T(8,128)(2,1)}, bf16[288,1024]{1,0:T(8,128)(2,1)S(1)}, u32[]{:S(2)}, u32[]{:S(2)}) collective-permute-start(bf16[288,1024]{1,0:T(8,128)(2,1)} %get-tuple-element.92), channel_id=1, source_target_pairs={{0,4},{1,8},{2,12},{3,0},{4,5},{5,9},{6,13},{7,1},{8,6},{9,10},{10... | collective-permute-start | bytes 1769480 | tf_op jit(solution)/shard_map/ppermute | solution.py:881
  65.3 59.1 %collective-permute-start.7 = (bf16[288,1024]{1,0:T(8,128)(2,1)}, bf16[288,1024]{1,0:T(8,128)(2,1)S(1)}, u32[]{:S(2)}, u32[]{:S(2)}) collective-permute-start(bf16[288,1024]{1,0:T(8,128)(2,1)} %get-tuple-element.93), channel_id=1, source_target_pairs={{0,8},{1,12},{2,0},{3,4},{4,9},{5,13},{6,1},{7,5},{8,10},{9,14},{1... | collective-permute-start | bytes 1769480 | tf_op jit(solution)/shard_map/ppermute | solution.py:881
  67.2 57.2 %collective-permute-start.8 = (bf16[288,1024]{1,0:T(8,128)(2,1)}, bf16[288,1024]{1,0:T(8,128)(2,1)S(1)}, u32[]{:S(2)}, u32[]{:S(2)}) collective-permute-start(bf16[288,1024]{1,0:T(8,128)(2,1)} %get-tuple-element.94), channel_id=1, source_target_pairs={{0,12},{1,0},{2,4},{3,8},{4,13},{5,1},{6,5},{7,9},{8,14},{9,2},{10... | collective-permute-start | bytes 1769480 | tf_op jit(solution)/shard_map/ppermute | solution.py:881
  69.8 35.3 %copy-start.21 = (bf16[72,1024]{1,0:T(8,128)(2,1)}, bf16[72,1024]{1,0:T(8,128)(2,1)S(1)}, u32[]{:S(2)}) copy-start(bf16[72,1024]{1,0:T(8,128)(2,1)S(1)} %collective-permute-done.2.refs_1_) | copy-start | bytes 442372
  69.8 29.4 %collective-permute-start.3 = (bf16[72,1024]{1,0:T(8,128)(2,1)}, bf16[72,1024]{1,0:T(8,128)(2,1)S(1)}, u32[]{:S(2)}, u32[]{:S(2)}) collective-permute-start(bf16[72,1024]{1,0:T(8,128)(2,1)} %get-tuple-element.87), channel_id=1, source_target_pairs={{0,8},{4,12},{8,0},{12,4},{1,9},{5,13},{9,1},{13,5},{2,10},{6,14},... | collective-permute-start | bytes 442376 | tf_op jit(solution)/shard_map/ppermute | solution.py:887
  99.1 6.0 %copy-start.22 = (bf16[72,1024]{1,0:T(8,128)(2,1)}, bf16[72,1024]{1,0:T(8,128)(2,1)S(1)}, u32[]{:S(2)}) copy-start(bf16[72,1024]{1,0:T(8,128)(2,1)S(1)} %collective-permute-done.3.refs_2_) | copy-start | bytes 442372
  99.1 6.0 %collective-permute-start.4 = (bf16[72,1024]{1,0:T(8,128)(2,1)}, bf16[72,1024]{1,0:T(8,128)(2,1)S(1)}, u32[]{:S(2)}, u32[]{:S(2)}) collective-permute-start(bf16[72,1024]{1,0:T(8,128)(2,1)} %get-tuple-element.88), channel_id=1, source_target_pairs={{0,12},{4,0},{8,4},{12,8},{1,13},{5,1},{9,5},{13,9},{2,14},{6,2},{... | collective-permute-start | bytes 442376 | tf_op jit(solution)/shard_map/ppermute | solution.py:887
  116.8 21.7 %copy-start.11 = (bf16[288,1024]{1,0:T(8,128)(2,1)S(1)}, bf16[288,1024]{1,0:T(8,128)(2,1)}, u32[]{:S(2)}) copy-start(bf16[288,1024]{1,0:T(8,128)(2,1)} %get-tuple-element.96.low_ref) | copy-start | bytes 1769476
  116.8 27.5 %collective-permute-start.9 = (bf16[288,1024]{1,0:T(8,128)(2,1)}, bf16[288,1024]{1,0:T(8,128)(2,1)S(1)}, u32[]{:S(2)}, u32[]{:S(2)}) collective-permute-start(bf16[288,1024]{1,0:T(8,128)(2,1)} %get-tuple-element.96.low_ref), channel_id=1, source_target_pairs={{0,0},{1,4},{2,8},{3,12},{4,1},{5,5},{6,9},{7,13},{8,2},{9,6},{10,... | collective-permute-start | bytes 1769480 | tf_op jit(solution)/shard_map/ppermute | solution.py:892
  118.7 5.7 %copy-start.10 = (bf16[288,1024]{1,0:T(8,128)(2,1)}, bf16[288,1024]{1,0:T(8,128)(2,1)S(1)}, u32[]{:S(2)}) copy-start(bf16[288,1024]{1,0:T(8,128)(2,1)S(1)} %collective-permute-done.5.rest_0_) | copy-start | bytes 1769476
  118.7 80.2 %collective-permute-start.10 = (bf16[288,1024]{1,0:T(8,128)(2,1)}, bf16[288,1024]{1,0:T(8,128)(2,1)}, u32[]{:S(2)}, u32[]{:S(2)}) collective-permute-start(bf16[288,1024]{1,0:T(8,128)(2,1)} %get-tuple-element.96.low_ref), channel_id=1, source_target_pairs={{0,1},{1,5},{2,9},{3,13},{4,2},{5,6},{6,10},{7,14},{8,3},{9,7},{10... | collective-permute-start | bytes 1769480 | tf_op jit(solution)/shard_map/ppermute | solution.py:892
  123.2 1.2 copy-start.12
  123.2 77.2 %collective-permute-start.11 = (bf16[288,1024]{1,0:T(8,128)(2,1)}, bf16[288,1024]{1,0:T(8,128)(2,1)}, u32[]{:S(2)}, u32[]{:S(2)}) collective-permute-start(bf16[288,1024]{1,0:T(8,128)(2,1)} %get-tuple-element.96.low_ref), channel_id=1, source_target_pairs={{0,2},{1,6},{2,10},{3,14},{4,3},{5,7},{6,11},{7,15},{8,0},{9,4},{1... | collective-permute-start | bytes 1769480 | tf_op jit(solution)/shard_map/ppermute | solution.py:892
  124.4 0.8 copy-start.13
  125.2 0.8 copy-start.14
  138.5 67.9 %collective-permute-start.12 = (bf16[288,1024]{1,0:T(8,128)(2,1)S(1)}, bf16[288,1024]{1,0:T(8,128)(2,1)S(1)}, u32[]{:S(2)}, u32[]{:S(2)}) collective-permute-start(bf16[288,1024]{1,0:T(8,128)(2,1)S(1)} %copy-done.11), channel_id=1, source_target_pairs={{0,3},{1,7},{2,11},{3,15},{4,0},{5,4},{6,8},{7,12},{8,1},{9,5},{10... | collective-permute-start | bytes 1769480 | tf_op jit(solution)/shard_map/ppermute | solution.py:893
  144.4 12.2 %copy-start.15 = (bf16[288,1024]{1,0:T(8,128)(2,1)}, bf16[288,1024]{1,0:T(8,128)(2,1)S(1)}, u32[]{:S(2)}) copy-start(bf16[288,1024]{1,0:T(8,128)(2,1)S(1)} %collective-permute-done.9.refs_0_) | copy-start | bytes 1769476
  156.6 49.8 %collective-permute-start.13 = (bf16[72,1024]{1,0:T(8,128)(2,1)}, bf16[72,1024]{1,0:T(8,128)(2,1)S(1)}, u32[]{:S(2)}, u32[]{:S(2)}) collective-permute-start(bf16[72,1024]{1,0:T(8,128)(2,1)} %get-tuple-element.108), channel_id=1, source_target_pairs={{0,12},{4,0},{8,4},{12,8},{1,13},{5,1},{9,5},{13,9},{2,14},{6,2},{... | collective-permute-start | bytes 442376 | tf_op jit(solution)/shard_map/ppermute | solution.py:899
  197.8 20.2 %collective-permute-start.14 = (bf16[72,1024]{1,0:T(8,128)(2,1)}, bf16[72,1024]{1,0:T(8,128)(2,1)S(1)}, u32[]{:S(2)}, u32[]{:S(2)}) collective-permute-start(bf16[72,1024]{1,0:T(8,128)(2,1)} %get-tuple-element.115), channel_id=1, source_target_pairs={{0,8},{4,12},{8,0},{12,4},{1,9},{5,13},{9,1},{13,5},{2,10},{6,14},... | collective-permute-start | bytes 442376 | tf_op jit(solution)/shard_map/ppermute | solution.py:899
  198.9 31.2 %collective-permute-start.15 = (bf16[72,1024]{1,0:T(8,128)(2,1)}, bf16[72,1024]{1,0:T(8,128)(2,1)S(1)}, u32[]{:S(2)}, u32[]{:S(2)}) collective-permute-start(bf16[72,1024]{1,0:T(8,128)(2,1)} %get-tuple-element.116), channel_id=1, source_target_pairs={{0,4},{4,8},{8,12},{12,0},{1,5},{5,9},{9,13},{13,1},{2,6},{6,10},{... | collective-permute-start | bytes 442376 | tf_op jit(solution)/shard_map/ppermute | solution.py:899
  206.4 0.8 copy-start.16
  206.4 11.6 %copy-start.24 = (bf16[72,1024]{1,0:T(8,128)(2,1)}, bf16[72,1024]{1,0:T(8,128)(2,1)S(1)}, u32[]{:S(2)}) copy-start(bf16[72,1024]{1,0:T(8,128)(2,1)S(1)} %collective-permute-done.13.refs_1_) | copy-start | bytes 442372
  218.0 18.7 %copy-start.25 = (bf16[72,1024]{1,0:T(8,128)(2,1)}, bf16[72,1024]{1,0:T(8,128)(2,1)S(1)}, u32[]{:S(2)}) copy-start(bf16[72,1024]{1,0:T(8,128)(2,1)S(1)} %collective-permute-done.14.refs_2_) | copy-start | bytes 442372
  230.1 6.7 %copy-start.26 = (bf16[72,1024]{1,0:T(8,128)(2,1)}, bf16[72,1024]{1,0:T(8,128)(2,1)S(1)}, u32[]{:S(2)}) copy-start(bf16[72,1024]{1,0:T(8,128)(2,1)S(1)} %collective-permute-done.15.refs_3_) | copy-start | bytes 442372
  236.8 21.6 %copy-start.30 = (bf16[8,144,1024]{2,1,0:T(8,128)(2,1)S(1)}, bf16[8,144,1024]{2,1,0:T(8,128)(2,1)}, u32[]{:S(2)}) copy-start(bf16[8,144,1024]{2,1,0:T(8,128)(2,1)} %get-tuple-element.130) | copy-start | bytes 7077892
  258.4 7.8 %copy-start.32 = (bf16[8,24,1024]{2,1,0:T(8,128)(2,1)S(1)}, bf16[8,24,1024]{2,1,0:T(8,128)(2,1)}, u32[]{:S(2)}) copy-start(bf16[8,24,1024]{2,1,0:T(8,128)(2,1)} %get-tuple-element.129) | copy-start | bytes 1179652
  258.4 17.1 %copy-start.31 = (bf16[8,24,1024]{2,1,0:T(8,128)(2,1)S(1)}, bf16[8,24,1024]{2,1,0:T(8,128)(2,1)}, u32[]{:S(2)}) copy-start(bf16[8,24,1024]{2,1,0:T(8,128)(2,1)} %get-tuple-element.133) | copy-start | bytes 1179652
  263.3 13.5 %copy-start.1 = (bf16[1024,1024]{1,0:T(8,128)(2,1)}, bf16[1024,1024]{1,0:T(8,128)(2,1)S(1)}, u32[]{:S(2)}) copy-start(bf16[1024,1024]{1,0:T(8,128)(2,1)S(1)} %bitcast_convert_fusion.own) | copy-start | bytes 6291460
  263.4 13.4 %collective-permute-start.16 = (bf16[512,1024]{1,0:T(8,128)(2,1)S(1)}, bf16[512,1024]{1,0:T(8,128)(2,1)S(1)}, u32[]{:S(2)}, u32[]{:S(2)}) collective-permute-start(bf16[512,1024]{1,0:T(8,128)(2,1)S(1)} %dynamic-slice_bitcast_fusion.1), channel_id=1, source_target_pairs={{0,16},{16,0},{1,17},{17,1},{2,18},{18,2},{3,19},{19,3},{4,20},{20... | collective-permute-start | bytes 3145736 | tf_op jit(solution)/shard_map/ppermute | solution.py:675
  266.2 32.0 %collective-permute-start.17 = (bf16[8,24,1024]{2,1,0:T(8,128)(2,1)S(1)}, bf16[8,24,1024]{2,1,0:T(8,128)(2,1)S(1)}, u32[]{:S(2)}, u32[]{:S(2)}) collective-permute-start(bf16[8,24,1024]{2,1,0:T(8,128)(2,1)S(1)} %copy-done.32), channel_id=1, source_target_pairs={{0,4},{4,8},{8,12},{1,5},{5,9},{9,13},{2,6},{6,10},{10,14},{3,7},{... | collective-permute-start | bytes 1179656 | tf_op jit(solution)/shard_map/ppermute | solution.py:916
  275.5 22.7 %collective-permute-start.18 = (bf16[8,24,1024]{2,1,0:T(8,128)(2,1)S(1)}, bf16[8,24,1024]{2,1,0:T(8,128)(2,1)S(1)}, u32[]{:S(2)}, u32[]{:S(2)}) collective-permute-start(bf16[8,24,1024]{2,1,0:T(8,128)(2,1)S(1)} %copy-done.31), channel_id=1, source_target_pairs={{4,0},{8,4},{12,8},{5,1},{9,5},{13,9},{6,2},{10,6},{14,10},{7,3},{... | collective-permute-start | bytes 1179656 | tf_op jit(solution)/shard_map/ppermute | solution.py:917
  276.9 1.0 copy-start.9
  280.6 35.1 %all-to-all-start = ((bf16[64,8,1024]{2,1,0:T(8,128)(2,1)}), bf16[64,8,1024]{2,1,0:T(8,128)(2,1)S(1)}, u32[]{:S(2)}, u32[]{:S(2)}) async-start(bf16[64,8,1024]{2,1,0:T(8,128)(2,1)} %bitcast.80), calls=%async_computation | async-start | bytes 2097152 | tf_op jit(solution)/shard_map/all_to_all | solution.py:926
  297.9 51.4 %reduce-scatter.5.cloned.1.call-start = ((), (), s32[]{:S(2)}) async-start(), calls=%async_computation.8 | async-start | bytes 983040 | tf_op jit(solution)/shard_map/reduce_scatter | solution.py:934
  298.2 0.7 copy-start.33
  298.9 0.7 copy-start.34
  315.7 1.0 copy-start.4
  325.0 5.4 %copy-start = (bf16[1024,1024]{1,0:T(8,128)(2,1)}, bf16[1024,1024]{1,0:T(8,128)(2,1)S(1)}, u32[]{:S(2)}) copy-start(bf16[1024,1024]{1,0:T(8,128)(2,1)S(1)} %convolution_convert_fusion.own) | copy-start | bytes 6291460
  325.0 2.8 copy-start.18
  326.0 4.3 collective-permute-start.19
  327.8 2.2 collective-permute-start.20
  330.6 1.0 copy-start.8
  358.6 22.3 %all-to-all-start.1 = ((bf16[64,8,1152]{2,1,0:T(8,128)(2,1)}), bf16[64,8,1152]{2,1,0:T(8,128)(2,1)S(1)}, u32[]{:S(2)}, u32[]{:S(2)}) async-start(bf16[64,8,1152]{2,1,0:T(8,128)(2,1)} %bitcast.24), calls=%async_computation.2 | async-start | bytes 2359296 | tf_op jit(solution)/shard_map/all_to_all | solution.py:939
  365.1 72.1 %all-gather.7.cloned.1.call-start = ((), (), s32[]{:S(2)}) async-start(), calls=%async_computation.10 | async-start | bytes 1671168 | tf_op jit(solution)/shard_map/all_gather | solution.py:946
  380.9 1.0 copy-start.3
  410.5 29.4 %copy-start.2 = (bf16[64,8,1152]{2,1,0:T(8,128)(2,1)}, bf16[64,8,1152]{2,1,0:T(8,128)(2,1)S(1)}, u32[]{:S(2)}) copy-start(bf16[64,8,1152]{2,1,0:T(8,128)(2,1)S(1)} %all_to_all.26) | copy-start | bytes 3538948
  410.5 21.4 %all-to-all-start.4 = ((bf16[64,8,1024]{2,1,0:T(8,128)(2,1)}), bf16[64,8,1024]{2,1,0:T(8,128)(2,1)S(1)}, u32[]{:S(2)}, u32[]{:S(2)}) async-start(bf16[64,8,1024]{2,1,0:T(8,128)(2,1)} %sum_and_copy.2), calls=%async_computation.6 | async-start | bytes 2097152 | tf_op jit(solution)/shard_map/all_to_all | solution.py:935
  417.7 28.1 %collective-permute-start.21 = (bf16[512,1152]{1,0:T(8,128)(2,1)S(1)}, bf16[512,1152]{1,0:T(8,128)(2,1)S(1)}, u32[]{:S(2)}, u32[]{:S(2)}) collective-permute-start(bf16[512,1152]{1,0:T(8,128)(2,1)S(1)} %bitcast.78), channel_id=1, source_target_pairs={{0,16},{16,0},{1,17},{17,1},{2,18},{18,2},{3,19},{19,3},{4,20},{20... | collective-permute-start | bytes 3538952 | tf_op jit(solution)/shard_map/ppermute | solution.py:675
  431.9 5.4 %copy-start.6 = (bf16[64,8,1024]{2,1,0:T(8,128)(2,1)}, bf16[64,8,1024]{2,1,0:T(8,128)(2,1)S(1)}, u32[]{:S(2)}) copy-start(bf16[64,8,1024]{2,1,0:T(8,128)(2,1)S(1)} %all-to-all-done.4) | copy-start | bytes 3145732
  431.9 8.4 %collective-permute-start.22 = (bf16[512,1024]{1,0:T(8,128)(2,1)S(1)}, bf16[512,1024]{1,0:T(8,128)(2,1)}, u32[]{:S(2)}, u32[]{:S(2)}) collective-permute-start(bf16[512,1024]{1,0:T(8,128)(2,1)S(1)} %bitcast.83), channel_id=1, source_target_pairs={{0,16},{16,0},{1,17},{17,1},{2,18},{18,2},{3,19},{19,3},{4,20},{20... | collective-permute-start | bytes 3145736 | tf_op jit(solution)/shard_map/ppermute | solution.py:675
  437.2 19.8 %collective-permute-start.23 = (bf16[4,32,6144]{2,1,0:T(8,128)(2,1)}, bf16[4,32,6144]{2,1,0:T(8,128)(2,1)}, u32[]{:S(2)}, u32[]{:S(2)}) collective-permute-start(bf16[4,32,6144]{2,1,0:T(8,128)(2,1)} %bitcast.91), channel_id=1, source_target_pairs={{0,16},{16,0},{1,17},{17,1},{2,18},{18,2},{3,19},{19,3},{4,20},{20... | collective-permute-start | bytes 4718600 | tf_op jit(solution)/shard_map/ppermute | solution.py:675
  445.8 1.0 copy-start.7
  446.8 2.8 copy-start.19
  (3 other events, 1.9 us)
Sparse Core Ops, SparseCore 0:
  11.3 79.3 all-gather.4
  236.9 57.6 reduce-scatter.2
  327.9 21.3 reduce-scatter.4
  367.8 50.0 all-gather.6

commit v8 on v6

--- a/solution.py
+++ b/solution.py
@@ -612,7 +612,6 @@
             *[(r, None, None) for r in returned],
         ],
         outs=[(shape((slots, cells, ch), F32), whole, by_order)],
-        cost=9 * 10**9,
         name="feature_backward",
     )(order)[0]
 
@@ -764,29 +763,32 @@
     )(place)
 
 
-def finish_post(gathered, n):
-    share, width = gathered.shape
+def finish_post(place, gathered, n, earlier=()):
+    groups, per, width = gathered.shape
+    share = 2 * groups * per
     ch = width // (n + 2)
-    per = 64
-
-    def kernel(x, reduce_out, expand_out, read_out):
-        reduce_out[...] = x[:, :ch].astype(F32)
+
+    def kernel(place_ref, x, *outs):
+        reduce_out, expand_out, read_out = outs[len(earlier) :]
+        reduce_out[...] = x[0, :, :ch].astype(F32)
         for q in range(n):
-            expand_out[q] = x[:, ch + q * share : ch + (q + 1) * share].astype(F32)
-        read_out[...] = x[:, 2 * ch :].astype(F32)
-
-    return call(
-        kernel,
-        grid=(share // per,),
-        ins=[(gathered, (per, width), lambda i: (i, 0))],
+            expand_out[q] = x[0, :, ch + q * share : ch + (q + 1) * share].astype(F32)
+        read_out[...] = x[0, :, 2 * ch :].astype(F32)
+
+    at = lambda i, c: (2 * i + c[0], 0)
+    return call(
+        kernel,
+        grid=(groups,),
+        prefetch=1,
+        ins=[(gathered, (1, per, width), lambda i, c: (i, 0, 0))],
         outs=[
-            (shape((share, ch), F32), (per, ch), lambda i: (i, 0)),
-            (shape((n, share, share), F32), (n, per, share), lambda i: (0, i, 0)),
-            (shape((share, n * ch), F32), (per, n * ch), lambda i: (i, 0)),
-        ],
-        cost=6 * 10**9,
+            (shape((share, ch), F32), (per, ch), at),
+            (shape((n, share, share), F32), (n, per, share), lambda i, c: (0, 2 * i + c[0], 0)),
+            (shape((share, n * ch), F32), (per, n * ch), at),
+        ],
+        aliased=earlier,
         name="finish_post",
-    )()
+    )(place)
 
 
 def after(values, *earlier):
@@ -827,7 +829,6 @@
     row = lax.axis_index("rows").astype(jnp.int32)
     chan = lax.axis_index("chan").astype(jnp.int32)
     core = lax.axis_index("core").astype(jnp.int32)
-    eighth = lax.axis_index(("x", "core"))
     ch = pre_reduce.shape[0]
     slots, high, wide = features.shape[0], features.shape[1], features.shape[2]
     part = slots // n
@@ -859,38 +860,34 @@
     shards = jnp.concatenate(
         [post_reduce, jnp.concatenate([square[q] for q in range(n)], axis=1), jnp.pad(gain_row, ((0, 63), (0, 0)))], axis=0
     )
-    eighths = shards.reshape(8, -1, ch)
-    full = lax.all_gather(lax.dynamic_index_in_dim(eighths, eighth, 0, keepdims=False), ("chan", "x", "core"), axis=0, tiled=True)
+    shard = lax.dynamic_index_in_dim(shards.reshape(2, -1, ch), core, 0, keepdims=False)
+    full = lax.all_gather(shard, ("chan", "core"), axis=0, tiled=True)
     full = full.reshape(n, 2 * share + 64, ch)
     flat_features = features.reshape(slots * cells, ch)
     reduced = dot(flat_features, pre_reduce).reshape(slots, cells, ch)
     live = (jnp.arange(SLOT)[None, :] < counts[:, None]).astype(F32).reshape(slots)
     select = place.T * jnp.tile(live.astype(BF), 16)[None, :]
     cot_rows = cotangent.transpose(1, 2, 0, 3).reshape(-1, out_share)
-    cots = lax.all_to_all(cotangent_by_image(after(cot_rows, reduced), select), "chan", 0, 0, tiled=False)
-
-    fixed = (reduced, above, below, features, pre_reduce, pre_taps, pre_expand, pre_gain_row, pool_m)
-    half = n // 2
-    kept, pooled = (), []
-    for h in range(2):
-        *kept, = pre_forward(order[h * half : (h + 1) * half], *fixed, earlier=tuple(kept))
-        pooled += kept[4:]
-        kept = kept[:4]
-    convolved, convolved_act, normal_pre, pre_std = kept
-
+    cots = lax.all_to_all(cotangent_by_image(after(cot_rows, reduced, above, below), select), "chan", 0, 0, tiled=False)
+
+    convolved, convolved_act, normal_pre, pre_std, *pooled = pre_forward(
+        order, reduced, above, below, features, pre_reduce, pre_taps, pre_expand, pre_gain_row, pool_m
+    )
+
+    pooled = after(pooled, cots)
     moved = [lax.ppermute(pooled[k], ("rows", "chan"), spread(n, k)) for k in range(n)]
     flat, post_reduced, post_act, post_convolved, post_cact, post_normal, post_std, low = post_forward(
         source, moved, full, post_taps, pool
     )
     lows = [low] + [lax.ppermute(low, "chan", [(i, (i + k) % n) for i in range(n)]) for k in range(1, n)]
     refined_grad = readout_backward(low, readout, cots)
-    refined_grad, lows[1], lows[3] = lax.optimization_barrier((refined_grad, lows[1], lows[3]))
     post_expanded_grad, post_reduced_grad, post_taps_grad, post_gain_grad, *back = post_backward(
         source, refined_grad, full, post_taps, post_act, post_reduced, post_convolved, post_normal, post_std, pool
     )
 
     returned = [lax.ppermute(back[k], ("rows", "chan"), [(d, s) for s, d in spread(n, k)]) for k in range(n)]
 
+    flat = after(flat, lows)
     load = post_weight_grads(flat, post_reduced_grad, post_cact, post_expanded_grad, n)
 
     alive = jnp.broadcast_to(jnp.tile(live, 48)[:, None], (48 * slots, 1))
@@ -911,33 +908,40 @@
     pre_expand_grad = dot(act_rows, expanded_grad.reshape(-1, ch), TN).astype(BF)
     convolved_grad = after(convolved_grad, pre_expand_grad)
     reduced_grad, pre_taps_grad = pre_conv_backward(convolved_grad, grad_above, grad_below, reduced, pre_taps)
-    rest = after(rest, reduced_grad).reshape(n, 4, eight, 3 * ch).transpose(1, 0, 2, 3)
     small = small_rows(pre_taps_grad, pre_gain_grad, post_taps_grad, post_gain_grad)
-    flat_features = after(flat_features, rest, small)
-    rest = lax.psum_scatter(rest, "rows", scatter_dimension=0, tiled=False)
-
-    pre_reduce_grad = dot(flat_features, reduced_grad.reshape(-1, ch), TN).astype(BF)
-    feature_grad = feature_backward(order, after(reduced_grad, pre_reduce_grad), pre_reduce, returned, up_m).reshape(features.shape)
-
+    pre_reduce_grad = dot(after(flat_features, small), reduced_grad.reshape(-1, ch), TN).astype(BF)
+
+    chips = ("x", "rows", "chan")
     mine = [pre_reduce_grad, pre_expand_grad]
     theirs = [other_core(lax.dynamic_index_in_dim(g.reshape(2, ch // 2, ch), 1 - core, 0, keepdims=False)) for g in mine]
+    rest = after(rest, *mine).reshape(n, 4, eight, 3 * ch).transpose(1, 0, 2, 3)
+    theirs = after(theirs, rest)
+    rest = lax.psum_scatter(rest, "rows", scatter_dimension=0, tiled=False)
     load = join_halves(core_at, mine, theirs, small, other_core(small), 64)
-    chips = ("x", "rows", "chan")
-    pieces = after(lax.all_to_all(load, chips, 0, 0, tiled=False), feature_grad)
-
-    rest = lax.all_to_all(after(rest, feature_grad), "chan", 0, 0, tiled=False)
-    summed = jnp.sum(rest[:, :, : 2 * ch].astype(F32), axis=0).astype(BF)
-    rest = jnp.concatenate([summed] + [rest[c, :, 2 * ch :] for c in range(n)], axis=1)
-    rest = lax.all_gather(rest, ("x", "core", "rows"), axis=0, tiled=True)
-    post_reduce_out, post_expand_out, readout_out = finish_post(rest, n)
-
+    pieces = lax.all_to_all(load, chips, 0, 0, tiled=False)
+    feature_grad = feature_backward(order, after(reduced_grad, load), pre_reduce, returned, up_m).reshape(features.shape)
+
+    rest = after(rest, feature_grad)
+    block_at = lax.broadcasted_iota(jnp.int32, (1, 1, n * ch), 2) // ch
+    padded = jnp.where(block_at == chan, jnp.tile(rest[:, :, 2 * ch :], (1, 1, n)), jnp.zeros((), BF))
+    rest = jnp.concatenate([rest[:, :, : 2 * ch], padded], axis=2)
+    pieces = after(pieces, rest)
+    rest = lax.psum_scatter(rest, "chan", scatter_dimension=0, tiled=False)
     load = sum_and_copy(pieces)
-    load = lax.all_to_all(load, chips, 0, 0, tiled=False).reshape(ch // 2, -1)
-    theirs = other_core(load)
-    *own, small_own = finish_pre(core_at, load, ch)
-    theirs = after(theirs, small_own)
-    pre_reduce_out, pre_expand_out, small_their = finish_pre(1 - core_at, theirs, ch, earlier=tuple(own))
-    small_out = jnp.where(core == 0, small_own, small_their)
+    load_all = lax.all_to_all(load, chips, 0, 0, tiled=False).reshape(ch // 2, -1)
+    rest = lax.all_gather(rest, ("x", "rows"), axis=0, tiled=False).reshape(4, 4 * eight, -1)
+
+    def finish(kernel, values, *sizes):
+        theirs = other_core(values)
+        own = kernel(core_at, values, *sizes)
+        theirs = after(theirs, *own)
+        return own, theirs
+
+    own, theirs = finish(finish_pre, load_all, ch)
+    pre_reduce_out, pre_expand_out, small_their = finish_pre(1 - core_at, theirs, ch, earlier=tuple(own[:2]))
+    small_out = jnp.where(core == 0, own[2], small_their)
+    own, theirs = finish(finish_post, rest, n)
+    post_reduce_out, post_expand_out, readout_out = finish_post(1 - core_at, theirs, n, earlier=tuple(own))
     per = ch // LANES
     cut = [0, 9 * per, 10 * per, 19 * per, 20 * per]
     pre_conv_out, pre_gain_out, post_conv_out, post_gain_out = [small_out[a:b] for a, b in zip(cut, cut[1:])]

time: 388 us -> 397 us (1.023)
  waiting for transfers between devices: 48.1 us -> 117 us
  blocking collectives: 43.2 us -> 0 us
  starting transfers between devices: 78 us -> 69.8 us
  local copies, waits for them, and re-layouts: 24.5 us -> 19 us
    all_to_all x1 -> x0, blocking collectives: 43.2 us -> none  [body(): load = lax.all_to_all(load, chips, 0, 0, tiled=False).reshape(ch // 2, -1)]
    all_gather x2, waiting for transfers between devices: 0.01 us -> 41.3 us  [the longest x1 41.3 us: body(): lax.all_gather(rest, ('x', 'rows'), axis=0, tiled=False)]
    all_to_all x3, waiting for transfers between devices: 25.5 us -> 51.8 us  [the longest x1 25.1 us: body(): lax.all_to_all(load, chips, 0, 0, tiled=False).reshape(ch // 2, -1)]
    ppermute x4, starting transfers between devices: 19.2 us -> 6.12 us  [body(): lax.ppermute(back[k], ('rows', 'chan'), [(d, s) for s, d in spread(n, k)])]
    ppermute x4, waiting for transfers between devices: 4.8 us -> 14.5 us  [body(): lax.ppermute(pooled[k], ('rows', 'chan'), spread(n, k))]
    unnamed x72 -> x62, local copies, waits for them, and re-layouts: 12.6 us -> 4.52 us
    reduce_scatter x1, waiting for transfers between devices: 6.8 us -> 0.01 us  [body(): rest = lax.psum_scatter(rest, 'rows', scatter_dimension=0, tiled=False)]
    ppermute x1, waiting for transfers between devices: 4.86 us -> 0.01 us  [body(): above = lax.ppermute(features[:, -1], 'rows', down_pairs)]
  transfers between devices with their start and end apart: 26 -> 28, of which waited for: 10 -> 9; matrix products, arithmetic and copies ran while one was open for 8% -> 8% of each run, Pallas kernels for 38% -> 34%
where the time goes in v8:
time: 397 us; the launch traced here: 395 us
  Pallas kernels  155 us (39%)
  waiting for transfers between devices  117 us (29%)
  starting transfers between devices  69.8 us (18%)
  local copies, waits for them, and re-layouts  19 us (5%)
  matrix products  15.5 us (4%)
  between operations  14.2 us (4%)
  other arithmetic  5.15 us (1%)
    pallas_call x18, Pallas kernels, run(): pl.pallas_call(kernel, grid_spec=pltpu.PrefetchScalarGridSpec(num_scalar_...  155 us
    all_gather x1, waiting for transfers between devices, body(): lax.all_gather(rest, ('x', 'rows'), axis=0, tiled=False)  41.3 us
    all_to_all x1, waiting for transfers between devices, body(): lax.all_to_all(load, chips, 0, 0, tiled=False).reshape(ch // 2, -1)  25.1 us
    all_to_all x1, waiting for transfers between devices, body(): pieces = lax.all_to_all(load, chips, 0, 0, tiled=False)  18.1 us
    dot_general x3, matrix products, dot(): return lax.dot_general(a, b, (dims, ((), ())), preferred_element_type=F32)  15.5 us
    ppermute x4, waiting for transfers between devices, body(): lax.ppermute(pooled[k], ('rows', 'chan'), spread(n, k))  14.5 us
    ppermute x3, starting transfers between devices, body(): lax.ppermute(low, 'chan', [(i, (i + k) % n) for i in range(n)])  11 us
    ppermute x5, starting transfers between devices, other_core(): return lax.ppermute(values, 'core', [(0, 1), (1, 0)])  10.9 us
  transfers between devices with their start and end apart: 28, of which 9 were waited for; matrix products, arithmetic and copies ran while one was open for 8% of the time, Pallas kernels for 34%

profile of v8, /device:TPU:1, one launch (start us, length us, event | category | flops | bytes accessed | tf_op | source)
XLA Modules:
  0.0 395.4 jit_solution(7135139205532946636)
XLA Ops:
  7.2 0.8 subtract_convert_fusion
  8.0 1.1 fusion.10
  9.2 1.3 fusion.3
  10.5 0.9 constant_dynamic-slice_fusion
  11.4 1.2 slice_bitcast_fusion
  12.6 4.1 %collective-permute-start = (bf16[8,24,1024]{2,1,0:T(8,128)(2,1)S(1)}, bf16[8,24,1024]{2,1,0:T(8,128)(2,1)S(1)}, u32[]{:S(2)}, u32[]{:S(2)}) collective-permute-start(bf16[8,24,1024]{2,1,0:T(8,128)(2,1)S(1)} %get-tuple-element.158), channel_id=1, source_target_pairs={{0,4},{4,8},{8,12},{1,5},{5,9},{9,13},{2,6},{6,10},{10,14},{3,7},{... | collective-permute-start | bytes 1179656 | tf_op jit(solution)/shard_map/ppermute | solution.py:854
  16.6 1.3 collective-permute-start.1
  19.1 5.9 %fusion.1.red = f32[8,144,1024]{2,1,0:T(8,128)} fusion(bf16[8,144,1024]{2,1,0:T(8,128)(2,1)} %bitcast.67, bf16[1024,1024]{1,0:T(8,128)(2,1)S(1)} %copy-done.3), kind=kOutput, calls=%fused_computation.3 | convolution fusion | flops 2415919104 | bytes 9175040 | tf_op jit(solution)/shard_map/dot_general | solution.py:23
  24.9 3.4 collective-permute-done.1.down_ref
  28.3 4.4 %cotangent_by_image.1 = bf16[4,288,1024]{2,1,0:T(8,128)(2,1)} custom-call(bf16[1152,1024]{1,0:T(8,128)(2,1)} %bitcast.59, bf16[128,128]{1,0:T(8,128)(2,1)} %copy.43.sel), custom_call_target="tpu_custom_call" | custom-call | flops 1 | bytes 1 | tf_op jit(solution)/shard_map/cotangent_by_image/pallas_call | solution.py:67
  32.8 5.2 %all-to-all-start = ((bf16[4,288,1024]{2,1,0:T(8,128)(2,1)}), bf16[4,288,1024]{2,1,0:T(8,128)(2,1)S(1)}, u32[]{:S(2)}, u32[]{:S(2)}) async-start(bf16[4,288,1024]{2,1,0:T(8,128)(2,1)} %cotangent_by_image.1), calls=%async_computation | async-start | bytes 4718592 | tf_op jit(solution)/shard_map/all_to_all | solution.py:871
  39.2 24.8 %pre_forward.1 = (f32[8,144,1024]{2,1,0:T(8,128)}, bf16[8,144,1024]{2,1,0:T(8,128)(2,1)}, f32[8,144,1024]{2,1,0:T(8,128)}, f32[8,144,1]{2,1,0:T(8,128)}, bf16[72...) custom-call(s32[4]{0:T(128)} %and_select_fusion.order_ref, ...), custom_call_target="tpu_custom_call" | custom-call | flops 1 | bytes 1 | tf_op jit(solution)/shard_map/pre_forward/pallas_call | solution.py:67
  64.0 8.5 %all-to-all-done.cot = bf16[4,288,1024]{2,1,0:T(8,128)(2,1)S(1)} async-done(((bf16[4,288,1024]{2,1,0:T(8,128)(2,1)}), bf16[4,288,1024]{2,1,0:T(8,128)(2,1)S(1)}, u32[]{:S(2)}, u32[]{:S(2)}) %all-to-all-start) | async-done | bytes 2359328 | tf_op jit(solution)/shard_map/all_to_all | solution.py:871
  72.5 1.7 collective-permute-start.2
  74.2 2.6 collective-permute-start.3
  76.9 3.1 collective-permute-start.4
  80.0 1.7 collective-permute-start.5
  82.8 14.5 %collective-permute-done.3.refs_1_ = bf16[72,1024]{1,0:T(8,128)(2,1)S(1)} collective-permute-done((bf16[72,1024]{1,0:T(8,128)(2,1)}, bf16[72,1024]{1,0:T(8,128)(2,1)S(1)}, u32[]{:S(2)}, u32[]{:S(2)}) %collective-permute-start.3) | collective-permute-done | bytes 147488 | tf_op jit(solution)/shard_map/ppermute | solution.py:878
  98.0 11.1 %post_forward.1 = (bf16[288,1024]{1,0:T(8,128)(2,1)}, f32[288,1024]{1,0:T(8,128)}, bf16[288,1024]{1,0:T(8,128)(2,1)}, f32[288,1024]{1,0:T(8,128)}, bf16[288,1024...) custom-call(s32[4]{0:T(128)} %and_select_fusion.1.src, ...), custom_call_target="tpu_custom_call" | custom-call | flops 1 | bytes 1 | tf_op jit(solution)/shard_map/post_forward/pallas_call | solution.py:67
  109.1 4.3 %collective-permute-start.6 = (bf16[288,1024]{1,0:T(8,128)(2,1)}, bf16[288,1024]{1,0:T(8,128)(2,1)S(1)}, u32[]{:S(2)}, u32[]{:S(2)}) collective-permute-start(bf16[288,1024]{1,0:T(8,128)(2,1)} %get-tuple-element.105.low_ref.refs_0_), channel_id=1, source_target_pairs={{0,1},{1,2},{2,3},{3,0},{4,5},{5,6},{6,7},{7,4},{8,9},{9,10},{10,1... | collective-permute-start | bytes 1769480 | tf_op jit(solution)/shard_map/ppermute | solution.py:882
  113.4 4.7 %collective-permute-start.7 = (bf16[288,1024]{1,0:T(8,128)(2,1)}, bf16[288,1024]{1,0:T(8,128)(2,1)S(1)}, u32[]{:S(2)}, u32[]{:S(2)}) collective-permute-start(bf16[288,1024]{1,0:T(8,128)(2,1)} %get-tuple-element.105.low_ref.refs_0_), channel_id=1, source_target_pairs={{0,2},{1,3},{2,0},{3,1},{4,6},{5,7},{6,4},{7,5},{8,10},{9,11},{10,... | collective-permute-start | bytes 1769480 | tf_op jit(solution)/shard_map/ppermute | solution.py:882
  118.1 2.0 collective-permute-start.8
  120.1 10.9 %readout_backward.1.rg = f32[288,1024]{1,0:T(8,128)} custom-call(bf16[288,1024]{1,0:T(8,128)(2,1)} %get-tuple-element.105.low_ref.refs_0_, bf16[1024,4096]{1,0:T(8,128)(2,1)} %refs_5_.1, bf16[4,288,1024]{2,1,0:T(8,128)(2,1)} %copy-done), custom_call_target="tpu_custom_call" | custom-call | flops 1 | bytes 1 | tf_op jit(solution)/shard_map/readout_backward/pallas_call | solution.py:67
  131.0 12.2 %post_backward.1 = (bf16[288,1024]{1,0:T(8,128)(2,1)}, bf16[288,1024]{1,0:T(8,128)(2,1)}, f32[9,8,1024]{2,1,0:T(8,128)}, f32[8,1024]{1,0:T(8,128)}, bf16[72,1024...) custom-call(s32[4]{0:T(128)} %and_select_fusion.1.src, ...), custom_call_target="tpu_custom_call" | custom-call | flops 1 | bytes 1 | tf_op jit(solution)/shard_map/post_backward/pallas_call | solution.py:67
  143.2 1.6 collective-permute-start.9
  144.7 3.0 collective-permute-start.10
  148.3 1.0 collective-permute-start.12
  149.3 0.8 broadcast_in_dim_tile.5.refs_7_
  150.1 6.2 %post_weight_grads.1.old = bf16[8,4,32,3072]{3,2,1,0:T(8,128)(2,1)} custom-call(bf16[288,1024]{1,0:T(8,128)(2,1)} %get-tuple-element.94.x, bf16[288,1024]{1,0:T(8,128)(2,1)} %get-tuple-element.100.g, bf16[288,1024]{1,0:T(8,128)(2,1)} %get-tuple-element.101.a, bf16[288,1024]{1,0:T(8,128)(2,1)} %get-tuple-element.102.e), custom_call_target="tpu_custom_call" | custom-call | flops 1 | bytes 1 | tf_op jit(solution)/shard_map/post_weight_grads/pallas_call | solution.py:67
  156.4 10.8 %token_block.1 = (bf16[1152,1024]{1,0:T(8,128)(2,1)}, bf16[1152,1024]{1,0:T(8,128)(2,1)}, bf16[1152,1024]{1,0:T(8,128)(2,1)}) custom-call(s32[1]{0:T(128)} %bitcast.chan_ref, s32[4]{0:T(128)} %and_select_fusion.1.src, bf16[288,1024]{1,0:T(8,128)(2,1)} %get-tuple-element.105.low_ref.refs_0_, bf16[288,1024]{1,0:T(8,128)(2,1)} %copy-done.9, ...), custom_call_target="tpu_custom_call" | custom-call | flops 1 | bytes 1 | tf_op jit(solution)/shard_map/token_block/pallas_call | solution.py:67
  167.3 6.7 %readout_weight_grad.1 = bf16[8,4,32,3072]{3,2,1,0:T(8,128)(2,1)} custom-call(bf16[1152,1024]{1,0:T(8,128)(2,1)} %get-tuple-element.112.x, bf16[1152,1024]{1,0:T(8,128)(2,1)} %get-tuple-element.114.g, bf16[8,4,32,3072]{3,2,1,0:T(8,128)(2,1)} %post_weight_grads.1.old), custom_call_target="tpu_custom_call", output_to_operand_aliasing={{}: (2, {})} | custom-call | flops 1 | bytes 1 | tf_op jit(solution)/shard_map/readout_weight_grad/pallas_call | solution.py:67
  174.1 21.6 %pre_backward.1 = (bf16[8,144,1024]{2,1,0:T(8,128)(2,1)}, bf16[8,144,1024]{2,1,0:T(8,128)(2,1)}, bf16[8,24,1024]{2,1,0:T(8,128)(2,1)}, bf16[8,24,1024]{2,1,0:T(8,128)(2,1)}, f32[8,1024]{1,0:T(8,128)}) custom-call(s32[4]{0:T(128)} %and_select_fusion.order_ref, bf16[72,1024]{1,0:T(8,128)(2,1)} %copy-done.12, bf16[72,1024]{1,0:T(8,128)(2,1)} %copy-done.13, ...), custom_call_target="tpu_custom_call" | custom-call | flops 1 | bytes 1 | tf_op jit(solution)/shard_map/pre_backward/pallas_call | solution.py:67
  195.7 4.9 %collective-permute-start.13 = (bf16[8,24,1024]{2,1,0:T(8,128)(2,1)}, bf16[8,24,1024]{2,1,0:T(8,128)(2,1)S(1)}, u32[]{:S(2)}, u32[]{:S(2)}) collective-permute-start(bf16[8,24,1024]{2,1,0:T(8,128)(2,1)} %get-tuple-element.124), channel_id=1, source_target_pairs={{0,4},{4,8},{8,12},{1,5},{5,9},{9,13},{2,6},{6,10},{10,14},{3,7},{... | collective-permute-start | bytes 1179656 | tf_op jit(solution)/shard_map/ppermute | solution.py:905
  200.6 1.3 collective-permute-start.14
  201.9 4.9 %bitcast_convert_fusion.refs_1_ = bf16[1024,1024]{1,0:T(8,128)(2,1)S(1)} fusion(bf16[8,144,1024]{2,1,0:T(8,128)(2,1)S(1)} %copy-done.29, bf16[8,144,1024]{2,1,0:T(8,128)(2,1)} %get-tuple-element.126), kind=kOutput, calls=%fused_computation | convolution fusion | flops 2416967680 | bytes 6815744 | tf_op jit(solution)/shard_map/dot_general | solution.py:23
  206.8 1.1 dynamic-slice_bitcast_fusion
  207.9 3.0 collective-permute-start.16
  212.5 12.1 %pre_conv_backward.1 = (bf16[8,144,1024]{2,1,0:T(8,128)(2,1)}, f32[9,8,1024]{2,1,0:T(8,128)}) custom-call(bf16[8,144,1024]{2,1,0:T(8,128)(2,1)} %get-tuple-element.127.cg, bf16[8,24,1024]{2,1,0:T(8,128)(2,1)} %copy-done.17, bf16[8,24,1024]{2,1,0:T(8,128)(2,1)} %copy-done.18, f32[8,144,1024]{2,1,0:T(8,128)} %fusion.1.red, f32[9,1024]{1,0:T(8,128)} %reshape.199.tap), custom_call_target="tpu_custom_call" | custom-call | flops 1 | bytes 1 | tf_op jit(solution)/shard_map/pre_conv_backward/pallas_call | solution.py:67
  224.6 1.8 small_rows.1.refs_4_
  226.4 4.8 %convolution_convert_fusion.refs_0_ = bf16[1024,1024]{1,0:T(8,128)(2,1)S(1)} fusion(bf16[1152,1024]{1,0:T(8,128)(2,1)S(1)} %bitcast.68, bf16[1152,1024]{1,0:T(8,128)(2,1)} %bitcast.70), kind=kOutput, calls=%fused_computation.5 | convolution fusion | flops 2416967680 | bytes 6815744 | tf_op jit(solution)/shard_map/dot_general | solution.py:23
  231.3 2.8 copy_bitcast_fusion
  234.2 2.6 collective-permute-start.15
  236.9 2.2 collective-permute-done.15.refs_2_
  239.2 0.8 copy-done.8
  240.1 4.0 %join_halves.1 = bf16[512,2176]{1,0:T(8,128)(2,1)} custom-call(s32[1]{0:T(128)} %bitcast.14.core_ref.place_ref, bf16[1024,1024]{1,0:T(8,128)(2,1)} %copy-done.5, bf16[1024,1024]{1,0:T(8,128)(2,1)} %copy-done.4, bf16[512,1024]{1,0:T(8,128)(2,1)} %copy-done.8, bf16[512,1024]{1,0:T(8,128)(2,1)} %copy-done.7, f32[160,128]{1,0:T(8,128)} %small_rows.1.refs_4_, ...), custom_call_target="tpu_custom_call" | custom-call | flops 1 | bytes 1 | tf_op jit(solution)/shard_map/join_halves/pallas_call | solution.py:67
  244.1 7.4 %all-to-all-start.1 = ((bf16[64,8,2176]{2,1,0:T(8,128)(2,1)}), bf16[64,8,2176]{2,1,0:T(8,128)(2,1)S(1)}, u32[]{:S(2)}, u32[]{:S(2)}) async-start(bf16[64,8,2176]{2,1,0:T(8,128)(2,1)} %bitcast.63), calls=%async_computation.2 | async-start | bytes 4456448 | tf_op jit(solution)/shard_map/all_to_all | solution.py:921
  251.5 8.5 %feature_backward.1 = f32[8,144,1024]{2,1,0:T(8,128)} custom-call(s32[4]{0:T(128)} %and_select_fusion.order_ref, bf16[8,144,1024]{2,1,0:T(8,128)(2,1)} %get-tuple-element.138.rg, bf16[1024,1024]{1,0:T(8,128)(2,1)} %wr.3, bf16[288,72]{1,0:T(8,128)(2,1)} %constant.80.clone.refs_4_.up, bf16[72,1024]{1,0:T(8,128)(2,1)} %copy-done.12, ...), custom_call_target="tpu_custom_call" | custom-call | flops 1 | bytes 1 | tf_op jit(solution)/shard_map/feature_backward/pallas_call | solution.py:67
  260.1 0.8 slice.47
  260.9 0.9 slice.46
  261.9 0.8 pad_maximum_fusion
  262.7 18.1 %all-to-all-done.1.x = bf16[64,8,2176]{2,1,0:T(8,128)(2,1)S(1)} async-done(((bf16[64,8,2176]{2,1,0:T(8,128)(2,1)}), bf16[64,8,2176]{2,1,0:T(8,128)(2,1)S(1)}, u32[]{:S(2)}, u32[]{:S(2)}) %all-to-all-start.1) | async-done | bytes 2228256 | tf_op jit(solution)/shard_map/all_to_all | solution.py:921
  280.8 1.4 copy-done.2
  282.2 4.4 %sum_and_copy.1 = bf16[64,8,2176]{2,1,0:T(8,128)(2,1)} custom-call(bf16[64,8,2176]{2,1,0:T(8,128)(2,1)} %copy-done.2), custom_call_target="tpu_custom_call" | custom-call | flops 1 | bytes 1 | tf_op jit(solution)/shard_map/sum_and_copy/pallas_call | solution.py:67
  286.6 8.5 %all-to-all-start.2 = ((bf16[64,8,2176]{2,1,0:T(8,128)(2,1)}), bf16[64,8,2176]{2,1,0:T(8,128)(2,1)S(1)}, u32[]{:S(2)}, u32[]{:S(2)}) async-start(bf16[64,8,2176]{2,1,0:T(8,128)(2,1)} %sum_and_copy.1), calls=%async_computation.4 | async-start | bytes 4456448 | tf_op jit(solution)/shard_map/all_to_all | solution.py:931
  295.1 3.2 reduce-scatter.8.cloned.1.call-done
  298.4 25.1 %all-to-all-done.2 = bf16[64,8,2176]{2,1,0:T(8,128)(2,1)S(1)} async-done(((bf16[64,8,2176]{2,1,0:T(8,128)(2,1)}), bf16[64,8,2176]{2,1,0:T(8,128)(2,1)S(1)}, u32[]{:S(2)}, u32[]{:S(2)}) %all-to-all-start.2) | async-done | bytes 2228256 | tf_op jit(solution)/shard_map/all_to_all | solution.py:931
  323.5 3.6 collective-permute-start.18
  327.1 41.3 %all-gather.4.cloned.1.call-done = bf16[16,8,6144]{2,1,0:T(8,128)(2,1)} async-done(((bf16[1,8,6144]{2,1,0:T(8,128)(2,1)}), bf16[16,8,6144]{2,1,0:T(8,128)(2,1)}) %all-gather.4.cloned.1.call-update) | async-done | bytes 1572880 | tf_op jit(solution)/shard_map/all_gather | solution.py:932
  368.3 1.6 collective-permute-start.19
  370.0 3.9 finish_pre.2
  373.8 3.8 finish_post.2
  377.7 3.9 finish_pre.3
  381.6 1.0 broadcast_select_fusion.1
  385.1 3.8 finish_post.3
  (116 shorter events, 9.5 us)
Async XLA Ops:
  7.2 90.1 %all-gather.6.cloned.1.call-start = ((), (), s32[]{:S(2)}) async-start(), calls=%async_computation.10 | async-start | bytes 5308416 | tf_op jit(solution)/shard_map/all_gather | solution.py:864
  9.2 8.8 %copy-start.30 = (s32[2]{0:T(128)S(1)}, s32[2]{0:T(128)}, u32[]{:S(2)}) copy-start(s32[2]{0:T(128)} %param.16) | copy-start | bytes 28
  9.2 9.1 %copy-start.25 = (bf16[128,128]{1,0:T(8,128)(2,1)S(1)}, bf16[128,128]{1,0:T(8,128)(2,1)}, u32[]{:S(2)}) copy-start(bf16[128,128]{1,0:T(8,128)(2,1)} %constant.81.clone.refs_4_) | copy-start | bytes 98308
  9.2 9.9 %copy-start.3 = (bf16[1024,1024]{1,0:T(8,128)(2,1)S(1)}, bf16[1024,1024]{1,0:T(8,128)(2,1)}, u32[]{:S(2)}) copy-start(bf16[1024,1024]{1,0:T(8,128)(2,1)} %wr.3) | copy-start | bytes 6291460
  12.6 12.3 %collective-permute-start = (bf16[8,24,1024]{2,1,0:T(8,128)(2,1)S(1)}, bf16[8,24,1024]{2,1,0:T(8,128)(2,1)S(1)}, u32[]{:S(2)}, u32[]{:S(2)}) collective-permute-start(bf16[8,24,1024]{2,1,0:T(8,128)(2,1)S(1)} %get-tuple-element.158), channel_id=1, source_target_pairs={{0,4},{4,8},{8,12},{1,5},{5,9},{9,13},{2,6},{6,10},{10,14},{3,7},{... | collective-permute-start | bytes 1179656 | tf_op jit(solution)/shard_map/ppermute | solution.py:854
  16.6 11.7 %collective-permute-start.1 = (bf16[8,24,1024]{2,1,0:T(8,128)(2,1)S(1)}, bf16[8,24,1024]{2,1,0:T(8,128)(2,1)}, u32[]{:S(2)}, u32[]{:S(2)}) collective-permute-start(bf16[8,24,1024]{2,1,0:T(8,128)(2,1)S(1)} %get-tuple-element.157), channel_id=1, source_target_pairs={{4,0},{8,4},{12,8},{5,1},{9,5},{13,9},{6,2},{10,6},{14,10},{7,3},{... | collective-permute-start | bytes 1179656 | tf_op jit(solution)/shard_map/ppermute | solution.py:855
  24.9 7.8 %copy-start.16 = (bf16[8,24,1024]{2,1,0:T(8,128)(2,1)}, bf16[8,24,1024]{2,1,0:T(8,128)(2,1)S(1)}, u32[]{:S(2)}) copy-start(bf16[8,24,1024]{2,1,0:T(8,128)(2,1)S(1)} %collective-permute-done.up_ref) | copy-start | bytes 1179652
  32.8 5.2 %copy-start.27 = (bf16[3,3,1024]{2,1,0:T(4,128)(2,1)S(1)}, bf16[3,3,1024]{2,1,0:T(4,128)(2,1)}, u32[]{:S(2)}) copy-start(bf16[3,3,1024]{2,1,0:T(4,128)(2,1)} %param.18) | copy-start | bytes 55300
  32.8 39.7 %all-to-all-start = ((bf16[4,288,1024]{2,1,0:T(8,128)(2,1)}), bf16[4,288,1024]{2,1,0:T(8,128)(2,1)S(1)}, u32[]{:S(2)}, u32[]{:S(2)}) async-start(bf16[4,288,1024]{2,1,0:T(8,128)(2,1)} %cotangent_by_image.1), calls=%async_computation | async-start | bytes 4718592 | tf_op jit(solution)/shard_map/all_to_all | solution.py:871
  37.9 193.4 %reduce-scatter.4.cloned.1.call-start = ((), (), s32[]{:S(2)}) async-start(), calls=%async_computation.6 | async-start | bytes 7077888 | tf_op jit(solution)/shard_map/reduce_scatter | solution.py:900
  39.2 42.5 %copy-start.28 = (bf16[3,3,1024]{2,1,0:T(4,128)(2,1)S(1)}, bf16[3,3,1024]{2,1,0:T(4,128)(2,1)}, u32[]{:S(2)}) copy-start(bf16[3,3,1024]{2,1,0:T(4,128)(2,1)} %param.22) | copy-start | bytes 55300
  72.5 36.6 %copy-start = (bf16[4,288,1024]{2,1,0:T(8,128)(2,1)}, bf16[4,288,1024]{2,1,0:T(8,128)(2,1)S(1)}, u32[]{:S(2)}) copy-start(bf16[4,288,1024]{2,1,0:T(8,128)(2,1)S(1)} %all-to-all-done.cot) | copy-start | bytes 7077892
  72.5 10.3 %collective-permute-start.2 = (bf16[72,1024]{1,0:T(8,128)(2,1)}, bf16[72,1024]{1,0:T(8,128)(2,1)S(1)}, u32[]{:S(2)}, u32[]{:S(2)}) collective-permute-start(bf16[72,1024]{1,0:T(8,128)(2,1)} %get-tuple-element.88), channel_id=1, source_target_pairs={{0,0},{1,4},{2,8},{3,12},{4,1},{5,5},{6,9},{7,13},{8,2},{9,6},{10,... | collective-permute-start | bytes 442376 | tf_op jit(solution)/shard_map/ppermute | solution.py:878
  74.2 23.0 %collective-permute-start.3 = (bf16[72,1024]{1,0:T(8,128)(2,1)}, bf16[72,1024]{1,0:T(8,128)(2,1)S(1)}, u32[]{:S(2)}, u32[]{:S(2)}) collective-permute-start(bf16[72,1024]{1,0:T(8,128)(2,1)} %get-tuple-element.89), channel_id=1, source_target_pairs={{0,1},{1,5},{2,9},{3,13},{4,2},{5,6},{6,10},{7,14},{8,3},{9,7},{10... | collective-permute-start | bytes 442376 | tf_op jit(solution)/shard_map/ppermute | solution.py:878
  76.9 20.4 %collective-permute-start.4 = (bf16[72,1024]{1,0:T(8,128)(2,1)}, bf16[72,1024]{1,0:T(8,128)(2,1)S(1)}, u32[]{:S(2)}, u32[]{:S(2)}) collective-permute-start(bf16[72,1024]{1,0:T(8,128)(2,1)} %get-tuple-element.90), channel_id=1, source_target_pairs={{0,2},{1,6},{2,10},{3,14},{4,3},{5,7},{6,11},{7,15},{8,0},{9,4},{1... | collective-permute-start | bytes 442376 | tf_op jit(solution)/shard_map/ppermute | solution.py:878
  80.0 17.3 %collective-permute-start.5 = (bf16[72,1024]{1,0:T(8,128)(2,1)}, bf16[72,1024]{1,0:T(8,128)(2,1)S(1)}, u32[]{:S(2)}, u32[]{:S(2)}) collective-permute-start(bf16[72,1024]{1,0:T(8,128)(2,1)} %get-tuple-element.91), channel_id=1, source_target_pairs={{0,3},{1,7},{2,11},{3,15},{4,0},{5,4},{6,8},{7,12},{8,1},{9,5},{10... | collective-permute-start | bytes 442376 | tf_op jit(solution)/shard_map/ppermute | solution.py:878
  82.8 14.5 %copy-start.21 = (bf16[72,1024]{1,0:T(8,128)(2,1)}, bf16[72,1024]{1,0:T(8,128)(2,1)S(1)}, u32[]{:S(2)}) copy-start(bf16[72,1024]{1,0:T(8,128)(2,1)S(1)} %collective-permute-done.2.refs_0_) | copy-start | bytes 442372
  97.3 0.7 copy-start.22
  97.3 0.7 copy-start.23
  97.3 0.8 copy-start.24
  109.1 38.6 %collective-permute-start.6 = (bf16[288,1024]{1,0:T(8,128)(2,1)}, bf16[288,1024]{1,0:T(8,128)(2,1)S(1)}, u32[]{:S(2)}, u32[]{:S(2)}) collective-permute-start(bf16[288,1024]{1,0:T(8,128)(2,1)} %get-tuple-element.105.low_ref.refs_0_), channel_id=1, source_target_pairs={{0,1},{1,2},{2,3},{3,0},{4,5},{5,6},{6,7},{7,4},{8,9},{9,10},{10,1... | collective-permute-start | bytes 1769480 | tf_op jit(solution)/shard_map/ppermute | solution.py:882
  113.4 34.9 %collective-permute-start.7 = (bf16[288,1024]{1,0:T(8,128)(2,1)}, bf16[288,1024]{1,0:T(8,128)(2,1)S(1)}, u32[]{:S(2)}, u32[]{:S(2)}) collective-permute-start(bf16[288,1024]{1,0:T(8,128)(2,1)} %get-tuple-element.105.low_ref.refs_0_), channel_id=1, source_target_pairs={{0,2},{1,3},{2,0},{3,1},{4,6},{5,7},{6,4},{7,5},{8,10},{9,11},{10,... | collective-permute-start | bytes 1769480 | tf_op jit(solution)/shard_map/ppermute | solution.py:882
  118.1 32.0 %collective-permute-start.8 = (bf16[288,1024]{1,0:T(8,128)(2,1)}, bf16[288,1024]{1,0:T(8,128)(2,1)S(1)}, u32[]{:S(2)}, u32[]{:S(2)}) collective-permute-start(bf16[288,1024]{1,0:T(8,128)(2,1)} %get-tuple-element.105.low_ref.refs_0_), channel_id=1, source_target_pairs={{0,3},{1,0},{2,1},{3,2},{4,7},{5,4},{6,5},{7,6},{8,11},{9,8},{10,9... | collective-permute-start | bytes 1769480 | tf_op jit(solution)/shard_map/ppermute | solution.py:882
  143.2 13.2 %collective-permute-start.9 = (bf16[72,1024]{1,0:T(8,128)(2,1)}, bf16[72,1024]{1,0:T(8,128)(2,1)S(1)}, u32[]{:S(2)}, u32[]{:S(2)}) collective-permute-start(bf16[72,1024]{1,0:T(8,128)(2,1)} %get-tuple-element.103), channel_id=1, source_target_pairs={{0,0},{4,1},{8,2},{12,3},{1,4},{5,5},{9,6},{13,7},{2,8},{6,9},{10,... | collective-permute-start | bytes 442376 | tf_op jit(solution)/shard_map/ppermute | solution.py:888
  144.7 11.6 %collective-permute-start.10 = (bf16[72,1024]{1,0:T(8,128)(2,1)}, bf16[72,1024]{1,0:T(8,128)(2,1)S(1)}, u32[]{:S(2)}, u32[]{:S(2)}) collective-permute-start(bf16[72,1024]{1,0:T(8,128)(2,1)} %get-tuple-element.104), channel_id=1, source_target_pairs={{1,0},{5,1},{9,2},{13,3},{2,4},{6,5},{10,6},{14,7},{3,8},{7,9},{11... | collective-permute-start | bytes 442376 | tf_op jit(solution)/shard_map/ppermute | solution.py:888
  147.7 8.6 %copy-start.9 = (bf16[288,1024]{1,0:T(8,128)(2,1)}, bf16[288,1024]{1,0:T(8,128)(2,1)S(1)}, u32[]{:S(2)}) copy-start(bf16[288,1024]{1,0:T(8,128)(2,1)S(1)} %collective-permute-done.6.refs_1_) | copy-start | bytes 1769476
  147.7 19.5 %collective-permute-start.11 = (bf16[72,1024]{1,0:T(8,128)(2,1)}, bf16[72,1024]{1,0:T(8,128)(2,1)S(1)}, u32[]{:S(2)}, u32[]{:S(2)}) collective-permute-start(bf16[72,1024]{1,0:T(8,128)(2,1)} %get-tuple-element.110), channel_id=1, source_target_pairs={{2,0},{6,1},{10,2},{14,3},{3,4},{7,5},{11,6},{15,7},{0,8},{4,9},{8... | collective-permute-start | bytes 442376 | tf_op jit(solution)/shard_map/ppermute | solution.py:888
  148.3 8.1 %copy-start.10 = (bf16[288,1024]{1,0:T(8,128)(2,1)}, bf16[288,1024]{1,0:T(8,128)(2,1)S(1)}, u32[]{:S(2)}) copy-start(bf16[288,1024]{1,0:T(8,128)(2,1)S(1)} %collective-permute-done.7.refs_2_) | copy-start | bytes 1769476
  148.3 18.9 %collective-permute-start.12 = (bf16[72,1024]{1,0:T(8,128)(2,1)}, bf16[72,1024]{1,0:T(8,128)(2,1)S(1)}, u32[]{:S(2)}, u32[]{:S(2)}) collective-permute-start(bf16[72,1024]{1,0:T(8,128)(2,1)} %get-tuple-element.111), channel_id=1, source_target_pairs={{3,0},{7,1},{11,2},{15,3},{0,4},{4,5},{8,6},{12,7},{1,8},{5,9},{9,... | collective-permute-start | bytes 442376 | tf_op jit(solution)/shard_map/ppermute | solution.py:888
  150.1 6.3 %copy-start.11 = (bf16[288,1024]{1,0:T(8,128)(2,1)}, bf16[288,1024]{1,0:T(8,128)(2,1)S(1)}, u32[]{:S(2)}) copy-start(bf16[288,1024]{1,0:T(8,128)(2,1)S(1)} %collective-permute-done.8.refs_3_) | copy-start | bytes 1769476
  156.4 10.8 %copy-start.12 = (bf16[72,1024]{1,0:T(8,128)(2,1)}, bf16[72,1024]{1,0:T(8,128)(2,1)S(1)}, u32[]{:S(2)}) copy-start(bf16[72,1024]{1,0:T(8,128)(2,1)S(1)} %collective-permute-done.9.refs_0_) | copy-start | bytes 442372
  156.4 10.8 %copy-start.13 = (bf16[72,1024]{1,0:T(8,128)(2,1)}, bf16[72,1024]{1,0:T(8,128)(2,1)S(1)}, u32[]{:S(2)}) copy-start(bf16[72,1024]{1,0:T(8,128)(2,1)S(1)} %collective-permute-done.10.refs_1_) | copy-start | bytes 442372
  167.2 6.8 %copy-start.14 = (bf16[72,1024]{1,0:T(8,128)(2,1)}, bf16[72,1024]{1,0:T(8,128)(2,1)S(1)}, u32[]{:S(2)}) copy-start(bf16[72,1024]{1,0:T(8,128)(2,1)S(1)} %collective-permute-done.11.refs_2_) | copy-start | bytes 442372
  167.2 6.7 %copy-start.15 = (bf16[72,1024]{1,0:T(8,128)(2,1)}, bf16[72,1024]{1,0:T(8,128)(2,1)S(1)}, u32[]{:S(2)}) copy-start(bf16[72,1024]{1,0:T(8,128)(2,1)S(1)} %collective-permute-done.12.refs_3_) | copy-start | bytes 442372
  174.0 86.0 %reduce-scatter.6.cloned.1.call-start = ((), (), s32[]{:S(2)}) async-start(), calls=%async_computation.7 | async-start | bytes 983040 | tf_op jit(solution)/shard_map/reduce_scatter | solution.py:919
  174.1 27.8 %copy-start.29 = (bf16[8,144,1024]{2,1,0:T(8,128)(2,1)S(1)}, bf16[8,144,1024]{2,1,0:T(8,128)(2,1)}, u32[]{:S(2)}) copy-start(bf16[8,144,1024]{2,1,0:T(8,128)(2,1)} %get-tuple-element.125) | copy-start | bytes 7077892
  195.7 15.3 %collective-permute-start.13 = (bf16[8,24,1024]{2,1,0:T(8,128)(2,1)}, bf16[8,24,1024]{2,1,0:T(8,128)(2,1)S(1)}, u32[]{:S(2)}, u32[]{:S(2)}) collective-permute-start(bf16[8,24,1024]{2,1,0:T(8,128)(2,1)} %get-tuple-element.124), channel_id=1, source_target_pairs={{0,4},{4,8},{8,12},{1,5},{5,9},{9,13},{2,6},{6,10},{10,14},{3,7},{... | collective-permute-start | bytes 1179656 | tf_op jit(solution)/shard_map/ppermute | solution.py:905
  200.6 10.4 %collective-permute-start.14 = (bf16[8,24,1024]{2,1,0:T(8,128)(2,1)}, bf16[8,24,1024]{2,1,0:T(8,128)(2,1)S(1)}, u32[]{:S(2)}, u32[]{:S(2)}) collective-permute-start(bf16[8,24,1024]{2,1,0:T(8,128)(2,1)} %get-tuple-element.128), channel_id=1, source_target_pairs={{4,0},{8,4},{12,8},{5,1},{9,5},{13,9},{6,2},{10,6},{14,10},{7,3},{... | collective-permute-start | bytes 1179656 | tf_op jit(solution)/shard_map/ppermute | solution.py:906
  206.8 17.8 %copy-start.4 = (bf16[1024,1024]{1,0:T(8,128)(2,1)}, bf16[1024,1024]{1,0:T(8,128)(2,1)S(1)}, u32[]{:S(2)}) copy-start(bf16[1024,1024]{1,0:T(8,128)(2,1)S(1)} %bitcast_convert_fusion.refs_1_) | copy-start | bytes 6291460
  207.9 18.5 %copy-start.6 = (bf16[8,6,24,1024]{3,2,1,0:T(8,128)(2,1)S(1)}, bf16[8,6,24,1024]{3,2,1,0:T(8,128)(2,1)}, u32[]{:S(2)}) copy-start(bf16[8,6,24,1024]{3,2,1,0:T(8,128)(2,1)} %feat.1) | copy-start | bytes 7077892
  207.9 29.0 %collective-permute-start.16 = (bf16[512,1024]{1,0:T(8,128)(2,1)}, bf16[512,1024]{1,0:T(8,128)(2,1)S(1)}, u32[]{:S(2)}, u32[]{:S(2)}) collective-permute-start(bf16[512,1024]{1,0:T(8,128)(2,1)} %dynamic-slice_bitcast_fusion), channel_id=1, source_target_pairs={{0,16},{16,0},{1,17},{17,1},{2,18},{18,2},{3,19},{19,3},{4,20},{20... | collective-permute-start | bytes 3145736 | tf_op jit(solution)/shard_map/ppermute | solution.py:670
  211.0 0.7 copy-start.17
  211.7 0.7 copy-start.18
  231.2 8.0 %copy-start.5 = (bf16[1024,1024]{1,0:T(8,128)(2,1)}, bf16[1024,1024]{1,0:T(8,128)(2,1)S(1)}, u32[]{:S(2)}) copy-start(bf16[1024,1024]{1,0:T(8,128)(2,1)S(1)} %convolution_convert_fusion.refs_0_) | copy-start | bytes 6291460
  231.3 5.5 %copy-start.19 = (f32[160,128]{1,0:T(8,128)S(1)}, f32[160,128]{1,0:T(8,128)}, u32[]{:S(2)}) copy-start(f32[160,128]{1,0:T(8,128)} %small_rows.1.refs_4_) | copy-start | bytes 245764
  234.2 4.9 %collective-permute-start.15 = (bf16[512,1024]{1,0:T(8,128)(2,1)S(1)}, bf16[512,1024]{1,0:T(8,128)(2,1)S(1)}, u32[]{:S(2)}, u32[]{:S(2)}) collective-permute-start(bf16[512,1024]{1,0:T(8,128)(2,1)S(1)} %dynamic-slice_bitcast_fusion.1), channel_id=1, source_target_pairs={{0,16},{16,0},{1,17},{17,1},{2,18},{18,2},{3,19},{19,3},{4,20},{20... | collective-permute-start | bytes 3145736 | tf_op jit(solution)/shard_map/ppermute | solution.py:670
  236.8 2.4 collective-permute-start.17
  236.9 2.3 copy-start.7
  239.1 1.0 copy-start.8
  239.2 0.9 copy-start.26
  244.1 36.7 %all-to-all-start.1 = ((bf16[64,8,2176]{2,1,0:T(8,128)(2,1)}), bf16[64,8,2176]{2,1,0:T(8,128)(2,1)S(1)}, u32[]{:S(2)}, u32[]{:S(2)}) async-start(bf16[64,8,2176]{2,1,0:T(8,128)(2,1)} %bitcast.63), calls=%async_computation.2 | async-start | bytes 4456448 | tf_op jit(solution)/shard_map/all_to_all | solution.py:921
  251.5 46.9 %reduce-scatter.8.cloned.1.call-start = ((), (), s32[]{:S(2)}) async-start(), calls=%async_computation.8 | async-start | bytes 491520 | tf_op jit(solution)/shard_map/reduce_scatter | solution.py:929
  280.8 1.4 copy-start.2
  286.6 36.9 %all-to-all-start.2 = ((bf16[64,8,2176]{2,1,0:T(8,128)(2,1)}), bf16[64,8,2176]{2,1,0:T(8,128)(2,1)S(1)}, u32[]{:S(2)}, u32[]{:S(2)}) async-start(bf16[64,8,2176]{2,1,0:T(8,128)(2,1)} %sum_and_copy.1), calls=%async_computation.4 | async-start | bytes 4456448 | tf_op jit(solution)/shard_map/all_to_all | solution.py:931
  295.1 73.3 %all-gather.4.cloned.1.call-start = ((), (), s32[]{:S(2)}) async-start(), calls=%async_computation.9 | async-start | bytes 1671168 | tf_op jit(solution)/shard_map/all_gather | solution.py:932
  323.5 46.5 %copy-start.1 = (bf16[64,8,2176]{2,1,0:T(8,128)(2,1)}, bf16[64,8,2176]{2,1,0:T(8,128)(2,1)S(1)}, u32[]{:S(2)}) copy-start(bf16[64,8,2176]{2,1,0:T(8,128)(2,1)S(1)} %all-to-all-done.2) | copy-start | bytes 6684676
  323.5 54.2 %collective-permute-start.18 = (bf16[512,2176]{1,0:T(8,128)(2,1)S(1)}, bf16[512,2176]{1,0:T(8,128)(2,1)}, u32[]{:S(2)}, u32[]{:S(2)}) collective-permute-start(bf16[512,2176]{1,0:T(8,128)(2,1)S(1)} %bitcast.61), channel_id=1, source_target_pairs={{0,16},{16,0},{1,17},{17,1},{2,18},{18,2},{3,19},{19,3},{4,20},{20... | collective-permute-start | bytes 6684680 | tf_op jit(solution)/shard_map/ppermute | solution.py:670
  368.3 16.7 %collective-permute-start.19 = (bf16[4,32,6144]{2,1,0:T(8,128)(2,1)}, bf16[4,32,6144]{2,1,0:T(8,128)(2,1)}, u32[]{:S(2)}, u32[]{:S(2)}) collective-permute-start(bf16[4,32,6144]{2,1,0:T(8,128)(2,1)} %bitcast.71), channel_id=1, source_target_pairs={{0,16},{16,0},{1,17},{17,1},{2,18},{18,2},{3,19},{19,3},{4,20},{20... | collective-permute-start | bytes 4718600 | tf_op jit(solution)/shard_map/ppermute | solution.py:670
  377.7 3.9 copy-start.20
Sparse Core Ops, SparseCore 0:
  11.5 43.3 all-gather.5
  174.1 45.3 reduce-scatter.3
  234.3 21.9 reduce-scatter.5
  262.8 35.5 reduce-scatter.7
  300.6 67.6 all-gather.3

commit v9 on v8

--- a/solution.py
+++ b/solution.py
@@ -700,24 +700,27 @@
     width = len(mine) * ch + LANES
     count = small.shape[0]
     m = len(mine)
+    steps = 2
+    block = half // steps
 
     def kernel(core_ref, *refs):
         own, got = refs[:m], refs[m : 2 * m]
         sm, got_sm, out = refs[2 * m :]
         for i in range(m):
             out[:, i * ch : (i + 1) * ch] = (own[i][...].astype(F32) + got[i][...].astype(F32)).astype(BF)
-        first = (core_ref[0] == 0).astype(F32)
+        first = ((core_ref[0] == 0) & (pl.program_id(0) == 0)).astype(F32)
         total = (sm[...] + got_sm[...]) * first
-        pad = jnp.zeros((half - count, LANES), F32)
+        pad = jnp.zeros((block - count, LANES), F32)
         out[:, m * ch :] = jnp.concatenate([total, pad], 0).astype(BF)
 
     return call(
         kernel,
-        grid=(1,),
+        grid=(steps,),
         prefetch=1,
-        ins=[(v, (half, ch), lambda i, c: (c[0], 0)) for v in mine]
-        + [(v, None, None) for v in (*theirs, small, their_small)],
-        outs=[(shape((half, width), BF), None, None)],
+        ins=[(v, (block, ch), lambda i, c: (c[0] * steps + i, 0)) for v in mine]
+        + [(v, (block, ch), lambda i, c: (i, 0)) for v in theirs]
+        + [(v, None, None) for v in (small, their_small)],
+        outs=[(shape((half, width), BF), (block, width), lambda i, c: (i, 0))],
         name="join_halves",
     )(core)[0].reshape(parts, half // parts, width)
 
@@ -741,9 +744,35 @@
     )()[0]
 
 
+def sum_parts(blocks, n):
+    parts, rows, width = blocks.shape
+    ch = width // 3
+
+    def kernel(x, out):
+        for lanes in range(0, width, ch):
+            for at in range(lanes, lanes + ch, 2 * LANES):
+                cut = slice(at, at + 2 * LANES)
+                by_chan = [sum(x[p, :, cut].astype(F32) for p in range(c, parts, n)) for c in range(n)]
+                if lanes < 2 * ch:
+                    out[:, cut] = sum(by_chan).astype(BF)
+                else:
+                    for c in range(n):
+                        out[:, at + c * ch : at + c * ch + 2 * LANES] = by_chan[c].astype(BF)
+
+    return call(
+        kernel,
+        grid=(1,),
+        ins=[(blocks, None, None)],
+        outs=[(shape((rows, 2 * ch + n * ch), BF), None, None)],
+        name="sum_parts",
+    )()[0]
+
+
 def finish_pre(place, half_rows, ch, earlier=()):
     half, width = half_rows.shape
     m = (width - LANES) // ch
+    steps = 4
+    block = half // steps
 
     def kernel(place_ref, x, *outs):
         outs = outs[len(earlier) :]
@@ -753,11 +782,11 @@
 
     return call(
         kernel,
-        grid=(1,),
+        grid=(steps,),
         prefetch=1,
-        ins=[(half_rows, None, None)],
-        outs=[(shape((2 * half, ch), F32), (half, ch), lambda i, c: (c[0], 0)) for _ in range(m)]
-        + [(shape((half, LANES), F32), None, None)],
+        ins=[(half_rows, (block, width), lambda i, c: (i, 0))],
+        outs=[(shape((2 * half, ch), F32), (block, ch), lambda i, c: (c[0] * steps + i, 0)) for _ in range(m)]
+        + [(shape((half, LANES), F32), (block, LANES), lambda i, c: (i, 0))],
         aliased=earlier,
         name="finish_pre",
     )(place)
@@ -916,17 +945,13 @@
     theirs = [other_core(lax.dynamic_index_in_dim(g.reshape(2, ch // 2, ch), 1 - core, 0, keepdims=False)) for g in mine]
     rest = after(rest, *mine).reshape(n, 4, eight, 3 * ch).transpose(1, 0, 2, 3)
     theirs = after(theirs, rest)
-    rest = lax.psum_scatter(rest, "rows", scatter_dimension=0, tiled=False)
+    rest = lax.all_to_all(rest.reshape(4 * n, eight, 3 * ch), ("rows", "chan"), 0, 0, tiled=False)
     load = join_halves(core_at, mine, theirs, small, other_core(small), 64)
     pieces = lax.all_to_all(load, chips, 0, 0, tiled=False)
     feature_grad = feature_backward(order, after(reduced_grad, load), pre_reduce, returned, up_m).reshape(features.shape)
 
-    rest = after(rest, feature_grad)
-    block_at = lax.broadcasted_iota(jnp.int32, (1, 1, n * ch), 2) // ch
-    padded = jnp.where(block_at == chan, jnp.tile(rest[:, :, 2 * ch :], (1, 1, n)), jnp.zeros((), BF))
-    rest = jnp.concatenate([rest[:, :, : 2 * ch], padded], axis=2)
+    rest = sum_parts(after(rest, feature_grad), n)
     pieces = after(pieces, rest)
-    rest = lax.psum_scatter(rest, "chan", scatter_dimension=0, tiled=False)
     load = sum_and_copy(pieces)
     load_all = lax.all_to_all(load, chips, 0, 0, tiled=False).reshape(ch // 2, -1)
     rest = lax.all_gather(rest, ("x", "rows"), axis=0, tiled=False).reshape(4, 4 * eight, -1)

time: 397 us -> 387 us (0.975)
  waiting for transfers between devices: 117 us -> 102 us
  starting transfers between devices: 69.8 us -> 75.1 us
    all_gather x1, waiting for transfers between devices: 41.3 us -> 21 us  [body(): lax.all_gather(rest, ('x', 'rows'), axis=0, tiled=False)]
    all_to_all x0 -> x1, waiting for transfers between devices: none -> 7.02 us  [body(): lax.all_to_all(rest.reshape(4 * n, eight, 3 * ch), ('rows', 'chan'), 0, 0...]
    pallas_call x18 -> x19, Pallas kernels: 155 us -> 157 us  [run(): pl.pallas_call(kernel, grid_spec=pltpu.PrefetchScalarGridSpec(num_scalar_...]
  transfers between devices with their start and end apart: 28 -> 27, of which waited for: 9 -> 8; matrix products, arithmetic and copies ran while one was open for 8% -> 7% of each run, Pallas kernels for 34% -> 34%
where the time goes in v9:
time: 387 us; the launch traced here: 385 us
  Pallas kernels  157 us (41%)
  waiting for transfers between devices  102 us (26%)
  starting transfers between devices  75.1 us (19%)
  local copies, waits for them, and re-layouts  17.2 us (4%)
  matrix products  15.5 us (4%)
  between operations  14.1 us (4%)
  other arithmetic  4.29 us (1%)
    pallas_call x19, Pallas kernels, run(): pl.pallas_call(kernel, grid_spec=pltpu.PrefetchScalarGridSpec(num_scalar_...  157 us
    all_to_all x1, waiting for transfers between devices, body(): lax.all_to_all(load, chips, 0, 0, tiled=False).reshape(ch // 2, -1)  28.3 us
    all_gather x1, waiting for transfers between devices, body(): lax.all_gather(rest, ('x', 'rows'), axis=0, tiled=False)  21 us
    all_to_all x1, waiting for transfers between devices, body(): pieces = lax.all_to_all(load, chips, 0, 0, tiled=False)  17.3 us
    dot_general x3, matrix products, dot(): return lax.dot_general(a, b, (dims, ((), ())), preferred_element_type=F32)  15.5 us
    ppermute x4, waiting for transfers between devices, body(): lax.ppermute(pooled[k], ('rows', 'chan'), spread(n, k))  14.5 us
    ppermute x5, starting transfers between devices, other_core(): return lax.ppermute(values, 'core', [(0, 1), (1, 0)])  12 us
    ppermute x3, starting transfers between devices, body(): lax.ppermute(low, 'chan', [(i, (i + k) % n) for i in range(n)])  11 us
  transfers between devices with their start and end apart: 27, of which 8 were waited for; matrix products, arithmetic and copies ran while one was open for 7% of the time, Pallas kernels for 34%

profile of v9, /device:TPU:1, one launch (start us, length us, event | category | flops | bytes accessed | tf_op | source)
XLA Modules:
  0.0 385.1 jit_solution(10996338262580293099)
XLA Ops:
  7.2 0.8 subtract_convert_fusion
  8.0 1.1 fusion.6
  9.2 1.3 fusion.3
  10.5 0.9 constant_dynamic-slice_fusion
  11.4 1.2 slice_bitcast_fusion
  12.6 4.1 %collective-permute-start = (bf16[8,24,1024]{2,1,0:T(8,128)(2,1)S(1)}, bf16[8,24,1024]{2,1,0:T(8,128)(2,1)S(1)}, u32[]{:S(2)}, u32[]{:S(2)}) collective-permute-start(bf16[8,24,1024]{2,1,0:T(8,128)(2,1)S(1)} %get-tuple-element.158), channel_id=1, source_target_pairs={{0,4},{4,8},{8,12},{1,5},{5,9},{9,13},{2,6},{6,10},{10,14},{3,7},{... | collective-permute-start | bytes 1179656 | tf_op jit(solution)/shard_map/ppermute | solution.py:883
  16.6 1.3 collective-permute-start.1
  19.1 5.9 %fusion.1.red = f32[8,144,1024]{2,1,0:T(8,128)} fusion(bf16[8,144,1024]{2,1,0:T(8,128)(2,1)} %bitcast.64, bf16[1024,1024]{1,0:T(8,128)(2,1)S(1)} %copy-done.3), kind=kOutput, calls=%fused_computation.3 | convolution fusion | flops 2415919104 | bytes 9175040 | tf_op jit(solution)/shard_map/dot_general | solution.py:23
  24.9 3.4 collective-permute-done.1.down_ref
  28.3 4.4 %cotangent_by_image.1 = bf16[4,288,1024]{2,1,0:T(8,128)(2,1)} custom-call(bf16[1152,1024]{1,0:T(8,128)(2,1)} %bitcast.56, bf16[128,128]{1,0:T(8,128)(2,1)} %copy.38.sel), custom_call_target="tpu_custom_call" | custom-call | flops 1 | bytes 1 | tf_op jit(solution)/shard_map/cotangent_by_image/pallas_call | solution.py:67
  32.8 5.2 %all-to-all-start = ((bf16[4,288,1024]{2,1,0:T(8,128)(2,1)}), bf16[4,288,1024]{2,1,0:T(8,128)(2,1)S(1)}, u32[]{:S(2)}, u32[]{:S(2)}) async-start(bf16[4,288,1024]{2,1,0:T(8,128)(2,1)} %cotangent_by_image.1), calls=%async_computation | async-start | bytes 4718592 | tf_op jit(solution)/shard_map/all_to_all | solution.py:900
  39.1 24.8 %pre_forward.1 = (f32[8,144,1024]{2,1,0:T(8,128)}, bf16[8,144,1024]{2,1,0:T(8,128)(2,1)}, f32[8,144,1024]{2,1,0:T(8,128)}, f32[8,144,1]{2,1,0:T(8,128)}, bf16[72...) custom-call(s32[4]{0:T(128)} %and_select_fusion.order_ref, ...), custom_call_target="tpu_custom_call" | custom-call | flops 1 | bytes 1 | tf_op jit(solution)/shard_map/pre_forward/pallas_call | solution.py:67
  64.0 8.6 %all-to-all-done.cot = bf16[4,288,1024]{2,1,0:T(8,128)(2,1)S(1)} async-done(((bf16[4,288,1024]{2,1,0:T(8,128)(2,1)}), bf16[4,288,1024]{2,1,0:T(8,128)(2,1)S(1)}, u32[]{:S(2)}, u32[]{:S(2)}) %all-to-all-start) | async-done | bytes 2359328 | tf_op jit(solution)/shard_map/all_to_all | solution.py:900
  72.5 1.7 collective-permute-start.2
  74.2 2.6 collective-permute-start.3
  76.9 3.1 collective-permute-start.4
  80.0 1.7 collective-permute-start.5
  82.8 14.5 %collective-permute-done.3.refs_1_ = bf16[72,1024]{1,0:T(8,128)(2,1)S(1)} collective-permute-done((bf16[72,1024]{1,0:T(8,128)(2,1)}, bf16[72,1024]{1,0:T(8,128)(2,1)S(1)}, u32[]{:S(2)}, u32[]{:S(2)}) %collective-permute-start.3) | collective-permute-done | bytes 147488 | tf_op jit(solution)/shard_map/ppermute | solution.py:907
  98.0 11.1 %post_forward.1 = (bf16[288,1024]{1,0:T(8,128)(2,1)}, f32[288,1024]{1,0:T(8,128)}, bf16[288,1024]{1,0:T(8,128)(2,1)}, f32[288,1024]{1,0:T(8,128)}, bf16[288,1024...) custom-call(s32[4]{0:T(128)} %and_select_fusion.1.src, ...), custom_call_target="tpu_custom_call" | custom-call | flops 1 | bytes 1 | tf_op jit(solution)/shard_map/post_forward/pallas_call | solution.py:67
  109.1 4.3 %collective-permute-start.6 = (bf16[288,1024]{1,0:T(8,128)(2,1)}, bf16[288,1024]{1,0:T(8,128)(2,1)S(1)}, u32[]{:S(2)}, u32[]{:S(2)}) collective-permute-start(bf16[288,1024]{1,0:T(8,128)(2,1)} %get-tuple-element.105.low_ref.refs_0_), channel_id=1, source_target_pairs={{0,1},{1,2},{2,3},{3,0},{4,5},{5,6},{6,7},{7,4},{8,9},{9,10},{10,1... | collective-permute-start | bytes 1769480 | tf_op jit(solution)/shard_map/ppermute | solution.py:911
  113.4 4.7 %collective-permute-start.7 = (bf16[288,1024]{1,0:T(8,128)(2,1)}, bf16[288,1024]{1,0:T(8,128)(2,1)S(1)}, u32[]{:S(2)}, u32[]{:S(2)}) collective-permute-start(bf16[288,1024]{1,0:T(8,128)(2,1)} %get-tuple-element.105.low_ref.refs_0_), channel_id=1, source_target_pairs={{0,2},{1,3},{2,0},{3,1},{4,6},{5,7},{6,4},{7,5},{8,10},{9,11},{10,... | collective-permute-start | bytes 1769480 | tf_op jit(solution)/shard_map/ppermute | solution.py:911
  118.1 2.0 collective-permute-start.8
  120.1 10.9 %readout_backward.1.rg = f32[288,1024]{1,0:T(8,128)} custom-call(bf16[288,1024]{1,0:T(8,128)(2,1)} %get-tuple-element.105.low_ref.refs_0_, bf16[1024,4096]{1,0:T(8,128)(2,1)} %refs_5_.1, bf16[4,288,1024]{2,1,0:T(8,128)(2,1)} %copy-done), custom_call_target="tpu_custom_call" | custom-call | flops 1 | bytes 1 | tf_op jit(solution)/shard_map/readout_backward/pallas_call | solution.py:67
  130.9 12.2 %post_backward.1 = (bf16[288,1024]{1,0:T(8,128)(2,1)}, bf16[288,1024]{1,0:T(8,128)(2,1)}, f32[9,8,1024]{2,1,0:T(8,128)}, f32[8,1024]{1,0:T(8,128)}, bf16[72,1024...) custom-call(s32[4]{0:T(128)} %and_select_fusion.1.src, ...), custom_call_target="tpu_custom_call" | custom-call | flops 1 | bytes 1 | tf_op jit(solution)/shard_map/post_backward/pallas_call | solution.py:67
  143.2 1.6 collective-permute-start.9
  144.7 3.0 collective-permute-start.10
  148.3 1.0 collective-permute-start.12
  149.3 0.8 broadcast_in_dim_tile.5.refs_7_
  150.1 6.3 %post_weight_grads.1.old = bf16[8,4,32,3072]{3,2,1,0:T(8,128)(2,1)} custom-call(bf16[288,1024]{1,0:T(8,128)(2,1)} %get-tuple-element.94.x, bf16[288,1024]{1,0:T(8,128)(2,1)} %get-tuple-element.100.g, bf16[288,1024]{1,0:T(8,128)(2,1)} %get-tuple-element.101.a, bf16[288,1024]{1,0:T(8,128)(2,1)} %get-tuple-element.102.e), custom_call_target="tpu_custom_call" | custom-call | flops 1 | bytes 1 | tf_op jit(solution)/shard_map/post_weight_grads/pallas_call | solution.py:67
  156.5 10.8 %token_block.1 = (bf16[1152,1024]{1,0:T(8,128)(2,1)}, bf16[1152,1024]{1,0:T(8,128)(2,1)}, bf16[1152,1024]{1,0:T(8,128)(2,1)}) custom-call(s32[1]{0:T(128)} %bitcast.chan_ref, s32[4]{0:T(128)} %and_select_fusion.1.src, bf16[288,1024]{1,0:T(8,128)(2,1)} %get-tuple-element.105.low_ref.refs_0_, bf16[288,1024]{1,0:T(8,128)(2,1)} %copy-done.8, ...), custom_call_target="tpu_custom_call" | custom-call | flops 1 | bytes 1 | tf_op jit(solution)/shard_map/token_block/pallas_call | solution.py:67
  167.3 6.7 %readout_weight_grad.1 = bf16[8,4,32,3072]{3,2,1,0:T(8,128)(2,1)} custom-call(bf16[1152,1024]{1,0:T(8,128)(2,1)} %get-tuple-element.112.x, bf16[1152,1024]{1,0:T(8,128)(2,1)} %get-tuple-element.114.g, bf16[8,4,32,3072]{3,2,1,0:T(8,128)(2,1)} %post_weight_grads.1.old), custom_call_target="tpu_custom_call", output_to_operand_aliasing={{}: (2, {})} | custom-call | flops 1 | bytes 1 | tf_op jit(solution)/shard_map/readout_weight_grad/pallas_call | solution.py:67
  174.1 21.6 %pre_backward.1 = (bf16[8,144,1024]{2,1,0:T(8,128)(2,1)}, bf16[8,144,1024]{2,1,0:T(8,128)(2,1)}, bf16[8,24,1024]{2,1,0:T(8,128)(2,1)}, bf16[8,24,1024]{2,1,0:T(8,128)(2,1)}, f32[8,1024]{1,0:T(8,128)}) custom-call(s32[4]{0:T(128)} %and_select_fusion.order_ref, bf16[72,1024]{1,0:T(8,128)(2,1)} %copy-done.11, bf16[72,1024]{1,0:T(8,128)(2,1)} %copy-done.12, ...), custom_call_target="tpu_custom_call" | custom-call | flops 1 | bytes 1 | tf_op jit(solution)/shard_map/pre_backward/pallas_call | solution.py:67
  195.7 4.9 %collective-permute-start.13 = (bf16[8,24,1024]{2,1,0:T(8,128)(2,1)}, bf16[8,24,1024]{2,1,0:T(8,128)(2,1)S(1)}, u32[]{:S(2)}, u32[]{:S(2)}) collective-permute-start(bf16[8,24,1024]{2,1,0:T(8,128)(2,1)} %get-tuple-element.124), channel_id=1, source_target_pairs={{0,4},{4,8},{8,12},{1,5},{5,9},{9,13},{2,6},{6,10},{10,14},{3,7},{... | collective-permute-start | bytes 1179656 | tf_op jit(solution)/shard_map/ppermute | solution.py:934
  200.6 1.3 collective-permute-start.14
  201.9 4.9 %bitcast_convert_fusion.refs_1_ = bf16[1024,1024]{1,0:T(8,128)(2,1)S(1)} fusion(bf16[8,144,1024]{2,1,0:T(8,128)(2,1)S(1)} %copy-done.28, bf16[8,144,1024]{2,1,0:T(8,128)(2,1)} %get-tuple-element.126), kind=kOutput, calls=%fused_computation | convolution fusion | flops 2416967680 | bytes 6815744 | tf_op jit(solution)/shard_map/dot_general | solution.py:23
  206.8 1.1 dynamic-slice_bitcast_fusion
  207.9 3.0 collective-permute-start.16
  211.7 0.7 copy-done.17
  212.5 12.1 %pre_conv_backward.1 = (bf16[8,144,1024]{2,1,0:T(8,128)(2,1)}, f32[9,8,1024]{2,1,0:T(8,128)}) custom-call(bf16[8,144,1024]{2,1,0:T(8,128)(2,1)} %get-tuple-element.127.cg, bf16[8,24,1024]{2,1,0:T(8,128)(2,1)} %copy-done.16, bf16[8,24,1024]{2,1,0:T(8,128)(2,1)} %copy-done.17, f32[8,144,1024]{2,1,0:T(8,128)} %fusion.1.red, f32[9,1024]{1,0:T(8,128)} %reshape.160.tap), custom_call_target="tpu_custom_call" | custom-call | flops 1 | bytes 1 | tf_op jit(solution)/shard_map/pre_conv_backward/pallas_call | solution.py:67
  224.6 1.8 small_rows.1.refs_4_
  226.5 4.8 %convolution_convert_fusion.refs_0_ = bf16[1024,1024]{1,0:T(8,128)(2,1)S(1)} fusion(bf16[1152,1024]{1,0:T(8,128)(2,1)S(1)} %bitcast.65, bf16[1152,1024]{1,0:T(8,128)(2,1)} %bitcast.68), kind=kOutput, calls=%fused_computation.5 | convolution fusion | flops 2416967680 | bytes 6815744 | tf_op jit(solution)/shard_map/dot_general | solution.py:23
  231.3 1.0 dynamic-slice_bitcast_fusion.1
  232.3 2.5 collective-permute-start.15
  234.9 2.1 copy.40
  236.9 4.0 %all-to-all-start.2 = ((bf16[16,8,3072]{2,1,0:T(8,128)(2,1)}), bf16[16,8,3072]{2,1,0:T(8,128)(2,1)S(1)}, u32[]{:S(2)}, u32[]{:S(2)}) async-start(bf16[16,8,3072]{2,1,0:T(8,128)(2,1)} %bitcast.66), calls=%async_computation.3 | async-start | bytes 1572864 | tf_op jit(solution)/shard_map/all_to_all | solution.py:948
  241.5 0.9 collective-permute-done.17.refs_5_
  243.1 3.4 join_halves.1
  246.5 7.0 %all-to-all-done.2.x = bf16[16,8,3072]{2,1,0:T(8,128)(2,1)S(1)} async-done(((bf16[16,8,3072]{2,1,0:T(8,128)(2,1)}), bf16[16,8,3072]{2,1,0:T(8,128)(2,1)S(1)}, u32[]{:S(2)}, u32[]{:S(2)}) %all-to-all-start.2) | async-done | bytes 786464 | tf_op jit(solution)/shard_map/all_to_all | solution.py:948
  253.5 7.9 %all-to-all-start.1 = ((bf16[64,8,2176]{2,1,0:T(8,128)(2,1)}), bf16[64,8,2176]{2,1,0:T(8,128)(2,1)S(1)}, u32[]{:S(2)}, u32[]{:S(2)}) async-start(bf16[64,8,2176]{2,1,0:T(8,128)(2,1)} %bitcast.60), calls=%async_computation.2 | async-start | bytes 4456448 | tf_op jit(solution)/shard_map/all_to_all | solution.py:950
  261.4 8.5 %feature_backward.1 = f32[8,144,1024]{2,1,0:T(8,128)} custom-call(s32[4]{0:T(128)} %and_select_fusion.order_ref, bf16[8,144,1024]{2,1,0:T(8,128)(2,1)} %get-tuple-element.138.rg, bf16[1024,1024]{1,0:T(8,128)(2,1)} %wr.3, bf16[288,72]{1,0:T(8,128)(2,1)} %constant.64.clone.refs_4_.up, bf16[72,1024]{1,0:T(8,128)(2,1)} %copy-done.11, ...), custom_call_target="tpu_custom_call" | custom-call | flops 1 | bytes 1 | tf_op jit(solution)/shard_map/feature_backward/pallas_call | solution.py:67
  269.9 1.9 sum_parts.1
  271.8 17.3 %all-to-all-done.1.x = bf16[64,8,2176]{2,1,0:T(8,128)(2,1)S(1)} async-done(((bf16[64,8,2176]{2,1,0:T(8,128)(2,1)}), bf16[64,8,2176]{2,1,0:T(8,128)(2,1)S(1)}, u32[]{:S(2)}, u32[]{:S(2)}) %all-to-all-start.1) | async-done | bytes 2228256 | tf_op jit(solution)/shard_map/all_to_all | solution.py:950
  289.1 1.4 copy-done.2
  290.4 4.4 %sum_and_copy.1 = bf16[64,8,2176]{2,1,0:T(8,128)(2,1)} custom-call(bf16[64,8,2176]{2,1,0:T(8,128)(2,1)} %copy-done.2), custom_call_target="tpu_custom_call" | custom-call | flops 1 | bytes 1 | tf_op jit(solution)/shard_map/sum_and_copy/pallas_call | solution.py:67
  294.9 8.3 %all-to-all-start.3 = ((bf16[64,8,2176]{2,1,0:T(8,128)(2,1)}), bf16[64,8,2176]{2,1,0:T(8,128)(2,1)S(1)}, u32[]{:S(2)}, u32[]{:S(2)}) async-start(bf16[64,8,2176]{2,1,0:T(8,128)(2,1)} %sum_and_copy.1), calls=%async_computation.4 | async-start | bytes 4456448 | tf_op jit(solution)/shard_map/all_to_all | solution.py:956
  303.9 28.3 %all-to-all-done.3 = bf16[64,8,2176]{2,1,0:T(8,128)(2,1)S(1)} async-done(((bf16[64,8,2176]{2,1,0:T(8,128)(2,1)}), bf16[64,8,2176]{2,1,0:T(8,128)(2,1)S(1)}, u32[]{:S(2)}, u32[]{:S(2)}) %all-to-all-start.3) | async-done | bytes 2228256 | tf_op jit(solution)/shard_map/all_to_all | solution.py:956
  332.2 4.2 %collective-permute-start.18 = (bf16[512,2176]{1,0:T(8,128)(2,1)S(1)}, bf16[512,2176]{1,0:T(8,128)(2,1)}, u32[]{:S(2)}, u32[]{:S(2)}) collective-permute-start(bf16[512,2176]{1,0:T(8,128)(2,1)S(1)} %bitcast.58), channel_id=1, source_target_pairs={{0,16},{16,0},{1,17},{17,1},{2,18},{18,2},{3,19},{19,3},{4,20},{20... | collective-permute-start | bytes 6684680 | tf_op jit(solution)/shard_map/ppermute | solution.py:670
  336.3 21.0 %all-gather.7.cloned.1.call-done = bf16[128,6144]{1,0:T(8,128)(2,1)} async-done(((bf16[8,6144]{1,0:T(8,128)(2,1)}), bf16[128,6144]{1,0:T(8,128)(2,1)}) %all-gather.7.cloned.1.call-update) | async-done | bytes 1572880 | tf_op jit(solution)/shard_map/all_gather | solution.py:957
  357.3 1.6 collective-permute-start.19
  358.9 4.2 %finish_pre.2 = (f32[1024,1024]{1,0:T(8,128)}, f32[1024,1024]{1,0:T(8,128)}, f32[512,128]{1,0:T(8,128)}) custom-call(s32[1]{0:T(128)} %bitcast.14.core_ref.place_ref, bf16[512,2176]{1,0:T(8,128)(2,1)} %bitcast.59), custom_call_target="tpu_custom_call" | custom-call | flops 1 | bytes 1 | tf_op jit(solution)/shard_map/finish_pre/pallas_call | solution.py:67
  363.1 3.9 %finish_post.2 = (f32[256,1024]{1,0:T(8,128)}, f32[4,256,256]{2,1,0:T(8,128)}, f32[256,4096]{1,0:T(8,128)}) custom-call(s32[1]{0:T(128)} %bitcast.14.core_ref.place_ref, bf16[4,32,6144]{2,1,0:T(8,128)(2,1)} %bitcast.70), custom_call_target="tpu_custom_call" | custom-call | flops 1 | bytes 1 | tf_op jit(solution)/shard_map/finish_post/pallas_call | solution.py:67
  367.0 4.2 %finish_pre.3 = (f32[1024,1024]{1,0:T(8,128)}, f32[1024,1024]{1,0:T(8,128)}, f32[512,128]{1,0:T(8,128)}) custom-call(s32[1]{0:T(128)S(6)} %sub.21.place_ref, bf16[512,2176]{1,0:T(8,128)(2,1)} %collective-permute-done.18.x, f32[1024,1024]{1,0:T(8,128)} %get-tuple-element.141.outs_0_, ...), custom_call_target="tpu_custom_call", output_to_operand_aliasing={{0}: (2, {}), {1}: (3, {})} | custom-call | flops 1 | bytes 1 | tf_op jit(solution)/shard_map/finish_pre/pallas_call | solution.py:67
  371.2 1.0 broadcast_select_fusion
  374.7 3.8 finish_post.3
  (105 shorter events, 10.1 us)
Async XLA Ops:
  7.2 90.1 %all-gather.5.cloned.1.call-start = ((), (), s32[]{:S(2)}) async-start(), calls=%async_computation.6 | async-start | bytes 5308416 | tf_op jit(solution)/shard_map/all_gather | solution.py:893
  9.2 8.8 %copy-start.29 = (s32[2]{0:T(128)S(1)}, s32[2]{0:T(128)}, u32[]{:S(2)}) copy-start(s32[2]{0:T(128)} %param.16) | copy-start | bytes 28
  9.2 9.1 %copy-start.24 = (bf16[128,128]{1,0:T(8,128)(2,1)S(1)}, bf16[128,128]{1,0:T(8,128)(2,1)}, u32[]{:S(2)}) copy-start(bf16[128,128]{1,0:T(8,128)(2,1)} %constant.65.clone.refs_4_) | copy-start | bytes 98308
  9.2 9.9 %copy-start.3 = (bf16[1024,1024]{1,0:T(8,128)(2,1)S(1)}, bf16[1024,1024]{1,0:T(8,128)(2,1)}, u32[]{:S(2)}) copy-start(bf16[1024,1024]{1,0:T(8,128)(2,1)} %wr.3) | copy-start | bytes 6291460
  12.6 12.3 %collective-permute-start = (bf16[8,24,1024]{2,1,0:T(8,128)(2,1)S(1)}, bf16[8,24,1024]{2,1,0:T(8,128)(2,1)S(1)}, u32[]{:S(2)}, u32[]{:S(2)}) collective-permute-start(bf16[8,24,1024]{2,1,0:T(8,128)(2,1)S(1)} %get-tuple-element.158), channel_id=1, source_target_pairs={{0,4},{4,8},{8,12},{1,5},{5,9},{9,13},{2,6},{6,10},{10,14},{3,7},{... | collective-permute-start | bytes 1179656 | tf_op jit(solution)/shard_map/ppermute | solution.py:883
  16.6 11.7 %collective-permute-start.1 = (bf16[8,24,1024]{2,1,0:T(8,128)(2,1)S(1)}, bf16[8,24,1024]{2,1,0:T(8,128)(2,1)}, u32[]{:S(2)}, u32[]{:S(2)}) collective-permute-start(bf16[8,24,1024]{2,1,0:T(8,128)(2,1)S(1)} %get-tuple-element.157), channel_id=1, source_target_pairs={{4,0},{8,4},{12,8},{5,1},{9,5},{13,9},{6,2},{10,6},{14,10},{7,3},{... | collective-permute-start | bytes 1179656 | tf_op jit(solution)/shard_map/ppermute | solution.py:884
  24.9 7.8 %copy-start.15 = (bf16[8,24,1024]{2,1,0:T(8,128)(2,1)}, bf16[8,24,1024]{2,1,0:T(8,128)(2,1)S(1)}, u32[]{:S(2)}) copy-start(bf16[8,24,1024]{2,1,0:T(8,128)(2,1)S(1)} %collective-permute-done.up_ref) | copy-start | bytes 1179652
  32.8 5.2 %copy-start.26 = (bf16[3,3,1024]{2,1,0:T(4,128)(2,1)S(1)}, bf16[3,3,1024]{2,1,0:T(4,128)(2,1)}, u32[]{:S(2)}) copy-start(bf16[3,3,1024]{2,1,0:T(4,128)(2,1)} %param.18) | copy-start | bytes 55300
  32.8 39.7 %all-to-all-start = ((bf16[4,288,1024]{2,1,0:T(8,128)(2,1)}), bf16[4,288,1024]{2,1,0:T(8,128)(2,1)S(1)}, u32[]{:S(2)}, u32[]{:S(2)}) async-start(bf16[4,288,1024]{2,1,0:T(8,128)(2,1)} %cotangent_by_image.1), calls=%async_computation | async-start | bytes 4718592 | tf_op jit(solution)/shard_map/all_to_all | solution.py:900
  37.9 196.9 %reduce-scatter.2.cloned.1.call-start = ((), (), s32[]{:S(2)}) async-start(), calls=%async_computation.5 | async-start | bytes 7077888 | tf_op jit(solution)/shard_map/reduce_scatter | solution.py:929
  39.1 42.5 %copy-start.27 = (bf16[3,3,1024]{2,1,0:T(4,128)(2,1)S(1)}, bf16[3,3,1024]{2,1,0:T(4,128)(2,1)}, u32[]{:S(2)}) copy-start(bf16[3,3,1024]{2,1,0:T(4,128)(2,1)} %param.22) | copy-start | bytes 55300
  72.5 36.6 %copy-start = (bf16[4,288,1024]{2,1,0:T(8,128)(2,1)}, bf16[4,288,1024]{2,1,0:T(8,128)(2,1)S(1)}, u32[]{:S(2)}) copy-start(bf16[4,288,1024]{2,1,0:T(8,128)(2,1)S(1)} %all-to-all-done.cot) | copy-start | bytes 7077892
  72.5 10.3 %collective-permute-start.2 = (bf16[72,1024]{1,0:T(8,128)(2,1)}, bf16[72,1024]{1,0:T(8,128)(2,1)S(1)}, u32[]{:S(2)}, u32[]{:S(2)}) collective-permute-start(bf16[72,1024]{1,0:T(8,128)(2,1)} %get-tuple-element.88), channel_id=1, source_target_pairs={{0,0},{1,4},{2,8},{3,12},{4,1},{5,5},{6,9},{7,13},{8,2},{9,6},{10,... | collective-permute-start | bytes 442376 | tf_op jit(solution)/shard_map/ppermute | solution.py:907
  74.2 23.0 %collective-permute-start.3 = (bf16[72,1024]{1,0:T(8,128)(2,1)}, bf16[72,1024]{1,0:T(8,128)(2,1)S(1)}, u32[]{:S(2)}, u32[]{:S(2)}) collective-permute-start(bf16[72,1024]{1,0:T(8,128)(2,1)} %get-tuple-element.89), channel_id=1, source_target_pairs={{0,1},{1,5},{2,9},{3,13},{4,2},{5,6},{6,10},{7,14},{8,3},{9,7},{10... | collective-permute-start | bytes 442376 | tf_op jit(solution)/shard_map/ppermute | solution.py:907
  76.9 20.4 %collective-permute-start.4 = (bf16[72,1024]{1,0:T(8,128)(2,1)}, bf16[72,1024]{1,0:T(8,128)(2,1)S(1)}, u32[]{:S(2)}, u32[]{:S(2)}) collective-permute-start(bf16[72,1024]{1,0:T(8,128)(2,1)} %get-tuple-element.90), channel_id=1, source_target_pairs={{0,2},{1,6},{2,10},{3,14},{4,3},{5,7},{6,11},{7,15},{8,0},{9,4},{1... | collective-permute-start | bytes 442376 | tf_op jit(solution)/shard_map/ppermute | solution.py:907
  80.0 17.3 %collective-permute-start.5 = (bf16[72,1024]{1,0:T(8,128)(2,1)}, bf16[72,1024]{1,0:T(8,128)(2,1)S(1)}, u32[]{:S(2)}, u32[]{:S(2)}) collective-permute-start(bf16[72,1024]{1,0:T(8,128)(2,1)} %get-tuple-element.91), channel_id=1, source_target_pairs={{0,3},{1,7},{2,11},{3,15},{4,0},{5,4},{6,8},{7,12},{8,1},{9,5},{10... | collective-permute-start | bytes 442376 | tf_op jit(solution)/shard_map/ppermute | solution.py:907
  82.8 14.5 %copy-start.20 = (bf16[72,1024]{1,0:T(8,128)(2,1)}, bf16[72,1024]{1,0:T(8,128)(2,1)S(1)}, u32[]{:S(2)}) copy-start(bf16[72,1024]{1,0:T(8,128)(2,1)S(1)} %collective-permute-done.2.refs_0_) | copy-start | bytes 442372
  97.3 0.7 copy-start.21
  97.3 0.7 copy-start.22
  97.3 0.8 copy-start.23
  109.1 38.6 %collective-permute-start.6 = (bf16[288,1024]{1,0:T(8,128)(2,1)}, bf16[288,1024]{1,0:T(8,128)(2,1)S(1)}, u32[]{:S(2)}, u32[]{:S(2)}) collective-permute-start(bf16[288,1024]{1,0:T(8,128)(2,1)} %get-tuple-element.105.low_ref.refs_0_), channel_id=1, source_target_pairs={{0,1},{1,2},{2,3},{3,0},{4,5},{5,6},{6,7},{7,4},{8,9},{9,10},{10,1... | collective-permute-start | bytes 1769480 | tf_op jit(solution)/shard_map/ppermute | solution.py:911
  113.4 34.9 %collective-permute-start.7 = (bf16[288,1024]{1,0:T(8,128)(2,1)}, bf16[288,1024]{1,0:T(8,128)(2,1)S(1)}, u32[]{:S(2)}, u32[]{:S(2)}) collective-permute-start(bf16[288,1024]{1,0:T(8,128)(2,1)} %get-tuple-element.105.low_ref.refs_0_), channel_id=1, source_target_pairs={{0,2},{1,3},{2,0},{3,1},{4,6},{5,7},{6,4},{7,5},{8,10},{9,11},{10,... | collective-permute-start | bytes 1769480 | tf_op jit(solution)/shard_map/ppermute | solution.py:911
  118.1 32.0 %collective-permute-start.8 = (bf16[288,1024]{1,0:T(8,128)(2,1)}, bf16[288,1024]{1,0:T(8,128)(2,1)S(1)}, u32[]{:S(2)}, u32[]{:S(2)}) collective-permute-start(bf16[288,1024]{1,0:T(8,128)(2,1)} %get-tuple-element.105.low_ref.refs_0_), channel_id=1, source_target_pairs={{0,3},{1,0},{2,1},{3,2},{4,7},{5,4},{6,5},{7,6},{8,11},{9,8},{10,9... | collective-permute-start | bytes 1769480 | tf_op jit(solution)/shard_map/ppermute | solution.py:911
  143.2 13.3 %collective-permute-start.9 = (bf16[72,1024]{1,0:T(8,128)(2,1)}, bf16[72,1024]{1,0:T(8,128)(2,1)S(1)}, u32[]{:S(2)}, u32[]{:S(2)}) collective-permute-start(bf16[72,1024]{1,0:T(8,128)(2,1)} %get-tuple-element.103), channel_id=1, source_target_pairs={{0,0},{4,1},{8,2},{12,3},{1,4},{5,5},{9,6},{13,7},{2,8},{6,9},{10,... | collective-permute-start | bytes 442376 | tf_op jit(solution)/shard_map/ppermute | solution.py:917
  144.7 11.7 %collective-permute-start.10 = (bf16[72,1024]{1,0:T(8,128)(2,1)}, bf16[72,1024]{1,0:T(8,128)(2,1)S(1)}, u32[]{:S(2)}, u32[]{:S(2)}) collective-permute-start(bf16[72,1024]{1,0:T(8,128)(2,1)} %get-tuple-element.104), channel_id=1, source_target_pairs={{1,0},{5,1},{9,2},{13,3},{2,4},{6,5},{10,6},{14,7},{3,8},{7,9},{11... | collective-permute-start | bytes 442376 | tf_op jit(solution)/shard_map/ppermute | solution.py:917
  147.7 8.7 %copy-start.8 = (bf16[288,1024]{1,0:T(8,128)(2,1)}, bf16[288,1024]{1,0:T(8,128)(2,1)S(1)}, u32[]{:S(2)}) copy-start(bf16[288,1024]{1,0:T(8,128)(2,1)S(1)} %collective-permute-done.6.refs_1_) | copy-start | bytes 1769476
  147.7 19.5 %collective-permute-start.11 = (bf16[72,1024]{1,0:T(8,128)(2,1)}, bf16[72,1024]{1,0:T(8,128)(2,1)S(1)}, u32[]{:S(2)}, u32[]{:S(2)}) collective-permute-start(bf16[72,1024]{1,0:T(8,128)(2,1)} %get-tuple-element.110), channel_id=1, source_target_pairs={{2,0},{6,1},{10,2},{14,3},{3,4},{7,5},{11,6},{15,7},{0,8},{4,9},{8... | collective-permute-start | bytes 442376 | tf_op jit(solution)/shard_map/ppermute | solution.py:917
  148.3 8.1 %copy-start.9 = (bf16[288,1024]{1,0:T(8,128)(2,1)}, bf16[288,1024]{1,0:T(8,128)(2,1)S(1)}, u32[]{:S(2)}) copy-start(bf16[288,1024]{1,0:T(8,128)(2,1)S(1)} %collective-permute-done.7.refs_2_) | copy-start | bytes 1769476
  148.3 19.0 %collective-permute-start.12 = (bf16[72,1024]{1,0:T(8,128)(2,1)}, bf16[72,1024]{1,0:T(8,128)(2,1)S(1)}, u32[]{:S(2)}, u32[]{:S(2)}) collective-permute-start(bf16[72,1024]{1,0:T(8,128)(2,1)} %get-tuple-element.111), channel_id=1, source_target_pairs={{3,0},{7,1},{11,2},{15,3},{0,4},{4,5},{8,6},{12,7},{1,8},{5,9},{9,... | collective-permute-start | bytes 442376 | tf_op jit(solution)/shard_map/ppermute | solution.py:917
  150.1 6.3 %copy-start.10 = (bf16[288,1024]{1,0:T(8,128)(2,1)}, bf16[288,1024]{1,0:T(8,128)(2,1)S(1)}, u32[]{:S(2)}) copy-start(bf16[288,1024]{1,0:T(8,128)(2,1)S(1)} %collective-permute-done.8.refs_3_) | copy-start | bytes 1769476
  156.4 10.8 %copy-start.11 = (bf16[72,1024]{1,0:T(8,128)(2,1)}, bf16[72,1024]{1,0:T(8,128)(2,1)S(1)}, u32[]{:S(2)}) copy-start(bf16[72,1024]{1,0:T(8,128)(2,1)S(1)} %collective-permute-done.9.refs_0_) | copy-start | bytes 442372
  156.5 10.8 %copy-start.12 = (bf16[72,1024]{1,0:T(8,128)(2,1)}, bf16[72,1024]{1,0:T(8,128)(2,1)S(1)}, u32[]{:S(2)}) copy-start(bf16[72,1024]{1,0:T(8,128)(2,1)S(1)} %collective-permute-done.10.refs_1_) | copy-start | bytes 442372
  167.3 6.8 %copy-start.13 = (bf16[72,1024]{1,0:T(8,128)(2,1)}, bf16[72,1024]{1,0:T(8,128)(2,1)S(1)}, u32[]{:S(2)}) copy-start(bf16[72,1024]{1,0:T(8,128)(2,1)S(1)} %collective-permute-done.11.refs_2_) | copy-start | bytes 442372
  167.3 6.8 %copy-start.14 = (bf16[72,1024]{1,0:T(8,128)(2,1)}, bf16[72,1024]{1,0:T(8,128)(2,1)S(1)}, u32[]{:S(2)}) copy-start(bf16[72,1024]{1,0:T(8,128)(2,1)S(1)} %collective-permute-done.12.refs_3_) | copy-start | bytes 442372
  174.1 27.8 %copy-start.28 = (bf16[8,144,1024]{2,1,0:T(8,128)(2,1)S(1)}, bf16[8,144,1024]{2,1,0:T(8,128)(2,1)}, u32[]{:S(2)}) copy-start(bf16[8,144,1024]{2,1,0:T(8,128)(2,1)} %get-tuple-element.125) | copy-start | bytes 7077892
  195.7 15.3 %collective-permute-start.13 = (bf16[8,24,1024]{2,1,0:T(8,128)(2,1)}, bf16[8,24,1024]{2,1,0:T(8,128)(2,1)S(1)}, u32[]{:S(2)}, u32[]{:S(2)}) collective-permute-start(bf16[8,24,1024]{2,1,0:T(8,128)(2,1)} %get-tuple-element.124), channel_id=1, source_target_pairs={{0,4},{4,8},{8,12},{1,5},{5,9},{9,13},{2,6},{6,10},{10,14},{3,7},{... | collective-permute-start | bytes 1179656 | tf_op jit(solution)/shard_map/ppermute | solution.py:934
  200.6 10.4 %collective-permute-start.14 = (bf16[8,24,1024]{2,1,0:T(8,128)(2,1)}, bf16[8,24,1024]{2,1,0:T(8,128)(2,1)S(1)}, u32[]{:S(2)}, u32[]{:S(2)}) collective-permute-start(bf16[8,24,1024]{2,1,0:T(8,128)(2,1)} %get-tuple-element.128), channel_id=1, source_target_pairs={{4,0},{8,4},{12,8},{5,1},{9,5},{13,9},{6,2},{10,6},{14,10},{7,3},{... | collective-permute-start | bytes 1179656 | tf_op jit(solution)/shard_map/ppermute | solution.py:935
  206.8 17.8 %copy-start.4 = (bf16[1024,1024]{1,0:T(8,128)(2,1)}, bf16[1024,1024]{1,0:T(8,128)(2,1)S(1)}, u32[]{:S(2)}) copy-start(bf16[1024,1024]{1,0:T(8,128)(2,1)S(1)} %bitcast_convert_fusion.refs_1_) | copy-start | bytes 6291460
  207.9 18.5 %copy-start.6 = (bf16[8,6,24,1024]{3,2,1,0:T(8,128)(2,1)S(1)}, bf16[8,6,24,1024]{3,2,1,0:T(8,128)(2,1)}, u32[]{:S(2)}) copy-start(bf16[8,6,24,1024]{3,2,1,0:T(8,128)(2,1)} %feat.1) | copy-start | bytes 7077892
  207.9 33.6 %collective-permute-start.16 = (bf16[512,1024]{1,0:T(8,128)(2,1)}, bf16[512,1024]{1,0:T(8,128)(2,1)}, u32[]{:S(2)}, u32[]{:S(2)}) collective-permute-start(bf16[512,1024]{1,0:T(8,128)(2,1)} %dynamic-slice_bitcast_fusion), channel_id=1, source_target_pairs={{0,16},{16,0},{1,17},{17,1},{2,18},{18,2},{3,19},{19,3},{4,20},{20... | collective-permute-start | bytes 3145736 | tf_op jit(solution)/shard_map/ppermute | solution.py:670
  211.0 0.7 copy-start.16
  211.7 0.7 copy-start.17
  231.3 5.7 %copy-start.5 = (bf16[1024,1024]{1,0:T(8,128)(2,1)}, bf16[1024,1024]{1,0:T(8,128)(2,1)S(1)}, u32[]{:S(2)}) copy-start(bf16[1024,1024]{1,0:T(8,128)(2,1)S(1)} %convolution_convert_fusion.refs_0_) | copy-start | bytes 6291460
  231.3 9.6 %copy-start.18 = (f32[160,128]{1,0:T(8,128)S(1)}, f32[160,128]{1,0:T(8,128)}, u32[]{:S(2)}) copy-start(f32[160,128]{1,0:T(8,128)} %small_rows.1.refs_4_) | copy-start | bytes 245764
  232.3 9.2 %collective-permute-start.15 = (bf16[512,1024]{1,0:T(8,128)(2,1)}, bf16[512,1024]{1,0:T(8,128)(2,1)}, u32[]{:S(2)}, u32[]{:S(2)}) collective-permute-start(bf16[512,1024]{1,0:T(8,128)(2,1)} %dynamic-slice_bitcast_fusion.1), channel_id=1, source_target_pairs={{0,16},{16,0},{1,17},{17,1},{2,18},{18,2},{3,19},{19,3},{4,20},{20... | collective-permute-start | bytes 3145736 | tf_op jit(solution)/shard_map/ppermute | solution.py:670
  236.9 16.6 %all-to-all-start.2 = ((bf16[16,8,3072]{2,1,0:T(8,128)(2,1)}), bf16[16,8,3072]{2,1,0:T(8,128)(2,1)S(1)}, u32[]{:S(2)}, u32[]{:S(2)}) async-start(bf16[16,8,3072]{2,1,0:T(8,128)(2,1)} %bitcast.66), calls=%async_computation.3 | async-start | bytes 1572864 | tf_op jit(solution)/shard_map/all_to_all | solution.py:948
  240.9 1.5 collective-permute-start.17
  242.4 0.6 copy-start.25
  253.5 16.4 %copy-start.7 = (bf16[16,8,3072]{2,1,0:T(8,128)(2,1)}, bf16[16,8,3072]{2,1,0:T(8,128)(2,1)S(1)}, u32[]{:S(2)}) copy-start(bf16[16,8,3072]{2,1,0:T(8,128)(2,1)S(1)} %all-to-all-done.2.x) | copy-start | bytes 2359300
  253.5 35.5 %all-to-all-start.1 = ((bf16[64,8,2176]{2,1,0:T(8,128)(2,1)}), bf16[64,8,2176]{2,1,0:T(8,128)(2,1)S(1)}, u32[]{:S(2)}, u32[]{:S(2)}) async-start(bf16[64,8,2176]{2,1,0:T(8,128)(2,1)} %bitcast.60), calls=%async_computation.2 | async-start | bytes 4456448 | tf_op jit(solution)/shard_map/all_to_all | solution.py:950
  289.1 1.4 copy-start.2
  294.9 37.3 %all-to-all-start.3 = ((bf16[64,8,2176]{2,1,0:T(8,128)(2,1)}), bf16[64,8,2176]{2,1,0:T(8,128)(2,1)S(1)}, u32[]{:S(2)}, u32[]{:S(2)}) async-start(bf16[64,8,2176]{2,1,0:T(8,128)(2,1)} %sum_and_copy.1), calls=%async_computation.4 | async-start | bytes 4456448 | tf_op jit(solution)/shard_map/all_to_all | solution.py:956
  303.1 54.2 %all-gather.7.cloned.1.call-start = ((), (), s32[]{:S(2)}) async-start(), calls=%async_computation.7 | async-start | bytes 1671168 | tf_op jit(solution)/shard_map/all_gather | solution.py:957
  332.1 26.8 %copy-start.1 = (bf16[64,8,2176]{2,1,0:T(8,128)(2,1)}, bf16[64,8,2176]{2,1,0:T(8,128)(2,1)S(1)}, u32[]{:S(2)}) copy-start(bf16[64,8,2176]{2,1,0:T(8,128)(2,1)S(1)} %all-to-all-done.3) | copy-start | bytes 6684676
  332.2 34.8 %collective-permute-start.18 = (bf16[512,2176]{1,0:T(8,128)(2,1)S(1)}, bf16[512,2176]{1,0:T(8,128)(2,1)}, u32[]{:S(2)}, u32[]{:S(2)}) collective-permute-start(bf16[512,2176]{1,0:T(8,128)(2,1)S(1)} %bitcast.58), channel_id=1, source_target_pairs={{0,16},{16,0},{1,17},{17,1},{2,18},{18,2},{3,19},{19,3},{4,20},{20... | collective-permute-start | bytes 6684680 | tf_op jit(solution)/shard_map/ppermute | solution.py:670
  357.3 17.4 %collective-permute-start.19 = (bf16[4,32,6144]{2,1,0:T(8,128)(2,1)}, bf16[4,32,6144]{2,1,0:T(8,128)(2,1)}, u32[]{:S(2)}, u32[]{:S(2)}) collective-permute-start(bf16[4,32,6144]{2,1,0:T(8,128)(2,1)} %bitcast.69), channel_id=1, source_target_pairs={{0,16},{16,0},{1,17},{17,1},{2,18},{18,2},{3,19},{19,3},{4,20},{20... | collective-permute-start | bytes 4718600 | tf_op jit(solution)/shard_map/ppermute | solution.py:670
  367.0 4.2 %copy-start.19 = (f32[512,128]{1,0:T(8,128)S(1)}, f32[512,128]{1,0:T(8,128)}, u32[]{:S(2)}) copy-start(f32[512,128]{1,0:T(8,128)} %get-tuple-element.143) | copy-start | bytes 786436
Sparse Core Ops, SparseCore 0:
  11.5 43.4 all-gather.4
  174.2 45.4 reduce-scatter.1
  306.7 50.5 all-gather.6
